TPU v7x, 128 devices: a whole 4x4x4 slice. The times are simulated.
128 devices in a mesh: seq: 32 (over x, y, z_hi), tp: 4 (over z_lo, core).
Axes of the slice: x: 4, y: 4, z: 4 (z_hi: 2, z_lo: 2; z = z_hi * 2 + z_lo), core: 2. Of those that a mesh axis runs over, the one named last changes fastest.
Arguments:
- layer_in: bfloat16 [8192, 4096], P('seq'), may hold values from -24 to 24
- w_value: bfloat16 [4096, 4096], P(None, 'tp'), may hold values from -0.09375 to 0.09375
- short_taps: float32 [7, 4096], P(None, 'tp'), may hold values from -2 to 2
- long_filters: float32 [2, 4096, 8192], P(None, ('tp', 'seq')), may hold values from -0.046875 to 0.046875
- gate_proj: bfloat16 [8192, 4096], P('seq', 'tp'), may hold values from -6 to 6
- grad_out: bfloat16 [8192, 4096], P('seq', 'tp'), may hold values from -8 to 8
Outputs:
- grad_input: bfloat16 [8192, 4096], P('seq', 'tp')
- grad_weight: float32 [4096, 4096], P('seq', 'tp')
- grad_taps: float32 [7, 4096], P(None, 'tp')
- grad_filters: float32 [2, 4096, 8192], P(None, ('tp', 'seq'))
- grad_gate: bfloat16 [8192, 4096], P('seq', 'tp')
All inputs are finite; a program needn't handle non-finite values.
Results may differ from a plain program's by a relative error of at most 0.0062.
Values may be sent and summed in bfloat16 or wider, within the bound.
No kernel may reach another device: no remote copies, remote signals or barrier semaphores. Data moves between devices by JAX's collectives and lax.ppermute only.
A program may use at most 128 MiB of HBM per device.

v0:
```python
import math

import jax
import jax.numpy as jnp
from jax import lax
from jax.sharding import PartitionSpec as P

highest = lax.Precision.HIGHEST


def settle(value):
    return lax.optimization_barrier(value).astype(jnp.float32)


def silu_slope(value):
    sig_part = jax.nn.sigmoid(value)
    return sig_part * (1.0 + value * (1.0 - sig_part))


def angles(height, breadth, modulus):
    products = (
        lax.broadcasted_iota(jnp.int32, (height, breadth), 0)
        * lax.broadcasted_iota(jnp.int32, (height, breadth), 1)
        % modulus
    )
    return -2.0 * math.pi / modulus * products.astype(jnp.float32)


def dft_tables(fft_length):
    inner_len = 128
    outer_len = fft_length // inner_len
    first_angle = angles(outer_len, outer_len, outer_len)
    second_angle = angles(inner_len, inner_len, inner_len)
    twist_angle = angles(outer_len, inner_len, fft_length)
    return (
        jnp.cos(first_angle),
        jnp.sin(first_angle),
        jnp.cos(second_angle),
        jnp.sin(second_angle),
        jnp.cos(twist_angle),
        jnp.sin(twist_angle),
    )


def mult(form, left, right):
    return jnp.einsum(form, left, right, precision=highest)


def forward_real(signal, tables):
    cos_first, sin_first, cos_second, sin_second, cos_twist, sin_twist = tables
    channels = signal.shape[0]
    blocks = signal.reshape(channels, cos_first.shape[0], cos_second.shape[0])
    section_re = mult("kn,cnm->ckm", cos_first, blocks)
    section_im = mult("kn,cnm->ckm", sin_first, blocks)
    turned_re = section_re * cos_twist - section_im * sin_twist
    turned_im = section_re * sin_twist + section_im * cos_twist
    spec_re = mult("ckm,mj->ckj", turned_re, cos_second) - mult(
        "ckm,mj->ckj", turned_im, sin_second
    )
    spec_im = mult("ckm,mj->ckj", turned_re, sin_second) + mult(
        "ckm,mj->ckj", turned_im, cos_second
    )
    return (spec_re, spec_im)


def inverse_steps(spec_re, spec_im, tables):
    cos_first, sin_first, cos_second, sin_second, cos_twist, sin_twist = tables
    section_re = mult("ckj,jm->ckm", spec_re, cos_second) + mult("ckj,jm->ckm", spec_im, sin_second)
    section_im = mult("ckj,jm->ckm", spec_im, cos_second) - mult("ckj,jm->ckm", spec_re, sin_second)
    turned_re = section_re * cos_twist + section_im * sin_twist
    turned_im = section_im * cos_twist - section_re * sin_twist
    return (turned_re, turned_im)


def inverse_complex(spec_re, spec_im, tables):
    cos_first, sin_first = (tables[0], tables[1])
    turned_re, turned_im = inverse_steps(spec_re, spec_im, tables)
    channels = spec_re.shape[0]
    fft_length = spec_re.shape[1] * spec_re.shape[2]
    out_re = mult("nk,ckm->cnm", cos_first, turned_re) + mult("nk,ckm->cnm", sin_first, turned_im)
    out_im = mult("nk,ckm->cnm", cos_first, turned_im) - mult("nk,ckm->cnm", sin_first, turned_re)
    return (
        out_re.reshape(channels, fft_length) / fft_length,
        out_im.reshape(channels, fft_length) / fft_length,
    )


def inverse_real(spec_re, spec_im, tables):
    cos_first, sin_first = (tables[0], tables[1])
    turned_re, turned_im = inverse_steps(spec_re, spec_im, tables)
    channels = spec_re.shape[0]
    fft_length = spec_re.shape[1] * spec_re.shape[2]
    out_re = mult("nk,ckm->cnm", cos_first, turned_re) + mult("nk,ckm->cnm", sin_first, turned_im)
    return out_re.reshape(channels, fft_length) / fft_length


def wrap_kernel(filters):
    forward = filters[0]
    backward = filters[1]
    lead_tap = forward[:, :1] + backward[:, :1]
    zero_col = jnp.zeros_like(lead_tap)
    return jnp.concatenate(
        [lead_tap, forward[:, 1:], zero_col, jnp.flip(backward[:, 1:], axis=1)], axis=1
    )


def mixer_core(short_conv, slope_in, filters):
    length = short_conv.shape[1]
    fft_length = 2 * length
    tables = dft_tables(fft_length)
    pooled = jnp.sum(jax.nn.silu(short_conv), axis=1) / length
    mean_grad = jnp.sum(slope_in, axis=1)
    zero_pad = jnp.zeros_like(short_conv)
    short_re, short_im = forward_real(jnp.concatenate([short_conv, zero_pad], axis=1), tables)
    grads_re, grads_im = forward_real(jnp.concatenate([slope_in, zero_pad], axis=1), tables)
    kernel_re, kernel_im = forward_real(wrap_kernel(filters), tables)
    joint_re = (
        short_re * kernel_re - short_im * kernel_im - (kernel_re * grads_im - kernel_im * grads_re)
    )
    joint_im = (
        short_re * kernel_im + short_im * kernel_re + (kernel_re * grads_re + kernel_im * grads_im)
    )
    out_re, out_im = inverse_complex(joint_re, joint_im, tables)
    lag_grads = inverse_real(
        short_re * grads_re + short_im * grads_im, short_re * grads_im - short_im * grads_re, tables
    )
    mixed_out = (out_re[:, :length] + pooled[:, None]).astype(jnp.bfloat16)
    slope_back = (
        out_im[:, :length] + (mean_grad / length)[:, None] * silu_slope(short_conv)
    ).astype(jnp.bfloat16)
    reverse_part = jnp.concatenate(
        [lag_grads[:, :1], jnp.flip(lag_grads[:, length + 1 :], axis=1)], axis=1
    )
    grad_filters = jnp.stack([lag_grads[:, :length], reverse_part])
    return (mixed_out, slope_back, grad_filters)


def local(layer_in, w_value, short_taps, long_filters, gate_proj, grad_out):
    values = jnp.dot(layer_in, w_value, preferred_element_type=jnp.float32).astype(jnp.bfloat16)
    tap_count = short_taps.shape[0]
    tap_reach = tap_count // 2
    own_values, own_gate, own_grads = (
        lax.all_to_all(values.T, "seq", split_axis=0, concat_axis=1, tiled=True),
        lax.all_to_all(gate_proj.T, "seq", split_axis=0, concat_axis=1, tiled=True),
        lax.all_to_all(grad_out.T, "seq", split_axis=0, concat_axis=1, tiled=True),
    )
    own_width = own_values.shape[0]
    length = own_values.shape[1]
    own_taps = lax.dynamic_slice_in_dim(short_taps, lax.axis_index("seq") * own_width, own_width, 1)
    value_pad = jnp.pad(own_values.astype(jnp.float32), ((0, 0), (tap_reach, tap_reach)))
    conv_sum = sum(
        (
            own_taps[offset][:, None] * value_pad[:, offset : offset + length]
            for offset in range(tap_count)
        )
    )
    short_conv = settle(conv_sum.astype(jnp.bfloat16))
    gate_sig = jax.nn.sigmoid(own_gate.astype(jnp.float32))
    slope_in = settle((own_grads.astype(jnp.float32) * gate_sig).astype(jnp.bfloat16))
    mixed_half, slope_half, grad_filters = mixer_core(short_conv, slope_in, long_filters)
    mixed_out = settle(mixed_half)
    slope_back = settle(slope_half)
    gate_back = (own_grads.astype(jnp.float32) * mixed_out * gate_sig * (1.0 - gate_sig)).astype(
        jnp.bfloat16
    )
    slope_pad = jnp.pad(slope_back, ((0, 0), (tap_reach, tap_reach)))
    value_back = sum(
        (
            own_taps[offset][:, None]
            * slope_pad[:, 2 * tap_reach - offset : 2 * tap_reach - offset + length]
            for offset in range(tap_count)
        )
    )
    value_back = value_back.astype(jnp.bfloat16)
    taps_part = jnp.stack(
        [
            jnp.sum(slope_back * value_pad[:, offset : offset + length], axis=1)
            for offset in range(tap_count)
        ]
    )
    grad_taps = lax.all_gather(taps_part, "seq", axis=1, tiled=True)
    back_values, back_gate = (
        lax.all_to_all(value_back, "seq", split_axis=1, concat_axis=0, tiled=True),
        lax.all_to_all(gate_back, "seq", split_axis=1, concat_axis=0, tiled=True),
    )
    grad_v = back_values.T
    grad_gate = back_gate.T
    input_term = lax.dot_general(
        grad_v, w_value, (((1,), (1,)), ((), ())), preferred_element_type=jnp.float32
    )
    grad_input = lax.psum_scatter(input_term, "tp", scatter_dimension=1, tiled=True).astype(
        jnp.bfloat16
    )
    grad_weight = lax.psum_scatter(
        lax.dot_general(
            layer_in, grad_v, (((0,), (0,)), ((), ())), preferred_element_type=jnp.float32
        ),
        "seq",
        scatter_dimension=0,
        tiled=True,
    )
    return (grad_input, grad_weight, grad_taps, grad_filters, grad_gate)


def solution(mesh):
    in_specs = (
        P("seq", None),
        P(None, "tp"),
        P(None, "tp"),
        P(None, ("tp", "seq"), None),
        P("seq", "tp"),
        P("seq", "tp"),
    )
    out_specs = (
        P("seq", "tp"),
        P("seq", "tp"),
        P(None, "tp"),
        P(None, ("tp", "seq"), None),
        P("seq", "tp"),
    )
    return jax.shard_map(local, mesh=mesh, in_specs=in_specs, out_specs=out_specs, check_vma=False)
```

profile of v0, /device:TPU:0, one launch (start us, length us, event | category | flops | bytes accessed | tf_op | source)
XLA Modules:
  0.0 674.3 jit_solution(11655589107655142125)
XLA Ops:
  9.4 10.8 %all-to-all-start.2 = ((bf16[32,32,256]{2,1,0:T(8,128)(2,1)}), bf16[32,32,256]{2,1,0:T(8,128)(2,1)}, u32[]{:S(2)}, u32[]{:S(2)}) async-start(bf16[32,32,256]{2,1,0:T(8,128)(2,1)} %bitcast.21), calls=%async_computation.2 | async-start | bytes 1048576 | tf_op jit(solution)/shard_map/all_to_all | solution.py:144
  24.1 21.7 %reverse = f32[32,8192]{1,0:T(8,128)} reverse(f32[32,8192]{1,0:T(8,128)S(1)} %bitcast.279), dimensions={1} | reverse | bytes 2097152
  45.8 2.7 slice.196
  48.5 4.0 concatenate.13
  54.4 5.0 fusion.72
  59.4 5.0 fusion.95
  64.6 6.0 fusion.44
  70.6 5.0 convolution_subtract_fusion.3
  75.7 6.6 convolution_convert_fusion
  82.2 5.0 fusion.46
  88.2 18.6 %convolution_add_fusion.4 = f32[32,128,128]{2,1,0:T(8,128)} fusion(f32[32,128,128]{2,1,0:T(8,128)} %fusion.46, f32[32,128,128]{2,1,0:T(8,128)} %fusion.72, f32[32,128,128]{2,1,0:T(8,128)} %fusion.95, f32[128,128]{0,1:T(8,128)S(1)} %copy.79, f32[128,128]{0,1:T(8,128)S(1)} %copy.77), kind=kOutput, calls=%fused_computation.58 | convolution fusion | flops 807632896 | bytes 8519680 | tf_op jit(solution)/shard_map/ckm,mj->ckj/dot_general | solution.py:46
  106.8 9.8 %all-to-all-start.1 = ((bf16[32,32,256]{2,1,0:T(8,128)(2,1)}), bf16[32,32,256]{2,1,0:T(8,128)(2,1)}, u32[]{:S(2)}, u32[]{:S(2)}) async-start(bf16[32,32,256]{2,1,0:T(8,128)(2,1)} %bitcast.18), calls=%async_computation.1 | async-start | bytes 1048576 | tf_op jit(solution)/shard_map/all_to_all | solution.py:145
  118.9 10.8 %all-to-all-done.1 = bf16[32,32,256]{2,1,0:T(8,128)(2,1)} async-done(((bf16[32,32,256]{2,1,0:T(8,128)(2,1)}), bf16[32,32,256]{2,1,0:T(8,128)(2,1)}, u32[]{:S(2)}, u32[]{:S(2)}) %all-to-all-start.1) | async-done | bytes 524320 | tf_op jit(solution)/shard_map/all_to_all | solution.py:145
  129.7 4.6 all-to-all-start
  137.1 5.0 fusion.67
  142.3 5.0 fusion.90
  151.5 4.0 fusion.75
  155.5 3.7 fusion.98
  159.2 3.8 fusion.38
  163.0 3.9 fusion.40
  166.9 3.8 fusion.50
  170.7 3.7 fusion.52
  174.4 4.0 convolution_subtract_fusion.4
  178.4 3.8 convolution_add_fusion.2
  182.2 3.8 convolution_subtract_fusion.2
  186.1 6.9 %multiply_subtract_fusion = (f32[32,128,128]{2,1,0:T(8,128)}, f32[32,128,128]{2,1,0:T(8,128)}, f32[32,128,128]{2,1,0:T(8,128)S(1)}, f32[32,128,128]{2,1,0:T(8,128)S(1)}) fusion(f32[32,128,128]{2,1,0:T(8,128)S(1)} %convolution_subtract_fusion.2, f32[32,128,128]{2,1,0:T(8,128)S(1)} %convolution_subtract_fusion.4, ...), kind=kOutput, calls=%fused_computation.33 | convolution fusion | flops 818118656 | bytes 25296896 | tf_op jit(solution)/shard_map/ckm,mj->ckj/dot_general | solution.py:46
  195.3 2.3 fusion.86
  204.4 3.8 multiply_bitcast_fusion.2
  208.1 2.9 copy.104
  211.1 2.9 copy.160
  215.2 3.7 fusion.27
  218.9 21.7 %all_to_all.77 = bf16[32,32,256]{2,0,1:T(8,128)(2,1)S(1)} all-to-all(bf16[32,32,256]{2,0,1:T(8,128)(2,1)S(1)} %bitcast.285), channel_id=1, replica_groups=mesh['seq'=32,'tp'=4] {'seq'}, dimensions={1} | all-to-all | bytes 1048576 | tf_op jit(solution)/shard_map/all_to_all | solution.py:183
  241.4 7.7 %fusion.271 = f32[256,4096]{1,0:T(8,128)} fusion(bf16[1024,256]{1,0:T(8,128)(2,1)S(1)} %bitcast.281, bf16[4096,1024]{1,0:T(8,128)(2,1)} %param.7), kind=kOutput, calls=%fused_computation.311 | convolution fusion | flops 2147483648 | bytes 13107200 | tf_op jit(solution)/shard_map/dot_general | solution.py:188
  249.4 9.7 %convolution_bitcast_fusion = f32[4096,1024]{0,1:T(8,128)} fusion(bf16[1024,256]{1,0:T(8,128)(2,1)} %bitcast.282, bf16[256,4096]{1,0:T(8,128)(2,1)S(1)} %copy-done), kind=kOutput, calls=%fused_computation | convolution fusion | flops 2147483648 | bytes 19398656 | tf_op jit(solution)/shard_map/dot_general | solution.py:195
  259.2 4.0 fusion.79
  270.0 2.5 fusion.6
  272.5 3.5 multiply_bitcast_fusion.1
  276.0 2.9 copy.111
  279.0 2.8 copy.159
  284.5 30.5 %reverse.1 = f32[32,8192]{1,0:T(8,128)} reverse(f32[32,8192]{1,0:T(8,128)} %bitcast.280), dimensions={1} | reverse | bytes 2097152
  315.0 2.8 slice.197
  317.8 3.9 fusion.35
  321.8 3.6 multiply_bitcast_fusion
  325.3 2.9 copy.112
  328.3 2.9 copy.158
  332.4 4.6 all-to-all-start.4
  337.1 96.6 %all-gather = f32[32,32,7]{1,2,0:T(8,128)S(1)} all-gather(f32[1,32,7]{1,2,0:T(8,128)S(1)} %bitcast.289), channel_id=1, replica_groups=mesh['seq'=32,'tp'=4] {'seq'}, dimensions={0}, use_global_device_ids=true | all-gather | bytes 29568 | tf_op jit(solution)/shard_map/all_gather | solution.py:181
  441.6 223.3 %reduce-scatter.5.cloned.1.call-done = f32[128,1024]{0,1:T(8,128)} async-done(((f32[4096,1024]{0,1:T(8,128)}), f32[128,1024]{0,1:T(8,128)}) %reduce-scatter.5.cloned.1.call-update) | async-done | bytes 524304 | tf_op jit(solution)/shard_map/reduce_scatter | solution.py:194
  (110 shorter events, 50.6 us)
Async XLA Ops:
  7.2 68.5 %copy-start = (bf16[256,4096]{1,0:T(8,128)(2,1)S(1)}, bf16[256,4096]{1,0:T(8,128)(2,1)}, u32[]{:S(2)}) copy-start(bf16[256,4096]{1,0:T(8,128)(2,1)} %param.6) | copy-start | bytes 6291460
  9.4 97.5 %all-to-all-start.2 = ((bf16[32,32,256]{2,1,0:T(8,128)(2,1)}), bf16[32,32,256]{2,1,0:T(8,128)(2,1)}, u32[]{:S(2)}, u32[]{:S(2)}) async-start(bf16[32,32,256]{2,1,0:T(8,128)(2,1)} %bitcast.21), calls=%async_computation.2 | async-start | bytes 1048576 | tf_op jit(solution)/shard_map/all_to_all | solution.py:144
  45.8 2.7 copy-start.21
  64.6 6.0 copy-start.6
  64.6 6.0 copy-start.7
  82.2 5.0 copy-start.23
  106.8 22.8 %all-to-all-start.1 = ((bf16[32,32,256]{2,1,0:T(8,128)(2,1)}), bf16[32,32,256]{2,1,0:T(8,128)(2,1)}, u32[]{:S(2)}, u32[]{:S(2)}) async-start(bf16[32,32,256]{2,1,0:T(8,128)(2,1)} %bitcast.18), calls=%async_computation.1 | async-start | bytes 1048576 | tf_op jit(solution)/shard_map/all_to_all | solution.py:145
  129.7 17.6 %all-to-all-start = ((bf16[32,32,256]{2,1,0:T(8,128)(2,1)}), bf16[32,32,256]{2,1,0:T(8,128)(2,1)}, u32[]{:S(2)}, u32[]{:S(2)}) async-start(bf16[32,32,256]{2,1,0:T(8,128)(2,1)} %bitcast.287), calls=%async_computation | async-start | bytes 1048576 | tf_op jit(solution)/shard_map/all_to_all | solution.py:143
  134.3 305.3 %reduce-scatter.3.cloned.1.call-start = ((), (), s32[]{:S(2)}) async-start(), calls=%async_computation.7 | async-start | bytes 5242880 | tf_op jit(solution)/shard_map/reduce_scatter | solution.py:191
  135.6 1.0 copy-start.11
  148.5 2.0 copy-start.13
  150.3 0.8 copy-start.18
  163.0 3.9 copy-start.5
  163.0 3.9 copy-start.8
  182.2 3.8 copy-start.16
  182.2 3.8 copy-start.17
  199.9 4.5 copy-start.1
  202.2 2.2 copy-start.3
  211.1 2.9 copy-start.19
  213.9 1.2 copy-start.14
  240.6 0.8 copy-start.22
  249.1 415.8 %reduce-scatter.5.cloned.1.call-start = ((), (), s32[]{:S(2)}) async-start(), calls=%async_computation.8 | async-start | bytes 17301504 | tf_op jit(solution)/shard_map/reduce_scatter | solution.py:194
  259.1 4.0 copy-start.10
  265.4 2.3 copy-start.9
  281.8 1.3 copy-start.15
  315.0 2.8 copy-start.2
  317.8 4.0 copy-start.4
  328.3 3.0 copy-start.12
  331.5 102.9 %copy-start.20 = (f32[32,8191]{1,0:T(8,128)S(1)}, f32[32,8191]{1,0:T(8,128)}, u32[]{:S(2)}) copy-start(f32[32,8191]{1,0:T(8,128)} %slice.197) | copy-start | bytes 3145348
  332.4 105.1 %all-to-all-start.4 = ((bf16[32,32,256]{2,0,1:T(8,128)(2,1)}), bf16[32,32,256]{2,0,1:T(8,128)(2,1)}, u32[]{:S(2)}, u32[]{:S(2)}) async-start(bf16[32,32,256]{2,0,1:T(8,128)(2,1)} %bitcast.284), calls=%async_computation.6 | async-start | bytes 1048576 | tf_op jit(solution)/shard_map/all_to_all | solution.py:184
Sparse Core Ops, SparseCore 0:
  249.2 41.1 reduce-scatter.2
  293.0 371.9 reduce-scatter.4
where the time goes:
time: 687 us; the launch traced here: 674 us
  waiting for transfers between devices  234 us (34%)
  matrix products  159 us (23%)
  blocking collectives  118 us (17%)
  local copies, waits for them, and re-layouts  101 us (15%)
  starting transfers between devices  30.2 us (4%)
  other arithmetic  16.1 us (2%)
  between operations  15.1 us (2%)
    reduce_scatter x1, waiting for transfers between devices, local(): lax.psum_scatter(lax.dot_general(layer_in, grad_v, (((0,), (0,)), ((), ()...  223 us
    dot_general x32, matrix products, mult(): return jnp.einsum(form, left, right, precision=highest)  135 us
    all_gather x1, blocking collectives, local(): grad_taps = lax.all_gather(taps_part, 'seq', axis=1, tiled=True)  96.6 us
    unnamed x65, local copies, waits for them, and re-layouts  81.3 us
    all_to_all x1, blocking collectives, local(): lax.all_to_all(value_back, 'seq', split_axis=1, concat_axis=0, tiled=True)  21.7 us
  transfers between devices with their start and end apart: 6, of which 2 were waited for; matrix products, arithmetic and copies ran while one was open for 28% of the time, Pallas kernels for 0%

commit v1 on v0

v1 whole, which is shorter than its diff:
```python
import functools
import math

import jax
import jax.numpy as jnp
import ml_dtypes
import numpy as np
from jax import lax
from jax.experimental import pallas as pl
from jax.experimental.pallas import tpu as pltpu
from jax.sharding import PartitionSpec as P

LANES = 128
ROWS = 64
LENGTH = ROWS * LANES
TAPS = 7
REACH = TAPS // 2
BATCH = 4


def halves(table):
    high = table.astype(ml_dtypes.bfloat16)
    low = (table - high.astype(np.float64)).astype(ml_dtypes.bfloat16)
    return high, low


@functools.lru_cache(maxsize=None)
def tables(blocks):
    half = np.arange(ROWS) + 0.5
    natural = np.arange(ROWS)
    split = (2 * np.arange(blocks)[None, :] + np.arange(2)[:, None]).reshape(-1)

    def first(order):
        turn = 2.0 * math.pi / LANES * np.outer(half, order)
        return halves(np.concatenate([np.cos(turn), -np.sin(turn)], axis=0))

    def last(order):
        turn = 2.0 * math.pi / LANES * np.outer(order, half)
        return halves(np.concatenate([np.cos(turn), -np.sin(turn)], axis=1) / LENGTH)

    split_high, split_low = first(split)
    nat_high, nat_low = first(natural)
    first_split = np.concatenate([split_high, split_low], axis=1)
    first_nat = np.concatenate([nat_high, nat_low, nat_high, nat_low], axis=1)
    inv_split_high, inv_split_low = last(split)
    inv_nat_high, inv_nat_low = last(natural)
    last_split = np.concatenate([inv_split_high, inv_split_high, inv_split_low], axis=1)
    last_nat = np.concatenate([inv_nat_high, inv_nat_high, inv_nat_low], axis=1)
    twist = 2.0 * math.pi / (2 * LENGTH) * np.outer(half, np.arange(LANES))
    twist = np.stack([np.cos(twist), -np.sin(twist)]).astype(np.float32)
    grid = 2.0 * math.pi / LANES * np.outer(np.arange(LANES), np.arange(LANES))
    cos, sin = np.cos(grid), np.sin(grid)

    def stacked(table):
        high, low = halves(table)
        return np.concatenate([high, high, low], axis=0)

    forward = np.block([[cos, -sin], [sin, cos]])
    mirror = np.block([[cos, sin], [sin, -cos]])
    inverse = np.block([[cos, sin], [-sin, cos]])
    pair = np.concatenate([stacked(forward), stacked(mirror)], axis=0)
    both = np.concatenate([stacked(inverse), stacked(np.block([[cos, sin], [sin, -cos]]))], axis=1)
    return {
        "first_split": first_split, "first_nat": first_nat, "twist": twist, "forward": stacked(forward), "pair": pair,
        "inverse": stacked(inverse), "both": both, "last_split": last_split, "last_nat": last_nat,
    }


def cut(value):
    high = value.astype(jnp.bfloat16)
    low = (value - high.astype(jnp.float32)).astype(jnp.bfloat16)
    return high, low


def store_parts(ref, row, col, real, imag):
    real_high, real_low = cut(real)
    imag_high, imag_low = cut(imag)
    parts = (real_high, imag_high, real_low, imag_low, real_high, imag_high)
    for at, part in enumerate(parts):
        ref[row:row + ROWS, col + at * LANES:col + (at + 1) * LANES] = part


def shifted(early, late, step):
    if step == 0:
        return early, late
    lane = lax.broadcasted_iota(jnp.int32, early.shape, 1)
    row = lax.broadcasted_iota(jnp.int32, early.shape, 0)
    count = early.shape[0]
    turned_early = pltpu.roll(early, (-step) % LANES, 1)
    turned_late = pltpu.roll(late, (-step) % LANES, 1)
    if step > 0:
        keep = lane < LANES - step
        beyond = jnp.where(row == count - 1, 0.0, pltpu.roll(turned_early, count - 1, 0))
        return jnp.where(keep, turned_early, turned_late), jnp.where(keep, turned_late, beyond)
    keep = lane >= -step
    before = jnp.where(row == 0, 0.0, pltpu.roll(turned_late, 1, 0))
    return jnp.where(keep, turned_early, before), jnp.where(keep, turned_late, turned_early)


def dot(left, right):
    return jnp.dot(left, right, preferred_element_type=jnp.float32)


QUADS = [[4 * q + place for place in range(4)] for q in range(8)]
LEAGUES = [[4 * q + 2 * pair + z for q in range(8) for z in range(2)] for pair in range(2)]
PLANES = [[2 * j + z for j in range(16)] for z in range(2)]


def twisted(array, col, twist_ref):
    real = array[:ROWS, col * LANES:(col + 1) * LANES]
    imag = array[ROWS:, col * LANES:(col + 1) * LANES]
    return real * twist_ref[0] - imag * twist_ref[1], real * twist_ref[1] + imag * twist_ref[0]


def untwisted(array, twist_ref):
    real, imag = array[:, :LANES], array[:, LANES:]
    return jnp.concatenate(
        [real * twist_ref[0] + imag * twist_ref[1], imag * twist_ref[0] - real * twist_ref[1]], axis=0)


def finish(table_ref, one, two):
    high, low = cut(jnp.concatenate([one, two], axis=1))
    return dot(table_ref[...], jnp.concatenate([high, low, high], axis=0))


def spectra_kernel(filters_ref, first_nat_ref, twist_ref, pair_ref, out_ref, kernel_buf):
    for q in range(BATCH):
        at = (pl.program_id(0) % (8 // BATCH)) * BATCH + q
        plus = filters_ref[0, 0, pl.ds(at, ROWS, stride=8), :]
        minus = filters_ref[1, 0, pl.ds(at, ROWS, stride=8), :]
        high, low = cut(jnp.concatenate([plus, minus], axis=1))
        section = dot(first_nat_ref[...], jnp.concatenate([high, high, low, low], axis=0))
        store_parts(kernel_buf, q * ROWS, 0, *twisted(section, 0, twist_ref))
        store_parts(kernel_buf, q * ROWS, 6 * LANES, *twisted(section, 1, twist_ref))
    out_ref[...] = dot(kernel_buf[...], pair_ref[...])


def lag_kernel(lag_ref, twist_ref, both_ref, last_nat_ref, out_ref):
    parts = lag_ref[...]
    unmixed = dot(jnp.concatenate([parts, parts[:, :2 * LANES]], axis=1), both_ref[...])
    for q in range(BATCH):
        at = (pl.program_id(0) % (8 // BATCH)) * BATCH + q
        rows = slice(q * ROWS, (q + 1) * ROWS)
        pair = finish(last_nat_ref, untwisted(unmixed[rows, :2 * LANES], twist_ref),
                      untwisted(unmixed[rows, 2 * LANES:], twist_ref))
        out_ref[0, 0, pl.ds(at, ROWS, stride=8), :] = pair[:, :LANES]
        out_ref[1, 0, pl.ds(at, ROWS, stride=8), :] = pair[:, LANES:]


def mixer_kernel(
    taps_ref, arrived_ref, spectra_ref, first_split_ref, twist_ref, forward_ref, inverse_ref, last_split_ref,
    back_ref, lag_ref,
    values_buf, slopes_buf, back_buf, mixed_buf, taps_buf, extra_buf, signal_buf, product_buf,
):
    blocks, width = arrived_ref.shape[0], arrived_ref.shape[1] // 2
    step = pl.program_id(0)

    @pl.when(step == 0)
    def _():
        for h in range(2):
            part = slice(h * LANES, (h + 1) * LANES)
            values_buf[h] = arrived_ref[:, :width, part].astype(jnp.float32).reshape(blocks * width, LANES)
            slopes_buf[h] = arrived_ref[:, width:, part].astype(jnp.float32).reshape(blocks * width, LANES)

    pooled = []
    for q in range(BATCH):
        c = step * BATCH + q
        early = values_buf[0, pl.ds(c, blocks, stride=width), :]
        late = values_buf[1, pl.ds(c, blocks, stride=width), :]
        sum_early, sum_late = None, None
        for k in range(TAPS):
            one, two = shifted(early, late, k - REACH)
            tap = taps_ref[k, c]
            sum_early = tap * one if k == 0 else sum_early + tap * one
            sum_late = tap * two if k == 0 else sum_late + tap * two
        short = jnp.concatenate([sum_early, sum_late], axis=0).astype(jnp.bfloat16)
        conv = short.astype(jnp.float32)
        slope = jnp.concatenate(
            [slopes_buf[h, pl.ds(c, blocks, stride=width), :] for h in range(2)], axis=0)
        sig = jax.nn.sigmoid(conv)
        pooled.append(jnp.sum(conv * sig, keepdims=True) / LENGTH)
        mean_grad = jnp.sum(slope, keepdims=True) / LENGTH
        extra_buf[q] = mean_grad * (sig * (1.0 + conv * (1.0 - sig)))
        both = jnp.concatenate([short, slope.astype(jnp.bfloat16)], axis=1)
        section = dot(first_split_ref[...], jnp.concatenate([both, both], axis=0))
        store_parts(signal_buf, q * ROWS, 0, *twisted(section, 0, twist_ref))
        store_parts(signal_buf, (BATCH + q) * ROWS, 0, *twisted(section, 1, twist_ref))

    spec = dot(signal_buf[...], forward_ref[...])
    for q in range(BATCH):
        rows = slice(q * ROWS, (q + 1) * ROWS)
        slope_rows = slice((BATCH + q) * ROWS, (BATCH + q + 1) * ROWS)
        short_re, short_im = spec[rows, :LANES], spec[rows, LANES:]
        slope_re, slope_im = spec[slope_rows, :LANES], spec[slope_rows, LANES:]
        filt_re, filt_im = spectra_ref[rows, :LANES], spectra_ref[rows, LANES:]
        store_parts(product_buf, (2 * q) * ROWS, 0,
                    short_re * filt_re - short_im * filt_im, short_re * filt_im + short_im * filt_re)
        store_parts(product_buf, (2 * q + 1) * ROWS, 0,
                    slope_re * filt_re + slope_im * filt_im, slope_im * filt_re - slope_re * filt_im)
        real_high, real_low = cut(slope_re * short_re + slope_im * short_im)
        imag_high, imag_low = cut(slope_im * short_re - slope_re * short_im)
        for at, part in enumerate((real_high, imag_high, real_low, imag_low)):
            lag_ref[rows, at * LANES:(at + 1) * LANES] = part

    unmixed = dot(product_buf[...], inverse_ref[...])
    for q in range(BATCH):
        c = step * BATCH + q
        rows = 2 * q * ROWS
        long_pair = finish(last_split_ref, untwisted(unmixed[rows:rows + ROWS], twist_ref),
                           untwisted(unmixed[rows + ROWS:rows + 2 * ROWS], twist_ref))
        mixed = long_pair[:, :LANES] + pooled[q]
        slope_back = (long_pair[:, LANES:] + extra_buf[q]).astype(jnp.bfloat16).astype(jnp.float32)
        early = values_buf[0, pl.ds(c, blocks, stride=width), :]
        late = values_buf[1, pl.ds(c, blocks, stride=width), :]
        sum_early, sum_late = None, None
        for k in range(TAPS):
            one, two = shifted(slope_back[:blocks], slope_back[blocks:], REACH - k)
            tap = taps_ref[k, c]
            sum_early = tap * one if k == 0 else sum_early + tap * one
            sum_late = tap * two if k == 0 else sum_late + tap * two
            taps_buf[k, pl.ds(c, 1), :] = jnp.sum(one * early + two * late, axis=0, keepdims=True)
        for h, part in enumerate((sum_early, sum_late)):
            back_buf[h, pl.ds(c, blocks, stride=width), :] = part
            mixed_buf[h, pl.ds(c, blocks, stride=width), :] = mixed[h * blocks:(h + 1) * blocks]

    @pl.when(step == pl.num_programs(0) - 1)
    def _():
        for q in range(blocks // 4):
            for place in range(4):
                rows = slice((4 * q + place) * width, (4 * q + place + 1) * width)
                for h in range(2):
                    part = back_buf[h, rows, :].astype(jnp.bfloat16)
                    lanes = slice((2 * place + h) * LANES, (2 * place + h + 1) * LANES)
                    back_ref[2 * q, :, lanes] = part
                    back_ref[2 * q + 1, :, lanes] = part
                    at = 8 + 2 * (place // 2) + h
                    back_ref[2 * q + place % 2, :, at * LANES:(at + 1) * LANES] = (
                        mixed_buf[h, rows, :].astype(jnp.bfloat16))
        lane = lax.broadcasted_iota(jnp.int32, (width, LANES), 1)
        packed = jnp.zeros((width, LANES), jnp.float32)
        for k in range(TAPS):
            rest = jnp.sum(taps_buf[k], axis=1, keepdims=True)
            for p in range(3):
                piece = rest.astype(jnp.bfloat16).astype(jnp.float32)
                packed = jnp.where(lane == 8 * p + k, piece, packed)
                rest = rest - piece
        for d in range(blocks // 2):
            back_ref[d, :, 12 * LANES:] = packed.astype(jnp.bfloat16)


def whole(shape):
    return pl.BlockSpec(shape, lambda *_: (0,) * len(shape))


def call(kernel, name, flops, nbytes, vmem=16, **kwargs):
    return pl.pallas_call(
        kernel, name=name,
        compiler_params=pltpu.CompilerParams(
            dimension_semantics=("arbitrary",), vmem_limit_bytes=vmem * 1024 * 1024),
        cost_estimate=pl.CostEstimate(flops=flops, bytes_accessed=nbytes, transcendentals=0), **kwargs)


def tables_of(names, blocks=LENGTH // 256):
    chosen = [jnp.asarray(tables(blocks)[name]) for name in names]
    return chosen, [whole(table.shape) for table in chosen]


PER_TILE = pl.BlockSpec((2, 1, ROWS * 8, LANES), lambda i: (0, i // (8 // BATCH), 0, 0))


def spectra_of(filters):
    width = filters.shape[1]
    tiles = width // 8
    view = filters.reshape(2, tiles, 8, ROWS, LANES).transpose(0, 1, 3, 2, 4).reshape(2, tiles, ROWS * 8, LANES)
    consts, specs = tables_of(("first_nat", "twist", "pair"))
    return call(
        spectra_kernel, "spectra", 3_000_000_000, 5_000_000, vmem=56,
        grid=(width // BATCH,), in_specs=[PER_TILE] + specs,
        out_specs=pl.BlockSpec((BATCH * ROWS, 2 * LANES), lambda i: (i, 0)),
        out_shape=jax.ShapeDtypeStruct((width * ROWS, 2 * LANES), jnp.float32),
        scratch_shapes=[pltpu.VMEM((BATCH * ROWS, 12 * LANES), jnp.bfloat16)],
    )(view, *consts)


def filter_grads(lag):
    width = lag.shape[0] // ROWS
    tiles = width // 8
    consts, specs = tables_of(("twist", "both", "last_nat"))
    out = call(
        lag_kernel, "filter_grads", 3_000_000_000, 5_000_000,
        grid=(width // BATCH,),
        in_specs=[pl.BlockSpec((BATCH * ROWS, 4 * LANES), lambda i: (i, 0))] + specs,
        out_specs=PER_TILE,
        out_shape=jax.ShapeDtypeStruct((2, tiles, ROWS * 8, LANES), jnp.float32),
    )(lag, *consts)
    return out.reshape(2, tiles, ROWS, 8, LANES).transpose(0, 1, 3, 2, 4).reshape(2, width, LENGTH)


def mixer(own_taps, arrived, spectra):
    blocks, width, span = arrived.shape[0], arrived.shape[1] // 2, arrived.shape[2]
    consts, specs = tables_of(("first_split", "twist", "forward", "inverse", "last_split"))
    back_shape = (blocks // 2, width, 6 * span + LANES)
    rows = (2, blocks * width, LANES)
    return call(
        mixer_kernel, "mixer", 3_000_000_000, 8_000_000, vmem=56,
        grid=(width // BATCH,),
        in_specs=[pl.BlockSpec(memory_space=pltpu.SMEM), whole(arrived.shape),
                  pl.BlockSpec((BATCH * ROWS, 2 * LANES), lambda i: (i, 0))] + specs,
        out_specs=[whole(back_shape), pl.BlockSpec((BATCH * ROWS, 4 * LANES), lambda i: (i, 0))],
        out_shape=[
            jax.ShapeDtypeStruct(back_shape, jnp.bfloat16),
            jax.ShapeDtypeStruct((width * ROWS, 4 * LANES), jnp.bfloat16),
        ],
        scratch_shapes=[
            pltpu.VMEM(rows, jnp.float32),
            pltpu.VMEM(rows, jnp.float32),
            pltpu.VMEM(rows, jnp.float32),
            pltpu.VMEM(rows, jnp.float32),
            pltpu.VMEM((TAPS, width, LANES), jnp.float32),
            pltpu.VMEM((BATCH, ROWS, LANES), jnp.float32),
            pltpu.VMEM((2 * BATCH * ROWS, 6 * LANES), jnp.bfloat16),
            pltpu.VMEM((2 * BATCH * ROWS, 6 * LANES), jnp.bfloat16),
        ],
    )(own_taps, arrived, spectra, *consts)


STREAMS = 4


def send_kernel(rows_ref, *refs):
    weight_refs, (gate_ref, grad_ref, out_ref, total_ref) = refs[:STREAMS], refs[STREAMS:]
    blocks, width, span = out_ref.shape[0], out_ref.shape[1] // 2, out_ref.shape[2]
    step, steps = pl.program_id(0), pl.num_programs(0)
    count = blocks * gate_ref.shape[1] // total_ref.shape[1]
    sig = jax.nn.sigmoid(gate_ref[...].astype(jnp.float32))
    slopes = (grad_ref[...].astype(jnp.float32) * sig).T.astype(jnp.bfloat16)
    out_ref[pl.ds(step * count, count), width:, :] = slopes.reshape(count, width, span)
    part = weight_refs[0].shape[0]
    term = dot(rows_ref[:, :part], weight_refs[0][...])
    for j in range(1, STREAMS):
        term = term + dot(rows_ref[:, j * part:(j + 1) * part], weight_refs[j][...])

    @pl.when(step == 0)
    def _():
        total_ref[...] = term

    @pl.when((step > 0) & (step < steps - 1))
    def _():
        total_ref[...] += term

    @pl.when(step == steps - 1)
    def _():
        total = total_ref[...] + term
        out_ref[:, :width, :] = total.T.astype(jnp.bfloat16).reshape(blocks, width, span)


def sends(layer_in, w_value, gate, grads, count, steps=4):
    span, depth = layer_in.shape
    channels = w_value.shape[1]
    width = channels // count
    block = pl.BlockSpec((span, channels // steps), lambda i: (0, i))
    streams = [pl.BlockSpec((depth // (steps * STREAMS), channels), functools.partial(lambda j, i: (STREAMS * i + j, 0), j))
               for j in range(STREAMS)]
    return call(
        send_kernel, "sends", 2 * span * depth * channels, 12_500_000, vmem=56, grid=(steps,),
        in_specs=[pl.BlockSpec((span, depth // steps), lambda i: (0, i))] + streams + [block, block],
        out_specs=whole((count, 2 * width, span)),
        out_shape=jax.ShapeDtypeStruct((count, 2 * width, span), jnp.bfloat16),
        scratch_shapes=[pltpu.VMEM((span, channels), jnp.float32)],
    )(layer_in, *[w_value] * STREAMS, gate, grads)


def quarter_kernel(place_ref, rows_ref, others_ref, same_ref, cross_ref, other_ref):
    z = place_ref[0] % 2
    for y in range(4):
        to = slice(y * LANES, (y + 1) * LANES)
        own = pl.ds(pl.multiple_of((2 * y + z) * LANES, LANES), LANES)
        same_ref[:, to] = rows_ref[:, own]
        other_ref[:, to] = others_ref[:, own]
        cross_ref[:, to] = rows_ref[:, pl.ds(pl.multiple_of((2 * y + 1 - z) * LANES, LANES), LANES)]


def quarters_of(place, layer_in):
    span, depth = layer_in.shape
    quarter = jax.ShapeDtypeStruct((span, depth // 4), jnp.bfloat16)
    return call(
        quarter_kernel, "quarters", 0, 5_000_000,
        grid_spec=pltpu.PrefetchScalarGridSpec(
            num_scalar_prefetch=1, grid=(2,),
            in_specs=[pl.BlockSpec((span, depth // 4), lambda i, place: (0, 2 * (place[1] % 2) + i)),
                      pl.BlockSpec((span, depth // 4), lambda i, place: (0, 2 - 2 * (place[1] % 2) + i))],
            out_specs=[pl.BlockSpec((span, 4 * LANES), lambda i, place: (0, i))] * 3),
        out_shape=[quarter] * 3,
    )(place, layer_in, layer_in)


def share_kernel(place_ref, back_ref, *refs):
    mine, other, out_ref = refs[:4], refs[4:8], refs[8]
    core = place_ref[1] % 2
    span = mine[0].shape[0]
    for half, rows in ((core, mine), (1 - core, other)):
        for two in range(4):
            lanes = slice(two * 256, (two + 1) * 256)
            product = None
            for j in range(4):
                at = pl.multiple_of((place_ref[0] ^ j) * span, span)
                term = dot(back_ref[:, pl.ds(at, span)], rows[j][:, lanes])
                product = term if product is None else product + term
            product = product.astype(jnp.bfloat16)
            out_ref[half * 8 + 2 * two] = product[:, :LANES]
            out_ref[half * 8 + 2 * two + 1] = product[:, LANES:]


def shares(place, back, mine, other):
    span, depth = mine[0].shape
    rows = back.shape[0]
    return call(
        share_kernel, "shares", 16 * rows * span * depth, 7_000_000, vmem=24, grid=(1,),
        in_specs=[pl.BlockSpec(memory_space=pltpu.SMEM), pl.BlockSpec((rows, 4 * span), lambda i: (0, 0))]
        + [whole(part.shape) for part in mine + other],
        out_specs=whole((16, rows, LANES)),
        out_shape=jax.ShapeDtypeStruct((16, rows, LANES), jnp.bfloat16),
    )(place, back, *mine, *other)


def merge(pair, mine, mate):
    first, second = jnp.where(pair == 0, mine, mate), jnp.where(pair == 0, mate, mine)
    half = mine.shape[0] // 2
    return jnp.concatenate([first[:half], second[:half], first[half:], second[half:]], axis=0)


def weight_kernel(place_ref, shares_ref, taps_ref, mate_ref, weight_ref, tap_sums_ref):
    for x in range(4):
        rows, lanes = slice(x * LANES, (x + 1) * LANES), slice(x * 2 * LANES, (x + 1) * 2 * LANES)
        totals = []
        for pair in range(2):
            total = shares_ref[pair, rows, :].astype(jnp.float32)
            for j in range(pair + 2, shares_ref.shape[0], 2):
                total = total + shares_ref[j, rows, :].astype(jnp.float32)
            totals.append(total)
        weight_ref[:, lanes] = merge(0, *totals).T
        packed = merge(place_ref[0] // 2, taps_ref[rows, :].astype(jnp.float32), mate_ref[rows, :].astype(jnp.float32)).T
        tap_sums_ref[:, lanes] = (packed[16:24] + packed[8:16] + packed[0:8])[:TAPS]


def close_weight(place, parts, back, mate):
    count, rows, span = parts.shape
    channels = 2 * rows
    return call(
        weight_kernel, "close_weight", 2_000_000, 3_000_000, grid=(1,),
        in_specs=[pl.BlockSpec(memory_space=pltpu.SMEM), whole(parts.shape),
                  pl.BlockSpec((rows, LANES), lambda i: (0, 12)), pl.BlockSpec((rows, LANES), lambda i: (0, 4))],
        out_specs=[whole((span, channels)), whole((TAPS, channels))],
        out_shape=[jax.ShapeDtypeStruct((span, channels), jnp.float32),
                   jax.ShapeDtypeStruct((TAPS, channels), jnp.float32)],
    )(place, parts, back, mate)


def input_kernel(place_ref, back_ref, mate_ref, weight_ref, send_ref, keep_ref, own_buf):
    @pl.when(pl.program_id(0) == 0)
    def _():
        pair = place_ref[0] // 2
        for at in range(8):
            rows = slice(at * 64, (at + 1) * 64)
            own_buf[pl.ds(pl.multiple_of(at * LANES + pair * 64, 64), 64), :] = back_ref[rows, :]
            own_buf[pl.ds(pl.multiple_of(at * LANES + (1 - pair) * 64, 64), 64), :] = mate_ref[rows, :]

    term = dot(weight_ref[...], own_buf[...])

    @pl.when(pl.program_id(0) < 2)
    def _():
        send_ref[0] = term.astype(jnp.bfloat16)

    @pl.when(pl.program_id(0) >= 2)
    def _():
        keep_ref[0] = term


def input_terms(place, back, mate, w_value):
    depth, channels = w_value.shape
    rows, span = depth // 4, 256
    return call(
        input_kernel, "input_terms", 2 * span * depth * channels, 12_000_000, vmem=24,
        grid_spec=pltpu.PrefetchScalarGridSpec(
            num_scalar_prefetch=1, grid=(4,),
            in_specs=[pl.BlockSpec((channels // 2, span), lambda i, place: (0, place[0])),
                      pl.BlockSpec((channels // 2, span), lambda i, place: (0, 0)),
                      pl.BlockSpec((rows, channels), lambda i, place: (place[1] ^ ((2 * i + 1 - i // 2) % 4), 0))],
            out_specs=[pl.BlockSpec((1, rows, span), lambda i, place: (jnp.minimum(i, 1), 0, 0)),
                       pl.BlockSpec((1, rows, span), lambda i, place: (jnp.maximum(i - 2, 0), 0, 0))],
            scratch_shapes=[pltpu.VMEM((channels, span), jnp.bfloat16)]),
        out_shape=[jax.ShapeDtypeStruct((2, rows, span), jnp.bfloat16),
                   jax.ShapeDtypeStruct((2, rows, span), jnp.float32)],
    )(place, back, mate, w_value)


def close_kernel(keep_ref, core_ref, chip_ref, out_ref):
    total = keep_ref[0] + core_ref[0].astype(jnp.float32) + chip_ref[...].astype(jnp.float32)
    out_ref[...] = total.T.astype(jnp.bfloat16)


def close_input(keep, core, chip):
    rows, span = chip.shape
    first = pl.BlockSpec((1, 512, span), lambda i: (0, i, 0))
    return call(
        close_kernel, "close_input", 1_000_000, 3_000_000, grid=(rows // 512,),
        in_specs=[first, first, pl.BlockSpec((512, span), lambda i: (i, 0))],
        out_specs=pl.BlockSpec((span, 512), lambda i: (0, i)),
        out_shape=jax.ShapeDtypeStruct((span, rows), jnp.bfloat16))(keep, core, chip)


def gate_kernel(place_ref, mixed_ref, mate_ref, gate_ref, grad_ref, out_ref):
    mixed = merge(place_ref[0] // 2, mixed_ref[...].astype(jnp.float32), mate_ref[...].astype(jnp.float32)).T
    sig = jax.nn.sigmoid(gate_ref[...].astype(jnp.float32))
    out_ref[...] = (grad_ref[...].astype(jnp.float32) * mixed * sig * (1.0 - sig)).astype(jnp.bfloat16)


def gate_grad(place, back, mate, gate, grads):
    span, channels = gate.shape
    block = pl.BlockSpec((span, channels // 4), lambda i, place: (0, i))
    return call(
        gate_kernel, "gate_grad", 2_000_000, 2_500_000,
        grid_spec=pltpu.PrefetchScalarGridSpec(
            num_scalar_prefetch=1, grid=(4,),
            in_specs=[pl.BlockSpec((LANES, span), lambda i, place: (i, 4 + place[0] // 2)),
                      pl.BlockSpec((LANES, span), lambda i, place: (i, 1)), block, block],
            out_specs=block),
        out_shape=jax.ShapeDtypeStruct(gate.shape, jnp.bfloat16))(place, back, mate, gate, grads)


def local(layer_in, w_value, short_taps, long_filters, gate_proj, grad_out):
    seq_count = lax.axis_size("seq")
    seq_at, tp_at = lax.axis_index("seq"), lax.axis_index("tp")
    span, depth = layer_in.shape
    channels = w_value.shape[1]
    width = channels // seq_count
    quad_at = seq_at % 4
    place = jnp.stack([quad_at, tp_at]).astype(jnp.int32)
    cores, chips = [(0, 1), (1, 0), (2, 3), (3, 2)], [(0, 2), (2, 0), (1, 3), (3, 1)]

    def exchange(value, index_groups=None):
        return lax.all_to_all(
            value, "seq", split_axis=0, concat_axis=0, axis_index_groups=index_groups, tiled=True)

    def mates(value, step):
        return lax.ppermute(value, "seq", [(s, s ^ step) for s in range(seq_count)])

    outgoing = sends(layer_in, w_value, gate_proj, grad_out, seq_count)
    rows_in, outgoing = lax.optimization_barrier((layer_in, outgoing))
    arrived = exchange(outgoing)
    same, cross, other = quarters_of(place, rows_in)
    mine = [same, mates(cross, 1), mates(same, 2), mates(cross, 3)]
    other = [other] + [lax.ppermute(part, "tp", cores) for part in mine[1:]]
    spectra = spectra_of(long_filters)

    own_taps = lax.dynamic_slice_in_dim(short_taps, seq_at * width, width, 1)
    back, lag = mixer(own_taps, arrived, spectra)
    back, mine = lax.optimization_barrier((back, mine))
    back = exchange(back, LEAGUES).reshape(channels // 2, back.shape[2])
    grad_filters = filter_grads(lag)
    back, grad_filters, other = lax.optimization_barrier((back, grad_filters, other))
    mate = mates(jnp.concatenate([
        lax.dynamic_slice_in_dim(back, (quad_at ^ 2) * span, span, 1),
        lax.dynamic_slice_in_dim(back, 4 * span + (1 - quad_at // 2) * span, span, 1),
        back[:, 6 * span:]], axis=1), 2)

    parts = exchange(shares(place, back, mine, other), PLANES)
    send, keep = input_terms(place, back, mate, w_value)
    core = lax.ppermute(send, "tp", cores)
    chip = lax.ppermute((keep[1] + core[1].astype(jnp.float32)).astype(jnp.bfloat16), "tp", chips)
    grad_input = close_input(keep, core, chip)
    grad_gate = gate_grad(place, back, mate, gate_proj, grad_out)
    grad_weight, grad_taps = close_weight(place, parts, back, mate)
    return (grad_input, grad_weight, grad_taps, grad_filters, grad_gate)


def solution(mesh):
    in_specs = (
        P("seq", None),
        P(None, "tp"),
        P(None, "tp"),
        P(None, ("tp", "seq"), None),
        P("seq", "tp"),
        P("seq", "tp"),
    )
    out_specs = (
        P("seq", "tp"),
        P("seq", "tp"),
        P(None, "tp"),
        P(None, ("tp", "seq"), None),
        P("seq", "tp"),
    )
    return jax.shard_map(local, mesh=mesh, in_specs=in_specs, out_specs=out_specs, check_vma=False)
```

time: 687 us -> 157 us (0.23)
  the two profiles are of different devices: /device:TPU:0 before, /device:TPU:14 now
where the time goes in v1:
time: 157 us; the launch traced here: 156 us
  Pallas kernels  59.5 us (38%)
  waiting for transfers between devices  42.3 us (27%)
  starting transfers between devices  39 us (25%)
  local copies, waits for them, and re-layouts  12.5 us (8%)
  other arithmetic  1.91 us (1%)
    all_to_all x3, starting transfers between devices, exchange(): lax.all_to_all(value, 'seq', split_axis=0, concat_axis=0, axis_index_grou...  31.3 us
    ppermute x4, waiting for transfers between devices, mates(): return lax.ppermute(value, 'seq', [(s, s ^ step) for s in range(seq_count)])  21.1 us
    pallas_call x1, Pallas kernels, mixer(): call(mixer_kernel, 'mixer', 3000000000, 8000000, vmem=56, grid=(width //...  20.1 us
    unnamed x36, local copies, waits for them, and re-layouts  11.7 us
    all_to_all x3, waiting for transfers between devices, exchange(): lax.all_to_all(value, 'seq', split_axis=0, concat_axis=0, axis_index_grou...  10.8 us
    pallas_call x1, Pallas kernels, spectra_of(): call(spectra_kernel, 'spectra', 3000000000, 5000000, vmem=56, grid=(width...  8.8 us
    ppermute x1, waiting for transfers between devices, local(): lax.ppermute((keep[1] + core[1].astype(jnp.float32)).astype(jnp.bfloat16)...  7.75 us
    pallas_call x1, Pallas kernels, sends(): call(send_kernel, 'sends', 2 * span * depth * channels, 12500000, vmem=56...  7.35 us
  transfers between devices with their start and end apart: 12, of which 5 were waited for; matrix products, arithmetic and copies ran while one was open for 1% of the time, Pallas kernels for 32%

profile of v1, /device:TPU:14, one launch (start us, length us, event | category | flops | bytes accessed | tf_op | source)
XLA Modules:
  0.0 156.1 jit_solution(11096997979637374826)
XLA Ops:
  0.6 0.0 copy-start
  0.6 7.3 %sends.1 = bf16[32,64,256]{2,1,0:T(8,128)(2,1)} custom-call(bf16[256,4096]{1,0:T(8,128)(2,1)} %others_ref, bf16[4096,1024]{1,0:T(8,128)(2,1)} %weight_ref.1, bf16[4096,1024]{1,0:T(8,128)(2,1)} %weight_ref.1, bf16[4096,1024]{1,0:T(8,128)(2,1)} %weight_ref.1, bf16[4096,1024]{1,0:T(8,128)(2,1)} %weight_ref.1, bf16[256,1024]{1,0:T(8,128)(2,1)} %gate_ref.1, ...), custom_call_target="tpu_custom_call" | custom-call | flops 2147483648 | bytes 12500000 | tf_op jit(solution)/shard_map/sends/pallas_call | solution.py:364
  8.0 11.0 %all-to-all-start = ((bf16[32,64,256]{2,1,0:T(8,128)(2,1)}), bf16[32,64,256]{2,1,0:T(8,128)(2,1)}, u32[]{:S(2)}, u32[]{:S(2)}) async-start(bf16[32,64,256]{2,1,0:T(8,128)(2,1)} %sends.1), calls=%async_computation | async-start | bytes 2097152 | tf_op jit(solution)/shard_map/all_to_all | solution.py:542
  19.0 0.1 pad_add_fusion.place_ref
  19.1 2.0 %quarters.1 = (bf16[256,1024]{1,0:T(8,128)(2,1)S(1)}, bf16[256,1024]{1,0:T(8,128)(2,1)}, bf16[256,1024]{1,0:T(8,128)(2,1)S(1)}) custom-call(s32[2]{0:T(128)S(1)} %pad_add_fusion.place_ref, bf16[256,4096]{1,0:T(8,128)(2,1)S(1)} %copy-done.2, bf16[256,4096]{1,0:T(8,128)(2,1)S(1)} %copy-done.2), custom_call_target="tpu_custom_call" | custom-call | bytes 5000000 | tf_op jit(solution)/shard_map/quarters/pallas_call | solution.py:386
  21.1 3.0 %collective-permute-start.2 = (bf16[256,1024]{1,0:T(8,128)(2,1)}, bf16[256,1024]{1,0:T(8,128)(2,1)S(1)}, u32[]{:S(2)}, u32[]{:S(2)}) collective-permute-start(bf16[256,1024]{1,0:T(8,128)(2,1)} %get-tuple-element.31), channel_id=1, source_target_pairs={{0,12},{4,8},{8,4},{12,0},{16,28},{20,24},{24,20},{28,16},{32,44},... | collective-permute-start | bytes 1572872 | tf_op jit(solution)/shard_map/ppermute | solution.py:546
  24.0 0.6 collective-permute-start
  24.6 1.5 collective-permute-start.1
  26.1 0.7 constant_dynamic-slice_fusion.2.taps_ref
  26.7 8.8 %spectra.1.spectra_ref = f32[2048,256]{1,0:T(8,128)} custom-call(f32[2,4,512,128]{3,2,1,0:T(8,128)} %bitcast.21, bf16[128,256]{1,0:T(8,128)(2,1)} %constant.66.clone.first_nat_ref, f32[2,64,128]{2,1,0:T(8,128)} %constant.67.clone.twist_ref, bf16[1536,256]{1,0:T(8,128)(2,1)} %constant.68.clone.pair_ref), custom_call_target="tpu_custom_call" | custom-call | flops 3000000000 | bytes 5000000 | tf_op jit(solution)/shard_map/spectra/pallas_call | solution.py:276
  35.5 0.0 all-to-all-done.arrived_ref
  35.6 20.1 %mixer.1 = (bf16[16,32,1664]{2,1,0:T(8,128)(2,1)}, bf16[2048,512]{1,0:T(8,128)(2,1)}) custom-call(f32[7,32]{1,0:T(8,128)} %constant_dynamic-slice_fusion.2.taps_ref, bf16[32,64,256]{2,1,0:T(8,128)(2,1)} %all-to-all-done.arrived_ref, f32[2048,256]{1,0:T(8,128)} %spectra.1.spectra_ref, bf16[128,128]{1,0:T(8,128)(2,1)} %constant.69.clone.first_split_ref, ...), custom_call_target="tpu_custom_call" | custom-call | flops 3000000000 | bytes 8000000 | tf_op jit(solution)/shard_map/mixer/pallas_call | solution.py:304
  55.7 0.0 copy-start.12
  55.7 0.0 collective-permute-done.2.refs_3_
  55.7 0.0 copy-start.8
  55.7 0.5 collective-permute-done.refs_1_
  56.2 0.3 copy-done.12
  56.5 0.5 copy-done.10
  57.0 14.8 %all-to-all-start.1 = ((bf16[16,32,1664]{2,1,0:T(8,128)(2,1)}), bf16[16,32,1664]{2,1,0:T(8,128)(2,1)S(1)}, u32[]{:S(2)}, u32[]{:S(2)}) async-start(bf16[16,32,1664]{2,1,0:T(8,128)(2,1)} %get-tuple-element.32), calls=%async_computation.1 | async-start | bytes 3407872 | tf_op jit(solution)/shard_map/all_to_all | solution.py:542
  71.8 0.5 collective-permute-start.5
  72.3 0.1 collective-permute-start.3
  72.4 1.1 copy-done.14
  73.5 1.6 %copy-done.17 = bf16[2048,512]{1,0:T(8,128)(2,1)S(1)} copy-done((bf16[2048,512]{1,0:T(8,128)(2,1)S(1)}, bf16[2048,512]{1,0:T(8,128)(2,1)}, u32[]{:S(2)}) %copy-start.17) | copy-done | bytes 2097176
  75.1 6.2 %filter_grads.1 = f32[2,4,512,128]{3,2,1,0:T(8,128)} custom-call(bf16[2048,512]{1,0:T(8,128)(2,1)S(1)} %copy-done.17, f32[2,64,128]{2,1,0:T(8,128)S(1)} %copy-done.15, bf16[768,512]{1,0:T(8,128)(2,1)S(1)} %copy-done.14, bf16[64,384]{1,0:T(8,128)(2,1)S(1)} %copy-done.16), custom_call_target="tpu_custom_call" | custom-call | flops 3000000000 | bytes 5000000 | tf_op jit(solution)/shard_map/filter_grads/pallas_call | solution.py:289
  81.4 0.0 collective-permute-done.5.refs_7_
  81.4 10.8 %all-to-all-done.1 = bf16[16,32,1664]{2,1,0:T(8,128)(2,1)S(1)} async-done(((bf16[16,32,1664]{2,1,0:T(8,128)(2,1)}), bf16[16,32,1664]{2,1,0:T(8,128)(2,1)S(1)}, u32[]{:S(2)}, u32[]{:S(2)}) %all-to-all-start.1) | async-done | bytes 1703968 | tf_op jit(solution)/shard_map/all_to_all | solution.py:542
  92.2 0.9 pad_maximum_fusion
  93.1 1.0 collective-permute-start.6
  94.2 1.0 copy-done.11
  95.2 1.0 copy-done.13
  96.2 3.8 %shares.1 = bf16[16,512,128]{2,1,0:T(8,128)(2,1)S(1)} custom-call(s32[2]{0:T(128)S(1)} %pad_add_fusion.place_ref, bf16[512,1664]{1,0:T(8,128)(2,1)S(1)} %bitcast.17, bf16[256,1024]{1,0:T(8,128)(2,1)S(1)} %get-tuple-element.38.refs_0_, bf16[256,1024]{1,0:T(8,128)(2,1)S(1)} %copy-done.11, bf16[256,1024]{1,0:T(8,128)(2,1)S(1)} %copy-done.13, ...), custom_call_target="tpu_custom_call" | custom-call | flops 2147483648 | bytes 7000000 | tf_op jit(solution)/shard_map/shares/pallas_call | solution.py:417
  100.0 1.3 copy-done.3
  101.4 5.5 %all-to-all-start.2 = ((bf16[16,512,128]{2,1,0:T(8,128)(2,1)}), bf16[16,512,128]{2,1,0:T(8,128)(2,1)}, u32[]{:S(2)}, u32[]{:S(2)}) async-start(bf16[16,512,128]{2,1,0:T(8,128)(2,1)} %copy-done.3), calls=%async_computation.2 | async-start | bytes 4194304 | tf_op jit(solution)/shard_map/all_to_all | solution.py:542
  106.9 20.6 %collective-permute-done.6.mate_ref = bf16[512,640]{1,0:T(8,128)(2,1)S(1)} collective-permute-done((bf16[512,640]{1,0:T(8,128)(2,1)}, bf16[512,640]{1,0:T(8,128)(2,1)S(1)}, u32[]{:S(2)}, u32[]{:S(2)}) %collective-permute-start.6) | collective-permute-done | bytes 655392 | tf_op jit(solution)/shard_map/ppermute | solution.py:546
  127.4 3.4 %copy-done.1 = bf16[4096,1024]{1,0:T(8,128)(2,1)S(1)} copy-done((bf16[4096,1024]{1,0:T(8,128)(2,1)S(1)}, bf16[4096,1024]{1,0:T(8,128)(2,1)}, u32[]{:S(2)}) %copy-start.1) | copy-done | bytes 8388632
  130.8 3.9 %input_terms.1 = (bf16[2,1024,256]{2,1,0:T(8,128)(2,1)S(1)}, f32[2,1024,256]{2,1,0:T(8,128)S(1)}) custom-call(s32[2]{0:T(128)S(1)} %pad_add_fusion.place_ref, bf16[512,1664]{1,0:T(8,128)(2,1)S(1)} %bitcast.18, bf16[512,640]{1,0:T(8,128)(2,1)S(1)} %collective-permute-done.6.mate_ref, bf16[4096,1024]{1,0:T(8,128)(2,1)S(1)} %copy-done.1), custom_call_target="tpu_custom_call" | custom-call | flops 2147483648 | bytes 12000000 | tf_op jit(solution)/shard_map/input_terms/pallas_call | solution.py:482
  134.7 0.0 copy-start.6
  134.7 0.0 copy-start.7
  134.7 0.1 collective-permute-start.7
  134.8 2.6 %collective-permute-done.7.core_ref = bf16[2,1024,256]{2,1,0:T(8,128)(2,1)S(1)} collective-permute-done((bf16[2,1024,256]{2,1,0:T(8,128)(2,1)S(1)}, bf16[2,1024,256]{2,1,0:T(8,128)(2,1)S(1)}, u32[]{:S(2)}, u32[]{:S(2)}) %collective-permute-start.7) | collective-permute-done | bytes 1048608 | tf_op jit(solution)/shard_map/ppermute | solution.py:569
  137.5 0.9 fusion
  138.4 1.4 copy-done.4
  139.8 1.0 collective-permute-start.8
  140.8 2.6 %gate_grad.1 = bf16[256,1024]{1,0:T(8,128)(2,1)} custom-call(s32[2]{0:T(128)S(1)} %pad_add_fusion.place_ref, bf16[512,1664]{1,0:T(8,128)(2,1)S(1)} %bitcast.19, bf16[512,640]{1,0:T(8,128)(2,1)S(1)} %collective-permute-done.6.mate_ref, bf16[256,1024]{1,0:T(8,128)(2,1)S(1)} %copy-done.6, bf16[256,1024]{1,0:T(8,128)(2,1)S(1)} %copy-done.7), custom_call_target="tpu_custom_call" | custom-call | flops 2000000 | bytes 2500000 | tf_op jit(solution)/shard_map/gate_grad/pallas_call | solution.py:521
  143.4 0.0 all-to-all-done.2.shares_ref
  143.4 2.9 %close_weight.1 = (f32[128,1024]{1,0:T(8,128)}, f32[7,1024]{1,0:T(8,128)}) custom-call(s32[2]{0:T(128)S(1)} %pad_add_fusion.place_ref, bf16[16,512,128]{2,1,0:T(8,128)(2,1)} %all-to-all-done.2.shares_ref, bf16[512,1664]{1,0:T(8,128)(2,1)S(1)} %bitcast.20, bf16[512,640]{1,0:T(8,128)(2,1)S(1)} %collective-permute-done.6.mate_ref), custom_call_target="tpu_custom_call" | custom-call | flops 2000000 | bytes 3000000 | tf_op jit(solution)/shard_map/close_weight/pallas_call | solution.py:449
  146.3 7.7 %collective-permute-done.8.chip_ref = bf16[1024,256]{1,0:T(8,128)(2,1)} collective-permute-done((bf16[1024,256]{1,0:T(8,128)(2,1)}, bf16[1024,256]{1,0:T(8,128)(2,1)}, u32[]{:S(2)}, u32[]{:S(2)}) %collective-permute-start.8) | collective-permute-done | bytes 524320 | tf_op jit(solution)/shard_map/ppermute | solution.py:570
  154.1 2.0 %close_input.1 = bf16[256,1024]{1,0:T(8,128)(2,1)} custom-call(f32[2,1024,256]{2,1,0:T(8,128)S(1)} %copy-done.5, bf16[2,1024,256]{2,1,0:T(8,128)(2,1)S(1)} %collective-permute-done.7.core_ref, bf16[1024,256]{1,0:T(8,128)(2,1)} %collective-permute-done.8.chip_ref), custom_call_target="tpu_custom_call" | custom-call | flops 1000000 | bytes 3000000 | tf_op jit(solution)/shard_map/close_input/pallas_call | solution.py:505
  (28 shorter events, 0.1 us)
Async XLA Ops:
  0.6 25.4 %copy-start = (f32[7,1024]{1,0:T(8,128)S(1)}, f32[7,1024]{1,0:T(8,128)}, u32[]{:S(2)}) copy-start(f32[7,1024]{1,0:T(8,128)} %param.17) | copy-start | bytes 86020
  8.0 11.1 %copy-start.2 = (bf16[256,4096]{1,0:T(8,128)(2,1)S(1)}, bf16[256,4096]{1,0:T(8,128)(2,1)}, u32[]{:S(2)}) copy-start(bf16[256,4096]{1,0:T(8,128)(2,1)} %others_ref) | copy-start | bytes 6291460
  8.0 27.6 %all-to-all-start = ((bf16[32,64,256]{2,1,0:T(8,128)(2,1)}), bf16[32,64,256]{2,1,0:T(8,128)(2,1)}, u32[]{:S(2)}, u32[]{:S(2)}) async-start(bf16[32,64,256]{2,1,0:T(8,128)(2,1)} %sends.1), calls=%async_computation | async-start | bytes 2097152 | tf_op jit(solution)/shard_map/all_to_all | solution.py:542
  21.1 34.6 %collective-permute-start.2 = (bf16[256,1024]{1,0:T(8,128)(2,1)}, bf16[256,1024]{1,0:T(8,128)(2,1)S(1)}, u32[]{:S(2)}, u32[]{:S(2)}) collective-permute-start(bf16[256,1024]{1,0:T(8,128)(2,1)} %get-tuple-element.31), channel_id=1, source_target_pairs={{0,12},{4,8},{8,4},{12,0},{16,28},{20,24},{24,20},{28,16},{32,44},... | collective-permute-start | bytes 1572872 | tf_op jit(solution)/shard_map/ppermute | solution.py:546
  24.0 32.2 %collective-permute-start = (bf16[256,1024]{1,0:T(8,128)(2,1)}, bf16[256,1024]{1,0:T(8,128)(2,1)S(1)}, u32[]{:S(2)}, u32[]{:S(2)}) collective-permute-start(bf16[256,1024]{1,0:T(8,128)(2,1)} %get-tuple-element.31), channel_id=1, source_target_pairs={{0,4},{4,0},{8,12},{12,8},{16,20},{20,16},{24,28},{28,24},{32,36},... | collective-permute-start | bytes 1572872 | tf_op jit(solution)/shard_map/ppermute | solution.py:546
  24.6 31.1 %collective-permute-start.1 = (bf16[256,1024]{1,0:T(8,128)(2,1)S(1)}, bf16[256,1024]{1,0:T(8,128)(2,1)S(1)}, u32[]{:S(2)}, u32[]{:S(2)}) collective-permute-start(bf16[256,1024]{1,0:T(8,128)(2,1)S(1)} %get-tuple-element.38.refs_0_), channel_id=1, source_target_pairs={{0,8},{4,12},{8,0},{12,4},{16,24},{20,28},{24,16},{28,20},{32,40},... | collective-permute-start | bytes 1572872 | tf_op jit(solution)/shard_map/ppermute | solution.py:546
  55.6 16.8 %copy-start.15 = (f32[2,64,128]{2,1,0:T(8,128)S(1)}, f32[2,64,128]{2,1,0:T(8,128)}, u32[]{:S(2)}) copy-start(f32[2,64,128]{2,1,0:T(8,128)} %constant.67.clone.twist_ref) | copy-start | bytes 196612
  55.6 16.8 %copy-start.16 = (bf16[64,384]{1,0:T(8,128)(2,1)S(1)}, bf16[64,384]{1,0:T(8,128)(2,1)}, u32[]{:S(2)}) copy-start(bf16[64,384]{1,0:T(8,128)(2,1)} %constant.74.clone.last_nat_ref) | copy-start | bytes 147460
  55.7 0.8 copy-start.12
  55.7 25.7 %copy-start.8 = (bf16[256,1024]{1,0:T(8,128)(2,1)}, bf16[256,1024]{1,0:T(8,128)(2,1)S(1)}, u32[]{:S(2)}) copy-start(bf16[256,1024]{1,0:T(8,128)(2,1)S(1)} %collective-permute-done.2.refs_3_) | copy-start | bytes 1572868
  56.2 0.8 copy-start.10
  57.0 35.2 %all-to-all-start.1 = ((bf16[16,32,1664]{2,1,0:T(8,128)(2,1)}), bf16[16,32,1664]{2,1,0:T(8,128)(2,1)S(1)}, u32[]{:S(2)}, u32[]{:S(2)}) async-start(bf16[16,32,1664]{2,1,0:T(8,128)(2,1)} %get-tuple-element.32), calls=%async_computation.1 | async-start | bytes 3407872 | tf_op jit(solution)/shard_map/all_to_all | solution.py:542
  71.8 9.6 %collective-permute-start.4 = (bf16[256,1024]{1,0:T(8,128)(2,1)}, bf16[256,1024]{1,0:T(8,128)(2,1)}, u32[]{:S(2)}, u32[]{:S(2)}) collective-permute-start(bf16[256,1024]{1,0:T(8,128)(2,1)} %copy-done.12), channel_id=1, source_target_pairs={{0,1},{1,0},{2,3},{3,2},{4,5},{5,4},{6,7},{7,6},{8,9},{9,8},{10,11... | collective-permute-start | bytes 1572872 | tf_op jit(solution)/shard_map/ppermute | solution.py:553
  71.8 9.6 %collective-permute-start.5 = (bf16[256,1024]{1,0:T(8,128)(2,1)S(1)}, bf16[256,1024]{1,0:T(8,128)(2,1)}, u32[]{:S(2)}, u32[]{:S(2)}) collective-permute-start(bf16[256,1024]{1,0:T(8,128)(2,1)S(1)} %collective-permute-done.2.refs_3_), channel_id=1, source_target_pairs={{0,1},{1,0},{2,3},{3,2},{4,5},{5,4},{6,7},{7,6},{8,9},{9,8},{10,11... | collective-permute-start | bytes 1572872 | tf_op jit(solution)/shard_map/ppermute | solution.py:553
  72.3 9.1 %collective-permute-start.3 = (bf16[256,1024]{1,0:T(8,128)(2,1)}, bf16[256,1024]{1,0:T(8,128)(2,1)}, u32[]{:S(2)}, u32[]{:S(2)}) collective-permute-start(bf16[256,1024]{1,0:T(8,128)(2,1)} %copy-done.10), channel_id=1, source_target_pairs={{0,1},{1,0},{2,3},{3,2},{4,5},{5,4},{6,7},{7,6},{8,9},{9,8},{10,11... | collective-permute-start | bytes 1572872 | tf_op jit(solution)/shard_map/ppermute | solution.py:553
  72.4 1.1 copy-start.14
  73.5 1.6 %copy-start.17 = (bf16[2048,512]{1,0:T(8,128)(2,1)S(1)}, bf16[2048,512]{1,0:T(8,128)(2,1)}, u32[]{:S(2)}) copy-start(bf16[2048,512]{1,0:T(8,128)(2,1)} %get-tuple-element.33.lag_ref) | copy-start | bytes 6291460
  92.2 2.0 %copy-start.9 = (bf16[256,1024]{1,0:T(8,128)(2,1)S(1)}, bf16[256,1024]{1,0:T(8,128)(2,1)}, u32[]{:S(2)}) copy-start(bf16[256,1024]{1,0:T(8,128)(2,1)} %copy-done.8) | copy-start | bytes 1572868
  93.1 34.3 %collective-permute-start.6 = (bf16[512,640]{1,0:T(8,128)(2,1)}, bf16[512,640]{1,0:T(8,128)(2,1)S(1)}, u32[]{:S(2)}, u32[]{:S(2)}) collective-permute-start(bf16[512,640]{1,0:T(8,128)(2,1)} %pad_maximum_fusion), channel_id=1, source_target_pairs={{0,8},{4,12},{8,0},{12,4},{16,24},{20,28},{24,16},{28,20},{32,40},... | collective-permute-start | bytes 1966088 | tf_op jit(solution)/shard_map/ppermute | solution.py:546
  94.2 1.0 copy-start.11
  95.2 1.0 copy-start.13
  100.0 1.3 copy-start.3
  101.4 42.0 %all-to-all-start.2 = ((bf16[16,512,128]{2,1,0:T(8,128)(2,1)}), bf16[16,512,128]{2,1,0:T(8,128)(2,1)}, u32[]{:S(2)}, u32[]{:S(2)}) async-start(bf16[16,512,128]{2,1,0:T(8,128)(2,1)} %copy-done.3), calls=%async_computation.2 | async-start | bytes 4194304 | tf_op jit(solution)/shard_map/all_to_all | solution.py:542
  127.4 3.4 %copy-start.1 = (bf16[4096,1024]{1,0:T(8,128)(2,1)S(1)}, bf16[4096,1024]{1,0:T(8,128)(2,1)}, u32[]{:S(2)}) copy-start(bf16[4096,1024]{1,0:T(8,128)(2,1)} %weight_ref.1) | copy-start | bytes 25165828
  134.7 6.1 %copy-start.6 = (bf16[256,1024]{1,0:T(8,128)(2,1)S(1)}, bf16[256,1024]{1,0:T(8,128)(2,1)}, u32[]{:S(2)}) copy-start(bf16[256,1024]{1,0:T(8,128)(2,1)} %gate_ref.1) | copy-start | bytes 1572868
  134.7 6.1 %copy-start.7 = (bf16[256,1024]{1,0:T(8,128)(2,1)S(1)}, bf16[256,1024]{1,0:T(8,128)(2,1)}, u32[]{:S(2)}) copy-start(bf16[256,1024]{1,0:T(8,128)(2,1)} %grad_ref.1) | copy-start | bytes 1572868
  134.7 2.7 %collective-permute-start.7 = (bf16[2,1024,256]{2,1,0:T(8,128)(2,1)S(1)}, bf16[2,1024,256]{2,1,0:T(8,128)(2,1)S(1)}, u32[]{:S(2)}, u32[]{:S(2)}) collective-permute-start(bf16[2,1024,256]{2,1,0:T(8,128)(2,1)S(1)} %get-tuple-element.37), channel_id=1, source_target_pairs={{0,1},{1,0},{2,3},{3,2},{4,5},{5,4},{6,7},{7,6},{8,9},{9,8},{10,11... | collective-permute-start | bytes 3145736 | tf_op jit(solution)/shard_map/ppermute | solution.py:569
  138.4 1.4 copy-start.4
  139.8 14.3 %collective-permute-start.8 = (bf16[1024,256]{1,0:T(8,128)(2,1)}, bf16[1024,256]{1,0:T(8,128)(2,1)}, u32[]{:S(2)}, u32[]{:S(2)}) collective-permute-start(bf16[1024,256]{1,0:T(8,128)(2,1)} %fusion), channel_id=1, source_target_pairs={{0,2},{2,0},{1,3},{3,1},{4,6},{6,4},{5,7},{7,5},{8,10},{10,8},{9,1... | collective-permute-start | bytes 1572872 | tf_op jit(solution)/shard_map/ppermute | solution.py:570
  143.4 10.7 %copy-start.5 = (f32[2,1024,256]{2,1,0:T(8,128)S(1)}, f32[2,1024,256]{2,1,0:T(8,128)}, u32[]{:S(2)}) copy-start(f32[2,1024,256]{2,1,0:T(8,128)} %copy-done.4) | copy-start | bytes 6291460

commit v2 on v1

--- a/solution.py
+++ b/solution.py
@@ -16,6 +16,7 @@
 TAPS = 7
 REACH = TAPS // 2
 BATCH = 4
+GROUP, GROUPS = 2, 4
 
 
 def halves(table):
@@ -101,9 +102,11 @@
     return jnp.dot(left, right, preferred_element_type=jnp.float32)
 
 
-QUADS = [[4 * q + place for place in range(4)] for q in range(8)]
-LEAGUES = [[4 * q + 2 * pair + z for q in range(8) for z in range(2)] for pair in range(2)]
+Y_OF = ((1, 2), (0, 3))
+QUADS = [[(x * 4 + Y_OF[odd][pair]) * 2 + z for pair in range(2) for z in range(2)] for x in range(4) for odd in range(2)]
+LEAGUES = [[quad[2 * pair + z] for quad in QUADS for z in range(2)] for pair in range(2)]
 PLANES = [[2 * j + z for j in range(16)] for z in range(2)]
+MATE = 6
 
 
 def twisted(array, col, twist_ref):
@@ -162,72 +165,87 @@
             values_buf[h] = arrived_ref[:, :width, part].astype(jnp.float32).reshape(blocks * width, LANES)
             slopes_buf[h] = arrived_ref[:, width:, part].astype(jnp.float32).reshape(blocks * width, LANES)
 
-    pooled = []
-    for q in range(BATCH):
-        c = step * BATCH + q
-        early = values_buf[0, pl.ds(c, blocks, stride=width), :]
-        late = values_buf[1, pl.ds(c, blocks, stride=width), :]
-        sum_early, sum_late = None, None
-        for k in range(TAPS):
-            one, two = shifted(early, late, k - REACH)
-            tap = taps_ref[k, c]
-            sum_early = tap * one if k == 0 else sum_early + tap * one
-            sum_late = tap * two if k == 0 else sum_late + tap * two
-        short = jnp.concatenate([sum_early, sum_late], axis=0).astype(jnp.bfloat16)
-        conv = short.astype(jnp.float32)
-        slope = jnp.concatenate(
-            [slopes_buf[h, pl.ds(c, blocks, stride=width), :] for h in range(2)], axis=0)
-        sig = jax.nn.sigmoid(conv)
-        pooled.append(jnp.sum(conv * sig, keepdims=True) / LENGTH)
-        mean_grad = jnp.sum(slope, keepdims=True) / LENGTH
-        extra_buf[q] = mean_grad * (sig * (1.0 + conv * (1.0 - sig)))
-        both = jnp.concatenate([short, slope.astype(jnp.bfloat16)], axis=1)
-        section = dot(first_split_ref[...], jnp.concatenate([both, both], axis=0))
-        store_parts(signal_buf, q * ROWS, 0, *twisted(section, 0, twist_ref))
-        store_parts(signal_buf, (BATCH + q) * ROWS, 0, *twisted(section, 1, twist_ref))
-
-    spec = dot(signal_buf[...], forward_ref[...])
-    for q in range(BATCH):
-        rows = slice(q * ROWS, (q + 1) * ROWS)
-        slope_rows = slice((BATCH + q) * ROWS, (BATCH + q + 1) * ROWS)
-        short_re, short_im = spec[rows, :LANES], spec[rows, LANES:]
-        slope_re, slope_im = spec[slope_rows, :LANES], spec[slope_rows, LANES:]
-        filt_re, filt_im = spectra_ref[rows, :LANES], spectra_ref[rows, LANES:]
-        store_parts(product_buf, (2 * q) * ROWS, 0,
-                    short_re * filt_re - short_im * filt_im, short_re * filt_im + short_im * filt_re)
-        store_parts(product_buf, (2 * q + 1) * ROWS, 0,
-                    slope_re * filt_re + slope_im * filt_im, slope_im * filt_re - slope_re * filt_im)
-        real_high, real_low = cut(slope_re * short_re + slope_im * short_im)
-        imag_high, imag_low = cut(slope_im * short_re - slope_re * short_im)
-        for at, part in enumerate((real_high, imag_high, real_low, imag_low)):
-            lag_ref[rows, at * LANES:(at + 1) * LANES] = part
-
-    unmixed = dot(product_buf[...], inverse_ref[...])
-    for q in range(BATCH):
-        c = step * BATCH + q
-        rows = 2 * q * ROWS
-        long_pair = finish(last_split_ref, untwisted(unmixed[rows:rows + ROWS], twist_ref),
-                           untwisted(unmixed[rows + ROWS:rows + 2 * ROWS], twist_ref))
-        mixed = long_pair[:, :LANES] + pooled[q]
-        slope_back = (long_pair[:, LANES:] + extra_buf[q]).astype(jnp.bfloat16).astype(jnp.float32)
-        early = values_buf[0, pl.ds(c, blocks, stride=width), :]
-        late = values_buf[1, pl.ds(c, blocks, stride=width), :]
-        sum_early, sum_late = None, None
-        for k in range(TAPS):
-            one, two = shifted(slope_back[:blocks], slope_back[blocks:], REACH - k)
-            tap = taps_ref[k, c]
-            sum_early = tap * one if k == 0 else sum_early + tap * one
-            sum_late = tap * two if k == 0 else sum_late + tap * two
-            taps_buf[k, pl.ds(c, 1), :] = jnp.sum(one * early + two * late, axis=0, keepdims=True)
-        for h, part in enumerate((sum_early, sum_late)):
-            back_buf[h, pl.ds(c, blocks, stride=width), :] = part
-            mixed_buf[h, pl.ds(c, blocks, stride=width), :] = mixed[h * blocks:(h + 1) * blocks]
+    pooled = {}
+
+    def start(g):
+        for q in range(g * GROUP, (g + 1) * GROUP):
+            c = step * GROUP * GROUPS + q
+            early = values_buf[0, pl.ds(c, blocks, stride=width), :]
+            late = values_buf[1, pl.ds(c, blocks, stride=width), :]
+            sum_early, sum_late = None, None
+            for k in range(TAPS):
+                one, two = shifted(early, late, k - REACH)
+                tap = taps_ref[k, c]
+                sum_early = tap * one if k == 0 else sum_early + tap * one
+                sum_late = tap * two if k == 0 else sum_late + tap * two
+            short = jnp.concatenate([sum_early, sum_late], axis=0).astype(jnp.bfloat16)
+            conv = short.astype(jnp.float32)
+            slope = jnp.concatenate(
+                [slopes_buf[h, pl.ds(c, blocks, stride=width), :] for h in range(2)], axis=0)
+            sig = jax.nn.sigmoid(conv)
+            pooled[q] = jnp.sum(conv * sig, keepdims=True) / LENGTH
+            mean_grad = jnp.sum(slope, keepdims=True) / LENGTH
+            extra_buf[q] = mean_grad * (sig * (1.0 + conv * (1.0 - sig)))
+            both = jnp.concatenate([short, slope.astype(jnp.bfloat16)], axis=1)
+            section = dot(first_split_ref[...], jnp.concatenate([both, both], axis=0))
+            store_parts(signal_buf, 2 * q * ROWS, 0, *twisted(section, 0, twist_ref))
+            store_parts(signal_buf, (2 * q + 1) * ROWS, 0, *twisted(section, 1, twist_ref))
+
+    def multiply(g):
+        base = 2 * g * GROUP * ROWS
+        spec = dot(signal_buf[base:base + 2 * GROUP * ROWS], forward_ref[...])
+        for q in range(GROUP):
+            short, slope = spec[2 * q * ROWS:(2 * q + 1) * ROWS], spec[(2 * q + 1) * ROWS:(2 * q + 2) * ROWS]
+            rows = slice((g * GROUP + q) * ROWS, (g * GROUP + q + 1) * ROWS)
+            short_re, short_im = short[:, :LANES], short[:, LANES:]
+            slope_re, slope_im = slope[:, :LANES], slope[:, LANES:]
+            filt_re, filt_im = spectra_ref[rows, :LANES], spectra_ref[rows, LANES:]
+            store_parts(product_buf, base + 2 * q * ROWS, 0,
+                        short_re * filt_re - short_im * filt_im, short_re * filt_im + short_im * filt_re)
+            store_parts(product_buf, base + (2 * q + 1) * ROWS, 0,
+                        slope_re * filt_re + slope_im * filt_im, slope_im * filt_re - slope_re * filt_im)
+            real_high, real_low = cut(slope_re * short_re + slope_im * short_im)
+            imag_high, imag_low = cut(slope_im * short_re - slope_re * short_im)
+            for at, part in enumerate((real_high, imag_high, real_low, imag_low)):
+                lag_ref[rows, at * LANES:(at + 1) * LANES] = part
+
+    def end(g):
+        base = 2 * g * GROUP * ROWS
+        unmixed = dot(product_buf[base:base + 2 * GROUP * ROWS], inverse_ref[...])
+        for q in range(GROUP):
+            c = step * GROUP * GROUPS + g * GROUP + q
+            rows = 2 * q * ROWS
+            long_pair = finish(last_split_ref, untwisted(unmixed[rows:rows + ROWS], twist_ref),
+                               untwisted(unmixed[rows + ROWS:rows + 2 * ROWS], twist_ref))
+            mixed = long_pair[:, :LANES] + pooled[g * GROUP + q]
+            slope_back = long_pair[:, LANES:] + extra_buf[g * GROUP + q]
+            slope_back = slope_back.astype(jnp.bfloat16).astype(jnp.float32)
+            early = values_buf[0, pl.ds(c, blocks, stride=width), :]
+            late = values_buf[1, pl.ds(c, blocks, stride=width), :]
+            sum_early, sum_late = None, None
+            for k in range(TAPS):
+                one, two = shifted(slope_back[:blocks], slope_back[blocks:], REACH - k)
+                tap = taps_ref[k, c]
+                sum_early = tap * one if k == 0 else sum_early + tap * one
+                sum_late = tap * two if k == 0 else sum_late + tap * two
+                taps_buf[k, pl.ds(c, 1), :] = jnp.sum(one * early + two * late, axis=0, keepdims=True)
+            for h, part in enumerate((sum_early, sum_late)):
+                back_buf[h, pl.ds(c, blocks, stride=width), :] = part
+                mixed_buf[h, pl.ds(c, blocks, stride=width), :] = mixed[h * blocks:(h + 1) * blocks]
+
+    for turn in range(GROUPS + 2):
+        if turn >= 2:
+            end(turn - 2)
+        if 1 <= turn <= GROUPS:
+            multiply(turn - 1)
+        if turn < GROUPS:
+            start(turn)
 
     @pl.when(step == pl.num_programs(0) - 1)
     def _():
-        for q in range(blocks // 4):
-            for place in range(4):
-                rows = slice((4 * q + place) * width, (4 * q + place + 1) * width)
+        for q, quad in enumerate(QUADS):
+            for place, s in enumerate(quad):
+                rows = slice(s * width, (s + 1) * width)
                 for h in range(2):
                     part = back_buf[h, rows, :].astype(jnp.bfloat16)
                     lanes = slice((2 * place + h) * LANES, (2 * place + h + 1) * LANES)
@@ -255,8 +273,7 @@
 def call(kernel, name, flops, nbytes, vmem=16, **kwargs):
     return pl.pallas_call(
         kernel, name=name,
-        compiler_params=pltpu.CompilerParams(
-            dimension_semantics=("arbitrary",), vmem_limit_bytes=vmem * 1024 * 1024),
+        compiler_params=pltpu.CompilerParams(vmem_limit_bytes=vmem * 1024 * 1024),
         cost_estimate=pl.CostEstimate(flops=flops, bytes_accessed=nbytes, transcendentals=0), **kwargs)
 
 
@@ -300,13 +317,13 @@
     blocks, width, span = arrived.shape[0], arrived.shape[1] // 2, arrived.shape[2]
     consts, specs = tables_of(("first_split", "twist", "forward", "inverse", "last_split"))
     back_shape = (blocks // 2, width, 6 * span + LANES)
-    rows = (2, blocks * width, LANES)
+    rows, batch = (2, blocks * width, LANES), GROUP * GROUPS
     return call(
         mixer_kernel, "mixer", 3_000_000_000, 8_000_000, vmem=56,
-        grid=(width // BATCH,),
+        grid=(width // batch,),
         in_specs=[pl.BlockSpec(memory_space=pltpu.SMEM), whole(arrived.shape),
-                  pl.BlockSpec((BATCH * ROWS, 2 * LANES), lambda i: (i, 0))] + specs,
-        out_specs=[whole(back_shape), pl.BlockSpec((BATCH * ROWS, 4 * LANES), lambda i: (i, 0))],
+                  pl.BlockSpec((batch * ROWS, 2 * LANES), lambda i: (i, 0))] + specs,
+        out_specs=[whole(back_shape), pl.BlockSpec((batch * ROWS, 4 * LANES), lambda i: (i, 0))],
         out_shape=[
             jax.ShapeDtypeStruct(back_shape, jnp.bfloat16),
             jax.ShapeDtypeStruct((width * ROWS, 4 * LANES), jnp.bfloat16),
@@ -317,9 +334,9 @@
             pltpu.VMEM(rows, jnp.float32),
             pltpu.VMEM(rows, jnp.float32),
             pltpu.VMEM((TAPS, width, LANES), jnp.float32),
-            pltpu.VMEM((BATCH, ROWS, LANES), jnp.float32),
-            pltpu.VMEM((2 * BATCH * ROWS, 6 * LANES), jnp.bfloat16),
-            pltpu.VMEM((2 * BATCH * ROWS, 6 * LANES), jnp.bfloat16),
+            pltpu.VMEM((batch, ROWS, LANES), jnp.float32),
+            pltpu.VMEM((2 * batch * ROWS, 6 * LANES), jnp.bfloat16),
+            pltpu.VMEM((2 * batch * ROWS, 6 * LANES), jnp.bfloat16),
         ],
     )(own_taps, arrived, spectra, *consts)
 
@@ -394,104 +411,136 @@
     )(place, layer_in, layer_in)
 
 
-def share_kernel(place_ref, back_ref, *refs):
-    mine, other, out_ref = refs[:4], refs[4:8], refs[8]
-    core = place_ref[1] % 2
-    span = mine[0].shape[0]
-    for half, rows in ((core, mine), (1 - core, other)):
+def quad_place():
+    seq_at = lax.axis_index("seq")
+    return seq_at // 4 % 2 * 2 + seq_at % 2
+
+
+def share_kernel(back_ref, *refs):
+    parts, (out_ref, back_buf, rows_buf, out_buf, in_sem, out_sem) = refs[:8], refs[8:]
+    span = rows_buf.shape[1]
+    loads = [pltpu.make_async_copy(back_ref.at[:, pl.ds(0, 4 * span)], back_buf, in_sem.at[8])]
+    loads += [pltpu.make_async_copy(part, rows_buf.at[n], in_sem.at[n]) for n, part in enumerate(parts)]
+    for load in loads:
+        load.start()
+    loads[0].wait()
+    stores = []
+    for half in range(2):
+        for load in loads[1 + 4 * half:5 + 4 * half]:
+            load.wait()
+        first = 8 * (half ^ (lax.axis_index("tp") % 2))
         for two in range(4):
             lanes = slice(two * 256, (two + 1) * 256)
             product = None
             for j in range(4):
-                at = pl.multiple_of((place_ref[0] ^ j) * span, span)
-                term = dot(back_ref[:, pl.ds(at, span)], rows[j][:, lanes])
+                at = pl.multiple_of((quad_place() ^ j) * span, span)
+                term = dot(back_buf[:, pl.ds(at, span)], rows_buf[4 * half + j, :, lanes])
                 product = term if product is None else product + term
             product = product.astype(jnp.bfloat16)
-            out_ref[half * 8 + 2 * two] = product[:, :LANES]
-            out_ref[half * 8 + 2 * two + 1] = product[:, LANES:]
-
-
-def shares(place, back, mine, other):
+            n = 4 * half + two
+            out_buf[2 * n] = product[:, :LANES]
+            out_buf[2 * n + 1] = product[:, LANES:]
+            store = pltpu.make_async_copy(
+                out_buf.at[pl.ds(2 * n, 2)], out_ref.at[pl.ds(first + 2 * two, 2)], out_sem.at[n])
+            store.start()
+            stores.append(store)
+    for store in stores:
+        store.wait()
+
+
+def shares(back, mine, other):
     span, depth = mine[0].shape
     rows = back.shape[0]
     return call(
-        share_kernel, "shares", 16 * rows * span * depth, 7_000_000, vmem=24, grid=(1,),
-        in_specs=[pl.BlockSpec(memory_space=pltpu.SMEM), pl.BlockSpec((rows, 4 * span), lambda i: (0, 0))]
-        + [whole(part.shape) for part in mine + other],
-        out_specs=whole((16, rows, LANES)),
+        share_kernel, "shares", 16 * rows * span * depth, 7_000_000, vmem=32,
+        in_specs=[pl.BlockSpec(memory_space=pl.ANY)] * 9,
+        out_specs=pl.BlockSpec(memory_space=pl.ANY),
         out_shape=jax.ShapeDtypeStruct((16, rows, LANES), jnp.bfloat16),
-    )(place, back, *mine, *other)
+        scratch_shapes=[
+            pltpu.VMEM((rows, 4 * span), jnp.bfloat16), pltpu.VMEM((8, span, depth), jnp.bfloat16),
+            pltpu.VMEM((16, rows, LANES), jnp.bfloat16),
+            pltpu.SemaphoreType.DMA((9,)), pltpu.SemaphoreType.DMA((8,))],
+    )(back, *mine, *other)
 
 
 def merge(pair, mine, mate):
     first, second = jnp.where(pair == 0, mine, mate), jnp.where(pair == 0, mate, mine)
     half = mine.shape[0] // 2
-    return jnp.concatenate([first[:half], second[:half], first[half:], second[half:]], axis=0)
-
-
-def weight_kernel(place_ref, shares_ref, taps_ref, mate_ref, weight_ref, tap_sums_ref):
+    return jnp.concatenate([first[half:], first[:half], second[:half], second[half:]], axis=0)
+
+
+def weight_kernel(shares_ref, taps_ref, mate_ref, weight_ref, tap_sums_ref):
     for x in range(4):
         rows, lanes = slice(x * LANES, (x + 1) * LANES), slice(x * 2 * LANES, (x + 1) * 2 * LANES)
         totals = []
         for pair in range(2):
-            total = shares_ref[pair, rows, :].astype(jnp.float32)
-            for j in range(pair + 2, shares_ref.shape[0], 2):
-                total = total + shares_ref[j, rows, :].astype(jnp.float32)
-            totals.append(total)
+            terms = [shares_ref[j, rows, :].astype(jnp.float32) for j in range(16) if j % 4 // 2 == pair]
+            totals.append(sum(terms[1:], terms[0]))
         weight_ref[:, lanes] = merge(0, *totals).T
-        packed = merge(place_ref[0] // 2, taps_ref[rows, :].astype(jnp.float32), mate_ref[rows, :].astype(jnp.float32)).T
+        packed = merge(quad_place() // 2, taps_ref[rows, :].astype(jnp.float32), mate_ref[rows, :].astype(jnp.float32)).T
         tap_sums_ref[:, lanes] = (packed[16:24] + packed[8:16] + packed[0:8])[:TAPS]
 
 
-def close_weight(place, parts, back, mate):
+def close_weight(parts, back, mate):
     count, rows, span = parts.shape
     channels = 2 * rows
     return call(
         weight_kernel, "close_weight", 2_000_000, 3_000_000, grid=(1,),
-        in_specs=[pl.BlockSpec(memory_space=pltpu.SMEM), whole(parts.shape),
-                  pl.BlockSpec((rows, LANES), lambda i: (0, 12)), pl.BlockSpec((rows, LANES), lambda i: (0, 4))],
+        in_specs=[whole(parts.shape),
+                  pl.BlockSpec((rows, LANES), lambda i: (0, 12)), pl.BlockSpec((rows, LANES), lambda i: (0, 2))],
         out_specs=[whole((span, channels)), whole((TAPS, channels))],
         out_shape=[jax.ShapeDtypeStruct((span, channels), jnp.float32),
                    jax.ShapeDtypeStruct((TAPS, channels), jnp.float32)],
-    )(place, parts, back, mate)
-
-
-def input_kernel(place_ref, back_ref, mate_ref, weight_ref, send_ref, keep_ref, own_buf):
+    )(parts, back, mate)
+
+
+def input_kernel(place_ref, back_ref, mate_ref, *refs):
+    weight_refs, (send_ref, keep_ref, own_buf) = refs[:STREAMS], refs[STREAMS:]
+
     @pl.when(pl.program_id(0) == 0)
     def _():
         pair = place_ref[0] // 2
-        for at in range(8):
-            rows = slice(at * 64, (at + 1) * 64)
-            own_buf[pl.ds(pl.multiple_of(at * LANES + pair * 64, 64), 64), :] = back_ref[rows, :]
-            own_buf[pl.ds(pl.multiple_of(at * LANES + (1 - pair) * 64, 64), 64), :] = mate_ref[rows, :]
-
-    term = dot(weight_ref[...], own_buf[...])
+        for x in range(4):
+            for odd, mine, other in ((0, 1 + pair, 2 - pair), (1, 3 * pair, 3 - 3 * pair)):
+                rows = slice((2 * x + odd) * 64, (2 * x + odd + 1) * 64)
+                own_buf[pl.ds(pl.multiple_of((4 * x + mine) * 64, 64), 64), :] = back_ref[rows, :]
+                own_buf[pl.ds(pl.multiple_of((4 * x + other) * 64, 64), 64), :] = mate_ref[rows, :]
+
+    size = weight_refs[0].shape[0]
+    terms = [dot(weight_ref[...], own_buf[...]) for weight_ref in weight_refs]
 
     @pl.when(pl.program_id(0) < 2)
     def _():
-        send_ref[0] = term.astype(jnp.bfloat16)
+        for n, term in enumerate(terms):
+            send_ref[0, n * size:(n + 1) * size] = term.astype(jnp.bfloat16)
 
     @pl.when(pl.program_id(0) >= 2)
     def _():
-        keep_ref[0] = term
+        for n, term in enumerate(terms):
+            keep_ref[0, n * size:(n + 1) * size] = term
 
 
 def input_terms(place, back, mate, w_value):
     depth, channels = w_value.shape
     rows, span = depth // 4, 256
-    return call(
-        input_kernel, "input_terms", 2 * span * depth * channels, 12_000_000, vmem=24,
+
+    def stream(n):
+        return pl.BlockSpec(
+            (rows // STREAMS, channels),
+            lambda i, place: (STREAMS * (place[1] ^ ((2 * i + 1 - i // 2) % 4)) + n, 0))
+
+    return call(
+        input_kernel, "input_terms", 2 * span * depth * channels, 12_000_000, vmem=56,
         grid_spec=pltpu.PrefetchScalarGridSpec(
             num_scalar_prefetch=1, grid=(4,),
             in_specs=[pl.BlockSpec((channels // 2, span), lambda i, place: (0, place[0])),
-                      pl.BlockSpec((channels // 2, span), lambda i, place: (0, 0)),
-                      pl.BlockSpec((rows, channels), lambda i, place: (place[1] ^ ((2 * i + 1 - i // 2) % 4), 0))],
+                      pl.BlockSpec((channels // 2, span), lambda i, place: (0, 0))] + [stream(n) for n in range(STREAMS)],
             out_specs=[pl.BlockSpec((1, rows, span), lambda i, place: (jnp.minimum(i, 1), 0, 0)),
                        pl.BlockSpec((1, rows, span), lambda i, place: (jnp.maximum(i - 2, 0), 0, 0))],
             scratch_shapes=[pltpu.VMEM((channels, span), jnp.bfloat16)]),
         out_shape=[jax.ShapeDtypeStruct((2, rows, span), jnp.bfloat16),
                    jax.ShapeDtypeStruct((2, rows, span), jnp.float32)],
-    )(place, back, mate, w_value)
+    )(place, back, mate, *[w_value] * STREAMS)
 
 
 def close_kernel(keep_ref, core_ref, chip_ref, out_ref):
@@ -523,7 +572,7 @@
         grid_spec=pltpu.PrefetchScalarGridSpec(
             num_scalar_prefetch=1, grid=(4,),
             in_specs=[pl.BlockSpec((LANES, span), lambda i, place: (i, 4 + place[0] // 2)),
-                      pl.BlockSpec((LANES, span), lambda i, place: (i, 1)), block, block],
+                      pl.BlockSpec((LANES, span), lambda i, place: (i, 0)), block, block],
             out_specs=block),
         out_shape=jax.ShapeDtypeStruct(gate.shape, jnp.bfloat16))(place, back, mate, gate, grads)
 
@@ -534,7 +583,7 @@
     span, depth = layer_in.shape
     channels = w_value.shape[1]
     width = channels // seq_count
-    quad_at = seq_at % 4
+    quad_at = quad_place()
     place = jnp.stack([quad_at, tp_at]).astype(jnp.int32)
     cores, chips = [(0, 1), (1, 0), (2, 3), (3, 2)], [(0, 2), (2, 0), (1, 3), (3, 1)]
 
@@ -542,16 +591,22 @@
         return lax.all_to_all(
             value, "seq", split_axis=0, concat_axis=0, axis_index_groups=index_groups, tiled=True)
 
-    def mates(value, step):
-        return lax.ppermute(value, "seq", [(s, s ^ step) for s in range(seq_count)])
+    def mates(value):
+        return lax.ppermute(value, "seq", [(s, s ^ MATE) for s in range(seq_count)])
 
     outgoing = sends(layer_in, w_value, gate_proj, grad_out, seq_count)
     rows_in, outgoing = lax.optimization_barrier((layer_in, outgoing))
     arrived = exchange(outgoing)
     same, cross, other = quarters_of(place, rows_in)
-    mine = [same, mates(cross, 1), mates(same, 2), mates(cross, 3)]
+    spectra = spectra_of(long_filters)
+    same, cross, spectra = lax.optimization_barrier((same, cross, spectra))
+
+    def across(value, flip):
+        return lax.ppermute(
+            value, ("seq", "tp"), [(4 * s + t, 4 * (s ^ flip) + (t ^ 2)) for s in range(seq_count) for t in range(4)])
+
+    mine = [same, across(cross, 1), mates(same), across(cross, 1 ^ MATE)]
     other = [other] + [lax.ppermute(part, "tp", cores) for part in mine[1:]]
-    spectra = spectra_of(long_filters)
 
     own_taps = lax.dynamic_slice_in_dim(short_taps, seq_at * width, width, 1)
     back, lag = mixer(own_taps, arrived, spectra)
@@ -559,18 +614,21 @@
     back = exchange(back, LEAGUES).reshape(channels // 2, back.shape[2])
     grad_filters = filter_grads(lag)
     back, grad_filters, other = lax.optimization_barrier((back, grad_filters, other))
-    mate = mates(jnp.concatenate([
-        lax.dynamic_slice_in_dim(back, (quad_at ^ 2) * span, span, 1),
-        lax.dynamic_slice_in_dim(back, 4 * span + (1 - quad_at // 2) * span, span, 1),
-        back[:, 6 * span:]], axis=1), 2)
-
-    parts = exchange(shares(place, back, mine, other), PLANES)
+    mate = mates(lax.dynamic_slice_in_dim(back, (quad_at ^ 2) * span, span, 1))
+    mate_rest = jnp.concatenate([
+        lax.dynamic_slice_in_dim(back, 4 * span + (1 - quad_at // 2) * span, span, 1), back[:, 6 * span:]], axis=1)
+    outgoing = shares(back, mine, other)
+    outgoing, mate, mate_rest = lax.optimization_barrier((outgoing, mate, mate_rest))
+    mate_rest = mates(mate_rest)
+    parts = exchange(outgoing, PLANES)
+
     send, keep = input_terms(place, back, mate, w_value)
     core = lax.ppermute(send, "tp", cores)
     chip = lax.ppermute((keep[1] + core[1].astype(jnp.float32)).astype(jnp.bfloat16), "tp", chips)
     grad_input = close_input(keep, core, chip)
-    grad_gate = gate_grad(place, back, mate, gate_proj, grad_out)
-    grad_weight, grad_taps = close_weight(place, parts, back, mate)
+    grad_gate = gate_grad(place, back, mate_rest, gate_proj, grad_out)
+    parts, grad_input, grad_gate = lax.optimization_barrier((parts, grad_input, grad_gate))
+    grad_weight, grad_taps = close_weight(parts, back, mate_rest)
     return (grad_input, grad_weight, grad_taps, grad_filters, grad_gate)
 
 

time: 157 us -> 149 us (0.949)
  the two profiles are of different devices: /device:TPU:14 before, /device:TPU:0 now
where the time goes in v2:
time: 149 us; the launch traced here: 147 us
  Pallas kernels  63.1 us (42%)
  waiting for transfers between devices  38.8 us (26%)
  starting transfers between devices  36.1 us (24%)
  local copies, waits for them, and re-layouts  5.62 us (4%)
  other arithmetic  2.2 us (1%)
    all_to_all x3, starting transfers between devices, exchange(): lax.all_to_all(value, 'seq', split_axis=0, concat_axis=0, axis_index_grou...  21.1 us
    pallas_call x1, Pallas kernels, mixer(): call(mixer_kernel, 'mixer', 3000000000, 8000000, vmem=56, grid=(width //...  18.2 us
    all_to_all x3, waiting for transfers between devices, exchange(): lax.all_to_all(value, 'seq', split_axis=0, concat_axis=0, axis_index_grou...  18.2 us
    ppermute x3, waiting for transfers between devices, mates(): return lax.ppermute(value, 'seq', [(s, s ^ MATE) for s in range(seq_count)])  14.8 us
    pallas_call x1, Pallas kernels, spectra_of(): call(spectra_kernel, 'spectra', 3000000000, 5000000, vmem=56, grid=(width...  8.8 us
    ppermute x3, starting transfers between devices, mates(): return lax.ppermute(value, 'seq', [(s, s ^ MATE) for s in range(seq_count)])  8.63 us
    pallas_call x1, Pallas kernels, input_terms(): call(input_kernel, 'input_terms', 2 * span * depth * channels, 12000000,...  7.99 us
    pallas_call x1, Pallas kernels, sends(): call(send_kernel, 'sends', 2 * span * depth * channels, 12500000, vmem=56...  7.35 us
  transfers between devices with their start and end apart: 13, of which 5 were waited for; matrix products, arithmetic and copies ran while one was open for 2% of the time, Pallas kernels for 36%

profile of v2, /device:TPU:0, one launch (start us, length us, event | category | flops | bytes accessed | tf_op | source)
XLA Modules:
  0.0 146.7 jit_solution(15429347234832872855)
XLA Ops:
  0.6 0.0 copy-start
  0.6 7.4 %sends.1 = bf16[32,64,256]{2,1,0:T(8,128)(2,1)} custom-call(bf16[256,4096]{1,0:T(8,128)(2,1)} %others_ref, bf16[4096,1024]{1,0:T(8,128)(2,1)} %refs_3_.3, bf16[4096,1024]{1,0:T(8,128)(2,1)} %refs_3_.3, bf16[4096,1024]{1,0:T(8,128)(2,1)} %refs_3_.3, bf16[4096,1024]{1,0:T(8,128)(2,1)} %refs_3_.3, bf16[256,1024]{1,0:T(8,128)(2,1)} %gate_ref.1, ...), custom_call_target="tpu_custom_call" | custom-call | flops 2147483648 | bytes 12500000 | tf_op jit(solution)/shard_map/sends/pallas_call | solution.py:381
  8.0 11.0 %all-to-all-start = ((bf16[32,64,256]{2,1,0:T(8,128)(2,1)}), bf16[32,64,256]{2,1,0:T(8,128)(2,1)}, u32[]{:S(2)}, u32[]{:S(2)}) async-start(bf16[32,64,256]{2,1,0:T(8,128)(2,1)} %sends.1), calls=%async_computation | async-start | bytes 2097152 | tf_op jit(solution)/shard_map/all_to_all | solution.py:591
  19.0 0.1 pad_add_fusion.place_ref
  19.1 2.0 %quarters.1 = (bf16[256,1024]{1,0:T(8,128)(2,1)S(1)}, bf16[256,1024]{1,0:T(8,128)(2,1)}, bf16[256,1024]{1,0:T(8,128)(2,1)S(1)}) custom-call(s32[2]{0:T(128)S(1)} %pad_add_fusion.place_ref, bf16[256,4096]{1,0:T(8,128)(2,1)S(1)} %copy-done.3, bf16[256,4096]{1,0:T(8,128)(2,1)S(1)} %copy-done.3), custom_call_target="tpu_custom_call" | custom-call | bytes 5000000 | tf_op jit(solution)/shard_map/quarters/pallas_call | solution.py:403
  21.1 8.8 %spectra.1.spectra_ref = f32[2048,256]{1,0:T(8,128)} custom-call(f32[2,4,512,128]{3,2,1,0:T(8,128)} %bitcast.21, bf16[128,256]{1,0:T(8,128)(2,1)} %constant.77.clone.first_nat_ref, f32[2,64,128]{2,1,0:T(8,128)} %constant.78.clone.twist_ref, bf16[1536,256]{1,0:T(8,128)(2,1)} %constant.79.clone.pair_ref), custom_call_target="tpu_custom_call" | custom-call | flops 3000000000 | bytes 5000000 | tf_op jit(solution)/shard_map/spectra/pallas_call | solution.py:293
  29.9 3.4 %collective-permute-start = (bf16[256,1024]{1,0:T(8,128)(2,1)}, bf16[256,1024]{1,0:T(8,128)(2,1)S(1)}, u32[]{:S(2)}, u32[]{:S(2)}) collective-permute-start(bf16[256,1024]{1,0:T(8,128)(2,1)} %get-tuple-element.43), channel_id=1, source_target_pairs={{0,6},{1,7},{2,4},{3,5},{4,2},{5,3},{6,0},{7,1},{8,14},{9,15},{10,... | collective-permute-start | bytes 1572872 | tf_op jit(solution)/shard_map/ppermute | solution.py:605
  33.3 2.7 %collective-permute-start.1 = (bf16[256,1024]{1,0:T(8,128)(2,1)S(1)}, bf16[256,1024]{1,0:T(8,128)(2,1)S(1)}, u32[]{:S(2)}, u32[]{:S(2)}) collective-permute-start(bf16[256,1024]{1,0:T(8,128)(2,1)S(1)} %get-tuple-element.48.refs_0_), channel_id=1, source_target_pairs={{0,24},{4,28},{8,16},{12,20},{16,8},{20,12},{24,0},{28,4},{32,56},... | collective-permute-start | bytes 1572872 | tf_op jit(solution)/shard_map/ppermute | solution.py:595
  35.9 0.0 collective-permute-start.2
  36.0 0.7 constant_dynamic-slice_fusion.2.taps_ref
  36.6 1.5 %all-to-all-done.arrived_ref = bf16[32,64,256]{2,1,0:T(8,128)(2,1)} async-done(((bf16[32,64,256]{2,1,0:T(8,128)(2,1)}), bf16[32,64,256]{2,1,0:T(8,128)(2,1)}, u32[]{:S(2)}, u32[]{:S(2)}) %all-to-all-start) | async-done | bytes 1048608 | tf_op jit(solution)/shard_map/all_to_all | solution.py:591
  38.1 18.2 %mixer.1 = (bf16[16,32,1664]{2,1,0:T(8,128)(2,1)}, bf16[2048,512]{1,0:T(8,128)(2,1)}) custom-call(f32[7,32]{1,0:T(8,128)} %constant_dynamic-slice_fusion.2.taps_ref, bf16[32,64,256]{2,1,0:T(8,128)(2,1)} %all-to-all-done.arrived_ref, f32[2048,256]{1,0:T(8,128)} %spectra.1.spectra_ref, bf16[128,128]{1,0:T(8,128)(2,1)} %constant.80.clone.first_split_ref, ...), custom_call_target="tpu_custom_call" | custom-call | flops 3000000000 | bytes 8000000 | tf_op jit(solution)/shard_map/mixer/pallas_call | solution.py:321
  56.3 0.0 collective-permute-done.refs_1_
  56.3 0.0 collective-permute-done.1.refs_2_
  56.4 0.0 copy-start.8
  56.4 2.9 %collective-permute-done.2.refs_3_ = bf16[256,1024]{1,0:T(8,128)(2,1)S(1)} collective-permute-done((bf16[256,1024]{1,0:T(8,128)(2,1)}, bf16[256,1024]{1,0:T(8,128)(2,1)S(1)}, u32[]{:S(2)}, u32[]{:S(2)}) %collective-permute-start.2) | collective-permute-done | bytes 524320 | tf_op jit(solution)/shard_map/ppermute | solution.py:605
  59.3 0.8 copy-done.10
  60.1 5.7 %all-to-all-start.1 = ((bf16[16,32,1664]{2,1,0:T(8,128)(2,1)}), bf16[16,32,1664]{2,1,0:T(8,128)(2,1)S(1)}, u32[]{:S(2)}, u32[]{:S(2)}) async-start(bf16[16,32,1664]{2,1,0:T(8,128)(2,1)} %get-tuple-element.44), calls=%async_computation.1 | async-start | bytes 3407872 | tf_op jit(solution)/shard_map/all_to_all | solution.py:591
  65.8 0.0 collective-permute-start.3
  65.8 0.5 collective-permute-start.4
  66.3 0.1 collective-permute-start.5
  66.4 1.1 copy-done.14
  67.5 1.6 %copy-done.17 = bf16[2048,512]{1,0:T(8,128)(2,1)S(1)} copy-done((bf16[2048,512]{1,0:T(8,128)(2,1)S(1)}, bf16[2048,512]{1,0:T(8,128)(2,1)}, u32[]{:S(2)}) %copy-start.17) | copy-done | bytes 2097176
  69.1 6.2 %filter_grads.1 = f32[2,4,512,128]{3,2,1,0:T(8,128)} custom-call(bf16[2048,512]{1,0:T(8,128)(2,1)S(1)} %copy-done.17, f32[2,64,128]{2,1,0:T(8,128)S(1)} %copy-done.15, bf16[768,512]{1,0:T(8,128)(2,1)S(1)} %copy-done.14, bf16[64,384]{1,0:T(8,128)(2,1)S(1)} %copy-done.16), custom_call_target="tpu_custom_call" | custom-call | flops 3000000000 | bytes 5000000 | tf_op jit(solution)/shard_map/filter_grads/pallas_call | solution.py:306
  75.3 0.0 collective-permute-done.3.refs_5_
  75.3 0.0 collective-permute-done.4.refs_6_
  75.3 0.0 collective-permute-done.5.refs_7_
  75.3 16.7 %all-to-all-done.1 = bf16[16,32,1664]{2,1,0:T(8,128)(2,1)S(1)} async-done(((bf16[16,32,1664]{2,1,0:T(8,128)(2,1)}), bf16[16,32,1664]{2,1,0:T(8,128)(2,1)S(1)}, u32[]{:S(2)}, u32[]{:S(2)}) %all-to-all-start.1) | async-done | bytes 1703968 | tf_op jit(solution)/shard_map/all_to_all | solution.py:591
  92.2 3.0 %collective-permute-start.6 = (bf16[512,256]{1,0:T(8,128)(2,1)S(1)}, bf16[512,256]{1,0:T(8,128)(2,1)}, u32[]{:S(2)}, u32[]{:S(2)}) collective-permute-start(bf16[512,256]{1,0:T(8,128)(2,1)S(1)} %get-tuple-element.68), channel_id=1, source_target_pairs={{0,24},{4,28},{8,16},{12,20},{16,8},{20,12},{24,0},{28,4},{32,56},... | collective-permute-start | bytes 786440 | tf_op jit(solution)/shard_map/ppermute | solution.py:595
  95.1 0.8 pad_maximum_fusion
  95.9 6.2 %shares.1 = bf16[16,512,128]{2,1,0:T(8,128)(2,1)S(1)} custom-call(bf16[512,1664]{1,0:T(8,128)(2,1)S(1)} %bitcast.17, bf16[256,1024]{1,0:T(8,128)(2,1)S(1)} %get-tuple-element.48.refs_0_, bf16[256,1024]{1,0:T(8,128)(2,1)S(1)} %collective-permute-done.refs_1_, bf16[256,1024]{1,0:T(8,128)(2,1)S(1)} %copy-done.9, bf16[256,1024]{1,0:T(8,128)(2,1)S(1)} %copy-done.11, ...), custom_call_target="tpu_custom_call" | custom-call | flops 2147483648 | bytes 7000000 | tf_op jit(solution)/shard_map/shares/pallas_call | solution.py:454
  102.2 1.3 copy-done.4
  103.5 0.0 collective-permute-done.6.mate_ref
  103.5 4.4 %all-to-all-start.2 = ((bf16[16,512,128]{2,1,0:T(8,128)(2,1)}), bf16[16,512,128]{2,1,0:T(8,128)(2,1)}, u32[]{:S(2)}, u32[]{:S(2)}) async-start(bf16[16,512,128]{2,1,0:T(8,128)(2,1)} %copy-done.4), calls=%async_computation.2 | async-start | bytes 4194304 | tf_op jit(solution)/shard_map/all_to_all | solution.py:591
  107.9 0.0 copy-start.6
  107.9 0.0 copy-start.7
  107.9 8.0 %input_terms.1 = (bf16[2,1024,256]{2,1,0:T(8,128)(2,1)}, f32[2,1024,256]{2,1,0:T(8,128)}) custom-call(s32[2]{0:T(128)} %copy-done.12, bf16[512,1664]{1,0:T(8,128)(2,1)} %bitcast.18, bf16[512,256]{1,0:T(8,128)(2,1)} %collective-permute-done.6.mate_ref, bf16[4096,1024]{1,0:T(8,128)(2,1)} %refs_3_.3, bf16[4096,1024]{1,0:T(8,128)(2,1)} %refs_3_.3, ...), custom_call_target="tpu_custom_call" | custom-call | flops 2147483648 | bytes 12000000 | tf_op jit(solution)/shard_map/input_terms/pallas_call | solution.py:532
  116.0 0.1 collective-permute-start.7
  116.1 2.9 %collective-permute-done.7.core_ref = bf16[2,1024,256]{2,1,0:T(8,128)(2,1)S(1)} collective-permute-done((bf16[2,1024,256]{2,1,0:T(8,128)(2,1)}, bf16[2,1024,256]{2,1,0:T(8,128)(2,1)S(1)}, u32[]{:S(2)}, u32[]{:S(2)}) %collective-permute-start.7) | collective-permute-done | bytes 1048608 | tf_op jit(solution)/shard_map/ppermute | solution.py:626
  118.9 1.3 fusion
  120.3 2.3 %collective-permute-start.8 = (bf16[1024,256]{1,0:T(8,128)(2,1)S(1)}, bf16[1024,256]{1,0:T(8,128)(2,1)S(1)}, u32[]{:S(2)}, u32[]{:S(2)}) collective-permute-start(bf16[1024,256]{1,0:T(8,128)(2,1)S(1)} %fusion), channel_id=1, source_target_pairs={{0,2},{2,0},{1,3},{3,1},{4,6},{6,4},{5,7},{7,5},{8,10},{10,8},{9,1... | collective-permute-start | bytes 1572872 | tf_op jit(solution)/shard_map/ppermute | solution.py:627
  122.6 3.0 %collective-permute-start.9 = (bf16[512,384]{1,0:T(8,128)(2,1)S(1)}, bf16[512,384]{1,0:T(8,128)(2,1)S(1)}, u32[]{:S(2)}, u32[]{:S(2)}) collective-permute-start(bf16[512,384]{1,0:T(8,128)(2,1)S(1)} %copy-done.18), channel_id=1, source_target_pairs={{0,24},{4,28},{8,16},{12,20},{16,8},{20,12},{24,0},{28,4},{32,56},... | collective-permute-start | bytes 1179656 | tf_op jit(solution)/shard_map/ppermute | solution.py:595
  125.5 14.8 %collective-permute-done.9.mate_ref = bf16[512,384]{1,0:T(8,128)(2,1)S(1)} collective-permute-done((bf16[512,384]{1,0:T(8,128)(2,1)S(1)}, bf16[512,384]{1,0:T(8,128)(2,1)S(1)}, u32[]{:S(2)}, u32[]{:S(2)}) %collective-permute-start.9) | collective-permute-done | bytes 393248 | tf_op jit(solution)/shard_map/ppermute | solution.py:595
  140.3 2.6 %gate_grad.1 = bf16[256,1024]{1,0:T(8,128)(2,1)} custom-call(s32[2]{0:T(128)S(1)} %copy-done.13, bf16[512,1664]{1,0:T(8,128)(2,1)S(1)} %bitcast.19, bf16[512,384]{1,0:T(8,128)(2,1)S(1)} %collective-permute-done.9.mate_ref, bf16[256,1024]{1,0:T(8,128)(2,1)S(1)} %copy-done.6, bf16[256,1024]{1,0:T(8,128)(2,1)S(1)} %copy-done.7), custom_call_target="tpu_custom_call" | custom-call | flops 2000000 | bytes 2500000 | tf_op jit(solution)/shard_map/gate_grad/pallas_call | solution.py:570
  142.9 0.0 collective-permute-done.8.chip_ref
  142.9 1.0 close_input.1
  143.9 0.0 all-to-all-done.2.shares_ref
  143.9 2.8 %close_weight.1 = (f32[128,1024]{1,0:T(8,128)}, f32[7,1024]{1,0:T(8,128)}) custom-call(bf16[16,512,128]{2,1,0:T(8,128)(2,1)} %all-to-all-done.2.shares_ref, bf16[512,1664]{1,0:T(8,128)(2,1)S(1)} %bitcast.20, bf16[512,384]{1,0:T(8,128)(2,1)S(1)} %collective-permute-done.9.mate_ref), custom_call_target="tpu_custom_call" | custom-call | flops 2000000 | bytes 3000000 | tf_op jit(solution)/shard_map/close_weight/pallas_call | solution.py:487
  (32 shorter events, 0.1 us)
Async XLA Ops:
  0.6 35.3 %copy-start = (f32[7,1024]{1,0:T(8,128)S(1)}, f32[7,1024]{1,0:T(8,128)}, u32[]{:S(2)}) copy-start(f32[7,1024]{1,0:T(8,128)} %param.17) | copy-start | bytes 86020
  8.0 11.1 %copy-start.3 = (bf16[256,4096]{1,0:T(8,128)(2,1)S(1)}, bf16[256,4096]{1,0:T(8,128)(2,1)}, u32[]{:S(2)}) copy-start(bf16[256,4096]{1,0:T(8,128)(2,1)} %others_ref) | copy-start | bytes 6291460
  8.0 30.1 %all-to-all-start = ((bf16[32,64,256]{2,1,0:T(8,128)(2,1)}), bf16[32,64,256]{2,1,0:T(8,128)(2,1)}, u32[]{:S(2)}, u32[]{:S(2)}) async-start(bf16[32,64,256]{2,1,0:T(8,128)(2,1)} %sends.1), calls=%async_computation | async-start | bytes 2097152 | tf_op jit(solution)/shard_map/all_to_all | solution.py:591
  19.1 2.0 %copy-start.12 = (s32[2]{0:T(128)}, s32[2]{0:T(128)S(1)}, u32[]{:S(2)}) copy-start(s32[2]{0:T(128)S(1)} %pad_add_fusion.place_ref) | copy-start | bytes 28
  29.9 26.5 %collective-permute-start = (bf16[256,1024]{1,0:T(8,128)(2,1)}, bf16[256,1024]{1,0:T(8,128)(2,1)S(1)}, u32[]{:S(2)}, u32[]{:S(2)}) collective-permute-start(bf16[256,1024]{1,0:T(8,128)(2,1)} %get-tuple-element.43), channel_id=1, source_target_pairs={{0,6},{1,7},{2,4},{3,5},{4,2},{5,3},{6,0},{7,1},{8,14},{9,15},{10,... | collective-permute-start | bytes 1572872 | tf_op jit(solution)/shard_map/ppermute | solution.py:605
  33.3 23.1 %collective-permute-start.1 = (bf16[256,1024]{1,0:T(8,128)(2,1)S(1)}, bf16[256,1024]{1,0:T(8,128)(2,1)S(1)}, u32[]{:S(2)}, u32[]{:S(2)}) collective-permute-start(bf16[256,1024]{1,0:T(8,128)(2,1)S(1)} %get-tuple-element.48.refs_0_), channel_id=1, source_target_pairs={{0,24},{4,28},{8,16},{12,20},{16,8},{20,12},{24,0},{28,4},{32,56},... | collective-permute-start | bytes 1572872 | tf_op jit(solution)/shard_map/ppermute | solution.py:595
  35.9 23.4 %collective-permute-start.2 = (bf16[256,1024]{1,0:T(8,128)(2,1)}, bf16[256,1024]{1,0:T(8,128)(2,1)S(1)}, u32[]{:S(2)}, u32[]{:S(2)}) collective-permute-start(bf16[256,1024]{1,0:T(8,128)(2,1)} %get-tuple-element.43), channel_id=1, source_target_pairs={{0,30},{1,31},{2,28},{3,29},{4,26},{5,27},{6,24},{7,25},{8,22},{9,... | collective-permute-start | bytes 1572872 | tf_op jit(solution)/shard_map/ppermute | solution.py:605
  56.3 10.1 %copy-start.15 = (f32[2,64,128]{2,1,0:T(8,128)S(1)}, f32[2,64,128]{2,1,0:T(8,128)}, u32[]{:S(2)}) copy-start(f32[2,64,128]{2,1,0:T(8,128)} %constant.78.clone.twist_ref) | copy-start | bytes 196612
  56.3 10.1 %copy-start.16 = (bf16[64,384]{1,0:T(8,128)(2,1)S(1)}, bf16[64,384]{1,0:T(8,128)(2,1)}, u32[]{:S(2)}) copy-start(bf16[64,384]{1,0:T(8,128)(2,1)} %constant.85.clone.last_nat_ref) | copy-start | bytes 147460
  56.4 2.9 %copy-start.8 = (bf16[256,1024]{1,0:T(8,128)(2,1)}, bf16[256,1024]{1,0:T(8,128)(2,1)S(1)}, u32[]{:S(2)}) copy-start(bf16[256,1024]{1,0:T(8,128)(2,1)S(1)} %collective-permute-done.1.refs_2_) | copy-start | bytes 1572868
  59.3 0.8 copy-start.10
  60.1 32.0 %all-to-all-start.1 = ((bf16[16,32,1664]{2,1,0:T(8,128)(2,1)}), bf16[16,32,1664]{2,1,0:T(8,128)(2,1)S(1)}, u32[]{:S(2)}, u32[]{:S(2)}) async-start(bf16[16,32,1664]{2,1,0:T(8,128)(2,1)} %get-tuple-element.44), calls=%async_computation.1 | async-start | bytes 3407872 | tf_op jit(solution)/shard_map/all_to_all | solution.py:591
  65.8 9.5 %collective-permute-start.3 = (bf16[256,1024]{1,0:T(8,128)(2,1)S(1)}, bf16[256,1024]{1,0:T(8,128)(2,1)}, u32[]{:S(2)}, u32[]{:S(2)}) collective-permute-start(bf16[256,1024]{1,0:T(8,128)(2,1)S(1)} %collective-permute-done.refs_1_), channel_id=1, source_target_pairs={{0,1},{1,0},{2,3},{3,2},{4,5},{5,4},{6,7},{7,6},{8,9},{9,8},{10,11... | collective-permute-start | bytes 1572872 | tf_op jit(solution)/shard_map/ppermute | solution.py:609
  65.8 9.5 %collective-permute-start.4 = (bf16[256,1024]{1,0:T(8,128)(2,1)}, bf16[256,1024]{1,0:T(8,128)(2,1)}, u32[]{:S(2)}, u32[]{:S(2)}) collective-permute-start(bf16[256,1024]{1,0:T(8,128)(2,1)} %copy-done.8), channel_id=1, source_target_pairs={{0,1},{1,0},{2,3},{3,2},{4,5},{5,4},{6,7},{7,6},{8,9},{9,8},{10,11... | collective-permute-start | bytes 1572872 | tf_op jit(solution)/shard_map/ppermute | solution.py:609
  66.3 9.0 %collective-permute-start.5 = (bf16[256,1024]{1,0:T(8,128)(2,1)}, bf16[256,1024]{1,0:T(8,128)(2,1)}, u32[]{:S(2)}, u32[]{:S(2)}) collective-permute-start(bf16[256,1024]{1,0:T(8,128)(2,1)} %copy-done.10), channel_id=1, source_target_pairs={{0,1},{1,0},{2,3},{3,2},{4,5},{5,4},{6,7},{7,6},{8,9},{9,8},{10,11... | collective-permute-start | bytes 1572872 | tf_op jit(solution)/shard_map/ppermute | solution.py:609
  66.4 1.1 copy-start.14
  67.5 1.6 %copy-start.17 = (bf16[2048,512]{1,0:T(8,128)(2,1)S(1)}, bf16[2048,512]{1,0:T(8,128)(2,1)}, u32[]{:S(2)}) copy-start(bf16[2048,512]{1,0:T(8,128)(2,1)} %get-tuple-element.45.lag_ref) | copy-start | bytes 6291460
  92.1 10.1 %copy-start.1 = (bf16[16,32,1664]{2,1,0:T(8,128)(2,1)}, bf16[16,32,1664]{2,1,0:T(8,128)(2,1)S(1)}, u32[]{:S(2)}) copy-start(bf16[16,32,1664]{2,1,0:T(8,128)(2,1)S(1)} %all-to-all-done.1) | copy-start | bytes 5111812
  92.1 3.8 %copy-start.9 = (bf16[256,1024]{1,0:T(8,128)(2,1)S(1)}, bf16[256,1024]{1,0:T(8,128)(2,1)}, u32[]{:S(2)}) copy-start(bf16[256,1024]{1,0:T(8,128)(2,1)} %copy-done.8) | copy-start | bytes 1572868
  92.1 3.8 %copy-start.11 = (bf16[256,1024]{1,0:T(8,128)(2,1)S(1)}, bf16[256,1024]{1,0:T(8,128)(2,1)}, u32[]{:S(2)}) copy-start(bf16[256,1024]{1,0:T(8,128)(2,1)} %copy-done.10) | copy-start | bytes 1572868
  92.2 11.3 %collective-permute-start.6 = (bf16[512,256]{1,0:T(8,128)(2,1)S(1)}, bf16[512,256]{1,0:T(8,128)(2,1)}, u32[]{:S(2)}, u32[]{:S(2)}) collective-permute-start(bf16[512,256]{1,0:T(8,128)(2,1)S(1)} %get-tuple-element.68), channel_id=1, source_target_pairs={{0,24},{4,28},{8,16},{12,20},{16,8},{20,12},{24,0},{28,4},{32,56},... | collective-permute-start | bytes 786440 | tf_op jit(solution)/shard_map/ppermute | solution.py:595
  102.2 1.3 copy-start.4
  103.5 40.4 %all-to-all-start.2 = ((bf16[16,512,128]{2,1,0:T(8,128)(2,1)}), bf16[16,512,128]{2,1,0:T(8,128)(2,1)}, u32[]{:S(2)}, u32[]{:S(2)}) async-start(bf16[16,512,128]{2,1,0:T(8,128)(2,1)} %copy-done.4), calls=%async_computation.2 | async-start | bytes 4194304 | tf_op jit(solution)/shard_map/all_to_all | solution.py:591
  107.9 32.4 %copy-start.6 = (bf16[256,1024]{1,0:T(8,128)(2,1)S(1)}, bf16[256,1024]{1,0:T(8,128)(2,1)}, u32[]{:S(2)}) copy-start(bf16[256,1024]{1,0:T(8,128)(2,1)} %gate_ref.1) | copy-start | bytes 1572868
  107.9 32.4 %copy-start.7 = (bf16[256,1024]{1,0:T(8,128)(2,1)S(1)}, bf16[256,1024]{1,0:T(8,128)(2,1)}, u32[]{:S(2)}) copy-start(bf16[256,1024]{1,0:T(8,128)(2,1)} %grad_ref.1) | copy-start | bytes 1572868
  115.9 6.6 %copy-start.18 = (bf16[512,384]{1,0:T(8,128)(2,1)S(1)}, bf16[512,384]{1,0:T(8,128)(2,1)}, u32[]{:S(2)}) copy-start(bf16[512,384]{1,0:T(8,128)(2,1)} %pad_maximum_fusion) | copy-start | bytes 1179652
  115.9 24.4 %copy-start.2 = (bf16[16,32,1664]{2,1,0:T(8,128)(2,1)S(1)}, bf16[16,32,1664]{2,1,0:T(8,128)(2,1)}, u32[]{:S(2)}) copy-start(bf16[16,32,1664]{2,1,0:T(8,128)(2,1)} %copy-done.1) | copy-start | bytes 5111812
  116.0 24.4 %copy-start.13 = (s32[2]{0:T(128)S(1)}, s32[2]{0:T(128)}, u32[]{:S(2)}) copy-start(s32[2]{0:T(128)} %copy-done.12) | copy-start | bytes 28
  116.0 3.0 %collective-permute-start.7 = (bf16[2,1024,256]{2,1,0:T(8,128)(2,1)}, bf16[2,1024,256]{2,1,0:T(8,128)(2,1)S(1)}, u32[]{:S(2)}, u32[]{:S(2)}) collective-permute-start(bf16[2,1024,256]{2,1,0:T(8,128)(2,1)} %get-tuple-element.59), channel_id=1, source_target_pairs={{0,1},{1,0},{2,3},{3,2},{4,5},{5,4},{6,7},{7,6},{8,9},{9,8},{10,11... | collective-permute-start | bytes 3145736 | tf_op jit(solution)/shard_map/ppermute | solution.py:626
  120.3 22.6 %copy-start.5 = (f32[2,1024,256]{2,1,0:T(8,128)S(1)}, f32[2,1024,256]{2,1,0:T(8,128)}, u32[]{:S(2)}) copy-start(f32[2,1024,256]{2,1,0:T(8,128)} %get-tuple-element.58.keep_ref) | copy-start | bytes 6291460
  120.3 22.6 %collective-permute-start.8 = (bf16[1024,256]{1,0:T(8,128)(2,1)S(1)}, bf16[1024,256]{1,0:T(8,128)(2,1)S(1)}, u32[]{:S(2)}, u32[]{:S(2)}) collective-permute-start(bf16[1024,256]{1,0:T(8,128)(2,1)S(1)} %fusion), channel_id=1, source_target_pairs={{0,2},{2,0},{1,3},{3,1},{4,6},{6,4},{5,7},{7,5},{8,10},{10,8},{9,1... | collective-permute-start | bytes 1572872 | tf_op jit(solution)/shard_map/ppermute | solution.py:627
  122.6 17.7 %collective-permute-start.9 = (bf16[512,384]{1,0:T(8,128)(2,1)S(1)}, bf16[512,384]{1,0:T(8,128)(2,1)S(1)}, u32[]{:S(2)}, u32[]{:S(2)}) collective-permute-start(bf16[512,384]{1,0:T(8,128)(2,1)S(1)} %copy-done.18), channel_id=1, source_target_pairs={{0,24},{4,28},{8,16},{12,20},{16,8},{20,12},{24,0},{28,4},{32,56},... | collective-permute-start | bytes 1179656 | tf_op jit(solution)/shard_map/ppermute | solution.py:595

commit v3 on v2

--- a/solution.py
+++ b/solution.py
@@ -16,7 +16,7 @@
 TAPS = 7
 REACH = TAPS // 2
 BATCH = 4
-GROUP, GROUPS = 2, 4
+GROUP, GROUPS = 2, 8
 
 
 def halves(table):
@@ -319,7 +319,7 @@
     back_shape = (blocks // 2, width, 6 * span + LANES)
     rows, batch = (2, blocks * width, LANES), GROUP * GROUPS
     return call(
-        mixer_kernel, "mixer", 3_000_000_000, 8_000_000, vmem=56,
+        mixer_kernel, "mixer", 100_000_000, 1_000_000, vmem=56,
         grid=(width // batch,),
         in_specs=[pl.BlockSpec(memory_space=pltpu.SMEM), whole(arrived.shape),
                   pl.BlockSpec((batch * ROWS, 2 * LANES), lambda i: (i, 0))] + specs,
@@ -452,7 +452,7 @@
     span, depth = mine[0].shape
     rows = back.shape[0]
     return call(
-        share_kernel, "shares", 16 * rows * span * depth, 7_000_000, vmem=32,
+        share_kernel, "shares", 16 * rows * span * depth, 7_000_000, vmem=60,
         in_specs=[pl.BlockSpec(memory_space=pl.ANY)] * 9,
         out_specs=pl.BlockSpec(memory_space=pl.ANY),
         out_shape=jax.ShapeDtypeStruct((16, rows, LANES), jnp.bfloat16),
@@ -487,60 +487,71 @@
     return call(
         weight_kernel, "close_weight", 2_000_000, 3_000_000, grid=(1,),
         in_specs=[whole(parts.shape),
-                  pl.BlockSpec((rows, LANES), lambda i: (0, 12)), pl.BlockSpec((rows, LANES), lambda i: (0, 2))],
+                  pl.BlockSpec((rows, LANES), lambda i: (0, 12)), pl.BlockSpec((rows, LANES), lambda i: (0, 4))],
         out_specs=[whole((span, channels)), whole((TAPS, channels))],
         out_shape=[jax.ShapeDtypeStruct((span, channels), jnp.float32),
                    jax.ShapeDtypeStruct((TAPS, channels), jnp.float32)],
     )(parts, back, mate)
 
 
-def input_kernel(place_ref, back_ref, mate_ref, *refs):
-    weight_refs, (send_ref, keep_ref, own_buf) = refs[:STREAMS], refs[STREAMS:]
-
-    @pl.when(pl.program_id(0) == 0)
-    def _():
-        pair = place_ref[0] // 2
-        for x in range(4):
-            for odd, mine, other in ((0, 1 + pair, 2 - pair), (1, 3 * pair, 3 - 3 * pair)):
-                rows = slice((2 * x + odd) * 64, (2 * x + odd + 1) * 64)
-                own_buf[pl.ds(pl.multiple_of((4 * x + mine) * 64, 64), 64), :] = back_ref[rows, :]
-                own_buf[pl.ds(pl.multiple_of((4 * x + other) * 64, 64), 64), :] = mate_ref[rows, :]
-
-    size = weight_refs[0].shape[0]
-    terms = [dot(weight_ref[...], own_buf[...]) for weight_ref in weight_refs]
-
-    @pl.when(pl.program_id(0) < 2)
-    def _():
-        for n, term in enumerate(terms):
-            send_ref[0, n * size:(n + 1) * size] = term.astype(jnp.bfloat16)
-
-    @pl.when(pl.program_id(0) >= 2)
-    def _():
-        for n, term in enumerate(terms):
-            keep_ref[0, n * size:(n + 1) * size] = term
-
-
-def input_terms(place, back, mate, w_value):
+def input_kernel(
+    back_ref, mate_ref, weight_ref, send_ref, keep_ref,
+    mine_buf, mate_buf, own_buf, weight_buf, send_buf, keep_buf, own_sem, weight_sem, out_sem,
+):
+    span, rows = mine_buf.shape[1], weight_buf.shape[1]
+    part = rows // STREAMS
+    at = quad_place()
+    own = [
+        pltpu.make_async_copy(
+            back_ref.at[:, pl.ds(pl.multiple_of(at * span, span), span)], mine_buf, own_sem.at[0]),
+        pltpu.make_async_copy(mate_ref.at[:, pl.ds(0, span)], mate_buf, own_sem.at[1]),
+    ]
+    loads = []
+    for n, flip in enumerate((1, 3, 0, 2)):
+        base = (lax.axis_index("tp") ^ flip) * rows
+        loads.append([
+            pltpu.make_async_copy(
+                weight_ref.at[pl.ds(pl.multiple_of(base + j * part, part), part)],
+                weight_buf.at[n, pl.ds(j * part, part)], weight_sem.at[n, j]) for j in range(STREAMS)])
+    for load in own + sum(loads, []):
+        load.start()
+    for load in own:
+        load.wait()
+    pair = at // 2
+    for x in range(4):
+        for odd, mine, other in ((0, 1 + pair, 2 - pair), (1, 3 * pair, 3 - 3 * pair)):
+            rows_in = slice((2 * x + odd) * 64, (2 * x + odd + 1) * 64)
+            own_buf[pl.ds(pl.multiple_of((4 * x + mine) * 64, 64), 64), :] = mine_buf[rows_in, :]
+            own_buf[pl.ds(pl.multiple_of((4 * x + other) * 64, 64), 64), :] = mate_buf[rows_in, :]
+    stores = []
+    for n in range(4):
+        for load in loads[n]:
+            load.wait()
+        term = dot(weight_buf[n], own_buf[...])
+        buf, ref = (send_buf, send_ref) if n < 2 else (keep_buf, keep_ref)
+        buf[n % 2] = term.astype(buf.dtype)
+        store = pltpu.make_async_copy(buf.at[n % 2], ref.at[n % 2], out_sem.at[n])
+        store.start()
+        stores.append(store)
+    for store in stores:
+        store.wait()
+
+
+def input_terms(back, mate, w_value):
     depth, channels = w_value.shape
     rows, span = depth // 4, 256
-
-    def stream(n):
-        return pl.BlockSpec(
-            (rows // STREAMS, channels),
-            lambda i, place: (STREAMS * (place[1] ^ ((2 * i + 1 - i // 2) % 4)) + n, 0))
-
+    anywhere = pl.BlockSpec(memory_space=pl.ANY)
     return call(
         input_kernel, "input_terms", 2 * span * depth * channels, 12_000_000, vmem=56,
-        grid_spec=pltpu.PrefetchScalarGridSpec(
-            num_scalar_prefetch=1, grid=(4,),
-            in_specs=[pl.BlockSpec((channels // 2, span), lambda i, place: (0, place[0])),
-                      pl.BlockSpec((channels // 2, span), lambda i, place: (0, 0))] + [stream(n) for n in range(STREAMS)],
-            out_specs=[pl.BlockSpec((1, rows, span), lambda i, place: (jnp.minimum(i, 1), 0, 0)),
-                       pl.BlockSpec((1, rows, span), lambda i, place: (jnp.maximum(i - 2, 0), 0, 0))],
-            scratch_shapes=[pltpu.VMEM((channels, span), jnp.bfloat16)]),
+        in_specs=[anywhere] * 3, out_specs=[anywhere] * 2,
         out_shape=[jax.ShapeDtypeStruct((2, rows, span), jnp.bfloat16),
                    jax.ShapeDtypeStruct((2, rows, span), jnp.float32)],
-    )(place, back, mate, *[w_value] * STREAMS)
+        scratch_shapes=[
+            pltpu.VMEM((channels // 2, span), jnp.bfloat16), pltpu.VMEM((channels // 2, span), jnp.bfloat16),
+            pltpu.VMEM((channels, span), jnp.bfloat16), pltpu.VMEM((4, rows, channels), jnp.bfloat16),
+            pltpu.VMEM((2, rows, span), jnp.bfloat16), pltpu.VMEM((2, rows, span), jnp.float32),
+            pltpu.SemaphoreType.DMA((2,)), pltpu.SemaphoreType.DMA((4, STREAMS)), pltpu.SemaphoreType.DMA((4,))],
+    )(back, mate, w_value)
 
 
 def close_kernel(keep_ref, core_ref, chip_ref, out_ref):
@@ -572,7 +583,7 @@
         grid_spec=pltpu.PrefetchScalarGridSpec(
             num_scalar_prefetch=1, grid=(4,),
             in_specs=[pl.BlockSpec((LANES, span), lambda i, place: (i, 4 + place[0] // 2)),
-                      pl.BlockSpec((LANES, span), lambda i, place: (i, 0)), block, block],
+                      pl.BlockSpec((LANES, span), lambda i, place: (i, 1)), block, block],
             out_specs=block),
         out_shape=jax.ShapeDtypeStruct(gate.shape, jnp.bfloat16))(place, back, mate, gate, grads)
 
@@ -598,37 +609,37 @@
     rows_in, outgoing = lax.optimization_barrier((layer_in, outgoing))
     arrived = exchange(outgoing)
     same, cross, other = quarters_of(place, rows_in)
-    spectra = spectra_of(long_filters)
-    same, cross, spectra = lax.optimization_barrier((same, cross, spectra))
 
     def across(value, flip):
         return lax.ppermute(
             value, ("seq", "tp"), [(4 * s + t, 4 * (s ^ flip) + (t ^ 2)) for s in range(seq_count) for t in range(4)])
 
-    mine = [same, across(cross, 1), mates(same), across(cross, 1 ^ MATE)]
-    other = [other] + [lax.ppermute(part, "tp", cores) for part in mine[1:]]
+    first = across(cross, 1)
+    spectra = spectra_of(long_filters)
+    same, cross, spectra = lax.optimization_barrier((same, cross, spectra))
+    mine = [same, first, mates(same), across(cross, 1 ^ MATE)]
 
     own_taps = lax.dynamic_slice_in_dim(short_taps, seq_at * width, width, 1)
     back, lag = mixer(own_taps, arrived, spectra)
     back, mine = lax.optimization_barrier((back, mine))
+    other = [other] + [lax.ppermute(part, "tp", cores) for part in mine[1:]]
     back = exchange(back, LEAGUES).reshape(channels // 2, back.shape[2])
     grad_filters = filter_grads(lag)
     back, grad_filters, other = lax.optimization_barrier((back, grad_filters, other))
-    mate = mates(lax.dynamic_slice_in_dim(back, (quad_at ^ 2) * span, span, 1))
-    mate_rest = jnp.concatenate([
-        lax.dynamic_slice_in_dim(back, 4 * span + (1 - quad_at // 2) * span, span, 1), back[:, 6 * span:]], axis=1)
-    outgoing = shares(back, mine, other)
-    outgoing, mate, mate_rest = lax.optimization_barrier((outgoing, mate, mate_rest))
-    mate_rest = mates(mate_rest)
-    parts = exchange(outgoing, PLANES)
-
-    send, keep = input_terms(place, back, mate, w_value)
+    mate = mates(jnp.concatenate([
+        lax.dynamic_slice_in_dim(back, (quad_at ^ 2) * span, span, 1),
+        lax.dynamic_slice_in_dim(back, 4 * span + (1 - quad_at // 2) * span, span, 1),
+        back[:, 6 * span:]], axis=1))
+    parts = exchange(shares(back, mine, other), PLANES)
+
+    send, keep = input_terms(back, mate, w_value)
     core = lax.ppermute(send, "tp", cores)
-    chip = lax.ppermute((keep[1] + core[1].astype(jnp.float32)).astype(jnp.bfloat16), "tp", chips)
+    send = (keep[1] + core[1].astype(jnp.float32)).astype(jnp.bfloat16)
+    chip = lax.ppermute(send, "tp", chips)
     grad_input = close_input(keep, core, chip)
-    grad_gate = gate_grad(place, back, mate_rest, gate_proj, grad_out)
+    grad_gate = gate_grad(place, back, mate, gate_proj, grad_out)
     parts, grad_input, grad_gate = lax.optimization_barrier((parts, grad_input, grad_gate))
-    grad_weight, grad_taps = close_weight(parts, back, mate_rest)
+    grad_weight, grad_taps = close_weight(parts, back, mate)
     return (grad_input, grad_weight, grad_taps, grad_filters, grad_gate)
 
 

time: 149 us -> 158 us (1.060)
  the two profiles are of different devices: /device:TPU:0 before, /device:TPU:14 now
where the time goes in v3:
time: 158 us
  Pallas kernels  62.7 us (40%)
  waiting for transfers between devices  48.9 us (31%)
  starting transfers between devices  36.5 us (23%)
  local copies, waits for them, and re-layouts  7.1 us (4%)
    all_to_all x3, starting transfers between devices, exchange(): lax.all_to_all(value, 'seq', split_axis=0, concat_axis=0, axis_index_grou...  26.4 us
    ppermute x2, waiting for transfers between devices, mates(): return lax.ppermute(value, 'seq', [(s, s ^ MATE) for s in range(seq_count)])  19.1 us
    pallas_call x1, Pallas kernels, mixer(): call(mixer_kernel, 'mixer', 100000000, 1000000, vmem=56, grid=(width // b...  17.7 us
    all_to_all x3, waiting for transfers between devices, exchange(): lax.all_to_all(value, 'seq', split_axis=0, concat_axis=0, axis_index_grou...  14.2 us
    pallas_call x1, Pallas kernels, input_terms(): call(input_kernel, 'input_terms', 2 * span * depth * channels, 12000000,...  9.62 us
    pallas_call x1, Pallas kernels, spectra_of(): call(spectra_kernel, 'spectra', 3000000000, 5000000, vmem=56, grid=(width...  8.8 us
    ppermute x1, waiting for transfers between devices, local(): chip = lax.ppermute(send, 'tp', chips)  8.55 us
    pallas_call x1, Pallas kernels, sends(): call(send_kernel, 'sends', 2 * span * depth * channels, 12500000, vmem=56...  7.36 us
  transfers between devices with their start and end apart: 12, of which 5 were waited for; matrix products, arithmetic and copies ran while one was open for 1% of the time, Pallas kernels for 33%

profile of v3, /device:TPU:14, one launch (start us, length us, event | category | flops | bytes accessed | tf_op | source)
XLA Modules:
  0.0 157.6 jit_solution(11867518960115357832)
XLA Ops:
  0.6 0.0 copy-start
  0.6 7.4 %sends.1 = bf16[32,64,256]{2,1,0:T(8,128)(2,1)} custom-call(bf16[256,4096]{1,0:T(8,128)(2,1)} %others_ref, bf16[4096,1024]{1,0:T(8,128)(2,1)} %weight_ref.1, bf16[4096,1024]{1,0:T(8,128)(2,1)} %weight_ref.1, bf16[4096,1024]{1,0:T(8,128)(2,1)} %weight_ref.1, bf16[4096,1024]{1,0:T(8,128)(2,1)} %weight_ref.1, bf16[256,1024]{1,0:T(8,128)(2,1)} %gate_ref.1, ...), custom_call_target="tpu_custom_call" | custom-call | flops 2147483648 | bytes 12500000 | tf_op jit(solution)/shard_map/sends/pallas_call | solution.py:381
  8.0 11.0 %all-to-all-start = ((bf16[32,64,256]{2,1,0:T(8,128)(2,1)}), bf16[32,64,256]{2,1,0:T(8,128)(2,1)}, u32[]{:S(2)}, u32[]{:S(2)}) async-start(bf16[32,64,256]{2,1,0:T(8,128)(2,1)} %sends.1), calls=%async_computation | async-start | bytes 2097152 | tf_op jit(solution)/shard_map/all_to_all | solution.py:602
  19.1 0.1 pad_add_fusion.place_ref
  19.1 1.3 quarters.1
  20.5 0.8 copy-done.11
  21.3 3.1 %collective-permute-start = (bf16[256,1024]{1,0:T(8,128)(2,1)S(1)}, bf16[256,1024]{1,0:T(8,128)(2,1)S(1)}, u32[]{:S(2)}, u32[]{:S(2)}) collective-permute-start(bf16[256,1024]{1,0:T(8,128)(2,1)S(1)} %get-tuple-element.40), channel_id=1, source_target_pairs={{0,6},{1,7},{2,4},{3,5},{4,2},{5,3},{6,0},{7,1},{8,14},{9,15},{10,... | collective-permute-start | bytes 1572872 | tf_op jit(solution)/shard_map/ppermute | solution.py:614
  24.4 8.8 %spectra.1.spectra_ref = f32[2048,256]{1,0:T(8,128)} custom-call(f32[2,4,512,128]{3,2,1,0:T(8,128)} %bitcast.21, bf16[128,256]{1,0:T(8,128)(2,1)} %constant.77.clone.first_nat_ref, f32[2,64,128]{2,1,0:T(8,128)} %constant.78.clone.twist_ref, bf16[1536,256]{1,0:T(8,128)(2,1)} %constant.79.clone.pair_ref), custom_call_target="tpu_custom_call" | custom-call | flops 3000000000 | bytes 5000000 | tf_op jit(solution)/shard_map/spectra/pallas_call | solution.py:293
  33.3 1.5 collective-permute-start.1
  34.7 0.2 collective-permute-start.2
  34.9 0.7 constant_dynamic-slice_fusion.2.taps_ref
  35.6 0.0 all-to-all-done.arrived_ref
  35.6 17.7 %mixer.1 = (bf16[16,32,1664]{2,1,0:T(8,128)(2,1)}, bf16[2048,512]{1,0:T(8,128)(2,1)}) custom-call(f32[7,32]{1,0:T(8,128)} %constant_dynamic-slice_fusion.2.taps_ref, bf16[32,64,256]{2,1,0:T(8,128)(2,1)} %all-to-all-done.arrived_ref, f32[2048,256]{1,0:T(8,128)} %spectra.1.spectra_ref, bf16[128,128]{1,0:T(8,128)(2,1)} %constant.80.clone.first_split_ref, ...), custom_call_target="tpu_custom_call" | custom-call | flops 100000000 | bytes 1000000 | tf_op jit(solution)/shard_map/mixer/pallas_call | solution.py:321
  53.2 0.0 collective-permute-done.refs_1_
  53.3 0.0 copy-start.16
  53.3 0.0 collective-permute-done.1.refs_2_
  53.3 0.0 copy-start.17
  53.3 4.2 %collective-permute-done.2.refs_3_ = bf16[256,1024]{1,0:T(8,128)(2,1)S(1)} collective-permute-done((bf16[256,1024]{1,0:T(8,128)(2,1)S(1)}, bf16[256,1024]{1,0:T(8,128)(2,1)S(1)}, u32[]{:S(2)}, u32[]{:S(2)}) %collective-permute-start.2) | collective-permute-done | bytes 524320 | tf_op jit(solution)/shard_map/ppermute | solution.py:614
  57.5 0.8 copy-done.18
  58.3 6.6 %all-to-all-start.1 = ((bf16[16,32,1664]{2,1,0:T(8,128)(2,1)}), bf16[16,32,1664]{2,1,0:T(8,128)(2,1)S(1)}, u32[]{:S(2)}, u32[]{:S(2)}) async-start(bf16[16,32,1664]{2,1,0:T(8,128)(2,1)} %get-tuple-element.41), calls=%async_computation.1 | async-start | bytes 3407872 | tf_op jit(solution)/shard_map/all_to_all | solution.py:602
  64.8 0.0 collective-permute-start.3
  64.8 0.5 collective-permute-start.4
  65.4 0.1 collective-permute-start.5
  65.4 1.6 %copy-done.13 = bf16[2048,512]{1,0:T(8,128)(2,1)S(1)} copy-done((bf16[2048,512]{1,0:T(8,128)(2,1)S(1)}, bf16[2048,512]{1,0:T(8,128)(2,1)}, u32[]{:S(2)}) %copy-start.13) | copy-done | bytes 2097176
  67.0 1.1 copy-done.14
  68.2 6.2 %filter_grads.1 = f32[2,4,512,128]{3,2,1,0:T(8,128)} custom-call(bf16[2048,512]{1,0:T(8,128)(2,1)S(1)} %copy-done.13, f32[2,64,128]{2,1,0:T(8,128)S(1)} %copy-done.12, bf16[768,512]{1,0:T(8,128)(2,1)S(1)} %copy-done.14, bf16[64,384]{1,0:T(8,128)(2,1)S(1)} %copy-done.15), custom_call_target="tpu_custom_call" | custom-call | flops 3000000000 | bytes 5000000 | tf_op jit(solution)/shard_map/filter_grads/pallas_call | solution.py:306
  74.4 0.0 collective-permute-done.3.refs_5_
  74.4 0.0 collective-permute-done.4.refs_6_
  74.4 0.0 collective-permute-done.5.refs_7_
  74.4 14.2 %all-to-all-done.1 = bf16[16,32,1664]{2,1,0:T(8,128)(2,1)S(1)} async-done(((bf16[16,32,1664]{2,1,0:T(8,128)(2,1)}), bf16[16,32,1664]{2,1,0:T(8,128)(2,1)S(1)}, u32[]{:S(2)}, u32[]{:S(2)}) %all-to-all-start.1) | async-done | bytes 1703968 | tf_op jit(solution)/shard_map/all_to_all | solution.py:602
  88.7 0.1 constant_dynamic-slice_fusion.1
  88.7 0.1 pad_maximum_fusion
  88.8 2.4 %collective-permute-start.6 = (bf16[512,640]{1,0:T(8,128)(2,1)S(1)}, bf16[512,640]{1,0:T(8,128)(2,1)S(1)}, u32[]{:S(2)}, u32[]{:S(2)}) collective-permute-start(bf16[512,640]{1,0:T(8,128)(2,1)S(1)} %pad_maximum_fusion), channel_id=1, source_target_pairs={{0,24},{4,28},{8,16},{12,20},{16,8},{20,12},{24,0},{28,4},{32,56},... | collective-permute-start | bytes 1966088 | tf_op jit(solution)/shard_map/ppermute | solution.py:606
  91.2 5.4 %shares.1 = bf16[16,512,128]{2,1,0:T(8,128)(2,1)} custom-call(bf16[512,1664]{1,0:T(8,128)(2,1)} %bitcast.17, bf16[256,1024]{1,0:T(8,128)(2,1)} %copy-done.10, bf16[256,1024]{1,0:T(8,128)(2,1)} %copy-done.16, bf16[256,1024]{1,0:T(8,128)(2,1)} %copy-done.17, bf16[256,1024]{1,0:T(8,128)(2,1)} %copy-done.18, bf16[256,1024]{1,0:T(8,128)(2,1)} %copy-done.11, ...), custom_call_target="tpu_custom_call" | custom-call | flops 2147483648 | bytes 7000000 | tf_op jit(solution)/shard_map/shares/pallas_call | solution.py:454
  96.6 8.8 %all-to-all-start.2 = ((bf16[16,512,128]{2,1,0:T(8,128)(2,1)}), bf16[16,512,128]{2,1,0:T(8,128)(2,1)}, u32[]{:S(2)}, u32[]{:S(2)}) async-start(bf16[16,512,128]{2,1,0:T(8,128)(2,1)} %shares.1), calls=%async_computation.2 | async-start | bytes 4194304 | tf_op jit(solution)/shard_map/all_to_all | solution.py:602
  105.4 19.1 %collective-permute-done.6.mate_ref = bf16[512,640]{1,0:T(8,128)(2,1)S(1)} collective-permute-done((bf16[512,640]{1,0:T(8,128)(2,1)S(1)}, bf16[512,640]{1,0:T(8,128)(2,1)S(1)}, u32[]{:S(2)}, u32[]{:S(2)}) %collective-permute-start.6) | collective-permute-done | bytes 655392 | tf_op jit(solution)/shard_map/ppermute | solution.py:606
  124.5 0.8 copy-done.4
  125.4 9.6 %input_terms.1 = (bf16[2,1024,256]{2,1,0:T(8,128)(2,1)}, f32[2,1024,256]{2,1,0:T(8,128)}) custom-call(bf16[512,1664]{1,0:T(8,128)(2,1)} %bitcast.18, bf16[512,640]{1,0:T(8,128)(2,1)} %copy-done.4, bf16[4096,1024]{1,0:T(8,128)(2,1)} %weight_ref.1), custom_call_target="tpu_custom_call" | custom-call | flops 2147483648 | bytes 12000000 | tf_op jit(solution)/shard_map/input_terms/pallas_call | solution.py:544
  135.0 0.1 collective-permute-start.7
  135.1 2.9 %collective-permute-done.7.core_ref = bf16[2,1024,256]{2,1,0:T(8,128)(2,1)S(1)} collective-permute-done((bf16[2,1024,256]{2,1,0:T(8,128)(2,1)}, bf16[2,1024,256]{2,1,0:T(8,128)(2,1)S(1)}, u32[]{:S(2)}, u32[]{:S(2)}) %collective-permute-start.7) | collective-permute-done | bytes 1048608 | tf_op jit(solution)/shard_map/ppermute | solution.py:636
  137.9 1.4 fusion
  139.3 2.3 %collective-permute-start.8 = (bf16[1024,256]{1,0:T(8,128)(2,1)S(1)}, bf16[1024,256]{1,0:T(8,128)(2,1)S(1)}, u32[]{:S(2)}, u32[]{:S(2)}) collective-permute-start(bf16[1024,256]{1,0:T(8,128)(2,1)S(1)} %fusion), channel_id=1, source_target_pairs={{0,2},{2,0},{1,3},{3,1},{4,6},{6,4},{5,7},{7,5},{8,10},{10,8},{9,1... | collective-permute-start | bytes 1572872 | tf_op jit(solution)/shard_map/ppermute | solution.py:638
  141.6 1.1 copy-done.5
  142.7 2.6 %gate_grad.1 = bf16[256,1024]{1,0:T(8,128)(2,1)} custom-call(s32[2]{0:T(128)S(1)} %pad_add_fusion.place_ref, bf16[512,1664]{1,0:T(8,128)(2,1)S(1)} %bitcast.19, bf16[512,640]{1,0:T(8,128)(2,1)S(1)} %copy-done.5, bf16[256,1024]{1,0:T(8,128)(2,1)S(1)} %copy-done.8, bf16[256,1024]{1,0:T(8,128)(2,1)S(1)} %copy-done.9), custom_call_target="tpu_custom_call" | custom-call | flops 2000000 | bytes 2500000 | tf_op jit(solution)/shard_map/gate_grad/pallas_call | solution.py:581
  145.3 8.5 %collective-permute-done.8.chip_ref = bf16[1024,256]{1,0:T(8,128)(2,1)S(1)} collective-permute-done((bf16[1024,256]{1,0:T(8,128)(2,1)S(1)}, bf16[1024,256]{1,0:T(8,128)(2,1)S(1)}, u32[]{:S(2)}, u32[]{:S(2)}) %collective-permute-start.8) | collective-permute-done | bytes 524320 | tf_op jit(solution)/shard_map/ppermute | solution.py:638
  153.8 1.0 close_input.1
  154.8 0.0 all-to-all-done.2.shares_ref
  154.9 2.8 %close_weight.1 = (f32[128,1024]{1,0:T(8,128)}, f32[7,1024]{1,0:T(8,128)}) custom-call(bf16[16,512,128]{2,1,0:T(8,128)(2,1)} %all-to-all-done.2.shares_ref, bf16[512,1664]{1,0:T(8,128)(2,1)S(1)} %bitcast.20, bf16[512,640]{1,0:T(8,128)(2,1)S(1)} %copy-done.6), custom_call_target="tpu_custom_call" | custom-call | flops 2000000 | bytes 3000000 | tf_op jit(solution)/shard_map/close_weight/pallas_call | solution.py:487
  (36 shorter events, 0.1 us)
Async XLA Ops:
  0.6 34.3 %copy-start = (f32[7,1024]{1,0:T(8,128)S(1)}, f32[7,1024]{1,0:T(8,128)}, u32[]{:S(2)}) copy-start(f32[7,1024]{1,0:T(8,128)} %param.17) | copy-start | bytes 86020
  8.0 11.1 %copy-start.3 = (bf16[256,4096]{1,0:T(8,128)(2,1)S(1)}, bf16[256,4096]{1,0:T(8,128)(2,1)}, u32[]{:S(2)}) copy-start(bf16[256,4096]{1,0:T(8,128)(2,1)} %others_ref) | copy-start | bytes 6291460
  8.0 27.6 %all-to-all-start = ((bf16[32,64,256]{2,1,0:T(8,128)(2,1)}), bf16[32,64,256]{2,1,0:T(8,128)(2,1)}, u32[]{:S(2)}, u32[]{:S(2)}) async-start(bf16[32,64,256]{2,1,0:T(8,128)(2,1)} %sends.1), calls=%async_computation | async-start | bytes 2097152 | tf_op jit(solution)/shard_map/all_to_all | solution.py:602
  20.5 0.8 copy-start.11
  21.3 11.9 %copy-start.10 = (bf16[256,1024]{1,0:T(8,128)(2,1)}, bf16[256,1024]{1,0:T(8,128)(2,1)S(1)}, u32[]{:S(2)}) copy-start(bf16[256,1024]{1,0:T(8,128)(2,1)S(1)} %get-tuple-element.48.refs_0_) | copy-start | bytes 1572868
  21.3 31.9 %collective-permute-start = (bf16[256,1024]{1,0:T(8,128)(2,1)S(1)}, bf16[256,1024]{1,0:T(8,128)(2,1)S(1)}, u32[]{:S(2)}, u32[]{:S(2)}) collective-permute-start(bf16[256,1024]{1,0:T(8,128)(2,1)S(1)} %get-tuple-element.40), channel_id=1, source_target_pairs={{0,6},{1,7},{2,4},{3,5},{4,2},{5,3},{6,0},{7,1},{8,14},{9,15},{10,... | collective-permute-start | bytes 1572872 | tf_op jit(solution)/shard_map/ppermute | solution.py:614
  33.3 20.0 %collective-permute-start.1 = (bf16[256,1024]{1,0:T(8,128)(2,1)S(1)}, bf16[256,1024]{1,0:T(8,128)(2,1)S(1)}, u32[]{:S(2)}, u32[]{:S(2)}) collective-permute-start(bf16[256,1024]{1,0:T(8,128)(2,1)S(1)} %get-tuple-element.48.refs_0_), channel_id=1, source_target_pairs={{0,24},{4,28},{8,16},{12,20},{16,8},{20,12},{24,0},{28,4},{32,56},... | collective-permute-start | bytes 1572872 | tf_op jit(solution)/shard_map/ppermute | solution.py:606
  34.7 22.7 %collective-permute-start.2 = (bf16[256,1024]{1,0:T(8,128)(2,1)S(1)}, bf16[256,1024]{1,0:T(8,128)(2,1)S(1)}, u32[]{:S(2)}, u32[]{:S(2)}) collective-permute-start(bf16[256,1024]{1,0:T(8,128)(2,1)S(1)} %get-tuple-element.40), channel_id=1, source_target_pairs={{0,30},{1,31},{2,28},{3,29},{4,26},{5,27},{6,24},{7,25},{8,22},{9,... | collective-permute-start | bytes 1572872 | tf_op jit(solution)/shard_map/ppermute | solution.py:614
  53.2 12.2 %copy-start.12 = (f32[2,64,128]{2,1,0:T(8,128)S(1)}, f32[2,64,128]{2,1,0:T(8,128)}, u32[]{:S(2)}) copy-start(f32[2,64,128]{2,1,0:T(8,128)} %constant.78.clone.twist_ref) | copy-start | bytes 196612
  53.2 12.2 %copy-start.15 = (bf16[64,384]{1,0:T(8,128)(2,1)S(1)}, bf16[64,384]{1,0:T(8,128)(2,1)}, u32[]{:S(2)}) copy-start(bf16[64,384]{1,0:T(8,128)(2,1)} %constant.85.clone.last_nat_ref) | copy-start | bytes 147460
  53.3 4.2 %copy-start.16 = (bf16[256,1024]{1,0:T(8,128)(2,1)}, bf16[256,1024]{1,0:T(8,128)(2,1)S(1)}, u32[]{:S(2)}) copy-start(bf16[256,1024]{1,0:T(8,128)(2,1)S(1)} %collective-permute-done.refs_1_) | copy-start | bytes 1572868
  53.3 4.2 %copy-start.17 = (bf16[256,1024]{1,0:T(8,128)(2,1)}, bf16[256,1024]{1,0:T(8,128)(2,1)S(1)}, u32[]{:S(2)}) copy-start(bf16[256,1024]{1,0:T(8,128)(2,1)S(1)} %collective-permute-done.1.refs_2_) | copy-start | bytes 1572868
  57.4 0.8 copy-start.18
  58.3 30.4 %all-to-all-start.1 = ((bf16[16,32,1664]{2,1,0:T(8,128)(2,1)}), bf16[16,32,1664]{2,1,0:T(8,128)(2,1)S(1)}, u32[]{:S(2)}, u32[]{:S(2)}) async-start(bf16[16,32,1664]{2,1,0:T(8,128)(2,1)} %get-tuple-element.41), calls=%async_computation.1 | async-start | bytes 3407872 | tf_op jit(solution)/shard_map/all_to_all | solution.py:602
  64.8 9.6 %collective-permute-start.3 = (bf16[256,1024]{1,0:T(8,128)(2,1)}, bf16[256,1024]{1,0:T(8,128)(2,1)S(1)}, u32[]{:S(2)}, u32[]{:S(2)}) collective-permute-start(bf16[256,1024]{1,0:T(8,128)(2,1)} %copy-done.16), channel_id=1, source_target_pairs={{0,1},{1,0},{2,3},{3,2},{4,5},{5,4},{6,7},{7,6},{8,9},{9,8},{10,11... | collective-permute-start | bytes 1572872 | tf_op jit(solution)/shard_map/ppermute | solution.py:625
  64.8 9.6 %collective-permute-start.4 = (bf16[256,1024]{1,0:T(8,128)(2,1)}, bf16[256,1024]{1,0:T(8,128)(2,1)S(1)}, u32[]{:S(2)}, u32[]{:S(2)}) collective-permute-start(bf16[256,1024]{1,0:T(8,128)(2,1)} %copy-done.17), channel_id=1, source_target_pairs={{0,1},{1,0},{2,3},{3,2},{4,5},{5,4},{6,7},{7,6},{8,9},{9,8},{10,11... | collective-permute-start | bytes 1572872 | tf_op jit(solution)/shard_map/ppermute | solution.py:625
  65.4 9.1 %collective-permute-start.5 = (bf16[256,1024]{1,0:T(8,128)(2,1)}, bf16[256,1024]{1,0:T(8,128)(2,1)S(1)}, u32[]{:S(2)}, u32[]{:S(2)}) collective-permute-start(bf16[256,1024]{1,0:T(8,128)(2,1)} %copy-done.18), channel_id=1, source_target_pairs={{0,1},{1,0},{2,3},{3,2},{4,5},{5,4},{6,7},{7,6},{8,9},{9,8},{10,11... | collective-permute-start | bytes 1572872 | tf_op jit(solution)/shard_map/ppermute | solution.py:625
  65.4 1.6 %copy-start.13 = (bf16[2048,512]{1,0:T(8,128)(2,1)S(1)}, bf16[2048,512]{1,0:T(8,128)(2,1)}, u32[]{:S(2)}) copy-start(bf16[2048,512]{1,0:T(8,128)(2,1)} %get-tuple-element.42.lag_ref) | copy-start | bytes 6291460
  67.0 1.1 copy-start.14
  74.4 14.3 %copy-start.19 = (bf16[256,1024]{1,0:T(8,128)(2,1)}, bf16[256,1024]{1,0:T(8,128)(2,1)S(1)}, u32[]{:S(2)}) copy-start(bf16[256,1024]{1,0:T(8,128)(2,1)S(1)} %collective-permute-done.3.refs_5_) | copy-start | bytes 1572868
  74.4 14.2 %copy-start.20 = (bf16[256,1024]{1,0:T(8,128)(2,1)}, bf16[256,1024]{1,0:T(8,128)(2,1)S(1)}, u32[]{:S(2)}) copy-start(bf16[256,1024]{1,0:T(8,128)(2,1)S(1)} %collective-permute-done.4.refs_6_) | copy-start | bytes 1572868
  74.4 14.3 %copy-start.21 = (bf16[256,1024]{1,0:T(8,128)(2,1)}, bf16[256,1024]{1,0:T(8,128)(2,1)S(1)}, u32[]{:S(2)}) copy-start(bf16[256,1024]{1,0:T(8,128)(2,1)S(1)} %collective-permute-done.5.refs_7_) | copy-start | bytes 1572868
  88.6 2.5 %copy-start.1 = (bf16[16,32,1664]{2,1,0:T(8,128)(2,1)}, bf16[16,32,1664]{2,1,0:T(8,128)(2,1)S(1)}, u32[]{:S(2)}) copy-start(bf16[16,32,1664]{2,1,0:T(8,128)(2,1)S(1)} %all-to-all-done.1) | copy-start | bytes 5111812
  88.8 35.7 %collective-permute-start.6 = (bf16[512,640]{1,0:T(8,128)(2,1)S(1)}, bf16[512,640]{1,0:T(8,128)(2,1)S(1)}, u32[]{:S(2)}, u32[]{:S(2)}) collective-permute-start(bf16[512,640]{1,0:T(8,128)(2,1)S(1)} %pad_maximum_fusion), channel_id=1, source_target_pairs={{0,24},{4,28},{8,16},{12,20},{16,8},{20,12},{24,0},{28,4},{32,56},... | collective-permute-start | bytes 1966088 | tf_op jit(solution)/shard_map/ppermute | solution.py:606
  96.6 58.3 %all-to-all-start.2 = ((bf16[16,512,128]{2,1,0:T(8,128)(2,1)}), bf16[16,512,128]{2,1,0:T(8,128)(2,1)}, u32[]{:S(2)}, u32[]{:S(2)}) async-start(bf16[16,512,128]{2,1,0:T(8,128)(2,1)} %shares.1), calls=%async_computation.2 | async-start | bytes 4194304 | tf_op jit(solution)/shard_map/all_to_all | solution.py:602
  124.5 0.8 copy-start.4
  125.4 16.3 %copy-start.8 = (bf16[256,1024]{1,0:T(8,128)(2,1)S(1)}, bf16[256,1024]{1,0:T(8,128)(2,1)}, u32[]{:S(2)}) copy-start(bf16[256,1024]{1,0:T(8,128)(2,1)} %gate_ref.1) | copy-start | bytes 1572868
  125.4 16.3 %copy-start.9 = (bf16[256,1024]{1,0:T(8,128)(2,1)S(1)}, bf16[256,1024]{1,0:T(8,128)(2,1)}, u32[]{:S(2)}) copy-start(bf16[256,1024]{1,0:T(8,128)(2,1)} %grad_ref.1) | copy-start | bytes 1572868
  135.0 6.6 %copy-start.2 = (bf16[16,32,1664]{2,1,0:T(8,128)(2,1)S(1)}, bf16[16,32,1664]{2,1,0:T(8,128)(2,1)}, u32[]{:S(2)}) copy-start(bf16[16,32,1664]{2,1,0:T(8,128)(2,1)} %copy-done.1) | copy-start | bytes 5111812
  135.0 3.0 %collective-permute-start.7 = (bf16[2,1024,256]{2,1,0:T(8,128)(2,1)}, bf16[2,1024,256]{2,1,0:T(8,128)(2,1)S(1)}, u32[]{:S(2)}, u32[]{:S(2)}) collective-permute-start(bf16[2,1024,256]{2,1,0:T(8,128)(2,1)} %get-tuple-element.54), channel_id=1, source_target_pairs={{0,1},{1,0},{2,3},{3,2},{4,5},{5,4},{6,7},{7,6},{8,9},{9,8},{10,11... | collective-permute-start | bytes 3145736 | tf_op jit(solution)/shard_map/ppermute | solution.py:636
  139.3 14.5 %collective-permute-start.8 = (bf16[1024,256]{1,0:T(8,128)(2,1)S(1)}, bf16[1024,256]{1,0:T(8,128)(2,1)S(1)}, u32[]{:S(2)}, u32[]{:S(2)}) collective-permute-start(bf16[1024,256]{1,0:T(8,128)(2,1)S(1)} %fusion), channel_id=1, source_target_pairs={{0,2},{2,0},{1,3},{3,1},{4,6},{6,4},{5,7},{7,5},{8,10},{10,8},{9,1... | collective-permute-start | bytes 1572872 | tf_op jit(solution)/shard_map/ppermute | solution.py:638
  141.6 1.1 copy-start.5
  142.7 11.1 %copy-start.7 = (f32[2,1024,256]{2,1,0:T(8,128)S(1)}, f32[2,1024,256]{2,1,0:T(8,128)}, u32[]{:S(2)}) copy-start(f32[2,1024,256]{2,1,0:T(8,128)} %get-tuple-element.53.keep_ref) | copy-start | bytes 6291460
  145.3 9.6 %copy-start.6 = (bf16[512,640]{1,0:T(8,128)(2,1)S(1)}, bf16[512,640]{1,0:T(8,128)(2,1)}, u32[]{:S(2)}) copy-start(bf16[512,640]{1,0:T(8,128)(2,1)} %copy-done.4) | copy-start | bytes 1966084

commit v4 on v2

--- a/solution.py
+++ b/solution.py
@@ -16,7 +16,7 @@
 TAPS = 7
 REACH = TAPS // 2
 BATCH = 4
-GROUP, GROUPS = 2, 4
+GROUP, GROUPS = 2, 8
 
 
 def halves(table):
@@ -319,7 +319,7 @@
     back_shape = (blocks // 2, width, 6 * span + LANES)
     rows, batch = (2, blocks * width, LANES), GROUP * GROUPS
     return call(
-        mixer_kernel, "mixer", 3_000_000_000, 8_000_000, vmem=56,
+        mixer_kernel, "mixer", 100_000_000, 1_000_000, vmem=56,
         grid=(width // batch,),
         in_specs=[pl.BlockSpec(memory_space=pltpu.SMEM), whole(arrived.shape),
                   pl.BlockSpec((batch * ROWS, 2 * LANES), lambda i: (i, 0))] + specs,
@@ -452,7 +452,7 @@
     span, depth = mine[0].shape
     rows = back.shape[0]
     return call(
-        share_kernel, "shares", 16 * rows * span * depth, 7_000_000, vmem=32,
+        share_kernel, "shares", 16 * rows * span * depth, 7_000_000, vmem=60,
         in_specs=[pl.BlockSpec(memory_space=pl.ANY)] * 9,
         out_specs=pl.BlockSpec(memory_space=pl.ANY),
         out_shape=jax.ShapeDtypeStruct((16, rows, LANES), jnp.bfloat16),
@@ -487,16 +487,14 @@
     return call(
         weight_kernel, "close_weight", 2_000_000, 3_000_000, grid=(1,),
         in_specs=[whole(parts.shape),
-                  pl.BlockSpec((rows, LANES), lambda i: (0, 12)), pl.BlockSpec((rows, LANES), lambda i: (0, 2))],
+                  pl.BlockSpec((rows, LANES), lambda i: (0, 12)), pl.BlockSpec((rows, LANES), lambda i: (0, 4))],
         out_specs=[whole((span, channels)), whole((TAPS, channels))],
         out_shape=[jax.ShapeDtypeStruct((span, channels), jnp.float32),
                    jax.ShapeDtypeStruct((TAPS, channels), jnp.float32)],
     )(parts, back, mate)
 
 
-def input_kernel(place_ref, back_ref, mate_ref, *refs):
-    weight_refs, (send_ref, keep_ref, own_buf) = refs[:STREAMS], refs[STREAMS:]
-
+def input_kernel(place_ref, back_ref, mate_ref, weight_ref, send_ref, keep_ref, own_buf):
     @pl.when(pl.program_id(0) == 0)
     def _():
         pair = place_ref[0] // 2
@@ -506,41 +504,33 @@
                 own_buf[pl.ds(pl.multiple_of((4 * x + mine) * 64, 64), 64), :] = back_ref[rows, :]
                 own_buf[pl.ds(pl.multiple_of((4 * x + other) * 64, 64), 64), :] = mate_ref[rows, :]
 
-    size = weight_refs[0].shape[0]
-    terms = [dot(weight_ref[...], own_buf[...]) for weight_ref in weight_refs]
+    term = dot(weight_ref[...], own_buf[...])
 
     @pl.when(pl.program_id(0) < 2)
     def _():
-        for n, term in enumerate(terms):
-            send_ref[0, n * size:(n + 1) * size] = term.astype(jnp.bfloat16)
+        send_ref[0] = term.astype(jnp.bfloat16)
 
     @pl.when(pl.program_id(0) >= 2)
     def _():
-        for n, term in enumerate(terms):
-            keep_ref[0, n * size:(n + 1) * size] = term
+        keep_ref[0] = term
 
 
 def input_terms(place, back, mate, w_value):
     depth, channels = w_value.shape
     rows, span = depth // 4, 256
-
-    def stream(n):
-        return pl.BlockSpec(
-            (rows // STREAMS, channels),
-            lambda i, place: (STREAMS * (place[1] ^ ((2 * i + 1 - i // 2) % 4)) + n, 0))
-
-    return call(
-        input_kernel, "input_terms", 2 * span * depth * channels, 12_000_000, vmem=56,
+    return call(
+        input_kernel, "input_terms", 2 * span * depth * channels, 12_000_000, vmem=24,
         grid_spec=pltpu.PrefetchScalarGridSpec(
             num_scalar_prefetch=1, grid=(4,),
             in_specs=[pl.BlockSpec((channels // 2, span), lambda i, place: (0, place[0])),
-                      pl.BlockSpec((channels // 2, span), lambda i, place: (0, 0))] + [stream(n) for n in range(STREAMS)],
+                      pl.BlockSpec((channels // 2, span), lambda i, place: (0, 0)),
+                      pl.BlockSpec((rows, channels), lambda i, place: (place[1] ^ ((2 * i + 1 - i // 2) % 4), 0))],
             out_specs=[pl.BlockSpec((1, rows, span), lambda i, place: (jnp.minimum(i, 1), 0, 0)),
                        pl.BlockSpec((1, rows, span), lambda i, place: (jnp.maximum(i - 2, 0), 0, 0))],
             scratch_shapes=[pltpu.VMEM((channels, span), jnp.bfloat16)]),
         out_shape=[jax.ShapeDtypeStruct((2, rows, span), jnp.bfloat16),
                    jax.ShapeDtypeStruct((2, rows, span), jnp.float32)],
-    )(place, back, mate, *[w_value] * STREAMS)
+    )(place, back, mate, w_value)
 
 
 def close_kernel(keep_ref, core_ref, chip_ref, out_ref):
@@ -572,7 +562,7 @@
         grid_spec=pltpu.PrefetchScalarGridSpec(
             num_scalar_prefetch=1, grid=(4,),
             in_specs=[pl.BlockSpec((LANES, span), lambda i, place: (i, 4 + place[0] // 2)),
-                      pl.BlockSpec((LANES, span), lambda i, place: (i, 0)), block, block],
+                      pl.BlockSpec((LANES, span), lambda i, place: (i, 1)), block, block],
             out_specs=block),
         out_shape=jax.ShapeDtypeStruct(gate.shape, jnp.bfloat16))(place, back, mate, gate, grads)
 
@@ -598,37 +588,38 @@
     rows_in, outgoing = lax.optimization_barrier((layer_in, outgoing))
     arrived = exchange(outgoing)
     same, cross, other = quarters_of(place, rows_in)
-    spectra = spectra_of(long_filters)
-    same, cross, spectra = lax.optimization_barrier((same, cross, spectra))
 
     def across(value, flip):
         return lax.ppermute(
             value, ("seq", "tp"), [(4 * s + t, 4 * (s ^ flip) + (t ^ 2)) for s in range(seq_count) for t in range(4)])
 
-    mine = [same, across(cross, 1), mates(same), across(cross, 1 ^ MATE)]
-    other = [other] + [lax.ppermute(part, "tp", cores) for part in mine[1:]]
+    first = across(cross, 1)
+    spectra = spectra_of(long_filters)
+    same, cross, spectra = lax.optimization_barrier((same, cross, spectra))
+    mine = [same, first, mates(same), across(cross, 1 ^ MATE)]
 
     own_taps = lax.dynamic_slice_in_dim(short_taps, seq_at * width, width, 1)
     back, lag = mixer(own_taps, arrived, spectra)
     back, mine = lax.optimization_barrier((back, mine))
+    other = [other] + [lax.ppermute(part, "tp", cores) for part in mine[1:]]
     back = exchange(back, LEAGUES).reshape(channels // 2, back.shape[2])
     grad_filters = filter_grads(lag)
     back, grad_filters, other = lax.optimization_barrier((back, grad_filters, other))
-    mate = mates(lax.dynamic_slice_in_dim(back, (quad_at ^ 2) * span, span, 1))
-    mate_rest = jnp.concatenate([
-        lax.dynamic_slice_in_dim(back, 4 * span + (1 - quad_at // 2) * span, span, 1), back[:, 6 * span:]], axis=1)
-    outgoing = shares(back, mine, other)
-    outgoing, mate, mate_rest = lax.optimization_barrier((outgoing, mate, mate_rest))
-    mate_rest = mates(mate_rest)
+    mate = mates(jnp.concatenate([
+        lax.dynamic_slice_in_dim(back, (quad_at ^ 2) * span, span, 1),
+        lax.dynamic_slice_in_dim(back, 4 * span + (1 - quad_at // 2) * span, span, 1),
+        back[:, 6 * span:]], axis=1))
+    outgoing, mate = lax.optimization_barrier((shares(back, mine, other), mate))
     parts = exchange(outgoing, PLANES)
 
     send, keep = input_terms(place, back, mate, w_value)
     core = lax.ppermute(send, "tp", cores)
-    chip = lax.ppermute((keep[1] + core[1].astype(jnp.float32)).astype(jnp.bfloat16), "tp", chips)
+    send = (keep[1] + core[1].astype(jnp.float32)).astype(jnp.bfloat16)
+    chip = lax.ppermute(send, "tp", chips)
     grad_input = close_input(keep, core, chip)
-    grad_gate = gate_grad(place, back, mate_rest, gate_proj, grad_out)
+    grad_gate = gate_grad(place, back, mate, gate_proj, grad_out)
     parts, grad_input, grad_gate = lax.optimization_barrier((parts, grad_input, grad_gate))
-    grad_weight, grad_taps = close_weight(parts, back, mate_rest)
+    grad_weight, grad_taps = close_weight(parts, back, mate)
     return (grad_input, grad_weight, grad_taps, grad_filters, grad_gate)
 
 

time: 149 us -> 144 us (0.966)
  Pallas kernels: 63.1 us -> 57 us
  local copies, waits for them, and re-layouts: 5.62 us -> 8.5 us
  waiting for transfers between devices: 38.8 us -> 41.2 us
  other arithmetic: 2.2 us -> 0.27 us
    ppermute x1, waiting for transfers between devices: 0.01 us -> 9.64 us  [local(): chip = lax.ppermute(send, 'tp', chips)]
    ppermute x3 -> x2, waiting for transfers between devices: 14.8 us -> 5.32 us  [mates(): return lax.ppermute(value, 'seq', [(s, s ^ MATE) for s in range(seq_count)])]
    pallas_call x1, Pallas kernels: 7.99 us -> 3.87 us  [input_terms(): call(input_kernel, 'input_terms', 2 * span * depth * channels, 12000000,...]
    ppermute x3 -> x2, starting transfers between devices: 8.63 us -> 5.63 us  [mates(): return lax.ppermute(value, 'seq', [(s, s ^ MATE) for s in range(seq_count)])]
    unnamed x38, local copies, waits for them, and re-layouts: 4.9 us -> 7.75 us
    all_to_all x3, starting transfers between devices: 21.1 us -> 23 us  [exchange(): lax.all_to_all(value, 'seq', split_axis=0, concat_axis=0, axis_index_grou...]
    all_to_all x3, waiting for transfers between devices: 18.2 us -> 20.1 us  [exchange(): lax.all_to_all(value, 'seq', split_axis=0, concat_axis=0, axis_index_grou...]
  transfers between devices with their start and end apart: 13 -> 12, of which waited for: 5 -> 7; matrix products, arithmetic and copies ran while one was open for 2% -> 1% of each run, Pallas kernels for 36% -> 33%
where the time goes in v4:
time: 144 us; the launch traced here: 143 us
  Pallas kernels  57 us (40%)
  waiting for transfers between devices  41.2 us (29%)
  starting transfers between devices  35.2 us (24%)
  local copies, waits for them, and re-layouts  8.5 us (6%)
    all_to_all x3, starting transfers between devices, exchange(): lax.all_to_all(value, 'seq', split_axis=0, concat_axis=0, axis_index_grou...  23 us
    all_to_all x3, waiting for transfers between devices, exchange(): lax.all_to_all(value, 'seq', split_axis=0, concat_axis=0, axis_index_grou...  20.1 us
    pallas_call x1, Pallas kernels, mixer(): call(mixer_kernel, 'mixer', 100000000, 1000000, vmem=56, grid=(width // b...  17.7 us
    ppermute x1, waiting for transfers between devices, local(): chip = lax.ppermute(send, 'tp', chips)  9.64 us
    pallas_call x1, Pallas kernels, spectra_of(): call(spectra_kernel, 'spectra', 3000000000, 5000000, vmem=56, grid=(width...  8.8 us
    unnamed x38, local copies, waits for them, and re-layouts  7.75 us
    pallas_call x1, Pallas kernels, sends(): call(send_kernel, 'sends', 2 * span * depth * channels, 12500000, vmem=56...  7.41 us
    pallas_call x1, Pallas kernels, filter_grads(): call(lag_kernel, 'filter_grads', 3000000000, 5000000, grid=(width // BATC...  6.22 us
  transfers between devices with their start and end apart: 12, of which 7 were waited for; matrix products, arithmetic and copies ran while one was open for 1% of the time, Pallas kernels for 33%

profile of v4, /device:TPU:0, one launch (start us, length us, event | category | flops | bytes accessed | tf_op | source)
XLA Modules:
  0.0 143.1 jit_solution(9207391189062661097)
XLA Ops:
  0.6 0.0 copy-start
  0.6 7.4 %sends.1 = bf16[32,64,256]{2,1,0:T(8,128)(2,1)} custom-call(bf16[256,4096]{1,0:T(8,128)(2,1)} %others_ref, bf16[4096,1024]{1,0:T(8,128)(2,1)} %weight_ref.1, bf16[4096,1024]{1,0:T(8,128)(2,1)} %weight_ref.1, bf16[4096,1024]{1,0:T(8,128)(2,1)} %weight_ref.1, bf16[4096,1024]{1,0:T(8,128)(2,1)} %weight_ref.1, bf16[256,1024]{1,0:T(8,128)(2,1)} %gate_ref.1, ...), custom_call_target="tpu_custom_call" | custom-call | flops 2147483648 | bytes 12500000 | tf_op jit(solution)/shard_map/sends/pallas_call | solution.py:381
  8.1 11.0 %all-to-all-start = ((bf16[32,64,256]{2,1,0:T(8,128)(2,1)}), bf16[32,64,256]{2,1,0:T(8,128)(2,1)}, u32[]{:S(2)}, u32[]{:S(2)}) async-start(bf16[32,64,256]{2,1,0:T(8,128)(2,1)} %sends.1), calls=%async_computation | async-start | bytes 2097152 | tf_op jit(solution)/shard_map/all_to_all | solution.py:581
  19.1 0.1 pad_add_fusion.place_ref
  19.2 1.3 quarters.1
  20.5 0.8 copy-done.8
  21.3 3.4 %collective-permute-start = (bf16[256,1024]{1,0:T(8,128)(2,1)S(1)}, bf16[256,1024]{1,0:T(8,128)(2,1)S(1)}, u32[]{:S(2)}, u32[]{:S(2)}) collective-permute-start(bf16[256,1024]{1,0:T(8,128)(2,1)S(1)} %get-tuple-element.42), channel_id=1, source_target_pairs={{0,6},{1,7},{2,4},{3,5},{4,2},{5,3},{6,0},{7,1},{8,14},{9,15},{10,... | collective-permute-start | bytes 1572872 | tf_op jit(solution)/shard_map/ppermute | solution.py:593
  24.7 8.8 %spectra.1.spectra_ref = f32[2048,256]{1,0:T(8,128)} custom-call(f32[2,4,512,128]{3,2,1,0:T(8,128)} %bitcast.21, bf16[128,256]{1,0:T(8,128)(2,1)} %constant.77.clone.first_nat_ref, f32[2,64,128]{2,1,0:T(8,128)} %constant.78.clone.twist_ref, bf16[1536,256]{1,0:T(8,128)(2,1)} %constant.79.clone.pair_ref), custom_call_target="tpu_custom_call" | custom-call | flops 3000000000 | bytes 5000000 | tf_op jit(solution)/shard_map/spectra/pallas_call | solution.py:293
  33.5 2.7 %collective-permute-start.1 = (bf16[256,1024]{1,0:T(8,128)(2,1)S(1)}, bf16[256,1024]{1,0:T(8,128)(2,1)S(1)}, u32[]{:S(2)}, u32[]{:S(2)}) collective-permute-start(bf16[256,1024]{1,0:T(8,128)(2,1)S(1)} %get-tuple-element.50.refs_0_), channel_id=1, source_target_pairs={{0,24},{4,28},{8,16},{12,20},{16,8},{20,12},{24,0},{28,4},{32,56},... | collective-permute-start | bytes 1572872 | tf_op jit(solution)/shard_map/ppermute | solution.py:585
  36.2 0.2 collective-permute-start.2
  36.4 0.7 constant_dynamic-slice_fusion.2.taps_ref
  37.0 1.1 all-to-all-done.arrived_ref
  38.1 17.7 %mixer.1 = (bf16[16,32,1664]{2,1,0:T(8,128)(2,1)}, bf16[2048,512]{1,0:T(8,128)(2,1)}) custom-call(f32[7,32]{1,0:T(8,128)} %constant_dynamic-slice_fusion.2.taps_ref, bf16[32,64,256]{2,1,0:T(8,128)(2,1)} %all-to-all-done.arrived_ref, f32[2048,256]{1,0:T(8,128)} %spectra.1.spectra_ref, bf16[128,128]{1,0:T(8,128)(2,1)} %constant.80.clone.first_split_ref, ...), custom_call_target="tpu_custom_call" | custom-call | flops 100000000 | bytes 1000000 | tf_op jit(solution)/shard_map/mixer/pallas_call | solution.py:321
  55.8 0.0 collective-permute-done.refs_1_
  55.8 0.0 copy-start.13
  55.9 0.0 collective-permute-done.1.refs_2_
  55.9 0.0 copy-start.14
  55.9 3.5 %collective-permute-done.2.refs_3_ = bf16[256,1024]{1,0:T(8,128)(2,1)S(1)} collective-permute-done((bf16[256,1024]{1,0:T(8,128)(2,1)S(1)}, bf16[256,1024]{1,0:T(8,128)(2,1)S(1)}, u32[]{:S(2)}, u32[]{:S(2)}) %collective-permute-start.2) | collective-permute-done | bytes 524320 | tf_op jit(solution)/shard_map/ppermute | solution.py:593
  59.4 0.8 copy-done.15
  60.2 5.9 %all-to-all-start.1 = ((bf16[16,32,1664]{2,1,0:T(8,128)(2,1)}), bf16[16,32,1664]{2,1,0:T(8,128)(2,1)S(1)}, u32[]{:S(2)}, u32[]{:S(2)}) async-start(bf16[16,32,1664]{2,1,0:T(8,128)(2,1)} %get-tuple-element.43), calls=%async_computation.1 | async-start | bytes 3407872 | tf_op jit(solution)/shard_map/all_to_all | solution.py:581
  66.0 0.0 collective-permute-start.3
  66.0 0.5 collective-permute-start.4
  66.5 0.1 collective-permute-start.5
  66.6 1.6 %copy-done.10 = bf16[2048,512]{1,0:T(8,128)(2,1)S(1)} copy-done((bf16[2048,512]{1,0:T(8,128)(2,1)S(1)}, bf16[2048,512]{1,0:T(8,128)(2,1)}, u32[]{:S(2)}) %copy-start.10) | copy-done | bytes 2097176
  68.2 1.1 copy-done.11
  69.3 6.2 %filter_grads.1 = f32[2,4,512,128]{3,2,1,0:T(8,128)} custom-call(bf16[2048,512]{1,0:T(8,128)(2,1)S(1)} %copy-done.10, f32[2,64,128]{2,1,0:T(8,128)S(1)} %copy-done.9, bf16[768,512]{1,0:T(8,128)(2,1)S(1)} %copy-done.11, bf16[64,384]{1,0:T(8,128)(2,1)S(1)} %copy-done.12), custom_call_target="tpu_custom_call" | custom-call | flops 3000000000 | bytes 5000000 | tf_op jit(solution)/shard_map/filter_grads/pallas_call | solution.py:306
  75.6 0.0 collective-permute-done.4.refs_6_
  75.6 16.7 %all-to-all-done.1 = bf16[16,32,1664]{2,1,0:T(8,128)(2,1)S(1)} async-done(((bf16[16,32,1664]{2,1,0:T(8,128)(2,1)}), bf16[16,32,1664]{2,1,0:T(8,128)(2,1)S(1)}, u32[]{:S(2)}, u32[]{:S(2)}) %all-to-all-start.1) | async-done | bytes 1703968 | tf_op jit(solution)/shard_map/all_to_all | solution.py:581
  92.3 0.1 constant_dynamic-slice_fusion.1
  92.4 0.1 pad_maximum_fusion
  92.5 2.9 %collective-permute-start.6 = (bf16[512,640]{1,0:T(8,128)(2,1)S(1)}, bf16[512,640]{1,0:T(8,128)(2,1)S(1)}, u32[]{:S(2)}, u32[]{:S(2)}) collective-permute-start(bf16[512,640]{1,0:T(8,128)(2,1)S(1)} %pad_maximum_fusion), channel_id=1, source_target_pairs={{0,24},{4,28},{8,16},{12,20},{16,8},{20,12},{24,0},{28,4},{32,56},... | collective-permute-start | bytes 1966088 | tf_op jit(solution)/shard_map/ppermute | solution.py:585
  95.4 5.4 %shares.1 = bf16[16,512,128]{2,1,0:T(8,128)(2,1)} custom-call(bf16[512,1664]{1,0:T(8,128)(2,1)} %bitcast.17, bf16[256,1024]{1,0:T(8,128)(2,1)} %copy-done.7, bf16[256,1024]{1,0:T(8,128)(2,1)} %copy-done.13, bf16[256,1024]{1,0:T(8,128)(2,1)} %copy-done.14, bf16[256,1024]{1,0:T(8,128)(2,1)} %copy-done.15, bf16[256,1024]{1,0:T(8,128)(2,1)} %copy-done.8, ...), custom_call_target="tpu_custom_call" | custom-call | flops 2147483648 | bytes 7000000 | tf_op jit(solution)/shard_map/shares/pallas_call | solution.py:454
  100.8 5.3 %collective-permute-done.6.mate_ref = bf16[512,640]{1,0:T(8,128)(2,1)S(1)} collective-permute-done((bf16[512,640]{1,0:T(8,128)(2,1)S(1)}, bf16[512,640]{1,0:T(8,128)(2,1)S(1)}, u32[]{:S(2)}, u32[]{:S(2)}) %collective-permute-start.6) | collective-permute-done | bytes 655392 | tf_op jit(solution)/shard_map/ppermute | solution.py:585
  106.2 6.2 %all-to-all-start.2 = ((bf16[16,512,128]{2,1,0:T(8,128)(2,1)}), bf16[16,512,128]{2,1,0:T(8,128)(2,1)}, u32[]{:S(2)}, u32[]{:S(2)}) async-start(bf16[16,512,128]{2,1,0:T(8,128)(2,1)} %shares.1), calls=%async_computation.2 | async-start | bytes 4194304 | tf_op jit(solution)/shard_map/all_to_all | solution.py:581
  112.4 0.0 copy-start.1
  112.4 3.4 %copy-done.1 = bf16[4096,1024]{1,0:T(8,128)(2,1)S(1)} copy-done((bf16[4096,1024]{1,0:T(8,128)(2,1)S(1)}, bf16[4096,1024]{1,0:T(8,128)(2,1)}, u32[]{:S(2)}) %copy-start.1) | copy-done | bytes 8388632
  115.7 3.9 %input_terms.1 = (bf16[2,1024,256]{2,1,0:T(8,128)(2,1)S(1)}, f32[2,1024,256]{2,1,0:T(8,128)S(1)}) custom-call(s32[2]{0:T(128)S(1)} %pad_add_fusion.place_ref, bf16[512,1664]{1,0:T(8,128)(2,1)S(1)} %bitcast.18, bf16[512,640]{1,0:T(8,128)(2,1)S(1)} %collective-permute-done.6.mate_ref, bf16[4096,1024]{1,0:T(8,128)(2,1)S(1)} %copy-done.1), custom_call_target="tpu_custom_call" | custom-call | flops 2147483648 | bytes 12000000 | tf_op jit(solution)/shard_map/input_terms/pallas_call | solution.py:521
  119.6 0.0 copy-start.5
  119.6 0.0 copy-start.6
  119.6 0.1 collective-permute-start.7
  119.7 2.6 %collective-permute-done.7.core_ref = bf16[2,1024,256]{2,1,0:T(8,128)(2,1)S(1)} collective-permute-done((bf16[2,1024,256]{2,1,0:T(8,128)(2,1)S(1)}, bf16[2,1024,256]{2,1,0:T(8,128)(2,1)S(1)}, u32[]{:S(2)}, u32[]{:S(2)}) %collective-permute-start.7) | collective-permute-done | bytes 1048608 | tf_op jit(solution)/shard_map/ppermute | solution.py:616
  122.4 0.1 fusion
  122.5 2.3 %collective-permute-start.8 = (bf16[1024,256]{1,0:T(8,128)(2,1)S(1)}, bf16[1024,256]{1,0:T(8,128)(2,1)S(1)}, u32[]{:S(2)}, u32[]{:S(2)}) collective-permute-start(bf16[1024,256]{1,0:T(8,128)(2,1)S(1)} %fusion), channel_id=1, source_target_pairs={{0,2},{2,0},{1,3},{3,1},{4,6},{6,4},{5,7},{7,5},{8,10},{10,8},{9,1... | collective-permute-start | bytes 1572872 | tf_op jit(solution)/shard_map/ppermute | solution.py:618
  124.8 2.6 %gate_grad.1 = bf16[256,1024]{1,0:T(8,128)(2,1)} custom-call(s32[2]{0:T(128)S(1)} %pad_add_fusion.place_ref, bf16[512,1664]{1,0:T(8,128)(2,1)S(1)} %bitcast.19, bf16[512,640]{1,0:T(8,128)(2,1)S(1)} %collective-permute-done.6.mate_ref, bf16[256,1024]{1,0:T(8,128)(2,1)S(1)} %copy-done.5, bf16[256,1024]{1,0:T(8,128)(2,1)S(1)} %copy-done.6), custom_call_target="tpu_custom_call" | custom-call | flops 2000000 | bytes 2500000 | tf_op jit(solution)/shard_map/gate_grad/pallas_call | solution.py:560
  127.4 9.6 %collective-permute-done.8.chip_ref = bf16[1024,256]{1,0:T(8,128)(2,1)S(1)} collective-permute-done((bf16[1024,256]{1,0:T(8,128)(2,1)S(1)}, bf16[1024,256]{1,0:T(8,128)(2,1)S(1)}, u32[]{:S(2)}, u32[]{:S(2)}) %collective-permute-start.8) | collective-permute-done | bytes 524320 | tf_op jit(solution)/shard_map/ppermute | solution.py:618
  137.1 1.0 close_input.1
  138.1 2.3 %all-to-all-done.2.shares_ref = bf16[16,512,128]{2,1,0:T(8,128)(2,1)} async-done(((bf16[16,512,128]{2,1,0:T(8,128)(2,1)}), bf16[16,512,128]{2,1,0:T(8,128)(2,1)}, u32[]{:S(2)}, u32[]{:S(2)}) %all-to-all-start.2) | async-done | bytes 2097184 | tf_op jit(solution)/shard_map/all_to_all | solution.py:581
  140.3 2.8 %close_weight.1 = (f32[128,1024]{1,0:T(8,128)}, f32[7,1024]{1,0:T(8,128)}) custom-call(bf16[16,512,128]{2,1,0:T(8,128)(2,1)} %all-to-all-done.2.shares_ref, bf16[512,1664]{1,0:T(8,128)(2,1)S(1)} %bitcast.20, bf16[512,640]{1,0:T(8,128)(2,1)S(1)} %collective-permute-done.6.mate_ref), custom_call_target="tpu_custom_call" | custom-call | flops 2000000 | bytes 3000000 | tf_op jit(solution)/shard_map/close_weight/pallas_call | solution.py:487
  (30 shorter events, 0.1 us)
Async XLA Ops:
  0.6 35.7 %copy-start = (f32[7,1024]{1,0:T(8,128)S(1)}, f32[7,1024]{1,0:T(8,128)}, u32[]{:S(2)}) copy-start(f32[7,1024]{1,0:T(8,128)} %param.17) | copy-start | bytes 86020
  8.1 11.1 %copy-start.4 = (bf16[256,4096]{1,0:T(8,128)(2,1)S(1)}, bf16[256,4096]{1,0:T(8,128)(2,1)}, u32[]{:S(2)}) copy-start(bf16[256,4096]{1,0:T(8,128)(2,1)} %others_ref) | copy-start | bytes 6291460
  8.1 30.1 %all-to-all-start = ((bf16[32,64,256]{2,1,0:T(8,128)(2,1)}), bf16[32,64,256]{2,1,0:T(8,128)(2,1)}, u32[]{:S(2)}, u32[]{:S(2)}) async-start(bf16[32,64,256]{2,1,0:T(8,128)(2,1)} %sends.1), calls=%async_computation | async-start | bytes 2097152 | tf_op jit(solution)/shard_map/all_to_all | solution.py:581
  20.5 0.8 copy-start.8
  21.3 12.2 %copy-start.7 = (bf16[256,1024]{1,0:T(8,128)(2,1)}, bf16[256,1024]{1,0:T(8,128)(2,1)S(1)}, u32[]{:S(2)}) copy-start(bf16[256,1024]{1,0:T(8,128)(2,1)S(1)} %get-tuple-element.50.refs_0_) | copy-start | bytes 1572868
  21.3 34.5 %collective-permute-start = (bf16[256,1024]{1,0:T(8,128)(2,1)S(1)}, bf16[256,1024]{1,0:T(8,128)(2,1)S(1)}, u32[]{:S(2)}, u32[]{:S(2)}) collective-permute-start(bf16[256,1024]{1,0:T(8,128)(2,1)S(1)} %get-tuple-element.42), channel_id=1, source_target_pairs={{0,6},{1,7},{2,4},{3,5},{4,2},{5,3},{6,0},{7,1},{8,14},{9,15},{10,... | collective-permute-start | bytes 1572872 | tf_op jit(solution)/shard_map/ppermute | solution.py:593
  33.5 22.4 %collective-permute-start.1 = (bf16[256,1024]{1,0:T(8,128)(2,1)S(1)}, bf16[256,1024]{1,0:T(8,128)(2,1)S(1)}, u32[]{:S(2)}, u32[]{:S(2)}) collective-permute-start(bf16[256,1024]{1,0:T(8,128)(2,1)S(1)} %get-tuple-element.50.refs_0_), channel_id=1, source_target_pairs={{0,24},{4,28},{8,16},{12,20},{16,8},{20,12},{24,0},{28,4},{32,56},... | collective-permute-start | bytes 1572872 | tf_op jit(solution)/shard_map/ppermute | solution.py:585
  36.2 23.2 %collective-permute-start.2 = (bf16[256,1024]{1,0:T(8,128)(2,1)S(1)}, bf16[256,1024]{1,0:T(8,128)(2,1)S(1)}, u32[]{:S(2)}, u32[]{:S(2)}) collective-permute-start(bf16[256,1024]{1,0:T(8,128)(2,1)S(1)} %get-tuple-element.42), channel_id=1, source_target_pairs={{0,30},{1,31},{2,28},{3,29},{4,26},{5,27},{6,24},{7,25},{8,22},{9,... | collective-permute-start | bytes 1572872 | tf_op jit(solution)/shard_map/ppermute | solution.py:593
  55.8 10.8 %copy-start.9 = (f32[2,64,128]{2,1,0:T(8,128)S(1)}, f32[2,64,128]{2,1,0:T(8,128)}, u32[]{:S(2)}) copy-start(f32[2,64,128]{2,1,0:T(8,128)} %constant.78.clone.twist_ref) | copy-start | bytes 196612
  55.8 10.8 %copy-start.12 = (bf16[64,384]{1,0:T(8,128)(2,1)S(1)}, bf16[64,384]{1,0:T(8,128)(2,1)}, u32[]{:S(2)}) copy-start(bf16[64,384]{1,0:T(8,128)(2,1)} %constant.85.clone.last_nat_ref) | copy-start | bytes 147460
  55.8 3.5 %copy-start.13 = (bf16[256,1024]{1,0:T(8,128)(2,1)}, bf16[256,1024]{1,0:T(8,128)(2,1)S(1)}, u32[]{:S(2)}) copy-start(bf16[256,1024]{1,0:T(8,128)(2,1)S(1)} %collective-permute-done.refs_1_) | copy-start | bytes 1572868
  55.9 3.5 %copy-start.14 = (bf16[256,1024]{1,0:T(8,128)(2,1)}, bf16[256,1024]{1,0:T(8,128)(2,1)S(1)}, u32[]{:S(2)}) copy-start(bf16[256,1024]{1,0:T(8,128)(2,1)S(1)} %collective-permute-done.1.refs_2_) | copy-start | bytes 1572868
  59.4 0.8 copy-start.15
  60.2 32.2 %all-to-all-start.1 = ((bf16[16,32,1664]{2,1,0:T(8,128)(2,1)}), bf16[16,32,1664]{2,1,0:T(8,128)(2,1)S(1)}, u32[]{:S(2)}, u32[]{:S(2)}) async-start(bf16[16,32,1664]{2,1,0:T(8,128)(2,1)} %get-tuple-element.43), calls=%async_computation.1 | async-start | bytes 3407872 | tf_op jit(solution)/shard_map/all_to_all | solution.py:581
  66.0 9.6 %collective-permute-start.3 = (bf16[256,1024]{1,0:T(8,128)(2,1)}, bf16[256,1024]{1,0:T(8,128)(2,1)S(1)}, u32[]{:S(2)}, u32[]{:S(2)}) collective-permute-start(bf16[256,1024]{1,0:T(8,128)(2,1)} %copy-done.13), channel_id=1, source_target_pairs={{0,1},{1,0},{2,3},{3,2},{4,5},{5,4},{6,7},{7,6},{8,9},{9,8},{10,11... | collective-permute-start | bytes 1572872 | tf_op jit(solution)/shard_map/ppermute | solution.py:604
  66.0 9.6 %collective-permute-start.4 = (bf16[256,1024]{1,0:T(8,128)(2,1)}, bf16[256,1024]{1,0:T(8,128)(2,1)S(1)}, u32[]{:S(2)}, u32[]{:S(2)}) collective-permute-start(bf16[256,1024]{1,0:T(8,128)(2,1)} %copy-done.14), channel_id=1, source_target_pairs={{0,1},{1,0},{2,3},{3,2},{4,5},{5,4},{6,7},{7,6},{8,9},{9,8},{10,11... | collective-permute-start | bytes 1572872 | tf_op jit(solution)/shard_map/ppermute | solution.py:604
  66.5 9.1 %collective-permute-start.5 = (bf16[256,1024]{1,0:T(8,128)(2,1)}, bf16[256,1024]{1,0:T(8,128)(2,1)S(1)}, u32[]{:S(2)}, u32[]{:S(2)}) collective-permute-start(bf16[256,1024]{1,0:T(8,128)(2,1)} %copy-done.15), channel_id=1, source_target_pairs={{0,1},{1,0},{2,3},{3,2},{4,5},{5,4},{6,7},{7,6},{8,9},{9,8},{10,11... | collective-permute-start | bytes 1572872 | tf_op jit(solution)/shard_map/ppermute | solution.py:604
  66.6 1.6 %copy-start.10 = (bf16[2048,512]{1,0:T(8,128)(2,1)S(1)}, bf16[2048,512]{1,0:T(8,128)(2,1)}, u32[]{:S(2)}) copy-start(bf16[2048,512]{1,0:T(8,128)(2,1)} %get-tuple-element.44.lag_ref) | copy-start | bytes 6291460
  68.2 1.1 copy-start.11
  75.6 16.7 %copy-start.16 = (bf16[256,1024]{1,0:T(8,128)(2,1)}, bf16[256,1024]{1,0:T(8,128)(2,1)S(1)}, u32[]{:S(2)}) copy-start(bf16[256,1024]{1,0:T(8,128)(2,1)S(1)} %collective-permute-done.3.refs_5_) | copy-start | bytes 1572868
  75.6 16.8 %copy-start.17 = (bf16[256,1024]{1,0:T(8,128)(2,1)}, bf16[256,1024]{1,0:T(8,128)(2,1)S(1)}, u32[]{:S(2)}) copy-start(bf16[256,1024]{1,0:T(8,128)(2,1)S(1)} %collective-permute-done.4.refs_6_) | copy-start | bytes 1572868
  75.6 16.8 %copy-start.18 = (bf16[256,1024]{1,0:T(8,128)(2,1)}, bf16[256,1024]{1,0:T(8,128)(2,1)S(1)}, u32[]{:S(2)}) copy-start(bf16[256,1024]{1,0:T(8,128)(2,1)S(1)} %collective-permute-done.5.refs_7_) | copy-start | bytes 1572868
  92.3 3.1 %copy-start.2 = (bf16[16,32,1664]{2,1,0:T(8,128)(2,1)}, bf16[16,32,1664]{2,1,0:T(8,128)(2,1)S(1)}, u32[]{:S(2)}) copy-start(bf16[16,32,1664]{2,1,0:T(8,128)(2,1)S(1)} %all-to-all-done.1) | copy-start | bytes 5111812
  92.5 13.7 %collective-permute-start.6 = (bf16[512,640]{1,0:T(8,128)(2,1)S(1)}, bf16[512,640]{1,0:T(8,128)(2,1)S(1)}, u32[]{:S(2)}, u32[]{:S(2)}) collective-permute-start(bf16[512,640]{1,0:T(8,128)(2,1)S(1)} %pad_maximum_fusion), channel_id=1, source_target_pairs={{0,24},{4,28},{8,16},{12,20},{16,8},{20,12},{24,0},{28,4},{32,56},... | collective-permute-start | bytes 1966088 | tf_op jit(solution)/shard_map/ppermute | solution.py:585
  100.8 11.5 %copy-start.3 = (bf16[16,32,1664]{2,1,0:T(8,128)(2,1)S(1)}, bf16[16,32,1664]{2,1,0:T(8,128)(2,1)}, u32[]{:S(2)}) copy-start(bf16[16,32,1664]{2,1,0:T(8,128)(2,1)} %copy-done.2) | copy-start | bytes 5111812
  106.2 34.2 %all-to-all-start.2 = ((bf16[16,512,128]{2,1,0:T(8,128)(2,1)}), bf16[16,512,128]{2,1,0:T(8,128)(2,1)}, u32[]{:S(2)}, u32[]{:S(2)}) async-start(bf16[16,512,128]{2,1,0:T(8,128)(2,1)} %shares.1), calls=%async_computation.2 | async-start | bytes 4194304 | tf_op jit(solution)/shard_map/all_to_all | solution.py:581
  112.4 3.4 %copy-start.1 = (bf16[4096,1024]{1,0:T(8,128)(2,1)S(1)}, bf16[4096,1024]{1,0:T(8,128)(2,1)}, u32[]{:S(2)}) copy-start(bf16[4096,1024]{1,0:T(8,128)(2,1)} %weight_ref.1) | copy-start | bytes 25165828
  119.6 5.2 %copy-start.5 = (bf16[256,1024]{1,0:T(8,128)(2,1)S(1)}, bf16[256,1024]{1,0:T(8,128)(2,1)}, u32[]{:S(2)}) copy-start(bf16[256,1024]{1,0:T(8,128)(2,1)} %gate_ref.1) | copy-start | bytes 1572868
  119.6 5.2 %copy-start.6 = (bf16[256,1024]{1,0:T(8,128)(2,1)S(1)}, bf16[256,1024]{1,0:T(8,128)(2,1)}, u32[]{:S(2)}) copy-start(bf16[256,1024]{1,0:T(8,128)(2,1)} %grad_ref.1) | copy-start | bytes 1572868
  119.6 2.7 %collective-permute-start.7 = (bf16[2,1024,256]{2,1,0:T(8,128)(2,1)S(1)}, bf16[2,1024,256]{2,1,0:T(8,128)(2,1)S(1)}, u32[]{:S(2)}, u32[]{:S(2)}) collective-permute-start(bf16[2,1024,256]{2,1,0:T(8,128)(2,1)S(1)} %get-tuple-element.58), channel_id=1, source_target_pairs={{0,1},{1,0},{2,3},{3,2},{4,5},{5,4},{6,7},{7,6},{8,9},{9,8},{10,11... | collective-permute-start | bytes 3145736 | tf_op jit(solution)/shard_map/ppermute | solution.py:616
  122.5 14.5 %collective-permute-start.8 = (bf16[1024,256]{1,0:T(8,128)(2,1)S(1)}, bf16[1024,256]{1,0:T(8,128)(2,1)S(1)}, u32[]{:S(2)}, u32[]{:S(2)}) collective-permute-start(bf16[1024,256]{1,0:T(8,128)(2,1)S(1)} %fusion), channel_id=1, source_target_pairs={{0,2},{2,0},{1,3},{3,1},{4,6},{6,4},{5,7},{7,5},{8,10},{10,8},{9,1... | collective-permute-start | bytes 1572872 | tf_op jit(solution)/shard_map/ppermute | solution.py:618

commit v5 on v4

--- a/solution.py
+++ b/solution.py
@@ -152,7 +152,7 @@
 
 def mixer_kernel(
     taps_ref, arrived_ref, spectra_ref, first_split_ref, twist_ref, forward_ref, inverse_ref, last_split_ref,
-    back_ref, lag_ref,
+    back_ref, lag_ref, taps_out_ref,
     values_buf, slopes_buf, back_buf, mixed_buf, taps_buf, extra_buf, signal_buf, product_buf,
 ):
     blocks, width = arrived_ref.shape[0], arrived_ref.shape[1] // 2
@@ -262,8 +262,9 @@
                 piece = rest.astype(jnp.bfloat16).astype(jnp.float32)
                 packed = jnp.where(lane == 8 * p + k, piece, packed)
                 rest = rest - piece
-        for d in range(blocks // 2):
-            back_ref[d, :, 12 * LANES:] = packed.astype(jnp.bfloat16)
+        packed = jnp.concatenate([packed, jnp.zeros((LANES - width, LANES), jnp.float32)], axis=0).T
+        rows = packed[:8] + pltpu.roll(packed[8:16], width, 1) + pltpu.roll(packed[16:24], 2 * width, 1)
+        taps_out_ref[...] = jnp.concatenate([rows, jnp.zeros_like(rows)], axis=0).astype(jnp.bfloat16)
 
 
 def whole(shape):
@@ -316,17 +317,18 @@
 def mixer(own_taps, arrived, spectra):
     blocks, width, span = arrived.shape[0], arrived.shape[1] // 2, arrived.shape[2]
     consts, specs = tables_of(("first_split", "twist", "forward", "inverse", "last_split"))
-    back_shape = (blocks // 2, width, 6 * span + LANES)
+    back_shape = (blocks // 2, width, 6 * span)
     rows, batch = (2, blocks * width, LANES), GROUP * GROUPS
     return call(
         mixer_kernel, "mixer", 100_000_000, 1_000_000, vmem=56,
         grid=(width // batch,),
         in_specs=[pl.BlockSpec(memory_space=pltpu.SMEM), whole(arrived.shape),
                   pl.BlockSpec((batch * ROWS, 2 * LANES), lambda i: (i, 0))] + specs,
-        out_specs=[whole(back_shape), pl.BlockSpec((batch * ROWS, 4 * LANES), lambda i: (i, 0))],
+        out_specs=[whole(back_shape), pl.BlockSpec((batch * ROWS, 4 * LANES), lambda i: (i, 0)), whole((16, LANES))],
         out_shape=[
             jax.ShapeDtypeStruct(back_shape, jnp.bfloat16),
             jax.ShapeDtypeStruct((width * ROWS, 4 * LANES), jnp.bfloat16),
+            jax.ShapeDtypeStruct((16, LANES), jnp.bfloat16),
         ],
         scratch_shapes=[
             pltpu.VMEM(rows, jnp.float32),
@@ -341,7 +343,7 @@
     )(own_taps, arrived, spectra, *consts)
 
 
-STREAMS = 4
+STREAMS = 8
 
 
 def send_kernel(rows_ref, *refs):
@@ -353,9 +355,14 @@
     slopes = (grad_ref[...].astype(jnp.float32) * sig).T.astype(jnp.bfloat16)
     out_ref[pl.ds(step * count, count), width:, :] = slopes.reshape(count, width, span)
     part = weight_refs[0].shape[0]
-    term = dot(rows_ref[:, :part], weight_refs[0][...])
-    for j in range(1, STREAMS):
-        term = term + dot(rows_ref[:, j * part:(j + 1) * part], weight_refs[j][...])
+    sides = []
+    for side in range(2):
+        refs = weight_refs[side::2]
+        term = dot(rows_ref[:, :part], refs[0][...])
+        for j in range(1, len(refs)):
+            term = term + dot(rows_ref[:, j * part:(j + 1) * part], refs[j][...])
+        sides.append(term)
+    term = jnp.concatenate(sides, axis=1)
 
     @pl.when(step == 0)
     def _():
@@ -376,7 +383,8 @@
     channels = w_value.shape[1]
     width = channels // count
     block = pl.BlockSpec((span, channels // steps), lambda i: (0, i))
-    streams = [pl.BlockSpec((depth // (steps * STREAMS), channels), functools.partial(lambda j, i: (STREAMS * i + j, 0), j))
+    streams = [pl.BlockSpec((2 * depth // (steps * STREAMS), channels // 2),
+                            functools.partial(lambda j, i: (STREAMS // 2 * i + j // 2, j % 2), j))
                for j in range(STREAMS)]
     return call(
         send_kernel, "sends", 2 * span * depth * channels, 12_500_000, vmem=56, grid=(steps,),
@@ -417,8 +425,8 @@
 
 
 def share_kernel(back_ref, *refs):
-    parts, (out_ref, back_buf, rows_buf, out_buf, in_sem, out_sem) = refs[:8], refs[8:]
-    span = rows_buf.shape[1]
+    parts, (taps_ref, out_ref, back_buf, rows_buf, out_buf, in_sem, out_sem) = refs[:8], refs[8:]
+    span, rows = rows_buf.shape[1], back_buf.shape[0]
     loads = [pltpu.make_async_copy(back_ref.at[:, pl.ds(0, 4 * span)], back_buf, in_sem.at[8])]
     loads += [pltpu.make_async_copy(part, rows_buf.at[n], in_sem.at[n]) for n, part in enumerate(parts)]
     for load in loads:
@@ -438,8 +446,9 @@
                 product = term if product is None else product + term
             product = product.astype(jnp.bfloat16)
             n = 4 * half + two
-            out_buf[2 * n] = product[:, :LANES]
-            out_buf[2 * n + 1] = product[:, LANES:]
+            for m in range(2):
+                out_buf[2 * n + m, :rows] = product[:, m * LANES:(m + 1) * LANES]
+                out_buf[2 * n + m, rows:] = taps_ref[...]
             store = pltpu.make_async_copy(
                 out_buf.at[pl.ds(2 * n, 2)], out_ref.at[pl.ds(first + 2 * two, 2)], out_sem.at[n])
             store.start()
@@ -448,19 +457,19 @@
         store.wait()
 
 
-def shares(back, mine, other):
+def shares(back, mine, other, taps):
     span, depth = mine[0].shape
     rows = back.shape[0]
     return call(
         share_kernel, "shares", 16 * rows * span * depth, 7_000_000, vmem=60,
-        in_specs=[pl.BlockSpec(memory_space=pl.ANY)] * 9,
+        in_specs=[pl.BlockSpec(memory_space=pl.ANY)] * 9 + [pl.BlockSpec(memory_space=pltpu.VMEM)],
         out_specs=pl.BlockSpec(memory_space=pl.ANY),
-        out_shape=jax.ShapeDtypeStruct((16, rows, LANES), jnp.bfloat16),
+        out_shape=jax.ShapeDtypeStruct((16, rows + 16, LANES), jnp.bfloat16),
         scratch_shapes=[
             pltpu.VMEM((rows, 4 * span), jnp.bfloat16), pltpu.VMEM((8, span, depth), jnp.bfloat16),
-            pltpu.VMEM((16, rows, LANES), jnp.bfloat16),
+            pltpu.VMEM((16, rows + 16, LANES), jnp.bfloat16),
             pltpu.SemaphoreType.DMA((9,)), pltpu.SemaphoreType.DMA((8,))],
-    )(back, *mine, *other)
+    )(back, *mine, *other, taps)
 
 
 def merge(pair, mine, mate):
@@ -469,29 +478,38 @@
     return jnp.concatenate([first[half:], first[:half], second[:half], second[half:]], axis=0)
 
 
-def weight_kernel(shares_ref, taps_ref, mate_ref, weight_ref, tap_sums_ref):
-    for x in range(4):
-        rows, lanes = slice(x * LANES, (x + 1) * LANES), slice(x * 2 * LANES, (x + 1) * 2 * LANES)
+def weight_kernel(*refs):
+    share_refs, (taps_ref, weight_ref, tap_sums_ref) = refs[:4], refs[4:]
+    for x, ref in enumerate(share_refs):
         totals = []
         for pair in range(2):
-            terms = [shares_ref[j, rows, :].astype(jnp.float32) for j in range(16) if j % 4 // 2 == pair]
+            terms = [ref[j].astype(jnp.float32) for j in range(16) if j % 4 // 2 == pair]
             totals.append(sum(terms[1:], terms[0]))
-        weight_ref[:, lanes] = merge(0, *totals).T
-        packed = merge(quad_place() // 2, taps_ref[rows, :].astype(jnp.float32), mate_ref[rows, :].astype(jnp.float32)).T
-        tap_sums_ref[:, lanes] = (packed[16:24] + packed[8:16] + packed[0:8])[:TAPS]
-
-
-def close_weight(parts, back, mate):
+        weight_ref[:, x * 2 * LANES:(x + 1) * 2 * LANES] = merge(0, *totals).T
+    z = lax.axis_index("seq") % 2
+    lane = lax.broadcasted_iota(jnp.int32, (8, LANES), 1)
+    for x in range(8):
+        row = jnp.zeros((8, LANES), jnp.float32)
+        for n in range(4):
+            packed = taps_ref[2 * x + n // 2].astype(jnp.float32)
+            packed = jnp.where(z == n % 2, packed[:8], packed[8:])
+            packed = packed + pltpu.roll(packed, LANES - 32, 1) + pltpu.roll(packed, LANES - 64, 1)
+            row = jnp.where(lane // 32 == n, packed if n == 0 else pltpu.roll(packed, 32 * n, 1), row)
+        tap_sums_ref[:, x * LANES:(x + 1) * LANES] = row[:TAPS]
+
+
+def close_weight(parts):
     count, rows, span = parts.shape
+    rows -= 16
     channels = 2 * rows
     return call(
         weight_kernel, "close_weight", 2_000_000, 3_000_000, grid=(1,),
-        in_specs=[whole(parts.shape),
-                  pl.BlockSpec((rows, LANES), lambda i: (0, 12)), pl.BlockSpec((rows, LANES), lambda i: (0, 4))],
+        in_specs=[pl.BlockSpec((count, LANES, span), functools.partial(lambda x, i: (0, x, 0), x)) for x in range(4)]
+        + [pl.BlockSpec((count, 16, span), lambda i: (0, rows // 16, 0))],
         out_specs=[whole((span, channels)), whole((TAPS, channels))],
         out_shape=[jax.ShapeDtypeStruct((span, channels), jnp.float32),
                    jax.ShapeDtypeStruct((TAPS, channels), jnp.float32)],
-    )(parts, back, mate)
+    )(*[parts] * 5)
 
 
 def input_kernel(place_ref, back_ref, mate_ref, weight_ref, send_ref, keep_ref, own_buf):
@@ -599,17 +617,18 @@
     mine = [same, first, mates(same), across(cross, 1 ^ MATE)]
 
     own_taps = lax.dynamic_slice_in_dim(short_taps, seq_at * width, width, 1)
-    back, lag = mixer(own_taps, arrived, spectra)
+    back, lag, taps = mixer(own_taps, arrived, spectra)
     back, mine = lax.optimization_barrier((back, mine))
     other = [other] + [lax.ppermute(part, "tp", cores) for part in mine[1:]]
     back = exchange(back, LEAGUES).reshape(channels // 2, back.shape[2])
     grad_filters = filter_grads(lag)
-    back, grad_filters, other = lax.optimization_barrier((back, grad_filters, other))
+    partner = lax.ppermute(taps, "seq", [(s, s ^ 1) for s in range(seq_count)])
+    taps = jnp.concatenate([taps[:8], partner[:8]], axis=0)
+    back, grad_filters, other, taps = lax.optimization_barrier((back, grad_filters, other, taps))
     mate = mates(jnp.concatenate([
         lax.dynamic_slice_in_dim(back, (quad_at ^ 2) * span, span, 1),
-        lax.dynamic_slice_in_dim(back, 4 * span + (1 - quad_at // 2) * span, span, 1),
-        back[:, 6 * span:]], axis=1))
-    outgoing, mate = lax.optimization_barrier((shares(back, mine, other), mate))
+        lax.dynamic_slice_in_dim(back, 4 * span + (1 - quad_at // 2) * span, span, 1)], axis=1))
+    outgoing, mate = lax.optimization_barrier((shares(back, mine, other, taps), mate))
     parts = exchange(outgoing, PLANES)
 
     send, keep = input_terms(place, back, mate, w_value)
@@ -619,7 +638,7 @@
     grad_input = close_input(keep, core, chip)
     grad_gate = gate_grad(place, back, mate, gate_proj, grad_out)
     parts, grad_input, grad_gate = lax.optimization_barrier((parts, grad_input, grad_gate))
-    grad_weight, grad_taps = close_weight(parts, back, mate)
+    grad_weight, grad_taps = close_weight(parts)
     return (grad_input, grad_weight, grad_taps, grad_filters, grad_gate)
 
 

time: 144 us -> 138 us (0.958)
  waiting for transfers between devices: 41.2 us -> 32.2 us
  starting transfers between devices: 35.2 us -> 38 us
    all_to_all x3, waiting for transfers between devices: 20.1 us -> 15 us  [exchange(): lax.all_to_all(value, 'seq', split_axis=0, concat_axis=0, axis_index_grou...]
    ppermute x0 -> x1, starting transfers between devices: none -> 2.97 us  [local(): partner = lax.ppermute(taps, 'seq', [(s, s ^ 1) for s in range(seq_count)])]
    ppermute x2, starting transfers between devices: 5.63 us -> 3.32 us  [mates(): return lax.ppermute(value, 'seq', [(s, s ^ MATE) for s in range(seq_count)])]
    ppermute x2, starting transfers between devices: 3.57 us -> 5.88 us  [across(): lax.ppermute(value, ('seq', 'tp'), [(4 * s + t, 4 * (s ^ flip) + (t ^ 2))...]
    ppermute x2, waiting for transfers between devices: 3.48 us -> 1.51 us  [across(): lax.ppermute(value, ('seq', 'tp'), [(4 * s + t, 4 * (s ^ flip) + (t ^ 2))...]
    ppermute x2, waiting for transfers between devices: 5.32 us -> 3.37 us  [mates(): return lax.ppermute(value, 'seq', [(s, s ^ MATE) for s in range(seq_count)])]
    unnamed x38 -> x34, local copies, waits for them, and re-layouts: 7.75 us -> 7.23 us
  transfers between devices with their start and end apart: 12 -> 13, of which waited for: 7 -> 8; matrix products, arithmetic and copies ran while one was open for 1% -> 1% of each run, Pallas kernels for 33% -> 35%
where the time goes in v5:
time: 138 us; the launch traced here: 137 us
  Pallas kernels  56.8 us (41%)
  starting transfers between devices  38 us (28%)
  waiting for transfers between devices  32.2 us (23%)
  local copies, waits for them, and re-layouts  7.93 us (6%)
    all_to_all x3, starting transfers between devices, exchange(): lax.all_to_all(value, 'seq', split_axis=0, concat_axis=0, axis_index_grou...  22.8 us
    pallas_call x1, Pallas kernels, mixer(): call(mixer_kernel, 'mixer', 100000000, 1000000, vmem=56, grid=(width // b...  17.6 us
    all_to_all x3, waiting for transfers between devices, exchange(): lax.all_to_all(value, 'seq', split_axis=0, concat_axis=0, axis_index_grou...  15 us
    ppermute x1, waiting for transfers between devices, local(): chip = lax.ppermute(send, 'tp', chips)  9.73 us
    pallas_call x1, Pallas kernels, spectra_of(): call(spectra_kernel, 'spectra', 3000000000, 5000000, vmem=56, grid=(width...  8.8 us
    pallas_call x1, Pallas kernels, sends(): call(send_kernel, 'sends', 2 * span * depth * channels, 12500000, vmem=56...  7.33 us
    unnamed x34, local copies, waits for them, and re-layouts  7.23 us
    pallas_call x1, Pallas kernels, filter_grads(): call(lag_kernel, 'filter_grads', 3000000000, 5000000, grid=(width // BATC...  6.21 us
  transfers between devices with their start and end apart: 13, of which 8 were waited for; matrix products, arithmetic and copies ran while one was open for 1% of the time, Pallas kernels for 35%

profile of v5, /device:TPU:0, one launch (start us, length us, event | category | flops | bytes accessed | tf_op | source)
XLA Modules:
  0.0 136.7 jit_solution(2769058311141340430)
XLA Ops:
  0.6 0.0 copy-start
  0.6 7.3 %sends.1 = bf16[32,64,256]{2,1,0:T(8,128)(2,1)} custom-call(bf16[256,4096]{1,0:T(8,128)(2,1)} %others_ref, bf16[4096,1024]{1,0:T(8,128)(2,1)} %weight_ref.1, bf16[4096,1024]{1,0:T(8,128)(2,1)} %weight_ref.1, bf16[4096,1024]{1,0:T(8,128)(2,1)} %weight_ref.1, bf16[4096,1024]{1,0:T(8,128)(2,1)} %weight_ref.1, bf16[4096,1024]{1,0:T(8,128)(2,1)} %weight_ref.1, ...), custom_call_target="tpu_custom_call" | custom-call | flops 2147483648 | bytes 12500000 | tf_op jit(solution)/shard_map/sends/pallas_call | solution.py:389
  8.0 11.0 %all-to-all-start = ((bf16[32,64,256]{2,1,0:T(8,128)(2,1)}), bf16[32,64,256]{2,1,0:T(8,128)(2,1)}, u32[]{:S(2)}, u32[]{:S(2)}) async-start(bf16[32,64,256]{2,1,0:T(8,128)(2,1)} %sends.1), calls=%async_computation | async-start | bytes 2097152 | tf_op jit(solution)/shard_map/all_to_all | solution.py:599
  19.0 0.1 pad_add_fusion.place_ref
  19.1 2.0 %quarters.1 = (bf16[256,1024]{1,0:T(8,128)(2,1)S(1)}, bf16[256,1024]{1,0:T(8,128)(2,1)}, bf16[256,1024]{1,0:T(8,128)(2,1)S(1)}) custom-call(s32[2]{0:T(128)S(1)} %pad_add_fusion.place_ref, bf16[256,4096]{1,0:T(8,128)(2,1)S(1)} %copy-done.2, bf16[256,4096]{1,0:T(8,128)(2,1)S(1)} %copy-done.2), custom_call_target="tpu_custom_call" | custom-call | bytes 5000000 | tf_op jit(solution)/shard_map/quarters/pallas_call | solution.py:411
  21.1 3.4 %collective-permute-start = (bf16[256,1024]{1,0:T(8,128)(2,1)}, bf16[256,1024]{1,0:T(8,128)(2,1)}, u32[]{:S(2)}, u32[]{:S(2)}) collective-permute-start(bf16[256,1024]{1,0:T(8,128)(2,1)} %get-tuple-element.44), channel_id=1, source_target_pairs={{0,6},{1,7},{2,4},{3,5},{4,2},{5,3},{6,0},{7,1},{8,14},{9,15},{10,... | collective-permute-start | bytes 1572872 | tf_op jit(solution)/shard_map/ppermute | solution.py:611
  24.4 8.8 %spectra.1.spectra_ref = f32[2048,256]{1,0:T(8,128)} custom-call(f32[2,4,512,128]{3,2,1,0:T(8,128)} %bitcast.19, bf16[128,256]{1,0:T(8,128)(2,1)} %constant.77.clone.first_nat_ref, f32[2,64,128]{2,1,0:T(8,128)} %constant.78.clone.twist_ref, bf16[1536,256]{1,0:T(8,128)(2,1)} %constant.79.clone.pair_ref), custom_call_target="tpu_custom_call" | custom-call | flops 3000000000 | bytes 5000000 | tf_op jit(solution)/shard_map/spectra/pallas_call | solution.py:294
  33.2 2.5 %collective-permute-start.2 = (bf16[256,1024]{1,0:T(8,128)(2,1)}, bf16[256,1024]{1,0:T(8,128)(2,1)S(1)}, u32[]{:S(2)}, u32[]{:S(2)}) collective-permute-start(bf16[256,1024]{1,0:T(8,128)(2,1)} %get-tuple-element.44), channel_id=1, source_target_pairs={{0,30},{1,31},{2,28},{3,29},{4,26},{5,27},{6,24},{7,25},{8,22},{9,... | collective-permute-start | bytes 1572872 | tf_op jit(solution)/shard_map/ppermute | solution.py:611
  35.8 0.6 collective-permute-start.1
  36.3 0.7 constant_dynamic-slice_fusion.2.taps_ref
  37.0 1.1 all-to-all-done.arrived_ref
  38.1 17.6 %mixer.1 = (bf16[16,32,1536]{2,1,0:T(8,128)(2,1)}, bf16[2048,512]{1,0:T(8,128)(2,1)}, bf16[16,128]{1,0:T(8,128)(2,1)}) custom-call(f32[7,32]{1,0:T(8,128)} %constant_dynamic-slice_fusion.2.taps_ref, bf16[32,64,256]{2,1,0:T(8,128)(2,1)} %all-to-all-done.arrived_ref, f32[2048,256]{1,0:T(8,128)} %spectra.1.spectra_ref, ...), custom_call_target="tpu_custom_call" | custom-call | flops 100000000 | bytes 1000000 | tf_op jit(solution)/shard_map/mixer/pallas_call | solution.py:322
  55.7 0.0 copy-start.11
  55.7 0.0 copy-start.12
  55.7 1.5 %collective-permute-done.refs_1_ = bf16[256,1024]{1,0:T(8,128)(2,1)} collective-permute-done((bf16[256,1024]{1,0:T(8,128)(2,1)}, bf16[256,1024]{1,0:T(8,128)(2,1)}, u32[]{:S(2)}, u32[]{:S(2)}) %collective-permute-start) | collective-permute-done | bytes 524320 | tf_op jit(solution)/shard_map/ppermute | solution.py:611
  57.2 1.6 %collective-permute-done.1.refs_2_ = bf16[256,1024]{1,0:T(8,128)(2,1)S(1)} collective-permute-done((bf16[256,1024]{1,0:T(8,128)(2,1)S(1)}, bf16[256,1024]{1,0:T(8,128)(2,1)S(1)}, u32[]{:S(2)}, u32[]{:S(2)}) %collective-permute-start.1) | collective-permute-done | bytes 524320 | tf_op jit(solution)/shard_map/ppermute | solution.py:603
  58.8 0.8 copy-done.15
  59.6 6.5 %all-to-all-start.1 = ((bf16[16,32,1536]{2,1,0:T(8,128)(2,1)}), bf16[16,32,1536]{2,1,0:T(8,128)(2,1)S(1)}, u32[]{:S(2)}, u32[]{:S(2)}) async-start(bf16[16,32,1536]{2,1,0:T(8,128)(2,1)} %get-tuple-element.45), calls=%async_computation.1 | async-start | bytes 3145728 | tf_op jit(solution)/shard_map/all_to_all | solution.py:599
  66.1 0.0 collective-permute-start.3
  66.1 0.5 collective-permute-start.4
  66.6 0.1 collective-permute-start.5
  66.7 3.0 %collective-permute-start.6 = (bf16[16,128]{1,0:T(8,128)(2,1)S(1)}, bf16[16,128]{1,0:T(8,128)(2,1)S(1)}, u32[]{:S(2)}, u32[]{:S(2)}) collective-permute-start(bf16[16,128]{1,0:T(8,128)(2,1)S(1)} %copy-done.13), channel_id=1, source_target_pairs={{0,4},{4,0},{8,12},{12,8},{16,20},{20,16},{24,28},{28,24},{32,36},... | collective-permute-start | bytes 12296 | tf_op jit(solution)/shard_map/ppermute | solution.py:625
  69.7 1.6 %copy-done.8 = bf16[2048,512]{1,0:T(8,128)(2,1)S(1)} copy-done((bf16[2048,512]{1,0:T(8,128)(2,1)S(1)}, bf16[2048,512]{1,0:T(8,128)(2,1)}, u32[]{:S(2)}) %copy-start.8) | copy-done | bytes 2097176
  71.3 6.2 %filter_grads.1 = f32[2,4,512,128]{3,2,1,0:T(8,128)} custom-call(bf16[2048,512]{1,0:T(8,128)(2,1)S(1)} %copy-done.8, f32[2,64,128]{2,1,0:T(8,128)S(1)} %copy-done.7, bf16[768,512]{1,0:T(8,128)(2,1)S(1)} %copy-done.11, bf16[64,384]{1,0:T(8,128)(2,1)S(1)} %copy-done.12), custom_call_target="tpu_custom_call" | custom-call | flops 3000000000 | bytes 5000000 | tf_op jit(solution)/shard_map/filter_grads/pallas_call | solution.py:307
  77.5 0.0 collective-permute-done.6
  77.5 0.6 pad_maximum_fusion.1.refs_8_
  78.1 0.0 collective-permute-done.4.refs_6_
  78.1 0.0 collective-permute-done.5.refs_7_
  78.1 12.4 %all-to-all-done.1 = bf16[16,32,1536]{2,1,0:T(8,128)(2,1)S(1)} async-done(((bf16[16,32,1536]{2,1,0:T(8,128)(2,1)}), bf16[16,32,1536]{2,1,0:T(8,128)(2,1)S(1)}, u32[]{:S(2)}, u32[]{:S(2)}) %all-to-all-start.1) | async-done | bytes 1572896 | tf_op jit(solution)/shard_map/all_to_all | solution.py:599
  90.6 2.8 %collective-permute-start.7 = (bf16[512,512]{1,0:T(8,128)(2,1)S(1)}, bf16[512,512]{1,0:T(8,128)(2,1)S(1)}, u32[]{:S(2)}, u32[]{:S(2)}) collective-permute-start(bf16[512,512]{1,0:T(8,128)(2,1)S(1)} %pad_maximum_fusion), channel_id=1, source_target_pairs={{0,24},{4,28},{8,16},{12,20},{16,8},{20,12},{24,0},{28,4},{32,56},... | collective-permute-start | bytes 1572872 | tf_op jit(solution)/shard_map/ppermute | solution.py:603
  93.4 6.1 %shares.1 = bf16[16,528,128]{2,1,0:T(8,128)(2,1)} custom-call(bf16[512,1536]{1,0:T(8,128)(2,1)} %bitcast.16, bf16[256,1024]{1,0:T(8,128)(2,1)} %copy-done.9, bf16[256,1024]{1,0:T(8,128)(2,1)} %collective-permute-done.refs_1_, bf16[256,1024]{1,0:T(8,128)(2,1)} %copy-done.15, bf16[256,1024]{1,0:T(8,128)(2,1)} %copy-done.14, bf16[256,1024]{1,0:T(8,128)(2,1)} %copy-done.10, ...), custom_call_target="tpu_custom_call" | custom-call | flops 2147483648 | bytes 7000000 | tf_op jit(solution)/shard_map/shares/pallas_call | solution.py:463
  99.5 1.8 %collective-permute-done.7.mate_ref = bf16[512,512]{1,0:T(8,128)(2,1)S(1)} collective-permute-done((bf16[512,512]{1,0:T(8,128)(2,1)S(1)}, bf16[512,512]{1,0:T(8,128)(2,1)S(1)}, u32[]{:S(2)}, u32[]{:S(2)}) %collective-permute-start.7) | collective-permute-done | bytes 524320 | tf_op jit(solution)/shard_map/ppermute | solution.py:603
  101.3 5.4 %all-to-all-start.2 = ((bf16[16,528,128]{2,1,0:T(8,128)(2,1)}), bf16[16,528,128]{2,1,0:T(8,128)(2,1)S(1)}, u32[]{:S(2)}, u32[]{:S(2)}) async-start(bf16[16,528,128]{2,1,0:T(8,128)(2,1)} %shares.1), calls=%async_computation.2 | async-start | bytes 4325376 | tf_op jit(solution)/shard_map/all_to_all | solution.py:599
  106.7 0.0 copy-start.1
  106.7 3.4 %copy-done.1 = bf16[4096,1024]{1,0:T(8,128)(2,1)S(1)} copy-done((bf16[4096,1024]{1,0:T(8,128)(2,1)S(1)}, bf16[4096,1024]{1,0:T(8,128)(2,1)}, u32[]{:S(2)}) %copy-start.1) | copy-done | bytes 8388632
  110.0 1.4 %copy-done.4 = bf16[16,32,1536]{2,1,0:T(8,128)(2,1)S(1)} copy-done((bf16[16,32,1536]{2,1,0:T(8,128)(2,1)S(1)}, bf16[16,32,1536]{2,1,0:T(8,128)(2,1)}, u32[]{:S(2)}) %copy-start.4) | copy-done | bytes 1572888
  111.5 3.8 %input_terms.1 = (bf16[2,1024,256]{2,1,0:T(8,128)(2,1)S(1)}, f32[2,1024,256]{2,1,0:T(8,128)S(1)}) custom-call(s32[2]{0:T(128)S(1)} %pad_add_fusion.place_ref, bf16[512,1536]{1,0:T(8,128)(2,1)S(1)} %bitcast.17, bf16[512,512]{1,0:T(8,128)(2,1)S(1)} %collective-permute-done.7.mate_ref, bf16[4096,1024]{1,0:T(8,128)(2,1)S(1)} %copy-done.1), custom_call_target="tpu_custom_call" | custom-call | flops 2147483648 | bytes 12000000 | tf_op jit(solution)/shard_map/input_terms/pallas_call | solution.py:539
  115.3 0.0 copy-start.5
  115.3 0.0 copy-start.6
  115.3 0.1 collective-permute-start.8
  115.4 2.6 %collective-permute-done.8.core_ref = bf16[2,1024,256]{2,1,0:T(8,128)(2,1)S(1)} collective-permute-done((bf16[2,1024,256]{2,1,0:T(8,128)(2,1)S(1)}, bf16[2,1024,256]{2,1,0:T(8,128)(2,1)S(1)}, u32[]{:S(2)}, u32[]{:S(2)}) %collective-permute-start.8) | collective-permute-done | bytes 1048608 | tf_op jit(solution)/shard_map/ppermute | solution.py:635
  118.1 0.1 fusion
  118.2 2.3 %collective-permute-start.9 = (bf16[1024,256]{1,0:T(8,128)(2,1)S(1)}, bf16[1024,256]{1,0:T(8,128)(2,1)S(1)}, u32[]{:S(2)}, u32[]{:S(2)}) collective-permute-start(bf16[1024,256]{1,0:T(8,128)(2,1)S(1)} %fusion), channel_id=1, source_target_pairs={{0,2},{2,0},{1,3},{3,1},{4,6},{6,4},{5,7},{7,5},{8,10},{10,8},{9,1... | collective-permute-start | bytes 1572872 | tf_op jit(solution)/shard_map/ppermute | solution.py:637
  120.5 2.5 %gate_grad.1 = bf16[256,1024]{1,0:T(8,128)(2,1)} custom-call(s32[2]{0:T(128)S(1)} %pad_add_fusion.place_ref, bf16[512,1536]{1,0:T(8,128)(2,1)S(1)} %bitcast.18, bf16[512,512]{1,0:T(8,128)(2,1)S(1)} %collective-permute-done.7.mate_ref, bf16[256,1024]{1,0:T(8,128)(2,1)S(1)} %copy-done.5, bf16[256,1024]{1,0:T(8,128)(2,1)S(1)} %copy-done.6), custom_call_target="tpu_custom_call" | custom-call | flops 2000000 | bytes 2500000 | tf_op jit(solution)/shard_map/gate_grad/pallas_call | solution.py:578
  123.0 9.7 %collective-permute-done.9.chip_ref = bf16[1024,256]{1,0:T(8,128)(2,1)S(1)} collective-permute-done((bf16[1024,256]{1,0:T(8,128)(2,1)S(1)}, bf16[1024,256]{1,0:T(8,128)(2,1)S(1)}, u32[]{:S(2)}, u32[]{:S(2)}) %collective-permute-start.9) | collective-permute-done | bytes 524320 | tf_op jit(solution)/shard_map/ppermute | solution.py:637
  132.7 1.0 close_input.1
  133.8 1.5 %all-to-all-done.2.refs_0_.refs_1_.refs_2_.refs_3_.refs_4_ = bf16[16,528,128]{2,1,0:T(8,128)(2,1)S(1)} async-done(((bf16[16,528,128]{2,1,0:T(8,128)(2,1)}), bf16[16,528,128]{2,1,0:T(8,128)(2,1)S(1)}, u32[]{:S(2)}, u32[]{:S(2)}) %all-to-all-start.2) | async-done | bytes 2162720 | tf_op jit(solution)/shard_map/all_to_all | solution.py:599
  135.2 1.5 %close_weight.1 = (f32[128,1024]{1,0:T(8,128)}, f32[7,1024]{1,0:T(8,128)}) custom-call(bf16[16,528,128]{2,1,0:T(8,128)(2,1)S(1)} %all-to-all-done.2.refs_0_.refs_1_.refs_2_.refs_3_.refs_4_, bf16[16,528,128]{2,1,0:T(8,128)(2,1)S(1)} %all-to-all-done.2.refs_0_.refs_1_.refs_2_.refs_3_.refs_4_, ...), custom_call_target="tpu_custom_call" | custom-call | flops 2000000 | bytes 3000000 | tf_op jit(solution)/shard_map/close_weight/pallas_call | solution.py:505
  (30 shorter events, 0.1 us)
Async XLA Ops:
  0.6 35.7 %copy-start = (f32[7,1024]{1,0:T(8,128)S(1)}, f32[7,1024]{1,0:T(8,128)}, u32[]{:S(2)}) copy-start(f32[7,1024]{1,0:T(8,128)} %param.17) | copy-start | bytes 86020
  8.0 11.1 %copy-start.2 = (bf16[256,4096]{1,0:T(8,128)(2,1)S(1)}, bf16[256,4096]{1,0:T(8,128)(2,1)}, u32[]{:S(2)}) copy-start(bf16[256,4096]{1,0:T(8,128)(2,1)} %others_ref) | copy-start | bytes 6291460
  8.0 30.1 %all-to-all-start = ((bf16[32,64,256]{2,1,0:T(8,128)(2,1)}), bf16[32,64,256]{2,1,0:T(8,128)(2,1)}, u32[]{:S(2)}, u32[]{:S(2)}) async-start(bf16[32,64,256]{2,1,0:T(8,128)(2,1)} %sends.1), calls=%async_computation | async-start | bytes 2097152 | tf_op jit(solution)/shard_map/all_to_all | solution.py:599
  21.1 12.2 %copy-start.10 = (bf16[256,1024]{1,0:T(8,128)(2,1)}, bf16[256,1024]{1,0:T(8,128)(2,1)S(1)}, u32[]{:S(2)}) copy-start(bf16[256,1024]{1,0:T(8,128)(2,1)S(1)} %get-tuple-element.54.refs_4_) | copy-start | bytes 1572868
  21.1 14.7 %copy-start.9 = (bf16[256,1024]{1,0:T(8,128)(2,1)}, bf16[256,1024]{1,0:T(8,128)(2,1)S(1)}, u32[]{:S(2)}) copy-start(bf16[256,1024]{1,0:T(8,128)(2,1)S(1)} %get-tuple-element.53.refs_0_) | copy-start | bytes 1572868
  21.1 36.2 %collective-permute-start = (bf16[256,1024]{1,0:T(8,128)(2,1)}, bf16[256,1024]{1,0:T(8,128)(2,1)}, u32[]{:S(2)}, u32[]{:S(2)}) collective-permute-start(bf16[256,1024]{1,0:T(8,128)(2,1)} %get-tuple-element.44), channel_id=1, source_target_pairs={{0,6},{1,7},{2,4},{3,5},{4,2},{5,3},{6,0},{7,1},{8,14},{9,15},{10,... | collective-permute-start | bytes 1572872 | tf_op jit(solution)/shard_map/ppermute | solution.py:611
  33.2 24.0 %collective-permute-start.2 = (bf16[256,1024]{1,0:T(8,128)(2,1)}, bf16[256,1024]{1,0:T(8,128)(2,1)S(1)}, u32[]{:S(2)}, u32[]{:S(2)}) collective-permute-start(bf16[256,1024]{1,0:T(8,128)(2,1)} %get-tuple-element.44), channel_id=1, source_target_pairs={{0,30},{1,31},{2,28},{3,29},{4,26},{5,27},{6,24},{7,25},{8,22},{9,... | collective-permute-start | bytes 1572872 | tf_op jit(solution)/shard_map/ppermute | solution.py:611
  35.8 23.1 %collective-permute-start.1 = (bf16[256,1024]{1,0:T(8,128)(2,1)S(1)}, bf16[256,1024]{1,0:T(8,128)(2,1)S(1)}, u32[]{:S(2)}, u32[]{:S(2)}) collective-permute-start(bf16[256,1024]{1,0:T(8,128)(2,1)S(1)} %get-tuple-element.53.refs_0_), channel_id=1, source_target_pairs={{0,24},{4,28},{8,16},{12,20},{16,8},{20,12},{24,0},{28,4},{32,56},... | collective-permute-start | bytes 1572872 | tf_op jit(solution)/shard_map/ppermute | solution.py:603
  55.7 11.0 %copy-start.13 = (bf16[16,128]{1,0:T(8,128)(2,1)S(1)}, bf16[16,128]{1,0:T(8,128)(2,1)}, u32[]{:S(2)}) copy-start(bf16[16,128]{1,0:T(8,128)(2,1)} %get-tuple-element.51) | copy-start | bytes 12292
  55.7 14.0 %copy-start.7 = (f32[2,64,128]{2,1,0:T(8,128)S(1)}, f32[2,64,128]{2,1,0:T(8,128)}, u32[]{:S(2)}) copy-start(f32[2,64,128]{2,1,0:T(8,128)} %constant.78.clone.twist_ref) | copy-start | bytes 196612
  55.7 14.0 %copy-start.11 = (bf16[768,512]{1,0:T(8,128)(2,1)S(1)}, bf16[768,512]{1,0:T(8,128)(2,1)}, u32[]{:S(2)}) copy-start(bf16[768,512]{1,0:T(8,128)(2,1)} %constant.84.clone.both_ref) | copy-start | bytes 2359300
  55.7 13.9 %copy-start.12 = (bf16[64,384]{1,0:T(8,128)(2,1)S(1)}, bf16[64,384]{1,0:T(8,128)(2,1)}, u32[]{:S(2)}) copy-start(bf16[64,384]{1,0:T(8,128)(2,1)} %constant.85.clone.last_nat_ref) | copy-start | bytes 147460
  57.2 1.6 %copy-start.14 = (bf16[256,1024]{1,0:T(8,128)(2,1)}, bf16[256,1024]{1,0:T(8,128)(2,1)S(1)}, u32[]{:S(2)}) copy-start(bf16[256,1024]{1,0:T(8,128)(2,1)S(1)} %collective-permute-done.2.refs_3_) | copy-start | bytes 1572868
  58.8 0.8 copy-start.15
  59.6 30.9 %all-to-all-start.1 = ((bf16[16,32,1536]{2,1,0:T(8,128)(2,1)}), bf16[16,32,1536]{2,1,0:T(8,128)(2,1)S(1)}, u32[]{:S(2)}, u32[]{:S(2)}) async-start(bf16[16,32,1536]{2,1,0:T(8,128)(2,1)} %get-tuple-element.45), calls=%async_computation.1 | async-start | bytes 3145728 | tf_op jit(solution)/shard_map/all_to_all | solution.py:599
  66.1 12.0 %collective-permute-start.3 = (bf16[256,1024]{1,0:T(8,128)(2,1)}, bf16[256,1024]{1,0:T(8,128)(2,1)S(1)}, u32[]{:S(2)}, u32[]{:S(2)}) collective-permute-start(bf16[256,1024]{1,0:T(8,128)(2,1)} %collective-permute-done.refs_1_), channel_id=1, source_target_pairs={{0,1},{1,0},{2,3},{3,2},{4,5},{5,4},{6,7},{7,6},{8,9},{9,8},{10,11... | collective-permute-start | bytes 1572872 | tf_op jit(solution)/shard_map/ppermute | solution.py:622
  66.1 12.0 %collective-permute-start.4 = (bf16[256,1024]{1,0:T(8,128)(2,1)}, bf16[256,1024]{1,0:T(8,128)(2,1)}, u32[]{:S(2)}, u32[]{:S(2)}) collective-permute-start(bf16[256,1024]{1,0:T(8,128)(2,1)} %copy-done.15), channel_id=1, source_target_pairs={{0,1},{1,0},{2,3},{3,2},{4,5},{5,4},{6,7},{7,6},{8,9},{9,8},{10,11... | collective-permute-start | bytes 1572872 | tf_op jit(solution)/shard_map/ppermute | solution.py:622
  66.6 11.5 %collective-permute-start.5 = (bf16[256,1024]{1,0:T(8,128)(2,1)}, bf16[256,1024]{1,0:T(8,128)(2,1)}, u32[]{:S(2)}, u32[]{:S(2)}) collective-permute-start(bf16[256,1024]{1,0:T(8,128)(2,1)} %copy-done.14), channel_id=1, source_target_pairs={{0,1},{1,0},{2,3},{3,2},{4,5},{5,4},{6,7},{7,6},{8,9},{9,8},{10,11... | collective-permute-start | bytes 1572872 | tf_op jit(solution)/shard_map/ppermute | solution.py:622
  66.7 10.8 %collective-permute-start.6 = (bf16[16,128]{1,0:T(8,128)(2,1)S(1)}, bf16[16,128]{1,0:T(8,128)(2,1)S(1)}, u32[]{:S(2)}, u32[]{:S(2)}) collective-permute-start(bf16[16,128]{1,0:T(8,128)(2,1)S(1)} %copy-done.13), channel_id=1, source_target_pairs={{0,4},{4,0},{8,12},{12,8},{16,20},{20,16},{24,28},{28,24},{32,36},... | collective-permute-start | bytes 12296 | tf_op jit(solution)/shard_map/ppermute | solution.py:625
  69.7 1.6 %copy-start.8 = (bf16[2048,512]{1,0:T(8,128)(2,1)S(1)}, bf16[2048,512]{1,0:T(8,128)(2,1)}, u32[]{:S(2)}) copy-start(bf16[2048,512]{1,0:T(8,128)(2,1)} %get-tuple-element.46.lag_ref) | copy-start | bytes 6291460
  78.1 15.3 %copy-start.16 = (bf16[256,1024]{1,0:T(8,128)(2,1)}, bf16[256,1024]{1,0:T(8,128)(2,1)S(1)}, u32[]{:S(2)}) copy-start(bf16[256,1024]{1,0:T(8,128)(2,1)S(1)} %collective-permute-done.3.refs_5_) | copy-start | bytes 1572868
  90.5 2.8 %copy-start.3 = (bf16[16,32,1536]{2,1,0:T(8,128)(2,1)}, bf16[16,32,1536]{2,1,0:T(8,128)(2,1)S(1)}, u32[]{:S(2)}) copy-start(bf16[16,32,1536]{2,1,0:T(8,128)(2,1)S(1)} %all-to-all-done.1) | copy-start | bytes 4718596
  90.6 10.7 %collective-permute-start.7 = (bf16[512,512]{1,0:T(8,128)(2,1)S(1)}, bf16[512,512]{1,0:T(8,128)(2,1)S(1)}, u32[]{:S(2)}, u32[]{:S(2)}) collective-permute-start(bf16[512,512]{1,0:T(8,128)(2,1)S(1)} %pad_maximum_fusion), channel_id=1, source_target_pairs={{0,24},{4,28},{8,16},{12,20},{16,8},{20,12},{24,0},{28,4},{32,56},... | collective-permute-start | bytes 1572872 | tf_op jit(solution)/shard_map/ppermute | solution.py:603
  101.3 34.0 %all-to-all-start.2 = ((bf16[16,528,128]{2,1,0:T(8,128)(2,1)}), bf16[16,528,128]{2,1,0:T(8,128)(2,1)S(1)}, u32[]{:S(2)}, u32[]{:S(2)}) async-start(bf16[16,528,128]{2,1,0:T(8,128)(2,1)} %shares.1), calls=%async_computation.2 | async-start | bytes 4325376 | tf_op jit(solution)/shard_map/all_to_all | solution.py:599
  106.7 3.4 %copy-start.1 = (bf16[4096,1024]{1,0:T(8,128)(2,1)S(1)}, bf16[4096,1024]{1,0:T(8,128)(2,1)}, u32[]{:S(2)}) copy-start(bf16[4096,1024]{1,0:T(8,128)(2,1)} %weight_ref.1) | copy-start | bytes 25165828
  110.0 1.4 %copy-start.4 = (bf16[16,32,1536]{2,1,0:T(8,128)(2,1)S(1)}, bf16[16,32,1536]{2,1,0:T(8,128)(2,1)}, u32[]{:S(2)}) copy-start(bf16[16,32,1536]{2,1,0:T(8,128)(2,1)} %copy-done.3) | copy-start | bytes 4718596
  115.3 5.2 %copy-start.5 = (bf16[256,1024]{1,0:T(8,128)(2,1)S(1)}, bf16[256,1024]{1,0:T(8,128)(2,1)}, u32[]{:S(2)}) copy-start(bf16[256,1024]{1,0:T(8,128)(2,1)} %gate_ref.1) | copy-start | bytes 1572868
  115.3 5.2 %copy-start.6 = (bf16[256,1024]{1,0:T(8,128)(2,1)S(1)}, bf16[256,1024]{1,0:T(8,128)(2,1)}, u32[]{:S(2)}) copy-start(bf16[256,1024]{1,0:T(8,128)(2,1)} %grad_ref.1) | copy-start | bytes 1572868
  115.3 2.7 %collective-permute-start.8 = (bf16[2,1024,256]{2,1,0:T(8,128)(2,1)S(1)}, bf16[2,1024,256]{2,1,0:T(8,128)(2,1)S(1)}, u32[]{:S(2)}, u32[]{:S(2)}) collective-permute-start(bf16[2,1024,256]{2,1,0:T(8,128)(2,1)S(1)} %get-tuple-element.62), channel_id=1, source_target_pairs={{0,1},{1,0},{2,3},{3,2},{4,5},{5,4},{6,7},{7,6},{8,9},{9,8},{10,11... | collective-permute-start | bytes 3145736 | tf_op jit(solution)/shard_map/ppermute | solution.py:635
  118.2 14.5 %collective-permute-start.9 = (bf16[1024,256]{1,0:T(8,128)(2,1)S(1)}, bf16[1024,256]{1,0:T(8,128)(2,1)S(1)}, u32[]{:S(2)}, u32[]{:S(2)}) collective-permute-start(bf16[1024,256]{1,0:T(8,128)(2,1)S(1)} %fusion), channel_id=1, source_target_pairs={{0,2},{2,0},{1,3},{3,1},{4,6},{6,4},{5,7},{7,5},{8,10},{10,8},{9,1... | collective-permute-start | bytes 1572872 | tf_op jit(solution)/shard_map/ppermute | solution.py:637

commit v6 on v5

--- a/solution.py
+++ b/solution.py
@@ -138,8 +138,8 @@
     out_ref[...] = dot(kernel_buf[...], pair_ref[...])
 
 
-def lag_kernel(lag_ref, twist_ref, both_ref, last_nat_ref, out_ref):
-    parts = lag_ref[...]
+def lag_kernel(lag_one_ref, lag_two_ref, twist_ref, both_ref, last_nat_ref, out_ref):
+    parts = jnp.where(pl.program_id(0) < pl.num_programs(0) // 2, lag_one_ref[...], lag_two_ref[...])
     unmixed = dot(jnp.concatenate([parts, parts[:, :2 * LANES]], axis=1), both_ref[...])
     for q in range(BATCH):
         at = (pl.program_id(0) % (8 // BATCH)) * BATCH + q
@@ -151,19 +151,19 @@
 
 
 def mixer_kernel(
-    taps_ref, arrived_ref, spectra_ref, first_split_ref, twist_ref, forward_ref, inverse_ref, last_split_ref,
+    first, taps_ref, arrived_ref, spectra_ref, first_split_ref, twist_ref, forward_ref, inverse_ref, last_split_ref,
     back_ref, lag_ref, taps_out_ref,
     values_buf, slopes_buf, back_buf, mixed_buf, taps_buf, extra_buf, signal_buf, product_buf,
 ):
-    blocks, width = arrived_ref.shape[0], arrived_ref.shape[1] // 2
+    blocks, total, width = arrived_ref.shape[0], arrived_ref.shape[1] // 2, back_ref.shape[1]
     step = pl.program_id(0)
 
     @pl.when(step == 0)
     def _():
         for h in range(2):
             part = slice(h * LANES, (h + 1) * LANES)
-            values_buf[h] = arrived_ref[:, :width, part].astype(jnp.float32).reshape(blocks * width, LANES)
-            slopes_buf[h] = arrived_ref[:, width:, part].astype(jnp.float32).reshape(blocks * width, LANES)
+            for buf, at in ((values_buf, first), (slopes_buf, total + first)):
+                buf[h] = arrived_ref[:, at:at + width, part].astype(jnp.float32).reshape(blocks * width, LANES)
 
     pooled = {}
 
@@ -175,7 +175,7 @@
             sum_early, sum_late = None, None
             for k in range(TAPS):
                 one, two = shifted(early, late, k - REACH)
-                tap = taps_ref[k, c]
+                tap = taps_ref[k, first + c]
                 sum_early = tap * one if k == 0 else sum_early + tap * one
                 sum_late = tap * two if k == 0 else sum_late + tap * two
             short = jnp.concatenate([sum_early, sum_late], axis=0).astype(jnp.bfloat16)
@@ -225,7 +225,7 @@
             sum_early, sum_late = None, None
             for k in range(TAPS):
                 one, two = shifted(slope_back[:blocks], slope_back[blocks:], REACH - k)
-                tap = taps_ref[k, c]
+                tap = taps_ref[k, first + c]
                 sum_early = tap * one if k == 0 else sum_early + tap * one
                 sum_late = tap * two if k == 0 else sum_late + tap * two
                 taps_buf[k, pl.ds(c, 1), :] = jnp.sum(one * early + two * late, axis=0, keepdims=True)
@@ -263,7 +263,8 @@
                 packed = jnp.where(lane == 8 * p + k, piece, packed)
                 rest = rest - piece
         packed = jnp.concatenate([packed, jnp.zeros((LANES - width, LANES), jnp.float32)], axis=0).T
-        rows = packed[:8] + pltpu.roll(packed[8:16], width, 1) + pltpu.roll(packed[16:24], 2 * width, 1)
+        rows = pltpu.roll(packed[8:16], total + first, 1) + pltpu.roll(packed[16:24], 2 * total + first, 1)
+        rows = rows + (pltpu.roll(packed[:8], first, 1) if first else packed[:8])
         taps_out_ref[...] = jnp.concatenate([rows, jnp.zeros_like(rows)], axis=0).astype(jnp.bfloat16)
 
 
@@ -300,30 +301,31 @@
     )(view, *consts)
 
 
-def filter_grads(lag):
-    width = lag.shape[0] // ROWS
-    tiles = width // 8
+def filter_grads(lag_one, lag_two):
+    width = 2 * lag_one.shape[0] // ROWS
+    tiles, steps = width // 8, width // BATCH // 2
     consts, specs = tables_of(("twist", "both", "last_nat"))
     out = call(
         lag_kernel, "filter_grads", 3_000_000_000, 5_000_000,
         grid=(width // BATCH,),
-        in_specs=[pl.BlockSpec((BATCH * ROWS, 4 * LANES), lambda i: (i, 0))] + specs,
+        in_specs=[pl.BlockSpec((BATCH * ROWS, 4 * LANES), lambda i: (jnp.minimum(i, steps - 1), 0)),
+                  pl.BlockSpec((BATCH * ROWS, 4 * LANES), lambda i: (jnp.maximum(i - steps, 0), 0))] + specs,
         out_specs=PER_TILE,
         out_shape=jax.ShapeDtypeStruct((2, tiles, ROWS * 8, LANES), jnp.float32),
-    )(lag, *consts)
+    )(lag_one, lag_two, *consts)
     return out.reshape(2, tiles, ROWS, 8, LANES).transpose(0, 1, 3, 2, 4).reshape(2, width, LENGTH)
 
 
-def mixer(own_taps, arrived, spectra):
-    blocks, width, span = arrived.shape[0], arrived.shape[1] // 2, arrived.shape[2]
+def mixer(own_taps, arrived, spectra, half):
+    blocks, width, span = arrived.shape[0], arrived.shape[1] // 4, arrived.shape[2]
     consts, specs = tables_of(("first_split", "twist", "forward", "inverse", "last_split"))
     back_shape = (blocks // 2, width, 6 * span)
     rows, batch = (2, blocks * width, LANES), GROUP * GROUPS
     return call(
-        mixer_kernel, "mixer", 100_000_000, 1_000_000, vmem=56,
+        functools.partial(mixer_kernel, half * width), "mixer", 9_000_000_000, 4_000_000, vmem=56,
         grid=(width // batch,),
         in_specs=[pl.BlockSpec(memory_space=pltpu.SMEM), whole(arrived.shape),
-                  pl.BlockSpec((batch * ROWS, 2 * LANES), lambda i: (i, 0))] + specs,
+                  pl.BlockSpec((batch * ROWS, 2 * LANES), lambda i: (half * (width // batch) + i, 0))] + specs,
         out_specs=[whole(back_shape), pl.BlockSpec((batch * ROWS, 4 * LANES), lambda i: (i, 0)), whole((16, LANES))],
         out_shape=[
             jax.ShapeDtypeStruct(back_shape, jnp.bfloat16),
@@ -424,67 +426,86 @@
     return seq_at // 4 % 2 * 2 + seq_at % 2
 
 
-def share_kernel(back_ref, *refs):
-    parts, (taps_ref, out_ref, back_buf, rows_buf, out_buf, in_sem, out_sem) = refs[:8], refs[8:]
-    span, rows = rows_buf.shape[1], back_buf.shape[0]
+def share_kernel(half, back_ref, *refs):
+    parts, refs = refs[:8], refs[8:]
+    if half:
+        taps_ref, _, out_ref, back_buf, rows_buf, out_buf, in_sem, out_sem = refs
+    else:
+        out_ref, back_buf, rows_buf, out_buf, in_sem, out_sem = refs
+    span, rows, sent = rows_buf.shape[1], back_buf.shape[0], out_buf.shape[1]
     loads = [pltpu.make_async_copy(back_ref.at[:, pl.ds(0, 4 * span)], back_buf, in_sem.at[8])]
     loads += [pltpu.make_async_copy(part, rows_buf.at[n], in_sem.at[n]) for n, part in enumerate(parts)]
     for load in loads:
         load.start()
     loads[0].wait()
     stores = []
-    for half in range(2):
-        for load in loads[1 + 4 * half:5 + 4 * half]:
+    for side in range(2):
+        for load in loads[1 + 4 * side:5 + 4 * side]:
             load.wait()
-        first = 8 * (half ^ (lax.axis_index("tp") % 2))
+        first = 8 * (side ^ (lax.axis_index("tp") % 2))
         for two in range(4):
             lanes = slice(two * 256, (two + 1) * 256)
             product = None
             for j in range(4):
                 at = pl.multiple_of((quad_place() ^ j) * span, span)
-                term = dot(back_buf[:, pl.ds(at, span)], rows_buf[4 * half + j, :, lanes])
+                term = dot(back_buf[:, pl.ds(at, span)], rows_buf[4 * side + j, :, lanes])
                 product = term if product is None else product + term
             product = product.astype(jnp.bfloat16)
-            n = 4 * half + two
+            n = 4 * side + two
             for m in range(2):
                 out_buf[2 * n + m, :rows] = product[:, m * LANES:(m + 1) * LANES]
-                out_buf[2 * n + m, rows:] = taps_ref[...]
+                if half:
+                    out_buf[2 * n + m, rows:] = taps_ref[...]
             store = pltpu.make_async_copy(
-                out_buf.at[pl.ds(2 * n, 2)], out_ref.at[pl.ds(first + 2 * two, 2)], out_sem.at[n])
+                out_buf.at[pl.ds(2 * n, 2)],
+                out_ref.at[pl.ds(first + 2 * two, 2), pl.ds(half * rows, sent)], out_sem.at[n])
             store.start()
             stores.append(store)
     for store in stores:
         store.wait()
 
 
-def shares(back, mine, other, taps):
+def shares(back, mine, other, taps=None, before=None):
     span, depth = mine[0].shape
     rows = back.shape[0]
-    return call(
-        share_kernel, "shares", 16 * rows * span * depth, 7_000_000, vmem=60,
-        in_specs=[pl.BlockSpec(memory_space=pl.ANY)] * 9 + [pl.BlockSpec(memory_space=pltpu.VMEM)],
-        out_specs=pl.BlockSpec(memory_space=pl.ANY),
-        out_shape=jax.ShapeDtypeStruct((16, rows + 16, LANES), jnp.bfloat16),
+    half = 0 if before is None else 1
+    operands = [back, *mine, *other] + ([taps, before] if half else [])
+    anywhere = pl.BlockSpec(memory_space=pl.ANY)
+    return call(
+        functools.partial(share_kernel, half), "shares", 16 * rows * span * depth, 7_000_000, vmem=60,
+        in_specs=[anywhere] * 9 + ([pl.BlockSpec(memory_space=pltpu.VMEM), anywhere] if half else []),
+        out_specs=anywhere,
+        out_shape=jax.ShapeDtypeStruct((16, 2 * rows + 16, LANES), jnp.bfloat16),
+        input_output_aliases={10: 0} if half else {},
         scratch_shapes=[
             pltpu.VMEM((rows, 4 * span), jnp.bfloat16), pltpu.VMEM((8, span, depth), jnp.bfloat16),
-            pltpu.VMEM((16, rows + 16, LANES), jnp.bfloat16),
+            pltpu.VMEM((16, rows + 16 * half, LANES), jnp.bfloat16),
             pltpu.SemaphoreType.DMA((9,)), pltpu.SemaphoreType.DMA((8,))],
-    )(back, *mine, *other, taps)
+    )(*operands)
 
 
 def merge(pair, mine, mate):
-    first, second = jnp.where(pair == 0, mine, mate), jnp.where(pair == 0, mate, mine)
-    half = mine.shape[0] // 2
-    return jnp.concatenate([first[half:], first[:half], second[:half], second[half:]], axis=0)
+    leagues = [[jnp.where(pair == 0, one, two) for one, two in zip(mine, mate)],
+               [jnp.where(pair == 0, two, one) for one, two in zip(mine, mate)]]
+    size = mine[0].shape[0] // 4
+    pieces = []
+    for y in range(4):
+        league, odd = y // 2, Y_OF[0][y // 2] != y
+        for z in range(2):
+            at = (2 * odd + z) * size
+            pieces += [leagues[league][half][at:at + size] for half in range(2)]
+    return jnp.concatenate(pieces, axis=0)
 
 
 def weight_kernel(*refs):
-    share_refs, (taps_ref, weight_ref, tap_sums_ref) = refs[:4], refs[4:]
-    for x, ref in enumerate(share_refs):
-        totals = []
+    share_refs, (taps_ref, weight_ref, tap_sums_ref) = refs[:8], refs[8:]
+    for x in range(4):
+        totals = [[], []]
         for pair in range(2):
-            terms = [ref[j].astype(jnp.float32) for j in range(16) if j % 4 // 2 == pair]
-            totals.append(sum(terms[1:], terms[0]))
+            for half in range(2):
+                ref = share_refs[4 * half + x]
+                terms = [ref[j].astype(jnp.float32) for j in range(16) if j % 4 // 2 == pair]
+                totals[pair].append(sum(terms[1:], terms[0]))
         weight_ref[:, x * 2 * LANES:(x + 1) * 2 * LANES] = merge(0, *totals).T
     z = lax.axis_index("seq") % 2
     lane = lax.broadcasted_iota(jnp.int32, (8, LANES), 1)
@@ -504,23 +525,28 @@
     channels = 2 * rows
     return call(
         weight_kernel, "close_weight", 2_000_000, 3_000_000, grid=(1,),
-        in_specs=[pl.BlockSpec((count, LANES, span), functools.partial(lambda x, i: (0, x, 0), x)) for x in range(4)]
+        in_specs=[pl.BlockSpec((count, 64, span), functools.partial(lambda n, i: (0, n, 0), n)) for n in range(8)]
         + [pl.BlockSpec((count, 16, span), lambda i: (0, rows // 16, 0))],
         out_specs=[whole((span, channels)), whole((TAPS, channels))],
         out_shape=[jax.ShapeDtypeStruct((span, channels), jnp.float32),
                    jax.ShapeDtypeStruct((TAPS, channels), jnp.float32)],
-    )(*[parts] * 5)
-
-
-def input_kernel(place_ref, back_ref, mate_ref, weight_ref, send_ref, keep_ref, own_buf):
+    )(*[parts] * 9)
+
+
+def input_kernel(place_ref, *refs):
+    back_refs, mate_refs, (weight_ref, send_ref, keep_ref, own_buf) = refs[:2], refs[2:4], refs[4:]
+
     @pl.when(pl.program_id(0) == 0)
     def _():
         pair = place_ref[0] // 2
-        for x in range(4):
-            for odd, mine, other in ((0, 1 + pair, 2 - pair), (1, 3 * pair, 3 - 3 * pair)):
-                rows = slice((2 * x + odd) * 64, (2 * x + odd + 1) * 64)
-                own_buf[pl.ds(pl.multiple_of((4 * x + mine) * 64, 64), 64), :] = back_ref[rows, :]
-                own_buf[pl.ds(pl.multiple_of((4 * x + other) * 64, 64), 64), :] = mate_ref[rows, :]
+        for half in range(2):
+            for x in range(4):
+                for odd, mine, other in ((0, 1 + pair, 2 - pair), (1, 3 * pair, 3 - 3 * pair)):
+                    for z in range(2):
+                        at = ((2 * x + odd) * 2 + z) * 16
+                        for ref, y in ((back_refs[half], mine), (mate_refs[half], other)):
+                            to = pl.multiple_of(((4 * x + y) * 2 + z) * 32 + half * 16, 16)
+                            own_buf[pl.ds(to, 16), :] = ref[at:at + 16, :]
 
     term = dot(weight_ref[...], own_buf[...])
 
@@ -533,22 +559,22 @@
         keep_ref[0] = term
 
 
-def input_terms(place, back, mate, w_value):
+def input_terms(place, backs, mates, w_value):
     depth, channels = w_value.shape
     rows, span = depth // 4, 256
     return call(
         input_kernel, "input_terms", 2 * span * depth * channels, 12_000_000, vmem=24,
         grid_spec=pltpu.PrefetchScalarGridSpec(
             num_scalar_prefetch=1, grid=(4,),
-            in_specs=[pl.BlockSpec((channels // 2, span), lambda i, place: (0, place[0])),
-                      pl.BlockSpec((channels // 2, span), lambda i, place: (0, 0)),
-                      pl.BlockSpec((rows, channels), lambda i, place: (place[1] ^ ((2 * i + 1 - i // 2) % 4), 0))],
+            in_specs=[pl.BlockSpec((channels // 4, span), lambda i, place: (0, place[0]))] * 2
+            + [pl.BlockSpec((channels // 4, span), lambda i, place: (0, 0))] * 2
+            + [pl.BlockSpec((rows, channels), lambda i, place: (place[1] ^ ((2 * i + 1 - i // 2) % 4), 0))],
             out_specs=[pl.BlockSpec((1, rows, span), lambda i, place: (jnp.minimum(i, 1), 0, 0)),
                        pl.BlockSpec((1, rows, span), lambda i, place: (jnp.maximum(i - 2, 0), 0, 0))],
             scratch_shapes=[pltpu.VMEM((channels, span), jnp.bfloat16)]),
         out_shape=[jax.ShapeDtypeStruct((2, rows, span), jnp.bfloat16),
                    jax.ShapeDtypeStruct((2, rows, span), jnp.float32)],
-    )(place, back, mate, w_value)
+    )(place, *backs, *mates, w_value)
 
 
 def close_kernel(keep_ref, core_ref, chip_ref, out_ref):
@@ -566,23 +592,25 @@
         out_shape=jax.ShapeDtypeStruct((span, rows), jnp.bfloat16))(keep, core, chip)
 
 
-def gate_kernel(place_ref, mixed_ref, mate_ref, gate_ref, grad_ref, out_ref):
-    mixed = merge(place_ref[0] // 2, mixed_ref[...].astype(jnp.float32), mate_ref[...].astype(jnp.float32)).T
+def gate_kernel(place_ref, one_ref, two_ref, mate_one_ref, mate_two_ref, gate_ref, grad_ref, out_ref):
+    mine = [ref[...].astype(jnp.float32) for ref in (one_ref, two_ref)]
+    mate = [ref[...].astype(jnp.float32) for ref in (mate_one_ref, mate_two_ref)]
+    mixed = merge(place_ref[0] // 2, mine, mate).T
     sig = jax.nn.sigmoid(gate_ref[...].astype(jnp.float32))
     out_ref[...] = (grad_ref[...].astype(jnp.float32) * mixed * sig * (1.0 - sig)).astype(jnp.bfloat16)
 
 
-def gate_grad(place, back, mate, gate, grads):
+def gate_grad(place, backs, mates, gate, grads):
     span, channels = gate.shape
     block = pl.BlockSpec((span, channels // 4), lambda i, place: (0, i))
     return call(
         gate_kernel, "gate_grad", 2_000_000, 2_500_000,
         grid_spec=pltpu.PrefetchScalarGridSpec(
             num_scalar_prefetch=1, grid=(4,),
-            in_specs=[pl.BlockSpec((LANES, span), lambda i, place: (i, 4 + place[0] // 2)),
-                      pl.BlockSpec((LANES, span), lambda i, place: (i, 1)), block, block],
+            in_specs=[pl.BlockSpec((64, span), lambda i, place: (i, 4 + place[0] // 2))] * 2
+            + [pl.BlockSpec((64, span), lambda i, place: (i, 1))] * 2 + [block, block],
             out_specs=block),
-        out_shape=jax.ShapeDtypeStruct(gate.shape, jnp.bfloat16))(place, back, mate, gate, grads)
+        out_shape=jax.ShapeDtypeStruct(gate.shape, jnp.bfloat16))(place, *backs, *mates, gate, grads)
 
 
 def local(layer_in, w_value, short_taps, long_filters, gate_proj, grad_out):
@@ -617,26 +645,40 @@
     mine = [same, first, mates(same), across(cross, 1 ^ MATE)]
 
     own_taps = lax.dynamic_slice_in_dim(short_taps, seq_at * width, width, 1)
-    back, lag, taps = mixer(own_taps, arrived, spectra)
-    back, mine = lax.optimization_barrier((back, mine))
+    def league(value):
+        return exchange(value, LEAGUES).reshape(channels // 4, value.shape[2])
+
+    def for_mate(back):
+        return mates(jnp.concatenate([
+            lax.dynamic_slice_in_dim(back, (quad_at ^ 2) * span, span, 1),
+            lax.dynamic_slice_in_dim(back, 4 * span + (1 - quad_at // 2) * span, span, 1)], axis=1))
+
+    back_one, lag_one, taps_one = mixer(own_taps, arrived, spectra, 0)
+    arrived, back_one = lax.optimization_barrier((arrived, back_one))
+    back_two, lag_two, taps_two = mixer(own_taps, arrived, spectra, 1)
+    back_one = league(back_one)
+    back_one, back_two, mine = lax.optimization_barrier((back_one, back_two, mine))
     other = [other] + [lax.ppermute(part, "tp", cores) for part in mine[1:]]
-    back = exchange(back, LEAGUES).reshape(channels // 2, back.shape[2])
-    grad_filters = filter_grads(lag)
+    back_two = league(back_two)
+    mate_one = for_mate(back_one)
+    grad_filters = filter_grads(lag_one, lag_two)
+    taps = taps_one + taps_two
     partner = lax.ppermute(taps, "seq", [(s, s ^ 1) for s in range(seq_count)])
     taps = jnp.concatenate([taps[:8], partner[:8]], axis=0)
-    back, grad_filters, other, taps = lax.optimization_barrier((back, grad_filters, other, taps))
-    mate = mates(jnp.concatenate([
-        lax.dynamic_slice_in_dim(back, (quad_at ^ 2) * span, span, 1),
-        lax.dynamic_slice_in_dim(back, 4 * span + (1 - quad_at // 2) * span, span, 1)], axis=1))
-    outgoing, mate = lax.optimization_barrier((shares(back, mine, other, taps), mate))
+    outgoing = shares(back_one, mine, other)
+    back_two, outgoing, mate_one, grad_filters, taps = lax.optimization_barrier(
+        (back_two, outgoing, mate_one, grad_filters, taps))
+    mate_two = for_mate(back_two)
+    outgoing, mate_two = lax.optimization_barrier((shares(back_two, mine, other, taps, outgoing), mate_two))
     parts = exchange(outgoing, PLANES)
-
-    send, keep = input_terms(place, back, mate, w_value)
+    backs, their = [back_one, back_two], [mate_one, mate_two]
+
+    send, keep = input_terms(place, backs, their, w_value)
     core = lax.ppermute(send, "tp", cores)
     send = (keep[1] + core[1].astype(jnp.float32)).astype(jnp.bfloat16)
     chip = lax.ppermute(send, "tp", chips)
     grad_input = close_input(keep, core, chip)
-    grad_gate = gate_grad(place, back, mate, gate_proj, grad_out)
+    grad_gate = gate_grad(place, backs, their, gate_proj, grad_out)
     parts, grad_input, grad_gate = lax.optimization_barrier((parts, grad_input, grad_gate))
     grad_weight, grad_taps = close_weight(parts)
     return (grad_input, grad_weight, grad_taps, grad_filters, grad_gate)

time: 138 us -> 141 us (1.022)
  waiting for transfers between devices: 32.2 us -> 25.3 us
  starting transfers between devices: 38 us -> 43.1 us
  Pallas kernels: 56.8 us -> 59.4 us
  local copies, waits for them, and re-layouts: 7.93 us -> 9.34 us
    all_to_all x3 -> x4, starting transfers between devices: 22.8 us -> 29.2 us  [exchange(): lax.all_to_all(value, 'seq', split_axis=0, concat_axis=0, axis_index_grou...]
    all_to_all x3 -> x4, waiting for transfers between devices: 15 us -> 9.06 us  [exchange(): lax.all_to_all(value, 'seq', split_axis=0, concat_axis=0, axis_index_grou...]
    pallas_call x2 -> x4, Pallas kernels: 23.7 us -> 26.1 us  [the longest x2 17.4 us: mixer(): call(functools.partial(mixer_kernel, half * width), 'mixer', 9000000000,...]
    ppermute x1, starting transfers between devices: 2.31 us -> 0.69 us  [local(): chip = lax.ppermute(send, 'tp', chips)]
    ppermute x2, waiting for transfers between devices: 1.51 us -> 0.01 us  [across(): lax.ppermute(value, ('seq', 'tp'), [(4 * s + t, 4 * (s ^ flip) + (t ^ 2))...]
    unnamed x34 -> x38, local copies, waits for them, and re-layouts: 7.23 us -> 8.63 us
    ppermute x2 -> x3, starting transfers between devices: 3.32 us -> 3.95 us  [mates(): return lax.ppermute(value, 'seq', [(s, s ^ MATE) for s in range(seq_count)])]
    ppermute x2 -> x3, waiting for transfers between devices: 3.37 us -> 2.8 us  [mates(): return lax.ppermute(value, 'seq', [(s, s ^ MATE) for s in range(seq_count)])]
  transfers between devices with their start and end apart: 13 -> 15, of which waited for: 8 -> 6; matrix products, arithmetic and copies ran while one was open for 1% -> 2% of each run, Pallas kernels for 35% -> 36%
where the time goes in v6:
time: 141 us; the launch traced here: 140 us
  Pallas kernels  59.4 us (42%)
  starting transfers between devices  43.1 us (31%)
  waiting for transfers between devices  25.3 us (18%)
  local copies, waits for them, and re-layouts  9.34 us (7%)
  other arithmetic  1.53 us (1%)
    all_to_all x4, starting transfers between devices, exchange(): lax.all_to_all(value, 'seq', split_axis=0, concat_axis=0, axis_index_grou...  29.2 us
    pallas_call x2, Pallas kernels, mixer(): call(functools.partial(mixer_kernel, half * width), 'mixer', 9000000000,...  17.4 us
    ppermute x1, waiting for transfers between devices, local(): chip = lax.ppermute(send, 'tp', chips)  10.8 us
    all_to_all x4, waiting for transfers between devices, exchange(): lax.all_to_all(value, 'seq', split_axis=0, concat_axis=0, axis_index_grou...  9.06 us
    pallas_call x1, Pallas kernels, spectra_of(): call(spectra_kernel, 'spectra', 3000000000, 5000000, vmem=56, grid=(width...  8.8 us
    pallas_call x2, Pallas kernels, shares(): call(functools.partial(share_kernel, half), 'shares', 16 * rows * span *...  8.67 us
    unnamed x38, local copies, waits for them, and re-layouts  8.63 us
    pallas_call x1, Pallas kernels, sends(): call(send_kernel, 'sends', 2 * span * depth * channels, 12500000, vmem=56...  7.34 us
  transfers between devices with their start and end apart: 15, of which 6 were waited for; matrix products, arithmetic and copies ran while one was open for 2% of the time, Pallas kernels for 36%

profile of v6, /device:TPU:0, one launch (start us, length us, event | category | flops | bytes accessed | tf_op | source)
XLA Modules:
  0.0 139.7 jit_solution(11656462692972706218)
XLA Ops:
  0.6 0.0 copy-start
  0.6 7.3 %sends.1 = bf16[32,64,256]{2,1,0:T(8,128)(2,1)} custom-call(bf16[256,4096]{1,0:T(8,128)(2,1)} %others_ref, bf16[4096,1024]{1,0:T(8,128)(2,1)} %refs_4_.3, bf16[4096,1024]{1,0:T(8,128)(2,1)} %refs_4_.3, bf16[4096,1024]{1,0:T(8,128)(2,1)} %refs_4_.3, bf16[4096,1024]{1,0:T(8,128)(2,1)} %refs_4_.3, bf16[4096,1024]{1,0:T(8,128)(2,1)} %refs_4_.3, ...), custom_call_target="tpu_custom_call" | custom-call | flops 2147483648 | bytes 12500000 | tf_op jit(solution)/shard_map/sends/pallas_call | solution.py:391
  8.0 11.0 %all-to-all-start = ((bf16[32,64,256]{2,1,0:T(8,128)(2,1)}), bf16[32,64,256]{2,1,0:T(8,128)(2,1)}, u32[]{:S(2)}, u32[]{:S(2)}) async-start(bf16[32,64,256]{2,1,0:T(8,128)(2,1)} %sends.1), calls=%async_computation | async-start | bytes 2097152 | tf_op jit(solution)/shard_map/all_to_all | solution.py:627
  19.0 0.1 pad_add_fusion.place_ref
  19.1 2.0 %quarters.1 = (bf16[256,1024]{1,0:T(8,128)(2,1)S(1)}, bf16[256,1024]{1,0:T(8,128)(2,1)}, bf16[256,1024]{1,0:T(8,128)(2,1)S(1)}) custom-call(s32[2]{0:T(128)S(1)} %pad_add_fusion.place_ref, bf16[256,4096]{1,0:T(8,128)(2,1)S(1)} %copy-done.2, bf16[256,4096]{1,0:T(8,128)(2,1)S(1)} %copy-done.2), custom_call_target="tpu_custom_call" | custom-call | bytes 5000000 | tf_op jit(solution)/shard_map/quarters/pallas_call | solution.py:413
  21.1 0.8 copy-done.10
  21.9 3.4 %collective-permute-start = (bf16[256,1024]{1,0:T(8,128)(2,1)}, bf16[256,1024]{1,0:T(8,128)(2,1)}, u32[]{:S(2)}, u32[]{:S(2)}) collective-permute-start(bf16[256,1024]{1,0:T(8,128)(2,1)} %get-tuple-element.51), channel_id=1, source_target_pairs={{0,6},{1,7},{2,4},{3,5},{4,2},{5,3},{6,0},{7,1},{8,14},{9,15},{10,... | collective-permute-start | bytes 1572872 | tf_op jit(solution)/shard_map/ppermute | solution.py:639
  25.3 8.8 %spectra.1.spectra_ref = f32[2048,256]{1,0:T(8,128)} custom-call(f32[2,4,512,128]{3,2,1,0:T(8,128)} %bitcast.24, bf16[128,256]{1,0:T(8,128)(2,1)} %constant.79.clone.first_nat_ref, f32[2,64,128]{2,1,0:T(8,128)} %constant.80.clone.twist_ref, bf16[1536,256]{1,0:T(8,128)(2,1)} %constant.81.clone.pair_ref), custom_call_target="tpu_custom_call" | custom-call | flops 3000000000 | bytes 5000000 | tf_op jit(solution)/shard_map/spectra/pallas_call | solution.py:295
  34.1 2.3 %collective-permute-start.2 = (bf16[256,1024]{1,0:T(8,128)(2,1)}, bf16[256,1024]{1,0:T(8,128)(2,1)}, u32[]{:S(2)}, u32[]{:S(2)}) collective-permute-start(bf16[256,1024]{1,0:T(8,128)(2,1)} %get-tuple-element.51), channel_id=1, source_target_pairs={{0,30},{1,31},{2,28},{3,29},{4,26},{5,27},{6,24},{7,25},{8,22},{9,... | collective-permute-start | bytes 1572872 | tf_op jit(solution)/shard_map/ppermute | solution.py:639
  36.4 0.6 collective-permute-start.1
  36.9 0.7 constant_dynamic-slice_fusion.4.taps_ref
  37.6 0.4 all-to-all-done.arrived_ref
  38.0 8.7 %mixer.2 = (bf16[16,16,1536]{2,1,0:T(8,128)(2,1)}, bf16[1024,512]{1,0:T(8,128)(2,1)}, bf16[16,128]{1,0:T(8,128)(2,1)}) custom-call(f32[7,32]{1,0:T(8,128)} %constant_dynamic-slice_fusion.4.taps_ref, bf16[32,64,256]{2,1,0:T(8,128)(2,1)} %all-to-all-done.arrived_ref, f32[2048,256]{1,0:T(8,128)} %spectra.1.spectra_ref, ...), custom_call_target="tpu_custom_call" | custom-call | flops 8999999488 | bytes 4000000 | tf_op jit(solution)/shard_map/mixer/pallas_call | solution.py:324
  46.7 6.4 %all-to-all-start.1 = ((bf16[16,16,1536]{2,1,0:T(8,128)(2,1)}), bf16[16,16,1536]{2,1,0:T(8,128)(2,1)S(1)}, u32[]{:S(2)}, u32[]{:S(2)}) async-start(bf16[16,16,1536]{2,1,0:T(8,128)(2,1)} %get-tuple-element.47), calls=%async_computation.1 | async-start | bytes 1572864 | tf_op jit(solution)/shard_map/all_to_all | solution.py:627
  53.1 8.7 %mixer.3 = (bf16[16,16,1536]{2,1,0:T(8,128)(2,1)}, bf16[1024,512]{1,0:T(8,128)(2,1)}, bf16[16,128]{1,0:T(8,128)(2,1)}) custom-call(f32[7,32]{1,0:T(8,128)} %constant_dynamic-slice_fusion.4.taps_ref, bf16[32,64,256]{2,1,0:T(8,128)(2,1)} %all-to-all-done.arrived_ref, f32[2048,256]{1,0:T(8,128)} %spectra.1.spectra_ref, ...), custom_call_target="tpu_custom_call" | custom-call | flops 8999999488 | bytes 4000000 | tf_op jit(solution)/shard_map/mixer/pallas_call | solution.py:324
  61.9 0.0 copy-start.13
  61.9 0.0 copy-start.16
  61.9 4.7 %all-to-all-done.1 = bf16[16,16,1536]{2,1,0:T(8,128)(2,1)S(1)} async-done(((bf16[16,16,1536]{2,1,0:T(8,128)(2,1)}), bf16[16,16,1536]{2,1,0:T(8,128)(2,1)S(1)}, u32[]{:S(2)}, u32[]{:S(2)}) %all-to-all-start.1) | async-done | bytes 786464 | tf_op jit(solution)/shard_map/all_to_all | solution.py:627
  66.6 5.9 %all-to-all-start.2 = ((bf16[16,16,1536]{2,1,0:T(8,128)(2,1)}), bf16[16,16,1536]{2,1,0:T(8,128)(2,1)S(1)}, u32[]{:S(2)}, u32[]{:S(2)}) async-start(bf16[16,16,1536]{2,1,0:T(8,128)(2,1)} %get-tuple-element.52), calls=%async_computation.2 | async-start | bytes 1572864 | tf_op jit(solution)/shard_map/all_to_all | solution.py:627
  72.5 0.7 add.43
  73.2 3.0 %collective-permute-start.7 = (bf16[16,128]{1,0:T(8,128)(2,1)S(1)}, bf16[16,128]{1,0:T(8,128)(2,1)S(1)}, u32[]{:S(2)}, u32[]{:S(2)}) collective-permute-start(bf16[16,128]{1,0:T(8,128)(2,1)S(1)} %add.43), channel_id=1, source_target_pairs={{0,4},{4,0},{8,12},{12,8},{16,20},{20,16},{24,28},{28,24},{32,36},... | collective-permute-start | bytes 12296 | tf_op jit(solution)/shard_map/ppermute | solution.py:666
  76.1 0.5 collective-permute-start.4
  76.7 1.1 collective-permute-start.6
  77.8 1.2 copy-done.14
  79.1 1.2 copy-done.15
  80.3 6.2 %filter_grads.1 = f32[2,4,512,128]{3,2,1,0:T(8,128)} custom-call(bf16[1024,512]{1,0:T(8,128)(2,1)S(1)} %copy-done.14, bf16[1024,512]{1,0:T(8,128)(2,1)S(1)} %copy-done.15, f32[2,64,128]{2,1,0:T(8,128)S(1)} %copy-done.12, bf16[768,512]{1,0:T(8,128)(2,1)S(1)} %copy-done.11, bf16[64,384]{1,0:T(8,128)(2,1)S(1)} %copy-done.13), custom_call_target="tpu_custom_call" | custom-call | flops 3000000000 | bytes 5000000 | tf_op jit(solution)/shard_map/filter_grads/pallas_call | solution.py:308
  86.5 0.6 pad_maximum_fusion.2.refs_8_
  87.1 0.8 copy-done.17
  88.0 4.0 %shares.2.refs_9_ = bf16[16,528,128]{2,1,0:T(8,128)(2,1)} custom-call(bf16[256,1536]{1,0:T(8,128)(2,1)} %bitcast.17, bf16[256,1024]{1,0:T(8,128)(2,1)} %copy-done.9, bf16[256,1024]{1,0:T(8,128)(2,1)} %collective-permute-done.refs_1_, bf16[256,1024]{1,0:T(8,128)(2,1)} %copy-done.16, bf16[256,1024]{1,0:T(8,128)(2,1)} %collective-permute-done.2.refs_3_, ...), custom_call_target="tpu_custom_call" | custom-call | flops 1073741824 | bytes 7000000 | tf_op jit(solution)/shard_map/shares/pallas_call | solution.py:474
  92.0 2.3 %collective-permute-start.8 = (bf16[256,512]{1,0:T(8,128)(2,1)S(1)}, bf16[256,512]{1,0:T(8,128)(2,1)S(1)}, u32[]{:S(2)}, u32[]{:S(2)}) collective-permute-start(bf16[256,512]{1,0:T(8,128)(2,1)S(1)} %pad_maximum_fusion.1), channel_id=1, source_target_pairs={{0,24},{4,28},{8,16},{12,20},{16,8},{20,12},{24,0},{28,4},{32,56},... | collective-permute-start | bytes 786440 | tf_op jit(solution)/shard_map/ppermute | solution.py:631
  94.3 4.7 %shares.3 = bf16[16,528,128]{2,1,0:T(8,128)(2,1)} custom-call(bf16[256,1536]{1,0:T(8,128)(2,1)} %bitcast.21, bf16[256,1024]{1,0:T(8,128)(2,1)} %copy-done.9, bf16[256,1024]{1,0:T(8,128)(2,1)} %collective-permute-done.refs_1_, bf16[256,1024]{1,0:T(8,128)(2,1)} %copy-done.16, ...), custom_call_target="tpu_custom_call", output_to_operand_aliasing={{}: (10, {})} | custom-call | flops 1073741824 | bytes 7000000 | tf_op jit(solution)/shard_map/shares/pallas_call | solution.py:474
  99.0 2.8 %collective-permute-done.8.refs_3_.mate_two_ref = bf16[256,512]{1,0:T(8,128)(2,1)S(1)} collective-permute-done((bf16[256,512]{1,0:T(8,128)(2,1)S(1)}, bf16[256,512]{1,0:T(8,128)(2,1)S(1)}, u32[]{:S(2)}, u32[]{:S(2)}) %collective-permute-start.8) | collective-permute-done | bytes 262176 | tf_op jit(solution)/shard_map/ppermute | solution.py:631
  101.8 6.0 %all-to-all-start.3 = ((bf16[16,528,128]{2,1,0:T(8,128)(2,1)}), bf16[16,528,128]{2,1,0:T(8,128)(2,1)S(1)}, u32[]{:S(2)}, u32[]{:S(2)}) async-start(bf16[16,528,128]{2,1,0:T(8,128)(2,1)} %shares.3), calls=%async_computation.3 | async-start | bytes 4325376 | tf_op jit(solution)/shard_map/all_to_all | solution.py:627
  107.8 0.0 copy-start.1
  107.8 3.4 %copy-done.1 = bf16[4096,1024]{1,0:T(8,128)(2,1)S(1)} copy-done((bf16[4096,1024]{1,0:T(8,128)(2,1)S(1)}, bf16[4096,1024]{1,0:T(8,128)(2,1)}, u32[]{:S(2)}) %copy-start.1) | copy-done | bytes 8388632
  111.2 1.1 copy-done.6
  112.3 4.0 %input_terms.1 = (bf16[2,1024,256]{2,1,0:T(8,128)(2,1)S(1)}, f32[2,1024,256]{2,1,0:T(8,128)S(1)}) custom-call(s32[2]{0:T(128)S(1)} %pad_add_fusion.place_ref, bf16[256,1536]{1,0:T(8,128)(2,1)S(1)} %bitcast.18, bf16[256,1536]{1,0:T(8,128)(2,1)S(1)} %bitcast.22, bf16[256,512]{1,0:T(8,128)(2,1)S(1)} %collective-permute-done.6.refs_2_.mate_one_ref, ...), custom_call_target="tpu_custom_call" | custom-call | flops 2147483648 | bytes 12000000 | tf_op jit(solution)/shard_map/input_terms/pallas_call | solution.py:565
  116.3 0.0 copy-start.7
  116.3 0.0 copy-start.8
  116.3 0.1 collective-permute-start.9
  116.4 2.6 %collective-permute-done.9.core_ref = bf16[2,1024,256]{2,1,0:T(8,128)(2,1)S(1)} collective-permute-done((bf16[2,1024,256]{2,1,0:T(8,128)(2,1)S(1)}, bf16[2,1024,256]{2,1,0:T(8,128)(2,1)S(1)}, u32[]{:S(2)}, u32[]{:S(2)}) %collective-permute-start.9) | collective-permute-done | bytes 1048608 | tf_op jit(solution)/shard_map/ppermute | solution.py:677
  119.0 0.1 fusion
  119.2 0.7 collective-permute-start.10
  119.9 2.5 %gate_grad.1 = bf16[256,1024]{1,0:T(8,128)(2,1)} custom-call(s32[2]{0:T(128)S(1)} %pad_add_fusion.place_ref, bf16[256,1536]{1,0:T(8,128)(2,1)S(1)} %bitcast.19, bf16[256,1536]{1,0:T(8,128)(2,1)S(1)} %bitcast.23, bf16[256,512]{1,0:T(8,128)(2,1)S(1)} %collective-permute-done.6.refs_2_.mate_one_ref, ...), custom_call_target="tpu_custom_call" | custom-call | flops 2000000 | bytes 2500000 | tf_op jit(solution)/shard_map/gate_grad/pallas_call | solution.py:606
  122.4 10.8 %collective-permute-done.10.chip_ref = bf16[1024,256]{1,0:T(8,128)(2,1)S(1)} collective-permute-done((bf16[1024,256]{1,0:T(8,128)(2,1)S(1)}, bf16[1024,256]{1,0:T(8,128)(2,1)S(1)}, u32[]{:S(2)}, u32[]{:S(2)}) %collective-permute-start.10) | collective-permute-done | bytes 524320 | tf_op jit(solution)/shard_map/ppermute | solution.py:679
  133.2 1.0 close_input.1
  134.2 4.0 %all-to-all-done.3.refs_0_.refs_1_.refs_2_.refs_3_.refs_4_.refs_5_.refs_6_.refs_7_.refs_8_ = bf16[16,528,128]{2,1,0:T(8,128)(2,1)S(1)} async-done(((bf16[16,528,128]{2,1,0:T(8,128)(2,1)}), bf16[16,528,128]{2,1,0:T(8,128)(2,1)S(1)}, u32[]{:S(2)}, u32[]{:S(2)}) %all-to-all-start.3) | async-done | bytes 2162720 | tf_op jit(solution)/shard_map/all_to_all | solution.py:627
  138.2 1.5 %close_weight.1 = (f32[128,1024]{1,0:T(8,128)}, f32[7,1024]{1,0:T(8,128)}) custom-call(bf16[16,528,128]{2,1,0:T(8,128)(2,1)S(1)} %all-to-all-done.3.refs_0_.refs_1_.refs_2_.refs_3_.refs_4_.refs_5_.refs_6_.refs_7_.refs_8_, bf16[16,528,128]{2,1,0:T(8,128)(2,1)S(1)} %all-to-all-done.3.refs_0_.refs_1_.refs_2_.refs_3_.refs_4_.refs_5_.refs_6_.refs_7_.refs_8_, ...), custom_call_target="tpu_custom_call" | custom-call | flops 2000000 | bytes 3000000 | tf_op jit(solution)/shard_map/close_weight/pallas_call | solution.py:526
  (43 shorter events, 0.2 us)
Async XLA Ops:
  0.6 36.3 %copy-start = (f32[7,1024]{1,0:T(8,128)S(1)}, f32[7,1024]{1,0:T(8,128)}, u32[]{:S(2)}) copy-start(f32[7,1024]{1,0:T(8,128)} %param.17) | copy-start | bytes 86020
  8.0 11.1 %copy-start.2 = (bf16[256,4096]{1,0:T(8,128)(2,1)S(1)}, bf16[256,4096]{1,0:T(8,128)(2,1)}, u32[]{:S(2)}) copy-start(bf16[256,4096]{1,0:T(8,128)(2,1)} %others_ref) | copy-start | bytes 6291460
  8.0 30.0 %all-to-all-start = ((bf16[32,64,256]{2,1,0:T(8,128)(2,1)}), bf16[32,64,256]{2,1,0:T(8,128)(2,1)}, u32[]{:S(2)}, u32[]{:S(2)}) async-start(bf16[32,64,256]{2,1,0:T(8,128)(2,1)} %sends.1), calls=%async_computation | async-start | bytes 2097152 | tf_op jit(solution)/shard_map/all_to_all | solution.py:627
  21.1 0.8 copy-start.10
  21.9 14.5 %copy-start.9 = (bf16[256,1024]{1,0:T(8,128)(2,1)}, bf16[256,1024]{1,0:T(8,128)(2,1)S(1)}, u32[]{:S(2)}) copy-start(bf16[256,1024]{1,0:T(8,128)(2,1)S(1)} %get-tuple-element.54.refs_0_) | copy-start | bytes 1572868
  21.9 40.0 %collective-permute-start = (bf16[256,1024]{1,0:T(8,128)(2,1)}, bf16[256,1024]{1,0:T(8,128)(2,1)}, u32[]{:S(2)}, u32[]{:S(2)}) collective-permute-start(bf16[256,1024]{1,0:T(8,128)(2,1)} %get-tuple-element.51), channel_id=1, source_target_pairs={{0,6},{1,7},{2,4},{3,5},{4,2},{5,3},{6,0},{7,1},{8,14},{9,15},{10,... | collective-permute-start | bytes 1572872 | tf_op jit(solution)/shard_map/ppermute | solution.py:639
  34.1 27.8 %collective-permute-start.2 = (bf16[256,1024]{1,0:T(8,128)(2,1)}, bf16[256,1024]{1,0:T(8,128)(2,1)}, u32[]{:S(2)}, u32[]{:S(2)}) collective-permute-start(bf16[256,1024]{1,0:T(8,128)(2,1)} %get-tuple-element.51), channel_id=1, source_target_pairs={{0,30},{1,31},{2,28},{3,29},{4,26},{5,27},{6,24},{7,25},{8,22},{9,... | collective-permute-start | bytes 1572872 | tf_op jit(solution)/shard_map/ppermute | solution.py:639
  36.4 25.5 %collective-permute-start.1 = (bf16[256,1024]{1,0:T(8,128)(2,1)S(1)}, bf16[256,1024]{1,0:T(8,128)(2,1)S(1)}, u32[]{:S(2)}, u32[]{:S(2)}) collective-permute-start(bf16[256,1024]{1,0:T(8,128)(2,1)S(1)} %get-tuple-element.54.refs_0_), channel_id=1, source_target_pairs={{0,24},{4,28},{8,16},{12,20},{16,8},{20,12},{24,0},{28,4},{32,56},... | collective-permute-start | bytes 1572872 | tf_op jit(solution)/shard_map/ppermute | solution.py:631
  46.7 19.9 %all-to-all-start.1 = ((bf16[16,16,1536]{2,1,0:T(8,128)(2,1)}), bf16[16,16,1536]{2,1,0:T(8,128)(2,1)S(1)}, u32[]{:S(2)}, u32[]{:S(2)}) async-start(bf16[16,16,1536]{2,1,0:T(8,128)(2,1)} %get-tuple-element.47), calls=%async_computation.1 | async-start | bytes 1572864 | tf_op jit(solution)/shard_map/all_to_all | solution.py:627
  53.1 19.4 %copy-start.18 = (bf16[16,128]{1,0:T(8,128)(2,1)S(1)}, bf16[16,128]{1,0:T(8,128)(2,1)}, u32[]{:S(2)}) copy-start(bf16[16,128]{1,0:T(8,128)(2,1)} %get-tuple-element.61) | copy-start | bytes 12292
  61.8 16.0 %copy-start.11 = (bf16[768,512]{1,0:T(8,128)(2,1)S(1)}, bf16[768,512]{1,0:T(8,128)(2,1)}, u32[]{:S(2)}) copy-start(bf16[768,512]{1,0:T(8,128)(2,1)} %constant.86.clone.both_ref) | copy-start | bytes 2359300
  61.9 16.0 %copy-start.12 = (f32[2,64,128]{2,1,0:T(8,128)S(1)}, f32[2,64,128]{2,1,0:T(8,128)}, u32[]{:S(2)}) copy-start(f32[2,64,128]{2,1,0:T(8,128)} %constant.80.clone.twist_ref) | copy-start | bytes 196612
  61.9 16.0 %copy-start.13 = (bf16[64,384]{1,0:T(8,128)(2,1)S(1)}, bf16[64,384]{1,0:T(8,128)(2,1)}, u32[]{:S(2)}) copy-start(bf16[64,384]{1,0:T(8,128)(2,1)} %constant.87.clone.last_nat_ref) | copy-start | bytes 147460
  61.9 4.7 %copy-start.16 = (bf16[256,1024]{1,0:T(8,128)(2,1)}, bf16[256,1024]{1,0:T(8,128)(2,1)S(1)}, u32[]{:S(2)}) copy-start(bf16[256,1024]{1,0:T(8,128)(2,1)S(1)} %collective-permute-done.1.refs_2_) | copy-start | bytes 1572868
  66.6 19.9 %copy-start.3 = (bf16[16,16,1536]{2,1,0:T(8,128)(2,1)}, bf16[16,16,1536]{2,1,0:T(8,128)(2,1)S(1)}, u32[]{:S(2)}) copy-start(bf16[16,16,1536]{2,1,0:T(8,128)(2,1)S(1)} %all-to-all-done.1) | copy-start | bytes 2359300
  66.6 25.3 %all-to-all-start.2 = ((bf16[16,16,1536]{2,1,0:T(8,128)(2,1)}), bf16[16,16,1536]{2,1,0:T(8,128)(2,1)S(1)}, u32[]{:S(2)}, u32[]{:S(2)}) async-start(bf16[16,16,1536]{2,1,0:T(8,128)(2,1)} %get-tuple-element.52), calls=%async_computation.2 | async-start | bytes 1572864 | tf_op jit(solution)/shard_map/all_to_all | solution.py:627
  73.2 13.3 %collective-permute-start.7 = (bf16[16,128]{1,0:T(8,128)(2,1)S(1)}, bf16[16,128]{1,0:T(8,128)(2,1)S(1)}, u32[]{:S(2)}, u32[]{:S(2)}) collective-permute-start(bf16[16,128]{1,0:T(8,128)(2,1)S(1)} %add.43), channel_id=1, source_target_pairs={{0,4},{4,0},{8,12},{12,8},{16,20},{20,16},{24,28},{28,24},{32,36},... | collective-permute-start | bytes 12296 | tf_op jit(solution)/shard_map/ppermute | solution.py:666
  76.1 11.0 %collective-permute-start.3 = (bf16[256,1024]{1,0:T(8,128)(2,1)}, bf16[256,1024]{1,0:T(8,128)(2,1)S(1)}, u32[]{:S(2)}, u32[]{:S(2)}) collective-permute-start(bf16[256,1024]{1,0:T(8,128)(2,1)} %collective-permute-done.refs_1_), channel_id=1, source_target_pairs={{0,1},{1,0},{2,3},{3,2},{4,5},{5,4},{6,7},{7,6},{8,9},{9,8},{10,11... | collective-permute-start | bytes 1572872 | tf_op jit(solution)/shard_map/ppermute | solution.py:661
  76.1 11.0 %collective-permute-start.4 = (bf16[256,1024]{1,0:T(8,128)(2,1)}, bf16[256,1024]{1,0:T(8,128)(2,1)}, u32[]{:S(2)}, u32[]{:S(2)}) collective-permute-start(bf16[256,1024]{1,0:T(8,128)(2,1)} %copy-done.16), channel_id=1, source_target_pairs={{0,1},{1,0},{2,3},{3,2},{4,5},{5,4},{6,7},{7,6},{8,9},{9,8},{10,11... | collective-permute-start | bytes 1572872 | tf_op jit(solution)/shard_map/ppermute | solution.py:661
  76.7 10.5 %collective-permute-start.5 = (bf16[256,1024]{1,0:T(8,128)(2,1)}, bf16[256,1024]{1,0:T(8,128)(2,1)}, u32[]{:S(2)}, u32[]{:S(2)}) collective-permute-start(bf16[256,1024]{1,0:T(8,128)(2,1)} %collective-permute-done.2.refs_3_), channel_id=1, source_target_pairs={{0,1},{1,0},{2,3},{3,2},{4,5},{5,4},{6,7},{7,6},{8,9},{9,8},{10,11... | collective-permute-start | bytes 1572872 | tf_op jit(solution)/shard_map/ppermute | solution.py:661
  76.7 15.2 %collective-permute-start.6 = (bf16[256,512]{1,0:T(8,128)(2,1)S(1)}, bf16[256,512]{1,0:T(8,128)(2,1)S(1)}, u32[]{:S(2)}, u32[]{:S(2)}) collective-permute-start(bf16[256,512]{1,0:T(8,128)(2,1)S(1)} %pad_maximum_fusion), channel_id=1, source_target_pairs={{0,24},{4,28},{8,16},{12,20},{16,8},{20,12},{24,0},{28,4},{32,56},... | collective-permute-start | bytes 786440 | tf_op jit(solution)/shard_map/ppermute | solution.py:631
  77.8 1.2 copy-start.14
  79.1 1.2 copy-start.15
  87.1 0.8 copy-start.17
  92.0 2.3 %copy-start.5 = (bf16[16,16,1536]{2,1,0:T(8,128)(2,1)}, bf16[16,16,1536]{2,1,0:T(8,128)(2,1)S(1)}, u32[]{:S(2)}) copy-start(bf16[16,16,1536]{2,1,0:T(8,128)(2,1)S(1)} %all-to-all-done.2) | copy-start | bytes 2359300
  92.0 9.8 %collective-permute-start.8 = (bf16[256,512]{1,0:T(8,128)(2,1)S(1)}, bf16[256,512]{1,0:T(8,128)(2,1)S(1)}, u32[]{:S(2)}, u32[]{:S(2)}) collective-permute-start(bf16[256,512]{1,0:T(8,128)(2,1)S(1)} %pad_maximum_fusion.1), channel_id=1, source_target_pairs={{0,24},{4,28},{8,16},{12,20},{16,8},{20,12},{24,0},{28,4},{32,56},... | collective-permute-start | bytes 786440 | tf_op jit(solution)/shard_map/ppermute | solution.py:631
  99.0 8.8 %copy-start.4 = (bf16[16,16,1536]{2,1,0:T(8,128)(2,1)S(1)}, bf16[16,16,1536]{2,1,0:T(8,128)(2,1)}, u32[]{:S(2)}) copy-start(bf16[16,16,1536]{2,1,0:T(8,128)(2,1)} %copy-done.3) | copy-start | bytes 2359300
  101.8 36.4 %all-to-all-start.3 = ((bf16[16,528,128]{2,1,0:T(8,128)(2,1)}), bf16[16,528,128]{2,1,0:T(8,128)(2,1)S(1)}, u32[]{:S(2)}, u32[]{:S(2)}) async-start(bf16[16,528,128]{2,1,0:T(8,128)(2,1)} %shares.3), calls=%async_computation.3 | async-start | bytes 4325376 | tf_op jit(solution)/shard_map/all_to_all | solution.py:627
  107.8 3.4 %copy-start.1 = (bf16[4096,1024]{1,0:T(8,128)(2,1)S(1)}, bf16[4096,1024]{1,0:T(8,128)(2,1)}, u32[]{:S(2)}) copy-start(bf16[4096,1024]{1,0:T(8,128)(2,1)} %refs_4_.3) | copy-start | bytes 25165828
  111.2 1.1 copy-start.6
  116.3 3.6 %copy-start.7 = (bf16[256,1024]{1,0:T(8,128)(2,1)S(1)}, bf16[256,1024]{1,0:T(8,128)(2,1)}, u32[]{:S(2)}) copy-start(bf16[256,1024]{1,0:T(8,128)(2,1)} %gate_ref.1) | copy-start | bytes 1572868
  116.3 3.6 %copy-start.8 = (bf16[256,1024]{1,0:T(8,128)(2,1)S(1)}, bf16[256,1024]{1,0:T(8,128)(2,1)}, u32[]{:S(2)}) copy-start(bf16[256,1024]{1,0:T(8,128)(2,1)} %grad_ref.1) | copy-start | bytes 1572868
  116.3 2.7 %collective-permute-start.9 = (bf16[2,1024,256]{2,1,0:T(8,128)(2,1)S(1)}, bf16[2,1024,256]{2,1,0:T(8,128)(2,1)S(1)}, u32[]{:S(2)}, u32[]{:S(2)}) collective-permute-start(bf16[2,1024,256]{2,1,0:T(8,128)(2,1)S(1)} %get-tuple-element.70), channel_id=1, source_target_pairs={{0,1},{1,0},{2,3},{3,2},{4,5},{5,4},{6,7},{7,6},{8,9},{9,8},{10,11... | collective-permute-start | bytes 3145736 | tf_op jit(solution)/shard_map/ppermute | solution.py:677
  119.2 14.0 %collective-permute-start.10 = (bf16[1024,256]{1,0:T(8,128)(2,1)S(1)}, bf16[1024,256]{1,0:T(8,128)(2,1)S(1)}, u32[]{:S(2)}, u32[]{:S(2)}) collective-permute-start(bf16[1024,256]{1,0:T(8,128)(2,1)S(1)} %fusion), channel_id=1, source_target_pairs={{0,2},{2,0},{1,3},{3,1},{4,6},{6,4},{5,7},{7,5},{8,10},{10,8},{9,1... | collective-permute-start | bytes 1572872 | tf_op jit(solution)/shard_map/ppermute | solution.py:679

commit v7 on v6

--- a/solution.py
+++ b/solution.py
@@ -661,13 +661,11 @@
     other = [other] + [lax.ppermute(part, "tp", cores) for part in mine[1:]]
     back_two = league(back_two)
     mate_one = for_mate(back_one)
-    grad_filters = filter_grads(lag_one, lag_two)
     taps = taps_one + taps_two
     partner = lax.ppermute(taps, "seq", [(s, s ^ 1) for s in range(seq_count)])
     taps = jnp.concatenate([taps[:8], partner[:8]], axis=0)
     outgoing = shares(back_one, mine, other)
-    back_two, outgoing, mate_one, grad_filters, taps = lax.optimization_barrier(
-        (back_two, outgoing, mate_one, grad_filters, taps))
+    back_two, outgoing, mate_one, taps = lax.optimization_barrier((back_two, outgoing, mate_one, taps))
     mate_two = for_mate(back_two)
     outgoing, mate_two = lax.optimization_barrier((shares(back_two, mine, other, taps, outgoing), mate_two))
     parts = exchange(outgoing, PLANES)
@@ -676,7 +674,9 @@
     send, keep = input_terms(place, backs, their, w_value)
     core = lax.ppermute(send, "tp", cores)
     send = (keep[1] + core[1].astype(jnp.float32)).astype(jnp.bfloat16)
+    send, lag_one, lag_two = lax.optimization_barrier((send, lag_one, lag_two))
     chip = lax.ppermute(send, "tp", chips)
+    grad_filters = filter_grads(lag_one, lag_two)
     grad_input = close_input(keep, core, chip)
     grad_gate = gate_grad(place, backs, their, gate_proj, grad_out)
     parts, grad_input, grad_gate = lax.optimization_barrier((parts, grad_input, grad_gate))

time: 141 us -> 134 us (0.950)
  the two profiles are of different devices: /device:TPU:0 before, /device:TPU:32 now
where the time goes in v7:
time: 134 us; the launch traced here: 133 us
  Pallas kernels  59.5 us (44%)
  starting transfers between devices  44.3 us (33%)
  waiting for transfers between devices  21.6 us (16%)
  local copies, waits for them, and re-layouts  6.11 us (5%)
    all_to_all x4, starting transfers between devices, exchange(): lax.all_to_all(value, 'seq', split_axis=0, concat_axis=0, axis_index_grou...  29.9 us
    pallas_call x2, Pallas kernels, mixer(): call(functools.partial(mixer_kernel, half * width), 'mixer', 9000000000,...  17.4 us
    all_to_all x4, waiting for transfers between devices, exchange(): lax.all_to_all(value, 'seq', split_axis=0, concat_axis=0, axis_index_grou...  10.3 us
    pallas_call x1, Pallas kernels, spectra_of(): call(spectra_kernel, 'spectra', 3000000000, 5000000, vmem=56, grid=(width...  8.8 us
    pallas_call x2, Pallas kernels, shares(): call(functools.partial(share_kernel, half), 'shares', 16 * rows * span *...  8.71 us
    pallas_call x1, Pallas kernels, sends(): call(send_kernel, 'sends', 2 * span * depth * channels, 12500000, vmem=56...  7.33 us
    pallas_call x1, Pallas kernels, filter_grads(): call(lag_kernel, 'filter_grads', 3000000000, 5000000, grid=(width // BATC...  6.25 us
    ppermute x3, starting transfers between devices, mates(): return lax.ppermute(value, 'seq', [(s, s ^ MATE) for s in range(seq_count)])  6.14 us
  transfers between devices with their start and end apart: 15, of which 7 were waited for; matrix products, arithmetic and copies ran while one was open for 1% of the time, Pallas kernels for 38%

profile of v7, /device:TPU:32, one launch (start us, length us, event | category | flops | bytes accessed | tf_op | source)
XLA Modules:
  0.0 133.3 jit_solution(14444149845118152039)
XLA Ops:
  0.6 0.0 copy-start
  0.6 7.3 %sends.1 = bf16[32,64,256]{2,1,0:T(8,128)(2,1)} custom-call(bf16[256,4096]{1,0:T(8,128)(2,1)} %others_ref, bf16[4096,1024]{1,0:T(8,128)(2,1)} %refs_4_.3, bf16[4096,1024]{1,0:T(8,128)(2,1)} %refs_4_.3, bf16[4096,1024]{1,0:T(8,128)(2,1)} %refs_4_.3, bf16[4096,1024]{1,0:T(8,128)(2,1)} %refs_4_.3, bf16[4096,1024]{1,0:T(8,128)(2,1)} %refs_4_.3, ...), custom_call_target="tpu_custom_call" | custom-call | flops 2147483648 | bytes 12500000 | tf_op jit(solution)/shard_map/sends/pallas_call | solution.py:391
  8.0 10.0 %all-to-all-start = ((bf16[32,64,256]{2,1,0:T(8,128)(2,1)}), bf16[32,64,256]{2,1,0:T(8,128)(2,1)}, u32[]{:S(2)}, u32[]{:S(2)}) async-start(bf16[32,64,256]{2,1,0:T(8,128)(2,1)} %sends.1), calls=%async_computation | async-start | bytes 2097152 | tf_op jit(solution)/shard_map/all_to_all | solution.py:627
  18.0 0.1 pad_add_fusion.place_ref
  18.1 2.0 %quarters.1 = (bf16[256,1024]{1,0:T(8,128)(2,1)S(1)}, bf16[256,1024]{1,0:T(8,128)(2,1)}, bf16[256,1024]{1,0:T(8,128)(2,1)S(1)}) custom-call(s32[2]{0:T(128)S(1)} %pad_add_fusion.place_ref, bf16[256,4096]{1,0:T(8,128)(2,1)S(1)} %copy-done.2, bf16[256,4096]{1,0:T(8,128)(2,1)S(1)} %copy-done.2), custom_call_target="tpu_custom_call" | custom-call | bytes 5000000 | tf_op jit(solution)/shard_map/quarters/pallas_call | solution.py:413
  20.1 0.8 copy-done.10
  20.9 2.2 %collective-permute-start = (bf16[256,1024]{1,0:T(8,128)(2,1)}, bf16[256,1024]{1,0:T(8,128)(2,1)S(1)}, u32[]{:S(2)}, u32[]{:S(2)}) collective-permute-start(bf16[256,1024]{1,0:T(8,128)(2,1)} %get-tuple-element.53), channel_id=1, source_target_pairs={{0,6},{1,7},{2,4},{3,5},{4,2},{5,3},{6,0},{7,1},{8,14},{9,15},{10,... | collective-permute-start | bytes 1572872 | tf_op jit(solution)/shard_map/ppermute | solution.py:639
  23.0 8.8 %spectra.1.spectra_ref = f32[2048,256]{1,0:T(8,128)} custom-call(f32[2,4,512,128]{3,2,1,0:T(8,128)} %bitcast.24, bf16[128,256]{1,0:T(8,128)(2,1)} %constant.79.clone.first_nat_ref, f32[2,64,128]{2,1,0:T(8,128)} %constant.80.clone.twist_ref, bf16[1536,256]{1,0:T(8,128)(2,1)} %constant.81.clone.pair_ref), custom_call_target="tpu_custom_call" | custom-call | flops 3000000000 | bytes 5000000 | tf_op jit(solution)/shard_map/spectra/pallas_call | solution.py:295
  31.8 2.3 %collective-permute-start.2 = (bf16[256,1024]{1,0:T(8,128)(2,1)}, bf16[256,1024]{1,0:T(8,128)(2,1)S(1)}, u32[]{:S(2)}, u32[]{:S(2)}) collective-permute-start(bf16[256,1024]{1,0:T(8,128)(2,1)} %get-tuple-element.53), channel_id=1, source_target_pairs={{0,30},{1,31},{2,28},{3,29},{4,26},{5,27},{6,24},{7,25},{8,22},{9,... | collective-permute-start | bytes 1572872 | tf_op jit(solution)/shard_map/ppermute | solution.py:639
  34.1 0.6 collective-permute-start.1
  34.7 0.7 constant_dynamic-slice_fusion.4.taps_ref
  35.4 2.0 %all-to-all-done.arrived_ref = bf16[32,64,256]{2,1,0:T(8,128)(2,1)} async-done(((bf16[32,64,256]{2,1,0:T(8,128)(2,1)}), bf16[32,64,256]{2,1,0:T(8,128)(2,1)}, u32[]{:S(2)}, u32[]{:S(2)}) %all-to-all-start) | async-done | bytes 1048608 | tf_op jit(solution)/shard_map/all_to_all | solution.py:627
  37.4 8.7 %mixer.2 = (bf16[16,16,1536]{2,1,0:T(8,128)(2,1)}, bf16[1024,512]{1,0:T(8,128)(2,1)}, bf16[16,128]{1,0:T(8,128)(2,1)}) custom-call(f32[7,32]{1,0:T(8,128)} %constant_dynamic-slice_fusion.4.taps_ref, bf16[32,64,256]{2,1,0:T(8,128)(2,1)} %all-to-all-done.arrived_ref, f32[2048,256]{1,0:T(8,128)} %spectra.1.spectra_ref, ...), custom_call_target="tpu_custom_call" | custom-call | flops 8999999488 | bytes 4000000 | tf_op jit(solution)/shard_map/mixer/pallas_call | solution.py:324
  46.1 7.3 %all-to-all-start.1 = ((bf16[16,16,1536]{2,1,0:T(8,128)(2,1)}), bf16[16,16,1536]{2,1,0:T(8,128)(2,1)S(1)}, u32[]{:S(2)}, u32[]{:S(2)}) async-start(bf16[16,16,1536]{2,1,0:T(8,128)(2,1)} %get-tuple-element.49), calls=%async_computation.1 | async-start | bytes 1572864 | tf_op jit(solution)/shard_map/all_to_all | solution.py:627
  53.3 8.7 %mixer.3 = (bf16[16,16,1536]{2,1,0:T(8,128)(2,1)}, bf16[1024,512]{1,0:T(8,128)(2,1)}, bf16[16,128]{1,0:T(8,128)(2,1)}) custom-call(f32[7,32]{1,0:T(8,128)} %constant_dynamic-slice_fusion.4.taps_ref, bf16[32,64,256]{2,1,0:T(8,128)(2,1)} %all-to-all-done.arrived_ref, f32[2048,256]{1,0:T(8,128)} %spectra.1.spectra_ref, ...), custom_call_target="tpu_custom_call" | custom-call | flops 8999999488 | bytes 4000000 | tf_op jit(solution)/shard_map/mixer/pallas_call | solution.py:324
  62.1 0.0 copy-start.17
  62.1 4.7 %all-to-all-done.1 = bf16[16,16,1536]{2,1,0:T(8,128)(2,1)S(1)} async-done(((bf16[16,16,1536]{2,1,0:T(8,128)(2,1)}), bf16[16,16,1536]{2,1,0:T(8,128)(2,1)S(1)}, u32[]{:S(2)}, u32[]{:S(2)}) %all-to-all-start.1) | async-done | bytes 786464 | tf_op jit(solution)/shard_map/all_to_all | solution.py:627
  66.8 4.0 %all-to-all-start.2 = ((bf16[16,16,1536]{2,1,0:T(8,128)(2,1)}), bf16[16,16,1536]{2,1,0:T(8,128)(2,1)S(1)}, u32[]{:S(2)}, u32[]{:S(2)}) async-start(bf16[16,16,1536]{2,1,0:T(8,128)(2,1)} %get-tuple-element.54), calls=%async_computation.2 | async-start | bytes 1572864 | tf_op jit(solution)/shard_map/all_to_all | solution.py:627
  70.8 0.5 collective-permute-start.4
  71.3 0.1 collective-permute-start.5
  71.5 2.8 %collective-permute-start.6 = (bf16[256,512]{1,0:T(8,128)(2,1)S(1)}, bf16[256,512]{1,0:T(8,128)(2,1)S(1)}, u32[]{:S(2)}, u32[]{:S(2)}) collective-permute-start(bf16[256,512]{1,0:T(8,128)(2,1)S(1)} %pad_maximum_fusion), channel_id=1, source_target_pairs={{0,24},{4,28},{8,16},{12,20},{16,8},{20,12},{24,0},{28,4},{32,56},... | collective-permute-start | bytes 786440 | tf_op jit(solution)/shard_map/ppermute | solution.py:631
  74.3 3.0 %collective-permute-start.7 = (bf16[16,128]{1,0:T(8,128)(2,1)S(1)}, bf16[16,128]{1,0:T(8,128)(2,1)S(1)}, u32[]{:S(2)}, u32[]{:S(2)}) collective-permute-start(bf16[16,128]{1,0:T(8,128)(2,1)S(1)} %add.43), channel_id=1, source_target_pairs={{0,4},{4,0},{8,12},{12,8},{16,20},{20,16},{24,28},{28,24},{32,36},... | collective-permute-start | bytes 12296 | tf_op jit(solution)/shard_map/ppermute | solution.py:665
  77.3 2.5 %collective-permute-done.7 = bf16[16,128]{1,0:T(8,128)(2,1)S(1)} collective-permute-done((bf16[16,128]{1,0:T(8,128)(2,1)S(1)}, bf16[16,128]{1,0:T(8,128)(2,1)S(1)}, u32[]{:S(2)}, u32[]{:S(2)}) %collective-permute-start.7) | collective-permute-done | bytes 4128 | tf_op jit(solution)/shard_map/ppermute | solution.py:665
  79.9 0.6 pad_maximum_fusion.2.refs_8_
  80.5 4.0 %shares.2.refs_9_ = bf16[16,528,128]{2,1,0:T(8,128)(2,1)} custom-call(bf16[256,1536]{1,0:T(8,128)(2,1)} %bitcast.17, bf16[256,1024]{1,0:T(8,128)(2,1)} %copy-done.9, bf16[256,1024]{1,0:T(8,128)(2,1)} %copy-done.16, bf16[256,1024]{1,0:T(8,128)(2,1)} %collective-permute-done.1.refs_2_, bf16[256,1024]{1,0:T(8,128)(2,1)} %copy-done.17, ...), custom_call_target="tpu_custom_call" | custom-call | flops 1073741824 | bytes 7000000 | tf_op jit(solution)/shard_map/shares/pallas_call | solution.py:474
  84.5 0.0 all-to-all-done.2
  84.6 2.8 %collective-permute-start.8 = (bf16[256,512]{1,0:T(8,128)(2,1)S(1)}, bf16[256,512]{1,0:T(8,128)(2,1)S(1)}, u32[]{:S(2)}, u32[]{:S(2)}) collective-permute-start(bf16[256,512]{1,0:T(8,128)(2,1)S(1)} %pad_maximum_fusion.1), channel_id=1, source_target_pairs={{0,24},{4,28},{8,16},{12,20},{16,8},{20,12},{24,0},{28,4},{32,56},... | collective-permute-start | bytes 786440 | tf_op jit(solution)/shard_map/ppermute | solution.py:631
  87.4 4.7 %shares.3 = bf16[16,528,128]{2,1,0:T(8,128)(2,1)} custom-call(bf16[256,1536]{1,0:T(8,128)(2,1)} %bitcast.21, bf16[256,1024]{1,0:T(8,128)(2,1)} %copy-done.9, bf16[256,1024]{1,0:T(8,128)(2,1)} %copy-done.16, bf16[256,1024]{1,0:T(8,128)(2,1)} %collective-permute-done.1.refs_2_, bf16[256,1024]{1,0:T(8,128)(2,1)} %copy-done.17, ...), custom_call_target="tpu_custom_call", output_to_operand_aliasing={{}: (10, {})} | custom-call | flops 1073741824 | bytes 7000000 | tf_op jit(solution)/shard_map/shares/pallas_call | solution.py:474
  92.1 0.0 copy-start.4
  92.1 0.9 collective-permute-done.8.refs_3_.mate_two_ref
  93.0 8.6 %all-to-all-start.3 = ((bf16[16,528,128]{2,1,0:T(8,128)(2,1)}), bf16[16,528,128]{2,1,0:T(8,128)(2,1)S(1)}, u32[]{:S(2)}, u32[]{:S(2)}) async-start(bf16[16,528,128]{2,1,0:T(8,128)(2,1)} %shares.3), calls=%async_computation.3 | async-start | bytes 4325376 | tf_op jit(solution)/shard_map/all_to_all | solution.py:627
  101.7 0.0 copy-start.1
  101.7 3.4 %copy-done.1 = bf16[4096,1024]{1,0:T(8,128)(2,1)S(1)} copy-done((bf16[4096,1024]{1,0:T(8,128)(2,1)S(1)}, bf16[4096,1024]{1,0:T(8,128)(2,1)}, u32[]{:S(2)}) %copy-start.1) | copy-done | bytes 8388632
  105.1 1.1 copy-done.6
  106.2 4.0 %input_terms.1 = (bf16[2,1024,256]{2,1,0:T(8,128)(2,1)S(1)}, f32[2,1024,256]{2,1,0:T(8,128)S(1)}) custom-call(s32[2]{0:T(128)S(1)} %pad_add_fusion.place_ref, bf16[256,1536]{1,0:T(8,128)(2,1)S(1)} %bitcast.18, bf16[256,1536]{1,0:T(8,128)(2,1)S(1)} %bitcast.22, bf16[256,512]{1,0:T(8,128)(2,1)S(1)} %collective-permute-done.6.refs_2_.mate_one_ref, ...), custom_call_target="tpu_custom_call" | custom-call | flops 2147483648 | bytes 12000000 | tf_op jit(solution)/shard_map/input_terms/pallas_call | solution.py:565
  110.2 0.1 collective-permute-start.9
  110.3 2.6 %collective-permute-done.9.core_ref = bf16[2,1024,256]{2,1,0:T(8,128)(2,1)S(1)} collective-permute-done((bf16[2,1024,256]{2,1,0:T(8,128)(2,1)S(1)}, bf16[2,1024,256]{2,1,0:T(8,128)(2,1)S(1)}, u32[]{:S(2)}, u32[]{:S(2)}) %collective-permute-start.9) | collective-permute-done | bytes 1048608 | tf_op jit(solution)/shard_map/ppermute | solution.py:675
  113.0 0.1 fusion
  113.1 0.0 copy-start.11
  113.1 0.0 copy-start.12
  113.1 0.0 copy-start.13
  113.2 0.1 collective-permute-start.10
  113.3 2.6 %gate_grad.1 = bf16[256,1024]{1,0:T(8,128)(2,1)} custom-call(s32[2]{0:T(128)S(1)} %pad_add_fusion.place_ref, bf16[256,1536]{1,0:T(8,128)(2,1)S(1)} %bitcast.19, bf16[256,1536]{1,0:T(8,128)(2,1)S(1)} %bitcast.23, bf16[256,512]{1,0:T(8,128)(2,1)S(1)} %collective-permute-done.6.refs_2_.mate_one_ref, ...), custom_call_target="tpu_custom_call" | custom-call | flops 2000000 | bytes 2500000 | tf_op jit(solution)/shard_map/gate_grad/pallas_call | solution.py:606
  115.9 6.3 %filter_grads.1 = f32[2,4,512,128]{3,2,1,0:T(8,128)} custom-call(bf16[1024,512]{1,0:T(8,128)(2,1)S(1)} %copy-done.14, bf16[1024,512]{1,0:T(8,128)(2,1)S(1)} %copy-done.15, f32[2,64,128]{2,1,0:T(8,128)S(1)} %copy-done.12, bf16[768,512]{1,0:T(8,128)(2,1)S(1)} %copy-done.11, bf16[64,384]{1,0:T(8,128)(2,1)S(1)} %copy-done.13), custom_call_target="tpu_custom_call" | custom-call | flops 3000000000 | bytes 5000000 | tf_op jit(solution)/shard_map/filter_grads/pallas_call | solution.py:308
  122.1 5.1 %collective-permute-done.10.chip_ref = bf16[1024,256]{1,0:T(8,128)(2,1)S(1)} collective-permute-done((bf16[1024,256]{1,0:T(8,128)(2,1)S(1)}, bf16[1024,256]{1,0:T(8,128)(2,1)S(1)}, u32[]{:S(2)}, u32[]{:S(2)}) %collective-permute-start.10) | collective-permute-done | bytes 524320 | tf_op jit(solution)/shard_map/ppermute | solution.py:678
  127.2 1.0 close_input.1
  128.2 3.6 %all-to-all-done.3.refs_0_.refs_1_.refs_2_.refs_3_.refs_4_.refs_5_.refs_6_.refs_7_.refs_8_ = bf16[16,528,128]{2,1,0:T(8,128)(2,1)S(1)} async-done(((bf16[16,528,128]{2,1,0:T(8,128)(2,1)}), bf16[16,528,128]{2,1,0:T(8,128)(2,1)S(1)}, u32[]{:S(2)}, u32[]{:S(2)}) %all-to-all-start.3) | async-done | bytes 2162720 | tf_op jit(solution)/shard_map/all_to_all | solution.py:627
  131.9 1.5 %close_weight.1 = (f32[128,1024]{1,0:T(8,128)}, f32[7,1024]{1,0:T(8,128)}) custom-call(bf16[16,528,128]{2,1,0:T(8,128)(2,1)S(1)} %all-to-all-done.3.refs_0_.refs_1_.refs_2_.refs_3_.refs_4_.refs_5_.refs_6_.refs_7_.refs_8_, bf16[16,528,128]{2,1,0:T(8,128)(2,1)S(1)} %all-to-all-done.3.refs_0_.refs_1_.refs_2_.refs_3_.refs_4_.refs_5_.refs_6_.refs_7_.refs_8_, ...), custom_call_target="tpu_custom_call" | custom-call | flops 2000000 | bytes 3000000 | tf_op jit(solution)/shard_map/close_weight/pallas_call | solution.py:526
  (45 shorter events, 0.2 us)
Async XLA Ops:
  0.6 34.1 %copy-start = (f32[7,1024]{1,0:T(8,128)S(1)}, f32[7,1024]{1,0:T(8,128)}, u32[]{:S(2)}) copy-start(f32[7,1024]{1,0:T(8,128)} %param.17) | copy-start | bytes 86020
  8.0 10.1 %copy-start.2 = (bf16[256,4096]{1,0:T(8,128)(2,1)S(1)}, bf16[256,4096]{1,0:T(8,128)(2,1)}, u32[]{:S(2)}) copy-start(bf16[256,4096]{1,0:T(8,128)(2,1)} %others_ref) | copy-start | bytes 6291460
  8.0 29.4 %all-to-all-start = ((bf16[32,64,256]{2,1,0:T(8,128)(2,1)}), bf16[32,64,256]{2,1,0:T(8,128)(2,1)}, u32[]{:S(2)}, u32[]{:S(2)}) async-start(bf16[32,64,256]{2,1,0:T(8,128)(2,1)} %sends.1), calls=%async_computation | async-start | bytes 2097152 | tf_op jit(solution)/shard_map/all_to_all | solution.py:627
  20.1 0.8 copy-start.10
  20.9 13.3 %copy-start.9 = (bf16[256,1024]{1,0:T(8,128)(2,1)}, bf16[256,1024]{1,0:T(8,128)(2,1)S(1)}, u32[]{:S(2)}) copy-start(bf16[256,1024]{1,0:T(8,128)(2,1)S(1)} %get-tuple-element.56.refs_0_) | copy-start | bytes 1572868
  20.9 41.2 %collective-permute-start = (bf16[256,1024]{1,0:T(8,128)(2,1)}, bf16[256,1024]{1,0:T(8,128)(2,1)S(1)}, u32[]{:S(2)}, u32[]{:S(2)}) collective-permute-start(bf16[256,1024]{1,0:T(8,128)(2,1)} %get-tuple-element.53), channel_id=1, source_target_pairs={{0,6},{1,7},{2,4},{3,5},{4,2},{5,3},{6,0},{7,1},{8,14},{9,15},{10,... | collective-permute-start | bytes 1572872 | tf_op jit(solution)/shard_map/ppermute | solution.py:639
  31.8 30.3 %collective-permute-start.2 = (bf16[256,1024]{1,0:T(8,128)(2,1)}, bf16[256,1024]{1,0:T(8,128)(2,1)S(1)}, u32[]{:S(2)}, u32[]{:S(2)}) collective-permute-start(bf16[256,1024]{1,0:T(8,128)(2,1)} %get-tuple-element.53), channel_id=1, source_target_pairs={{0,30},{1,31},{2,28},{3,29},{4,26},{5,27},{6,24},{7,25},{8,22},{9,... | collective-permute-start | bytes 1572872 | tf_op jit(solution)/shard_map/ppermute | solution.py:639
  34.1 28.0 %collective-permute-start.1 = (bf16[256,1024]{1,0:T(8,128)(2,1)S(1)}, bf16[256,1024]{1,0:T(8,128)(2,1)}, u32[]{:S(2)}, u32[]{:S(2)}) collective-permute-start(bf16[256,1024]{1,0:T(8,128)(2,1)S(1)} %get-tuple-element.56.refs_0_), channel_id=1, source_target_pairs={{0,24},{4,28},{8,16},{12,20},{16,8},{20,12},{24,0},{28,4},{32,56},... | collective-permute-start | bytes 1572872 | tf_op jit(solution)/shard_map/ppermute | solution.py:631
  46.1 20.8 %all-to-all-start.1 = ((bf16[16,16,1536]{2,1,0:T(8,128)(2,1)}), bf16[16,16,1536]{2,1,0:T(8,128)(2,1)S(1)}, u32[]{:S(2)}, u32[]{:S(2)}) async-start(bf16[16,16,1536]{2,1,0:T(8,128)(2,1)} %get-tuple-element.49), calls=%async_computation.1 | async-start | bytes 1572864 | tf_op jit(solution)/shard_map/all_to_all | solution.py:627
  62.1 12.2 %copy-start.18 = (bf16[16,128]{1,0:T(8,128)(2,1)S(1)}, bf16[16,128]{1,0:T(8,128)(2,1)}, u32[]{:S(2)}) copy-start(bf16[16,128]{1,0:T(8,128)(2,1)} %get-tuple-element.61) | copy-start | bytes 12292
  62.1 12.2 %copy-start.19 = (bf16[16,128]{1,0:T(8,128)(2,1)S(1)}, bf16[16,128]{1,0:T(8,128)(2,1)}, u32[]{:S(2)}) copy-start(bf16[16,128]{1,0:T(8,128)(2,1)} %get-tuple-element.62) | copy-start | bytes 12292
  62.1 18.4 %copy-start.16 = (bf16[256,1024]{1,0:T(8,128)(2,1)}, bf16[256,1024]{1,0:T(8,128)(2,1)S(1)}, u32[]{:S(2)}) copy-start(bf16[256,1024]{1,0:T(8,128)(2,1)S(1)} %collective-permute-done.refs_1_) | copy-start | bytes 1572868
  62.1 18.4 %copy-start.17 = (bf16[256,1024]{1,0:T(8,128)(2,1)}, bf16[256,1024]{1,0:T(8,128)(2,1)S(1)}, u32[]{:S(2)}) copy-start(bf16[256,1024]{1,0:T(8,128)(2,1)S(1)} %collective-permute-done.2.refs_3_) | copy-start | bytes 1572868
  66.8 13.7 %copy-start.3 = (bf16[16,16,1536]{2,1,0:T(8,128)(2,1)}, bf16[16,16,1536]{2,1,0:T(8,128)(2,1)S(1)}, u32[]{:S(2)}) copy-start(bf16[16,16,1536]{2,1,0:T(8,128)(2,1)S(1)} %all-to-all-done.1) | copy-start | bytes 2359300
  66.8 17.7 %all-to-all-start.2 = ((bf16[16,16,1536]{2,1,0:T(8,128)(2,1)}), bf16[16,16,1536]{2,1,0:T(8,128)(2,1)S(1)}, u32[]{:S(2)}, u32[]{:S(2)}) async-start(bf16[16,16,1536]{2,1,0:T(8,128)(2,1)} %get-tuple-element.54), calls=%async_computation.2 | async-start | bytes 1572864 | tf_op jit(solution)/shard_map/all_to_all | solution.py:627
  70.8 9.7 %collective-permute-start.3 = (bf16[256,1024]{1,0:T(8,128)(2,1)S(1)}, bf16[256,1024]{1,0:T(8,128)(2,1)}, u32[]{:S(2)}, u32[]{:S(2)}) collective-permute-start(bf16[256,1024]{1,0:T(8,128)(2,1)S(1)} %collective-permute-done.refs_1_), channel_id=1, source_target_pairs={{0,1},{1,0},{2,3},{3,2},{4,5},{5,4},{6,7},{7,6},{8,9},{9,8},{10,11... | collective-permute-start | bytes 1572872 | tf_op jit(solution)/shard_map/ppermute | solution.py:661
  70.8 9.6 %collective-permute-start.4 = (bf16[256,1024]{1,0:T(8,128)(2,1)}, bf16[256,1024]{1,0:T(8,128)(2,1)}, u32[]{:S(2)}, u32[]{:S(2)}) collective-permute-start(bf16[256,1024]{1,0:T(8,128)(2,1)} %collective-permute-done.1.refs_2_), channel_id=1, source_target_pairs={{0,1},{1,0},{2,3},{3,2},{4,5},{5,4},{6,7},{7,6},{8,9},{9,8},{10,11... | collective-permute-start | bytes 1572872 | tf_op jit(solution)/shard_map/ppermute | solution.py:661
  71.3 9.1 %collective-permute-start.5 = (bf16[256,1024]{1,0:T(8,128)(2,1)S(1)}, bf16[256,1024]{1,0:T(8,128)(2,1)}, u32[]{:S(2)}, u32[]{:S(2)}) collective-permute-start(bf16[256,1024]{1,0:T(8,128)(2,1)S(1)} %collective-permute-done.2.refs_3_), channel_id=1, source_target_pairs={{0,1},{1,0},{2,3},{3,2},{4,5},{5,4},{6,7},{7,6},{8,9},{9,8},{10,11... | collective-permute-start | bytes 1572872 | tf_op jit(solution)/shard_map/ppermute | solution.py:661
  71.5 13.1 %collective-permute-start.6 = (bf16[256,512]{1,0:T(8,128)(2,1)S(1)}, bf16[256,512]{1,0:T(8,128)(2,1)S(1)}, u32[]{:S(2)}, u32[]{:S(2)}) collective-permute-start(bf16[256,512]{1,0:T(8,128)(2,1)S(1)} %pad_maximum_fusion), channel_id=1, source_target_pairs={{0,24},{4,28},{8,16},{12,20},{16,8},{20,12},{24,0},{28,4},{32,56},... | collective-permute-start | bytes 786440 | tf_op jit(solution)/shard_map/ppermute | solution.py:631
  74.3 5.6 %collective-permute-start.7 = (bf16[16,128]{1,0:T(8,128)(2,1)S(1)}, bf16[16,128]{1,0:T(8,128)(2,1)S(1)}, u32[]{:S(2)}, u32[]{:S(2)}) collective-permute-start(bf16[16,128]{1,0:T(8,128)(2,1)S(1)} %add.43), channel_id=1, source_target_pairs={{0,4},{4,0},{8,12},{12,8},{16,20},{20,16},{24,28},{28,24},{32,36},... | collective-permute-start | bytes 12296 | tf_op jit(solution)/shard_map/ppermute | solution.py:665
  84.5 2.8 %copy-start.5 = (bf16[16,16,1536]{2,1,0:T(8,128)(2,1)}, bf16[16,16,1536]{2,1,0:T(8,128)(2,1)S(1)}, u32[]{:S(2)}) copy-start(bf16[16,16,1536]{2,1,0:T(8,128)(2,1)S(1)} %all-to-all-done.2) | copy-start | bytes 2359300
  84.6 8.4 %collective-permute-start.8 = (bf16[256,512]{1,0:T(8,128)(2,1)S(1)}, bf16[256,512]{1,0:T(8,128)(2,1)S(1)}, u32[]{:S(2)}, u32[]{:S(2)}) collective-permute-start(bf16[256,512]{1,0:T(8,128)(2,1)S(1)} %pad_maximum_fusion.1), channel_id=1, source_target_pairs={{0,24},{4,28},{8,16},{12,20},{16,8},{20,12},{24,0},{28,4},{32,56},... | collective-permute-start | bytes 786440 | tf_op jit(solution)/shard_map/ppermute | solution.py:631
  92.1 9.6 %copy-start.4 = (bf16[16,16,1536]{2,1,0:T(8,128)(2,1)S(1)}, bf16[16,16,1536]{2,1,0:T(8,128)(2,1)}, u32[]{:S(2)}) copy-start(bf16[16,16,1536]{2,1,0:T(8,128)(2,1)} %copy-done.3) | copy-start | bytes 2359300
  93.0 38.8 %all-to-all-start.3 = ((bf16[16,528,128]{2,1,0:T(8,128)(2,1)}), bf16[16,528,128]{2,1,0:T(8,128)(2,1)S(1)}, u32[]{:S(2)}, u32[]{:S(2)}) async-start(bf16[16,528,128]{2,1,0:T(8,128)(2,1)} %shares.3), calls=%async_computation.3 | async-start | bytes 4325376 | tf_op jit(solution)/shard_map/all_to_all | solution.py:627
  101.7 3.4 %copy-start.1 = (bf16[4096,1024]{1,0:T(8,128)(2,1)S(1)}, bf16[4096,1024]{1,0:T(8,128)(2,1)}, u32[]{:S(2)}) copy-start(bf16[4096,1024]{1,0:T(8,128)(2,1)} %refs_4_.3) | copy-start | bytes 25165828
  105.1 1.1 copy-start.6
  110.2 3.1 %copy-start.7 = (bf16[256,1024]{1,0:T(8,128)(2,1)S(1)}, bf16[256,1024]{1,0:T(8,128)(2,1)}, u32[]{:S(2)}) copy-start(bf16[256,1024]{1,0:T(8,128)(2,1)} %gate_ref.1) | copy-start | bytes 1572868
  110.2 3.0 %copy-start.8 = (bf16[256,1024]{1,0:T(8,128)(2,1)S(1)}, bf16[256,1024]{1,0:T(8,128)(2,1)}, u32[]{:S(2)}) copy-start(bf16[256,1024]{1,0:T(8,128)(2,1)} %grad_ref.1) | copy-start | bytes 1572868
  110.2 2.7 %collective-permute-start.9 = (bf16[2,1024,256]{2,1,0:T(8,128)(2,1)S(1)}, bf16[2,1024,256]{2,1,0:T(8,128)(2,1)S(1)}, u32[]{:S(2)}, u32[]{:S(2)}) collective-permute-start(bf16[2,1024,256]{2,1,0:T(8,128)(2,1)S(1)} %get-tuple-element.70), channel_id=1, source_target_pairs={{0,1},{1,0},{2,3},{3,2},{4,5},{5,4},{6,7},{7,6},{8,9},{9,8},{10,11... | collective-permute-start | bytes 3145736 | tf_op jit(solution)/shard_map/ppermute | solution.py:675
  113.1 2.7 %copy-start.11 = (bf16[768,512]{1,0:T(8,128)(2,1)S(1)}, bf16[768,512]{1,0:T(8,128)(2,1)}, u32[]{:S(2)}) copy-start(bf16[768,512]{1,0:T(8,128)(2,1)} %constant.86.clone.both_ref) | copy-start | bytes 2359300
  113.1 2.7 %copy-start.12 = (f32[2,64,128]{2,1,0:T(8,128)S(1)}, f32[2,64,128]{2,1,0:T(8,128)}, u32[]{:S(2)}) copy-start(f32[2,64,128]{2,1,0:T(8,128)} %constant.80.clone.twist_ref) | copy-start | bytes 196612
  113.1 2.7 %copy-start.13 = (bf16[64,384]{1,0:T(8,128)(2,1)S(1)}, bf16[64,384]{1,0:T(8,128)(2,1)}, u32[]{:S(2)}) copy-start(bf16[64,384]{1,0:T(8,128)(2,1)} %constant.87.clone.last_nat_ref) | copy-start | bytes 147460
  113.1 2.7 %copy-start.14 = (bf16[1024,512]{1,0:T(8,128)(2,1)S(1)}, bf16[1024,512]{1,0:T(8,128)(2,1)}, u32[]{:S(2)}) copy-start(bf16[1024,512]{1,0:T(8,128)(2,1)} %get-tuple-element.78.lag_one_ref) | copy-start | bytes 3145732
  113.2 2.7 %copy-start.15 = (bf16[1024,512]{1,0:T(8,128)(2,1)S(1)}, bf16[1024,512]{1,0:T(8,128)(2,1)}, u32[]{:S(2)}) copy-start(bf16[1024,512]{1,0:T(8,128)(2,1)} %get-tuple-element.79.lag_two_ref) | copy-start | bytes 3145732
  113.2 14.0 %collective-permute-start.10 = (bf16[1024,256]{1,0:T(8,128)(2,1)S(1)}, bf16[1024,256]{1,0:T(8,128)(2,1)S(1)}, u32[]{:S(2)}, u32[]{:S(2)}) collective-permute-start(bf16[1024,256]{1,0:T(8,128)(2,1)S(1)} %fusion), channel_id=1, source_target_pairs={{0,2},{2,0},{1,3},{3,1},{4,6},{6,4},{5,7},{7,5},{8,10},{10,8},{9,1... | collective-permute-start | bytes 1572872 | tf_op jit(solution)/shard_map/ppermute | solution.py:678

commit v8 on v7

--- a/solution.py
+++ b/solution.py
@@ -665,7 +665,7 @@
     partner = lax.ppermute(taps, "seq", [(s, s ^ 1) for s in range(seq_count)])
     taps = jnp.concatenate([taps[:8], partner[:8]], axis=0)
     outgoing = shares(back_one, mine, other)
-    back_two, outgoing, mate_one, taps = lax.optimization_barrier((back_two, outgoing, mate_one, taps))
+    back_two, outgoing, mate_one = lax.optimization_barrier((back_two, outgoing, mate_one))
     mate_two = for_mate(back_two)
     outgoing, mate_two = lax.optimization_barrier((shares(back_two, mine, other, taps, outgoing), mate_two))
     parts = exchange(outgoing, PLANES)

time: 134 us -> 134 us (level)
  the two profiles are of different devices: /device:TPU:32 before, /device:TPU:0 now
where the time goes in v8:
time: 134 us; the launch traced here: 133 us
  Pallas kernels  59.5 us (44%)
  starting transfers between devices  37.5 us (28%)
  waiting for transfers between devices  28.2 us (21%)
  local copies, waits for them, and re-layouts  6.1 us (5%)
    all_to_all x4, starting transfers between devices, exchange(): lax.all_to_all(value, 'seq', split_axis=0, concat_axis=0, axis_index_grou...  27.9 us
    pallas_call x2, Pallas kernels, mixer(): call(functools.partial(mixer_kernel, half * width), 'mixer', 9000000000,...  17.4 us
    all_to_all x4, waiting for transfers between devices, exchange(): lax.all_to_all(value, 'seq', split_axis=0, concat_axis=0, axis_index_grou...  11.9 us
    pallas_call x1, Pallas kernels, spectra_of(): call(spectra_kernel, 'spectra', 3000000000, 5000000, vmem=56, grid=(width...  8.81 us
    pallas_call x2, Pallas kernels, shares(): call(functools.partial(share_kernel, half), 'shares', 16 * rows * span *...  8.7 us
    pallas_call x1, Pallas kernels, sends(): call(send_kernel, 'sends', 2 * span * depth * channels, 12500000, vmem=56...  7.33 us
    pallas_call x1, Pallas kernels, filter_grads(): call(lag_kernel, 'filter_grads', 3000000000, 5000000, grid=(width // BATC...  6.25 us
    ppermute x2, starting transfers between devices, across(): lax.ppermute(value, ('seq', 'tp'), [(4 * s + t, 4 * (s ^ flip) + (t ^ 2))...  5.68 us
  transfers between devices with their start and end apart: 15, of which 9 were waited for; matrix products, arithmetic and copies ran while one was open for 1% of the time, Pallas kernels for 38%

profile of v8, /device:TPU:0, one launch (start us, length us, event | category | flops | bytes accessed | tf_op | source)
XLA Modules:
  0.0 133.2 jit_solution(9653644995408240124)
XLA Ops:
  0.6 0.0 copy-start
  0.6 7.3 %sends.1 = bf16[32,64,256]{2,1,0:T(8,128)(2,1)} custom-call(bf16[256,4096]{1,0:T(8,128)(2,1)} %others_ref, bf16[4096,1024]{1,0:T(8,128)(2,1)} %refs_4_.3, bf16[4096,1024]{1,0:T(8,128)(2,1)} %refs_4_.3, bf16[4096,1024]{1,0:T(8,128)(2,1)} %refs_4_.3, bf16[4096,1024]{1,0:T(8,128)(2,1)} %refs_4_.3, bf16[4096,1024]{1,0:T(8,128)(2,1)} %refs_4_.3, ...), custom_call_target="tpu_custom_call" | custom-call | flops 2147483648 | bytes 12500000 | tf_op jit(solution)/shard_map/sends/pallas_call | solution.py:391
  8.0 11.0 %all-to-all-start = ((bf16[32,64,256]{2,1,0:T(8,128)(2,1)}), bf16[32,64,256]{2,1,0:T(8,128)(2,1)}, u32[]{:S(2)}, u32[]{:S(2)}) async-start(bf16[32,64,256]{2,1,0:T(8,128)(2,1)} %sends.1), calls=%async_computation | async-start | bytes 2097152 | tf_op jit(solution)/shard_map/all_to_all | solution.py:627
  19.0 0.1 pad_add_fusion.place_ref
  19.1 2.0 %quarters.1 = (bf16[256,1024]{1,0:T(8,128)(2,1)S(1)}, bf16[256,1024]{1,0:T(8,128)(2,1)}, bf16[256,1024]{1,0:T(8,128)(2,1)S(1)}) custom-call(s32[2]{0:T(128)S(1)} %pad_add_fusion.place_ref, bf16[256,4096]{1,0:T(8,128)(2,1)S(1)} %copy-done.2, bf16[256,4096]{1,0:T(8,128)(2,1)S(1)} %copy-done.2), custom_call_target="tpu_custom_call" | custom-call | bytes 5000000 | tf_op jit(solution)/shard_map/quarters/pallas_call | solution.py:413
  21.1 0.8 copy-done.10
  21.9 3.4 %collective-permute-start = (bf16[256,1024]{1,0:T(8,128)(2,1)}, bf16[256,1024]{1,0:T(8,128)(2,1)S(1)}, u32[]{:S(2)}, u32[]{:S(2)}) collective-permute-start(bf16[256,1024]{1,0:T(8,128)(2,1)} %get-tuple-element.52), channel_id=1, source_target_pairs={{0,6},{1,7},{2,4},{3,5},{4,2},{5,3},{6,0},{7,1},{8,14},{9,15},{10,... | collective-permute-start | bytes 1572872 | tf_op jit(solution)/shard_map/ppermute | solution.py:639
  25.2 8.8 %spectra.1.spectra_ref = f32[2048,256]{1,0:T(8,128)} custom-call(f32[2,4,512,128]{3,2,1,0:T(8,128)} %bitcast.24, bf16[128,256]{1,0:T(8,128)(2,1)} %constant.79.clone.first_nat_ref, f32[2,64,128]{2,1,0:T(8,128)} %constant.80.clone.twist_ref, bf16[1536,256]{1,0:T(8,128)(2,1)} %constant.81.clone.pair_ref), custom_call_target="tpu_custom_call" | custom-call | flops 3000000000 | bytes 5000000 | tf_op jit(solution)/shard_map/spectra/pallas_call | solution.py:295
  34.1 2.3 %collective-permute-start.2 = (bf16[256,1024]{1,0:T(8,128)(2,1)}, bf16[256,1024]{1,0:T(8,128)(2,1)S(1)}, u32[]{:S(2)}, u32[]{:S(2)}) collective-permute-start(bf16[256,1024]{1,0:T(8,128)(2,1)} %get-tuple-element.52), channel_id=1, source_target_pairs={{0,30},{1,31},{2,28},{3,29},{4,26},{5,27},{6,24},{7,25},{8,22},{9,... | collective-permute-start | bytes 1572872 | tf_op jit(solution)/shard_map/ppermute | solution.py:639
  36.4 0.6 collective-permute-start.1
  36.9 0.7 constant_dynamic-slice_fusion.4.taps_ref
  37.6 0.4 all-to-all-done.arrived_ref
  38.0 8.7 %mixer.2 = (bf16[16,16,1536]{2,1,0:T(8,128)(2,1)}, bf16[1024,512]{1,0:T(8,128)(2,1)}, bf16[16,128]{1,0:T(8,128)(2,1)}) custom-call(f32[7,32]{1,0:T(8,128)} %constant_dynamic-slice_fusion.4.taps_ref, bf16[32,64,256]{2,1,0:T(8,128)(2,1)} %all-to-all-done.arrived_ref, f32[2048,256]{1,0:T(8,128)} %spectra.1.spectra_ref, ...), custom_call_target="tpu_custom_call" | custom-call | flops 8999999488 | bytes 4000000 | tf_op jit(solution)/shard_map/mixer/pallas_call | solution.py:324
  46.7 6.4 %all-to-all-start.1 = ((bf16[16,16,1536]{2,1,0:T(8,128)(2,1)}), bf16[16,16,1536]{2,1,0:T(8,128)(2,1)S(1)}, u32[]{:S(2)}, u32[]{:S(2)}) async-start(bf16[16,16,1536]{2,1,0:T(8,128)(2,1)} %get-tuple-element.48), calls=%async_computation.1 | async-start | bytes 1572864 | tf_op jit(solution)/shard_map/all_to_all | solution.py:627
  53.1 8.7 %mixer.3 = (bf16[16,16,1536]{2,1,0:T(8,128)(2,1)}, bf16[1024,512]{1,0:T(8,128)(2,1)}, bf16[16,128]{1,0:T(8,128)(2,1)}) custom-call(f32[7,32]{1,0:T(8,128)} %constant_dynamic-slice_fusion.4.taps_ref, bf16[32,64,256]{2,1,0:T(8,128)(2,1)} %all-to-all-done.arrived_ref, f32[2048,256]{1,0:T(8,128)} %spectra.1.spectra_ref, ...), custom_call_target="tpu_custom_call" | custom-call | flops 8999999488 | bytes 4000000 | tf_op jit(solution)/shard_map/mixer/pallas_call | solution.py:324
  61.9 0.0 copy-start.17
  61.9 4.7 %all-to-all-done.1 = bf16[16,16,1536]{2,1,0:T(8,128)(2,1)S(1)} async-done(((bf16[16,16,1536]{2,1,0:T(8,128)(2,1)}), bf16[16,16,1536]{2,1,0:T(8,128)(2,1)S(1)}, u32[]{:S(2)}, u32[]{:S(2)}) %all-to-all-start.1) | async-done | bytes 786464 | tf_op jit(solution)/shard_map/all_to_all | solution.py:627
  66.6 5.0 %all-to-all-start.2 = ((bf16[16,16,1536]{2,1,0:T(8,128)(2,1)}), bf16[16,16,1536]{2,1,0:T(8,128)(2,1)S(1)}, u32[]{:S(2)}, u32[]{:S(2)}) async-start(bf16[16,16,1536]{2,1,0:T(8,128)(2,1)} %get-tuple-element.53), calls=%async_computation.2 | async-start | bytes 1572864 | tf_op jit(solution)/shard_map/all_to_all | solution.py:627
  71.6 0.5 collective-permute-start.4
  72.1 0.1 collective-permute-start.5
  72.3 1.8 %collective-permute-start.6 = (bf16[256,512]{1,0:T(8,128)(2,1)S(1)}, bf16[256,512]{1,0:T(8,128)(2,1)S(1)}, u32[]{:S(2)}, u32[]{:S(2)}) collective-permute-start(bf16[256,512]{1,0:T(8,128)(2,1)S(1)} %pad_maximum_fusion), channel_id=1, source_target_pairs={{0,24},{4,28},{8,16},{12,20},{16,8},{20,12},{24,0},{28,4},{32,56},... | collective-permute-start | bytes 786440 | tf_op jit(solution)/shard_map/ppermute | solution.py:631
  74.0 1.3 %collective-permute-done.4.refs_6_ = bf16[256,1024]{1,0:T(8,128)(2,1)} collective-permute-done((bf16[256,1024]{1,0:T(8,128)(2,1)}, bf16[256,1024]{1,0:T(8,128)(2,1)}, u32[]{:S(2)}, u32[]{:S(2)}) %collective-permute-start.4) | collective-permute-done | bytes 524320 | tf_op jit(solution)/shard_map/ppermute | solution.py:661
  75.4 4.0 %shares.2.refs_9_ = bf16[16,528,128]{2,1,0:T(8,128)(2,1)} custom-call(bf16[256,1536]{1,0:T(8,128)(2,1)} %bitcast.17, bf16[256,1024]{1,0:T(8,128)(2,1)} %copy-done.9, bf16[256,1024]{1,0:T(8,128)(2,1)} %copy-done.16, bf16[256,1024]{1,0:T(8,128)(2,1)} %collective-permute-done.1.refs_2_, bf16[256,1024]{1,0:T(8,128)(2,1)} %copy-done.17, ...), custom_call_target="tpu_custom_call" | custom-call | flops 1073741824 | bytes 7000000 | tf_op jit(solution)/shard_map/shares/pallas_call | solution.py:474
  79.4 2.8 %collective-permute-done.6.refs_2_.mate_one_ref = bf16[256,512]{1,0:T(8,128)(2,1)S(1)} collective-permute-done((bf16[256,512]{1,0:T(8,128)(2,1)S(1)}, bf16[256,512]{1,0:T(8,128)(2,1)S(1)}, u32[]{:S(2)}, u32[]{:S(2)}) %collective-permute-start.6) | collective-permute-done | bytes 262176 | tf_op jit(solution)/shard_map/ppermute | solution.py:631
  82.2 5.3 %all-to-all-done.2 = bf16[16,16,1536]{2,1,0:T(8,128)(2,1)S(1)} async-done(((bf16[16,16,1536]{2,1,0:T(8,128)(2,1)}), bf16[16,16,1536]{2,1,0:T(8,128)(2,1)S(1)}, u32[]{:S(2)}, u32[]{:S(2)}) %all-to-all-start.2) | async-done | bytes 786464 | tf_op jit(solution)/shard_map/all_to_all | solution.py:627
  87.5 0.1 collective-permute-start.8
  87.6 0.6 collective-permute-start.7
  88.3 4.5 %collective-permute-done.7 = bf16[16,128]{1,0:T(8,128)(2,1)S(1)} collective-permute-done((bf16[16,128]{1,0:T(8,128)(2,1)S(1)}, bf16[16,128]{1,0:T(8,128)(2,1)S(1)}, u32[]{:S(2)}, u32[]{:S(2)}) %collective-permute-start.7) | collective-permute-done | bytes 4128 | tf_op jit(solution)/shard_map/ppermute | solution.py:665
  92.8 0.6 pad_maximum_fusion.2.refs_8_
  93.4 4.7 %shares.3 = bf16[16,528,128]{2,1,0:T(8,128)(2,1)} custom-call(bf16[256,1536]{1,0:T(8,128)(2,1)} %bitcast.21, bf16[256,1024]{1,0:T(8,128)(2,1)} %copy-done.9, bf16[256,1024]{1,0:T(8,128)(2,1)} %copy-done.16, bf16[256,1024]{1,0:T(8,128)(2,1)} %collective-permute-done.1.refs_2_, bf16[256,1024]{1,0:T(8,128)(2,1)} %copy-done.17, ...), custom_call_target="tpu_custom_call", output_to_operand_aliasing={{}: (10, {})} | custom-call | flops 1073741824 | bytes 7000000 | tf_op jit(solution)/shard_map/shares/pallas_call | solution.py:474
  98.1 0.0 copy-start.4
  98.2 5.5 %all-to-all-start.3 = ((bf16[16,528,128]{2,1,0:T(8,128)(2,1)}), bf16[16,528,128]{2,1,0:T(8,128)(2,1)S(1)}, u32[]{:S(2)}, u32[]{:S(2)}) async-start(bf16[16,528,128]{2,1,0:T(8,128)(2,1)} %shares.3), calls=%async_computation.3 | async-start | bytes 4325376 | tf_op jit(solution)/shard_map/all_to_all | solution.py:627
  103.7 3.4 %copy-done.1 = bf16[4096,1024]{1,0:T(8,128)(2,1)S(1)} copy-done((bf16[4096,1024]{1,0:T(8,128)(2,1)S(1)}, bf16[4096,1024]{1,0:T(8,128)(2,1)}, u32[]{:S(2)}) %copy-start.1) | copy-done | bytes 8388632
  107.1 1.1 copy-done.6
  108.2 4.0 %input_terms.1 = (bf16[2,1024,256]{2,1,0:T(8,128)(2,1)S(1)}, f32[2,1024,256]{2,1,0:T(8,128)S(1)}) custom-call(s32[2]{0:T(128)S(1)} %pad_add_fusion.place_ref, bf16[256,1536]{1,0:T(8,128)(2,1)S(1)} %bitcast.18, bf16[256,1536]{1,0:T(8,128)(2,1)S(1)} %bitcast.22, bf16[256,512]{1,0:T(8,128)(2,1)S(1)} %collective-permute-done.6.refs_2_.mate_one_ref, ...), custom_call_target="tpu_custom_call" | custom-call | flops 2147483648 | bytes 12000000 | tf_op jit(solution)/shard_map/input_terms/pallas_call | solution.py:565
  112.2 0.1 collective-permute-start.9
  112.3 2.6 %collective-permute-done.9.core_ref = bf16[2,1024,256]{2,1,0:T(8,128)(2,1)S(1)} collective-permute-done((bf16[2,1024,256]{2,1,0:T(8,128)(2,1)S(1)}, bf16[2,1024,256]{2,1,0:T(8,128)(2,1)S(1)}, u32[]{:S(2)}, u32[]{:S(2)}) %collective-permute-start.9) | collective-permute-done | bytes 1048608 | tf_op jit(solution)/shard_map/ppermute | solution.py:675
  114.9 0.1 fusion
  115.1 0.0 copy-start.11
  115.1 0.0 copy-start.12
  115.1 0.0 copy-start.13
  115.1 0.2 collective-permute-start.10
  115.3 2.5 %gate_grad.1 = bf16[256,1024]{1,0:T(8,128)(2,1)} custom-call(s32[2]{0:T(128)S(1)} %pad_add_fusion.place_ref, bf16[256,1536]{1,0:T(8,128)(2,1)S(1)} %bitcast.19, bf16[256,1536]{1,0:T(8,128)(2,1)S(1)} %bitcast.23, bf16[256,512]{1,0:T(8,128)(2,1)S(1)} %collective-permute-done.6.refs_2_.mate_one_ref, ...), custom_call_target="tpu_custom_call" | custom-call | flops 2000000 | bytes 2500000 | tf_op jit(solution)/shard_map/gate_grad/pallas_call | solution.py:606
  117.9 6.3 %filter_grads.1 = f32[2,4,512,128]{3,2,1,0:T(8,128)} custom-call(bf16[1024,512]{1,0:T(8,128)(2,1)S(1)} %copy-done.14, bf16[1024,512]{1,0:T(8,128)(2,1)S(1)} %copy-done.15, f32[2,64,128]{2,1,0:T(8,128)S(1)} %copy-done.12, bf16[768,512]{1,0:T(8,128)(2,1)S(1)} %copy-done.11, bf16[64,384]{1,0:T(8,128)(2,1)S(1)} %copy-done.13), custom_call_target="tpu_custom_call" | custom-call | flops 3000000000 | bytes 5000000 | tf_op jit(solution)/shard_map/filter_grads/pallas_call | solution.py:308
  124.2 5.0 %collective-permute-done.10.chip_ref = bf16[1024,256]{1,0:T(8,128)(2,1)S(1)} collective-permute-done((bf16[1024,256]{1,0:T(8,128)(2,1)S(1)}, bf16[1024,256]{1,0:T(8,128)(2,1)S(1)}, u32[]{:S(2)}, u32[]{:S(2)}) %collective-permute-start.10) | collective-permute-done | bytes 524320 | tf_op jit(solution)/shard_map/ppermute | solution.py:678
  129.2 1.0 close_input.1
  130.2 1.5 %all-to-all-done.3.refs_0_.refs_1_.refs_2_.refs_3_.refs_4_.refs_5_.refs_6_.refs_7_.refs_8_ = bf16[16,528,128]{2,1,0:T(8,128)(2,1)S(1)} async-done(((bf16[16,528,128]{2,1,0:T(8,128)(2,1)}), bf16[16,528,128]{2,1,0:T(8,128)(2,1)S(1)}, u32[]{:S(2)}, u32[]{:S(2)}) %all-to-all-start.3) | async-done | bytes 2162720 | tf_op jit(solution)/shard_map/all_to_all | solution.py:627
  131.7 1.5 %close_weight.1 = (f32[128,1024]{1,0:T(8,128)}, f32[7,1024]{1,0:T(8,128)}) custom-call(bf16[16,528,128]{2,1,0:T(8,128)(2,1)S(1)} %all-to-all-done.3.refs_0_.refs_1_.refs_2_.refs_3_.refs_4_.refs_5_.refs_6_.refs_7_.refs_8_, bf16[16,528,128]{2,1,0:T(8,128)(2,1)S(1)} %all-to-all-done.3.refs_0_.refs_1_.refs_2_.refs_3_.refs_4_.refs_5_.refs_6_.refs_7_.refs_8_, ...), custom_call_target="tpu_custom_call" | custom-call | flops 2000000 | bytes 3000000 | tf_op jit(solution)/shard_map/close_weight/pallas_call | solution.py:526
  (45 shorter events, 0.2 us)
Async XLA Ops:
  0.6 36.3 %copy-start = (f32[7,1024]{1,0:T(8,128)S(1)}, f32[7,1024]{1,0:T(8,128)}, u32[]{:S(2)}) copy-start(f32[7,1024]{1,0:T(8,128)} %param.17) | copy-start | bytes 86020
  8.0 11.1 %copy-start.2 = (bf16[256,4096]{1,0:T(8,128)(2,1)S(1)}, bf16[256,4096]{1,0:T(8,128)(2,1)}, u32[]{:S(2)}) copy-start(bf16[256,4096]{1,0:T(8,128)(2,1)} %others_ref) | copy-start | bytes 6291460
  8.0 30.0 %all-to-all-start = ((bf16[32,64,256]{2,1,0:T(8,128)(2,1)}), bf16[32,64,256]{2,1,0:T(8,128)(2,1)}, u32[]{:S(2)}, u32[]{:S(2)}) async-start(bf16[32,64,256]{2,1,0:T(8,128)(2,1)} %sends.1), calls=%async_computation | async-start | bytes 2097152 | tf_op jit(solution)/shard_map/all_to_all | solution.py:627
  21.1 0.8 copy-start.10
  21.9 14.5 %copy-start.9 = (bf16[256,1024]{1,0:T(8,128)(2,1)}, bf16[256,1024]{1,0:T(8,128)(2,1)S(1)}, u32[]{:S(2)}) copy-start(bf16[256,1024]{1,0:T(8,128)(2,1)S(1)} %get-tuple-element.55.refs_0_) | copy-start | bytes 1572868
  21.9 40.0 %collective-permute-start = (bf16[256,1024]{1,0:T(8,128)(2,1)}, bf16[256,1024]{1,0:T(8,128)(2,1)S(1)}, u32[]{:S(2)}, u32[]{:S(2)}) collective-permute-start(bf16[256,1024]{1,0:T(8,128)(2,1)} %get-tuple-element.52), channel_id=1, source_target_pairs={{0,6},{1,7},{2,4},{3,5},{4,2},{5,3},{6,0},{7,1},{8,14},{9,15},{10,... | collective-permute-start | bytes 1572872 | tf_op jit(solution)/shard_map/ppermute | solution.py:639
  34.1 27.8 %collective-permute-start.2 = (bf16[256,1024]{1,0:T(8,128)(2,1)}, bf16[256,1024]{1,0:T(8,128)(2,1)S(1)}, u32[]{:S(2)}, u32[]{:S(2)}) collective-permute-start(bf16[256,1024]{1,0:T(8,128)(2,1)} %get-tuple-element.52), channel_id=1, source_target_pairs={{0,30},{1,31},{2,28},{3,29},{4,26},{5,27},{6,24},{7,25},{8,22},{9,... | collective-permute-start | bytes 1572872 | tf_op jit(solution)/shard_map/ppermute | solution.py:639
  36.4 25.5 %collective-permute-start.1 = (bf16[256,1024]{1,0:T(8,128)(2,1)S(1)}, bf16[256,1024]{1,0:T(8,128)(2,1)}, u32[]{:S(2)}, u32[]{:S(2)}) collective-permute-start(bf16[256,1024]{1,0:T(8,128)(2,1)S(1)} %get-tuple-element.55.refs_0_), channel_id=1, source_target_pairs={{0,24},{4,28},{8,16},{12,20},{16,8},{20,12},{24,0},{28,4},{32,56},... | collective-permute-start | bytes 1572872 | tf_op jit(solution)/shard_map/ppermute | solution.py:631
  46.7 19.9 %all-to-all-start.1 = ((bf16[16,16,1536]{2,1,0:T(8,128)(2,1)}), bf16[16,16,1536]{2,1,0:T(8,128)(2,1)S(1)}, u32[]{:S(2)}, u32[]{:S(2)}) async-start(bf16[16,16,1536]{2,1,0:T(8,128)(2,1)} %get-tuple-element.48), calls=%async_computation.1 | async-start | bytes 1572864 | tf_op jit(solution)/shard_map/all_to_all | solution.py:627
  61.8 13.5 %copy-start.16 = (bf16[256,1024]{1,0:T(8,128)(2,1)}, bf16[256,1024]{1,0:T(8,128)(2,1)S(1)}, u32[]{:S(2)}) copy-start(bf16[256,1024]{1,0:T(8,128)(2,1)S(1)} %collective-permute-done.refs_1_) | copy-start | bytes 1572868
  61.9 13.5 %copy-start.17 = (bf16[256,1024]{1,0:T(8,128)(2,1)}, bf16[256,1024]{1,0:T(8,128)(2,1)S(1)}, u32[]{:S(2)}) copy-start(bf16[256,1024]{1,0:T(8,128)(2,1)S(1)} %collective-permute-done.2.refs_3_) | copy-start | bytes 1572868
  66.6 8.8 %copy-start.3 = (bf16[16,16,1536]{2,1,0:T(8,128)(2,1)}, bf16[16,16,1536]{2,1,0:T(8,128)(2,1)S(1)}, u32[]{:S(2)}) copy-start(bf16[16,16,1536]{2,1,0:T(8,128)(2,1)S(1)} %all-to-all-done.1) | copy-start | bytes 2359300
  66.6 20.9 %all-to-all-start.2 = ((bf16[16,16,1536]{2,1,0:T(8,128)(2,1)}), bf16[16,16,1536]{2,1,0:T(8,128)(2,1)S(1)}, u32[]{:S(2)}, u32[]{:S(2)}) async-start(bf16[16,16,1536]{2,1,0:T(8,128)(2,1)} %get-tuple-element.53), calls=%async_computation.2 | async-start | bytes 1572864 | tf_op jit(solution)/shard_map/all_to_all | solution.py:627
  71.6 2.4 %collective-permute-start.3 = (bf16[256,1024]{1,0:T(8,128)(2,1)S(1)}, bf16[256,1024]{1,0:T(8,128)(2,1)}, u32[]{:S(2)}, u32[]{:S(2)}) collective-permute-start(bf16[256,1024]{1,0:T(8,128)(2,1)S(1)} %collective-permute-done.refs_1_), channel_id=1, source_target_pairs={{0,1},{1,0},{2,3},{3,2},{4,5},{5,4},{6,7},{7,6},{8,9},{9,8},{10,11... | collective-permute-start | bytes 1572872 | tf_op jit(solution)/shard_map/ppermute | solution.py:661
  71.6 3.7 %collective-permute-start.4 = (bf16[256,1024]{1,0:T(8,128)(2,1)}, bf16[256,1024]{1,0:T(8,128)(2,1)}, u32[]{:S(2)}, u32[]{:S(2)}) collective-permute-start(bf16[256,1024]{1,0:T(8,128)(2,1)} %collective-permute-done.1.refs_2_), channel_id=1, source_target_pairs={{0,1},{1,0},{2,3},{3,2},{4,5},{5,4},{6,7},{7,6},{8,9},{9,8},{10,11... | collective-permute-start | bytes 1572872 | tf_op jit(solution)/shard_map/ppermute | solution.py:661
  72.1 3.2 %collective-permute-start.5 = (bf16[256,1024]{1,0:T(8,128)(2,1)S(1)}, bf16[256,1024]{1,0:T(8,128)(2,1)}, u32[]{:S(2)}, u32[]{:S(2)}) collective-permute-start(bf16[256,1024]{1,0:T(8,128)(2,1)S(1)} %collective-permute-done.2.refs_3_), channel_id=1, source_target_pairs={{0,1},{1,0},{2,3},{3,2},{4,5},{5,4},{6,7},{7,6},{8,9},{9,8},{10,11... | collective-permute-start | bytes 1572872 | tf_op jit(solution)/shard_map/ppermute | solution.py:661
  72.3 9.9 %collective-permute-start.6 = (bf16[256,512]{1,0:T(8,128)(2,1)S(1)}, bf16[256,512]{1,0:T(8,128)(2,1)S(1)}, u32[]{:S(2)}, u32[]{:S(2)}) collective-permute-start(bf16[256,512]{1,0:T(8,128)(2,1)S(1)} %pad_maximum_fusion), channel_id=1, source_target_pairs={{0,24},{4,28},{8,16},{12,20},{16,8},{20,12},{24,0},{28,4},{32,56},... | collective-permute-start | bytes 786440 | tf_op jit(solution)/shard_map/ppermute | solution.py:631
  75.4 12.2 %copy-start.18 = (bf16[16,128]{1,0:T(8,128)(2,1)S(1)}, bf16[16,128]{1,0:T(8,128)(2,1)}, u32[]{:S(2)}) copy-start(bf16[16,128]{1,0:T(8,128)(2,1)} %get-tuple-element.61) | copy-start | bytes 12292
  75.4 12.2 %copy-start.19 = (bf16[16,128]{1,0:T(8,128)(2,1)S(1)}, bf16[16,128]{1,0:T(8,128)(2,1)}, u32[]{:S(2)}) copy-start(bf16[16,128]{1,0:T(8,128)(2,1)} %get-tuple-element.62) | copy-start | bytes 12292
  87.5 6.0 %copy-start.5 = (bf16[16,16,1536]{2,1,0:T(8,128)(2,1)}, bf16[16,16,1536]{2,1,0:T(8,128)(2,1)S(1)}, u32[]{:S(2)}) copy-start(bf16[16,16,1536]{2,1,0:T(8,128)(2,1)S(1)} %all-to-all-done.2) | copy-start | bytes 2359300
  87.5 10.6 %collective-permute-start.8 = (bf16[256,512]{1,0:T(8,128)(2,1)S(1)}, bf16[256,512]{1,0:T(8,128)(2,1)S(1)}, u32[]{:S(2)}, u32[]{:S(2)}) collective-permute-start(bf16[256,512]{1,0:T(8,128)(2,1)S(1)} %pad_maximum_fusion.1), channel_id=1, source_target_pairs={{0,24},{4,28},{8,16},{12,20},{16,8},{20,12},{24,0},{28,4},{32,56},... | collective-permute-start | bytes 786440 | tf_op jit(solution)/shard_map/ppermute | solution.py:631
  87.6 5.2 %collective-permute-start.7 = (bf16[16,128]{1,0:T(8,128)(2,1)S(1)}, bf16[16,128]{1,0:T(8,128)(2,1)S(1)}, u32[]{:S(2)}, u32[]{:S(2)}) collective-permute-start(bf16[16,128]{1,0:T(8,128)(2,1)S(1)} %add.43), channel_id=1, source_target_pairs={{0,4},{4,0},{8,12},{12,8},{16,20},{20,16},{24,28},{28,24},{32,36},... | collective-permute-start | bytes 12296 | tf_op jit(solution)/shard_map/ppermute | solution.py:665
  98.1 5.5 %copy-start.4 = (bf16[16,16,1536]{2,1,0:T(8,128)(2,1)S(1)}, bf16[16,16,1536]{2,1,0:T(8,128)(2,1)}, u32[]{:S(2)}) copy-start(bf16[16,16,1536]{2,1,0:T(8,128)(2,1)} %copy-done.3) | copy-start | bytes 2359300
  98.2 33.5 %all-to-all-start.3 = ((bf16[16,528,128]{2,1,0:T(8,128)(2,1)}), bf16[16,528,128]{2,1,0:T(8,128)(2,1)S(1)}, u32[]{:S(2)}, u32[]{:S(2)}) async-start(bf16[16,528,128]{2,1,0:T(8,128)(2,1)} %shares.3), calls=%async_computation.3 | async-start | bytes 4325376 | tf_op jit(solution)/shard_map/all_to_all | solution.py:627
  103.7 3.4 %copy-start.1 = (bf16[4096,1024]{1,0:T(8,128)(2,1)S(1)}, bf16[4096,1024]{1,0:T(8,128)(2,1)}, u32[]{:S(2)}) copy-start(bf16[4096,1024]{1,0:T(8,128)(2,1)} %refs_4_.3) | copy-start | bytes 25165828
  107.1 1.1 copy-start.6
  112.2 3.2 %copy-start.7 = (bf16[256,1024]{1,0:T(8,128)(2,1)S(1)}, bf16[256,1024]{1,0:T(8,128)(2,1)}, u32[]{:S(2)}) copy-start(bf16[256,1024]{1,0:T(8,128)(2,1)} %gate_ref.1) | copy-start | bytes 1572868
  112.2 3.2 %copy-start.8 = (bf16[256,1024]{1,0:T(8,128)(2,1)S(1)}, bf16[256,1024]{1,0:T(8,128)(2,1)}, u32[]{:S(2)}) copy-start(bf16[256,1024]{1,0:T(8,128)(2,1)} %grad_ref.1) | copy-start | bytes 1572868
  112.2 2.7 %collective-permute-start.9 = (bf16[2,1024,256]{2,1,0:T(8,128)(2,1)S(1)}, bf16[2,1024,256]{2,1,0:T(8,128)(2,1)S(1)}, u32[]{:S(2)}, u32[]{:S(2)}) collective-permute-start(bf16[2,1024,256]{2,1,0:T(8,128)(2,1)S(1)} %get-tuple-element.68), channel_id=1, source_target_pairs={{0,1},{1,0},{2,3},{3,2},{4,5},{5,4},{6,7},{7,6},{8,9},{9,8},{10,11... | collective-permute-start | bytes 3145736 | tf_op jit(solution)/shard_map/ppermute | solution.py:675
  115.1 2.8 %copy-start.11 = (bf16[768,512]{1,0:T(8,128)(2,1)S(1)}, bf16[768,512]{1,0:T(8,128)(2,1)}, u32[]{:S(2)}) copy-start(bf16[768,512]{1,0:T(8,128)(2,1)} %constant.86.clone.both_ref) | copy-start | bytes 2359300
  115.1 2.8 %copy-start.12 = (f32[2,64,128]{2,1,0:T(8,128)S(1)}, f32[2,64,128]{2,1,0:T(8,128)}, u32[]{:S(2)}) copy-start(f32[2,64,128]{2,1,0:T(8,128)} %constant.80.clone.twist_ref) | copy-start | bytes 196612
  115.1 2.8 %copy-start.13 = (bf16[64,384]{1,0:T(8,128)(2,1)S(1)}, bf16[64,384]{1,0:T(8,128)(2,1)}, u32[]{:S(2)}) copy-start(bf16[64,384]{1,0:T(8,128)(2,1)} %constant.87.clone.last_nat_ref) | copy-start | bytes 147460
  115.1 2.8 %copy-start.14 = (bf16[1024,512]{1,0:T(8,128)(2,1)S(1)}, bf16[1024,512]{1,0:T(8,128)(2,1)}, u32[]{:S(2)}) copy-start(bf16[1024,512]{1,0:T(8,128)(2,1)} %get-tuple-element.76.lag_one_ref) | copy-start | bytes 3145732
  115.1 2.8 %copy-start.15 = (bf16[1024,512]{1,0:T(8,128)(2,1)S(1)}, bf16[1024,512]{1,0:T(8,128)(2,1)}, u32[]{:S(2)}) copy-start(bf16[1024,512]{1,0:T(8,128)(2,1)} %get-tuple-element.77.lag_two_ref) | copy-start | bytes 3145732
  115.1 14.0 %collective-permute-start.10 = (bf16[1024,256]{1,0:T(8,128)(2,1)S(1)}, bf16[1024,256]{1,0:T(8,128)(2,1)S(1)}, u32[]{:S(2)}, u32[]{:S(2)}) collective-permute-start(bf16[1024,256]{1,0:T(8,128)(2,1)S(1)} %fusion), channel_id=1, source_target_pairs={{0,2},{2,0},{1,3},{3,1},{4,6},{6,4},{5,7},{7,5},{8,10},{10,8},{9,1... | collective-permute-start | bytes 1572872 | tf_op jit(solution)/shard_map/ppermute | solution.py:678

commit v9 on v8

--- a/solution.py
+++ b/solution.py
@@ -429,10 +429,13 @@
 def share_kernel(half, back_ref, *refs):
     parts, refs = refs[:8], refs[8:]
     if half:
-        taps_ref, _, out_ref, back_buf, rows_buf, out_buf, in_sem, out_sem = refs
+        taps_ref, partner_ref, _, out_ref, back_buf, rows_buf, out_buf, in_sem, out_sem = refs
     else:
         out_ref, back_buf, rows_buf, out_buf, in_sem, out_sem = refs
     span, rows, sent = rows_buf.shape[1], back_buf.shape[0], out_buf.shape[1]
+    if half:
+        taps = [ref[...].astype(jnp.float32)[:8] for ref in (taps_ref, partner_ref)]
+        taps = jnp.concatenate(taps, axis=0).astype(jnp.bfloat16)
     loads = [pltpu.make_async_copy(back_ref.at[:, pl.ds(0, 4 * span)], back_buf, in_sem.at[8])]
     loads += [pltpu.make_async_copy(part, rows_buf.at[n], in_sem.at[n]) for n, part in enumerate(parts)]
     for load in loads:
@@ -455,7 +458,7 @@
             for m in range(2):
                 out_buf[2 * n + m, :rows] = product[:, m * LANES:(m + 1) * LANES]
                 if half:
-                    out_buf[2 * n + m, rows:] = taps_ref[...]
+                    out_buf[2 * n + m, rows:] = taps
             store = pltpu.make_async_copy(
                 out_buf.at[pl.ds(2 * n, 2)],
                 out_ref.at[pl.ds(first + 2 * two, 2), pl.ds(half * rows, sent)], out_sem.at[n])
@@ -469,14 +472,14 @@
     span, depth = mine[0].shape
     rows = back.shape[0]
     half = 0 if before is None else 1
-    operands = [back, *mine, *other] + ([taps, before] if half else [])
+    operands = [back, *mine, *other] + ([*taps, before] if half else [])
     anywhere = pl.BlockSpec(memory_space=pl.ANY)
     return call(
         functools.partial(share_kernel, half), "shares", 16 * rows * span * depth, 7_000_000, vmem=60,
-        in_specs=[anywhere] * 9 + ([pl.BlockSpec(memory_space=pltpu.VMEM), anywhere] if half else []),
+        in_specs=[anywhere] * 9 + ([pl.BlockSpec(memory_space=pltpu.VMEM)] * 2 + [anywhere] if half else []),
         out_specs=anywhere,
         out_shape=jax.ShapeDtypeStruct((16, 2 * rows + 16, LANES), jnp.bfloat16),
-        input_output_aliases={10: 0} if half else {},
+        input_output_aliases={11: 0} if half else {},
         scratch_shapes=[
             pltpu.VMEM((rows, 4 * span), jnp.bfloat16), pltpu.VMEM((8, span, depth), jnp.bfloat16),
             pltpu.VMEM((16, rows + 16 * half, LANES), jnp.bfloat16),
@@ -663,11 +666,10 @@
     mate_one = for_mate(back_one)
     taps = taps_one + taps_two
     partner = lax.ppermute(taps, "seq", [(s, s ^ 1) for s in range(seq_count)])
-    taps = jnp.concatenate([taps[:8], partner[:8]], axis=0)
     outgoing = shares(back_one, mine, other)
-    back_two, outgoing, mate_one = lax.optimization_barrier((back_two, outgoing, mate_one))
+    back_two, outgoing, mate_one, partner = lax.optimization_barrier((back_two, outgoing, mate_one, partner))
     mate_two = for_mate(back_two)
-    outgoing, mate_two = lax.optimization_barrier((shares(back_two, mine, other, taps, outgoing), mate_two))
+    outgoing, mate_two = lax.optimization_barrier((shares(back_two, mine, other, (taps, partner), outgoing), mate_two))
     parts = exchange(outgoing, PLANES)
     backs, their = [back_one, back_two], [mate_one, mate_two]
 

time: 134 us -> 131 us (0.978)
  waiting for transfers between devices: 28.2 us -> 24.9 us
    ppermute x1, waiting for transfers between devices: 4.55 us -> 0.01 us  [local(): partner = lax.ppermute(taps, 'seq', [(s, s ^ 1) for s in range(seq_count)])]
    ppermute x1, starting transfers between devices: 0.64 us -> 3.05 us  [local(): partner = lax.ppermute(taps, 'seq', [(s, s ^ 1) for s in range(seq_count)])]
    all_to_all x4, starting transfers between devices: 27.9 us -> 26.1 us  [exchange(): lax.all_to_all(value, 'seq', split_axis=0, concat_axis=0, axis_index_grou...]
    ppermute x3, waiting for transfers between devices: 1.35 us -> 0.01 us  [local(): other = [other] + [lax.ppermute(part, 'tp', cores) for part in mine[1:]]]
    unnamed x40 -> x44, local copies, waits for them, and re-layouts: 5.4 us -> 6.15 us
  transfers between devices with their start and end apart: 15 -> 15, of which waited for: 9 -> 8; matrix products, arithmetic and copies ran while one was open for 1% -> 1% of each run, Pallas kernels for 38% -> 39%
where the time goes in v9:
time: 131 us
  Pallas kernels  59.5 us (45%)
  starting transfers between devices  38.1 us (29%)
  waiting for transfers between devices  24.9 us (19%)
  local copies, waits for them, and re-layouts  6.85 us (5%)
    all_to_all x4, starting transfers between devices, exchange(): lax.all_to_all(value, 'seq', split_axis=0, concat_axis=0, axis_index_grou...  26.1 us
    pallas_call x2, Pallas kernels, mixer(): call(functools.partial(mixer_kernel, half * width), 'mixer', 9000000000,...  17.4 us
    all_to_all x4, waiting for transfers between devices, exchange(): lax.all_to_all(value, 'seq', split_axis=0, concat_axis=0, axis_index_grou...  13 us
    pallas_call x1, Pallas kernels, spectra_of(): call(spectra_kernel, 'spectra', 3000000000, 5000000, vmem=56, grid=(width...  8.8 us
    pallas_call x2, Pallas kernels, shares(): call(functools.partial(share_kernel, half), 'shares', 16 * rows * span *...  8.74 us
    pallas_call x1, Pallas kernels, sends(): call(send_kernel, 'sends', 2 * span * depth * channels, 12500000, vmem=56...  7.33 us
    pallas_call x1, Pallas kernels, filter_grads(): call(lag_kernel, 'filter_grads', 3000000000, 5000000, grid=(width // BATC...  6.25 us
    unnamed x44, local copies, waits for them, and re-layouts  6.15 us
  transfers between devices with their start and end apart: 15, of which 8 were waited for; matrix products, arithmetic and copies ran while one was open for 1% of the time, Pallas kernels for 39%

profile of v9, /device:TPU:0, one launch (start us, length us, event | category | flops | bytes accessed | tf_op | source)
XLA Modules:
  0.0 130.6 jit_solution(1035301576226627792)
XLA Ops:
  0.6 0.0 copy-start
  0.6 7.3 %sends.1 = bf16[32,64,256]{2,1,0:T(8,128)(2,1)} custom-call(bf16[256,4096]{1,0:T(8,128)(2,1)} %others_ref, bf16[4096,1024]{1,0:T(8,128)(2,1)} %refs_4_.3, bf16[4096,1024]{1,0:T(8,128)(2,1)} %refs_4_.3, bf16[4096,1024]{1,0:T(8,128)(2,1)} %refs_4_.3, bf16[4096,1024]{1,0:T(8,128)(2,1)} %refs_4_.3, bf16[4096,1024]{1,0:T(8,128)(2,1)} %refs_4_.3, ...), custom_call_target="tpu_custom_call" | custom-call | flops 2147483648 | bytes 12500000 | tf_op jit(solution)/shard_map/sends/pallas_call | solution.py:391
  8.0 11.0 %all-to-all-start = ((bf16[32,64,256]{2,1,0:T(8,128)(2,1)}), bf16[32,64,256]{2,1,0:T(8,128)(2,1)}, u32[]{:S(2)}, u32[]{:S(2)}) async-start(bf16[32,64,256]{2,1,0:T(8,128)(2,1)} %sends.1), calls=%async_computation | async-start | bytes 2097152 | tf_op jit(solution)/shard_map/all_to_all | solution.py:630
  19.0 0.1 pad_add_fusion.place_ref
  19.1 2.0 %quarters.1 = (bf16[256,1024]{1,0:T(8,128)(2,1)S(1)}, bf16[256,1024]{1,0:T(8,128)(2,1)}, bf16[256,1024]{1,0:T(8,128)(2,1)S(1)}) custom-call(s32[2]{0:T(128)S(1)} %pad_add_fusion.place_ref, bf16[256,4096]{1,0:T(8,128)(2,1)S(1)} %copy-done.2, bf16[256,4096]{1,0:T(8,128)(2,1)S(1)} %copy-done.2), custom_call_target="tpu_custom_call" | custom-call | bytes 5000000 | tf_op jit(solution)/shard_map/quarters/pallas_call | solution.py:413
  21.1 0.8 copy-done.10
  21.9 3.4 %collective-permute-start = (bf16[256,1024]{1,0:T(8,128)(2,1)}, bf16[256,1024]{1,0:T(8,128)(2,1)S(1)}, u32[]{:S(2)}, u32[]{:S(2)}) collective-permute-start(bf16[256,1024]{1,0:T(8,128)(2,1)} %get-tuple-element.53), channel_id=1, source_target_pairs={{0,6},{1,7},{2,4},{3,5},{4,2},{5,3},{6,0},{7,1},{8,14},{9,15},{10,... | collective-permute-start | bytes 1572872 | tf_op jit(solution)/shard_map/ppermute | solution.py:642
  25.3 8.8 %spectra.1.spectra_ref = f32[2048,256]{1,0:T(8,128)} custom-call(f32[2,4,512,128]{3,2,1,0:T(8,128)} %bitcast.24, bf16[128,256]{1,0:T(8,128)(2,1)} %constant.79.clone.first_nat_ref, f32[2,64,128]{2,1,0:T(8,128)} %constant.80.clone.twist_ref, bf16[1536,256]{1,0:T(8,128)(2,1)} %constant.81.clone.pair_ref), custom_call_target="tpu_custom_call" | custom-call | flops 3000000000 | bytes 5000000 | tf_op jit(solution)/shard_map/spectra/pallas_call | solution.py:295
  34.1 2.3 %collective-permute-start.2 = (bf16[256,1024]{1,0:T(8,128)(2,1)}, bf16[256,1024]{1,0:T(8,128)(2,1)S(1)}, u32[]{:S(2)}, u32[]{:S(2)}) collective-permute-start(bf16[256,1024]{1,0:T(8,128)(2,1)} %get-tuple-element.53), channel_id=1, source_target_pairs={{0,30},{1,31},{2,28},{3,29},{4,26},{5,27},{6,24},{7,25},{8,22},{9,... | collective-permute-start | bytes 1572872 | tf_op jit(solution)/shard_map/ppermute | solution.py:642
  36.4 0.6 collective-permute-start.1
  36.9 0.7 constant_dynamic-slice_fusion.4.taps_ref
  37.6 0.4 all-to-all-done.arrived_ref
  38.0 8.7 %mixer.2 = (bf16[16,16,1536]{2,1,0:T(8,128)(2,1)}, bf16[1024,512]{1,0:T(8,128)(2,1)}, bf16[16,128]{1,0:T(8,128)(2,1)}) custom-call(f32[7,32]{1,0:T(8,128)} %constant_dynamic-slice_fusion.4.taps_ref, bf16[32,64,256]{2,1,0:T(8,128)(2,1)} %all-to-all-done.arrived_ref, f32[2048,256]{1,0:T(8,128)} %spectra.1.spectra_ref, ...), custom_call_target="tpu_custom_call" | custom-call | flops 8999999488 | bytes 4000000 | tf_op jit(solution)/shard_map/mixer/pallas_call | solution.py:324
  46.7 6.4 %all-to-all-start.1 = ((bf16[16,16,1536]{2,1,0:T(8,128)(2,1)}), bf16[16,16,1536]{2,1,0:T(8,128)(2,1)S(1)}, u32[]{:S(2)}, u32[]{:S(2)}) async-start(bf16[16,16,1536]{2,1,0:T(8,128)(2,1)} %get-tuple-element.49), calls=%async_computation.1 | async-start | bytes 1572864 | tf_op jit(solution)/shard_map/all_to_all | solution.py:630
  53.1 8.7 %mixer.3 = (bf16[16,16,1536]{2,1,0:T(8,128)(2,1)}, bf16[1024,512]{1,0:T(8,128)(2,1)}, bf16[16,128]{1,0:T(8,128)(2,1)}) custom-call(f32[7,32]{1,0:T(8,128)} %constant_dynamic-slice_fusion.4.taps_ref, bf16[32,64,256]{2,1,0:T(8,128)(2,1)} %all-to-all-done.arrived_ref, f32[2048,256]{1,0:T(8,128)} %spectra.1.spectra_ref, ...), custom_call_target="tpu_custom_call" | custom-call | flops 8999999488 | bytes 4000000 | tf_op jit(solution)/shard_map/mixer/pallas_call | solution.py:324
  61.9 0.0 copy-start.17
  61.9 4.7 %all-to-all-done.1 = bf16[16,16,1536]{2,1,0:T(8,128)(2,1)S(1)} async-done(((bf16[16,16,1536]{2,1,0:T(8,128)(2,1)}), bf16[16,16,1536]{2,1,0:T(8,128)(2,1)S(1)}, u32[]{:S(2)}, u32[]{:S(2)}) %all-to-all-start.1) | async-done | bytes 786464 | tf_op jit(solution)/shard_map/all_to_all | solution.py:630
  66.6 5.0 %all-to-all-start.2 = ((bf16[16,16,1536]{2,1,0:T(8,128)(2,1)}), bf16[16,16,1536]{2,1,0:T(8,128)(2,1)S(1)}, u32[]{:S(2)}, u32[]{:S(2)}) async-start(bf16[16,16,1536]{2,1,0:T(8,128)(2,1)} %get-tuple-element.54), calls=%async_computation.2 | async-start | bytes 1572864 | tf_op jit(solution)/shard_map/all_to_all | solution.py:630
  71.6 0.5 collective-permute-start.4
  72.1 0.1 collective-permute-start.5
  72.3 1.8 %collective-permute-start.6 = (bf16[256,512]{1,0:T(8,128)(2,1)S(1)}, bf16[256,512]{1,0:T(8,128)(2,1)S(1)}, u32[]{:S(2)}, u32[]{:S(2)}) collective-permute-start(bf16[256,512]{1,0:T(8,128)(2,1)S(1)} %pad_maximum_fusion), channel_id=1, source_target_pairs={{0,24},{4,28},{8,16},{12,20},{16,8},{20,12},{24,0},{28,4},{32,56},... | collective-permute-start | bytes 786440 | tf_op jit(solution)/shard_map/ppermute | solution.py:634
  74.1 0.0 copy-start.18
  74.1 3.0 %collective-permute-start.7 = (bf16[16,128]{1,0:T(8,128)(2,1)S(1)}, bf16[16,128]{1,0:T(8,128)(2,1)S(1)}, u32[]{:S(2)}, u32[]{:S(2)}) collective-permute-start(bf16[16,128]{1,0:T(8,128)(2,1)S(1)} %add.43.refs_8_), channel_id=1, source_target_pairs={{0,4},{4,0},{8,12},{12,8},{16,20},{20,16},{24,28},{28,24},{32,36},... | collective-permute-start | bytes 12296 | tf_op jit(solution)/shard_map/ppermute | solution.py:668
  77.2 4.0 %shares.2.refs_10_ = bf16[16,528,128]{2,1,0:T(8,128)(2,1)} custom-call(bf16[256,1536]{1,0:T(8,128)(2,1)} %bitcast.17, bf16[256,1024]{1,0:T(8,128)(2,1)} %copy-done.9, bf16[256,1024]{1,0:T(8,128)(2,1)} %copy-done.16, bf16[256,1024]{1,0:T(8,128)(2,1)} %collective-permute-done.1.refs_2_, bf16[256,1024]{1,0:T(8,128)(2,1)} %copy-done.17, ...), custom_call_target="tpu_custom_call" | custom-call | flops 1073741824 | bytes 7000000 | tf_op jit(solution)/shard_map/shares/pallas_call | solution.py:477
  81.2 1.0 collective-permute-done.6.refs_2_.mate_one_ref
  82.2 5.3 %all-to-all-done.2 = bf16[16,16,1536]{2,1,0:T(8,128)(2,1)S(1)} async-done(((bf16[16,16,1536]{2,1,0:T(8,128)(2,1)}), bf16[16,16,1536]{2,1,0:T(8,128)(2,1)S(1)}, u32[]{:S(2)}, u32[]{:S(2)}) %all-to-all-start.2) | async-done | bytes 786464 | tf_op jit(solution)/shard_map/all_to_all | solution.py:630
  87.5 0.1 collective-permute-start.8
  87.6 0.7 copy-done.5
  88.4 4.7 %shares.3 = bf16[16,528,128]{2,1,0:T(8,128)(2,1)} custom-call(bf16[256,1536]{1,0:T(8,128)(2,1)} %bitcast.21, bf16[256,1024]{1,0:T(8,128)(2,1)} %copy-done.9, bf16[256,1024]{1,0:T(8,128)(2,1)} %copy-done.16, bf16[256,1024]{1,0:T(8,128)(2,1)} %collective-permute-done.1.refs_2_, bf16[256,1024]{1,0:T(8,128)(2,1)} %copy-done.17, ...), custom_call_target="tpu_custom_call", output_to_operand_aliasing={{}: (11, {})} | custom-call | flops 1073741824 | bytes 7000000 | tf_op jit(solution)/shard_map/shares/pallas_call | solution.py:477
  93.1 0.0 copy-start.4
  93.1 3.1 %collective-permute-done.8.refs_3_.mate_two_ref = bf16[256,512]{1,0:T(8,128)(2,1)S(1)} collective-permute-done((bf16[256,512]{1,0:T(8,128)(2,1)S(1)}, bf16[256,512]{1,0:T(8,128)(2,1)S(1)}, u32[]{:S(2)}, u32[]{:S(2)}) %collective-permute-start.8) | collective-permute-done | bytes 262176 | tf_op jit(solution)/shard_map/ppermute | solution.py:634
  96.2 3.7 %all-to-all-start.3 = ((bf16[16,528,128]{2,1,0:T(8,128)(2,1)}), bf16[16,528,128]{2,1,0:T(8,128)(2,1)S(1)}, u32[]{:S(2)}, u32[]{:S(2)}) async-start(bf16[16,528,128]{2,1,0:T(8,128)(2,1)} %shares.3), calls=%async_computation.3 | async-start | bytes 4325376 | tf_op jit(solution)/shard_map/all_to_all | solution.py:630
  100.0 3.4 %copy-done.1 = bf16[4096,1024]{1,0:T(8,128)(2,1)S(1)} copy-done((bf16[4096,1024]{1,0:T(8,128)(2,1)S(1)}, bf16[4096,1024]{1,0:T(8,128)(2,1)}, u32[]{:S(2)}) %copy-start.1) | copy-done | bytes 8388632
  103.4 1.1 copy-done.6
  104.5 4.0 %input_terms.1 = (bf16[2,1024,256]{2,1,0:T(8,128)(2,1)S(1)}, f32[2,1024,256]{2,1,0:T(8,128)S(1)}) custom-call(s32[2]{0:T(128)S(1)} %pad_add_fusion.place_ref, bf16[256,1536]{1,0:T(8,128)(2,1)S(1)} %bitcast.18, bf16[256,1536]{1,0:T(8,128)(2,1)S(1)} %bitcast.22, bf16[256,512]{1,0:T(8,128)(2,1)S(1)} %collective-permute-done.6.refs_2_.mate_one_ref, ...), custom_call_target="tpu_custom_call" | custom-call | flops 2147483648 | bytes 12000000 | tf_op jit(solution)/shard_map/input_terms/pallas_call | solution.py:568
  108.5 0.1 collective-permute-start.9
  108.6 2.6 %collective-permute-done.9.core_ref = bf16[2,1024,256]{2,1,0:T(8,128)(2,1)S(1)} collective-permute-done((bf16[2,1024,256]{2,1,0:T(8,128)(2,1)S(1)}, bf16[2,1024,256]{2,1,0:T(8,128)(2,1)S(1)}, u32[]{:S(2)}, u32[]{:S(2)}) %collective-permute-start.9) | collective-permute-done | bytes 1048608 | tf_op jit(solution)/shard_map/ppermute | solution.py:677
  111.2 0.1 fusion
  111.4 0.0 copy-start.11
  111.4 0.0 copy-start.12
  111.4 0.0 copy-start.13
  111.4 0.1 collective-permute-start.10
  111.5 2.6 %gate_grad.1 = bf16[256,1024]{1,0:T(8,128)(2,1)} custom-call(s32[2]{0:T(128)S(1)} %pad_add_fusion.place_ref, bf16[256,1536]{1,0:T(8,128)(2,1)S(1)} %bitcast.19, bf16[256,1536]{1,0:T(8,128)(2,1)S(1)} %bitcast.23, bf16[256,512]{1,0:T(8,128)(2,1)S(1)} %collective-permute-done.6.refs_2_.mate_one_ref, ...), custom_call_target="tpu_custom_call" | custom-call | flops 2000000 | bytes 2500000 | tf_op jit(solution)/shard_map/gate_grad/pallas_call | solution.py:609
  114.1 6.3 %filter_grads.1 = f32[2,4,512,128]{3,2,1,0:T(8,128)} custom-call(bf16[1024,512]{1,0:T(8,128)(2,1)S(1)} %copy-done.14, bf16[1024,512]{1,0:T(8,128)(2,1)S(1)} %copy-done.15, f32[2,64,128]{2,1,0:T(8,128)S(1)} %copy-done.12, bf16[768,512]{1,0:T(8,128)(2,1)S(1)} %copy-done.11, bf16[64,384]{1,0:T(8,128)(2,1)S(1)} %copy-done.13), custom_call_target="tpu_custom_call" | custom-call | flops 3000000000 | bytes 5000000 | tf_op jit(solution)/shard_map/filter_grads/pallas_call | solution.py:308
  120.4 5.1 %collective-permute-done.10.chip_ref = bf16[1024,256]{1,0:T(8,128)(2,1)S(1)} collective-permute-done((bf16[1024,256]{1,0:T(8,128)(2,1)S(1)}, bf16[1024,256]{1,0:T(8,128)(2,1)S(1)}, u32[]{:S(2)}, u32[]{:S(2)}) %collective-permute-start.10) | collective-permute-done | bytes 524320 | tf_op jit(solution)/shard_map/ppermute | solution.py:680
  125.5 1.0 close_input.1
  126.5 2.7 %all-to-all-done.3.refs_0_.refs_1_.refs_2_.refs_3_.refs_4_.refs_5_.refs_6_.refs_7_.refs_8_ = bf16[16,528,128]{2,1,0:T(8,128)(2,1)S(1)} async-done(((bf16[16,528,128]{2,1,0:T(8,128)(2,1)}), bf16[16,528,128]{2,1,0:T(8,128)(2,1)S(1)}, u32[]{:S(2)}, u32[]{:S(2)}) %all-to-all-start.3) | async-done | bytes 2162720 | tf_op jit(solution)/shard_map/all_to_all | solution.py:630
  129.1 1.5 %close_weight.1 = (f32[128,1024]{1,0:T(8,128)}, f32[7,1024]{1,0:T(8,128)}) custom-call(bf16[16,528,128]{2,1,0:T(8,128)(2,1)S(1)} %all-to-all-done.3.refs_0_.refs_1_.refs_2_.refs_3_.refs_4_.refs_5_.refs_6_.refs_7_.refs_8_, bf16[16,528,128]{2,1,0:T(8,128)(2,1)S(1)} %all-to-all-done.3.refs_0_.refs_1_.refs_2_.refs_3_.refs_4_.refs_5_.refs_6_.refs_7_.refs_8_, ...), custom_call_target="tpu_custom_call" | custom-call | flops 2000000 | bytes 3000000 | tf_op jit(solution)/shard_map/close_weight/pallas_call | solution.py:529
  (46 shorter events, 0.2 us)
Async XLA Ops:
  0.6 36.3 %copy-start = (f32[7,1024]{1,0:T(8,128)S(1)}, f32[7,1024]{1,0:T(8,128)}, u32[]{:S(2)}) copy-start(f32[7,1024]{1,0:T(8,128)} %param.17) | copy-start | bytes 86020
  8.0 11.1 %copy-start.2 = (bf16[256,4096]{1,0:T(8,128)(2,1)S(1)}, bf16[256,4096]{1,0:T(8,128)(2,1)}, u32[]{:S(2)}) copy-start(bf16[256,4096]{1,0:T(8,128)(2,1)} %others_ref) | copy-start | bytes 6291460
  8.0 30.0 %all-to-all-start = ((bf16[32,64,256]{2,1,0:T(8,128)(2,1)}), bf16[32,64,256]{2,1,0:T(8,128)(2,1)}, u32[]{:S(2)}, u32[]{:S(2)}) async-start(bf16[32,64,256]{2,1,0:T(8,128)(2,1)} %sends.1), calls=%async_computation | async-start | bytes 2097152 | tf_op jit(solution)/shard_map/all_to_all | solution.py:630
  21.1 0.8 copy-start.10
  21.9 14.5 %copy-start.9 = (bf16[256,1024]{1,0:T(8,128)(2,1)}, bf16[256,1024]{1,0:T(8,128)(2,1)S(1)}, u32[]{:S(2)}) copy-start(bf16[256,1024]{1,0:T(8,128)(2,1)S(1)} %get-tuple-element.56.refs_0_) | copy-start | bytes 1572868
  21.9 40.0 %collective-permute-start = (bf16[256,1024]{1,0:T(8,128)(2,1)}, bf16[256,1024]{1,0:T(8,128)(2,1)S(1)}, u32[]{:S(2)}, u32[]{:S(2)}) collective-permute-start(bf16[256,1024]{1,0:T(8,128)(2,1)} %get-tuple-element.53), channel_id=1, source_target_pairs={{0,6},{1,7},{2,4},{3,5},{4,2},{5,3},{6,0},{7,1},{8,14},{9,15},{10,... | collective-permute-start | bytes 1572872 | tf_op jit(solution)/shard_map/ppermute | solution.py:642
  34.1 27.9 %collective-permute-start.2 = (bf16[256,1024]{1,0:T(8,128)(2,1)}, bf16[256,1024]{1,0:T(8,128)(2,1)S(1)}, u32[]{:S(2)}, u32[]{:S(2)}) collective-permute-start(bf16[256,1024]{1,0:T(8,128)(2,1)} %get-tuple-element.53), channel_id=1, source_target_pairs={{0,30},{1,31},{2,28},{3,29},{4,26},{5,27},{6,24},{7,25},{8,22},{9,... | collective-permute-start | bytes 1572872 | tf_op jit(solution)/shard_map/ppermute | solution.py:642
  36.4 25.6 %collective-permute-start.1 = (bf16[256,1024]{1,0:T(8,128)(2,1)S(1)}, bf16[256,1024]{1,0:T(8,128)(2,1)}, u32[]{:S(2)}, u32[]{:S(2)}) collective-permute-start(bf16[256,1024]{1,0:T(8,128)(2,1)S(1)} %get-tuple-element.56.refs_0_), channel_id=1, source_target_pairs={{0,24},{4,28},{8,16},{12,20},{16,8},{20,12},{24,0},{28,4},{32,56},... | collective-permute-start | bytes 1572872 | tf_op jit(solution)/shard_map/ppermute | solution.py:634
  46.7 19.9 %all-to-all-start.1 = ((bf16[16,16,1536]{2,1,0:T(8,128)(2,1)}), bf16[16,16,1536]{2,1,0:T(8,128)(2,1)S(1)}, u32[]{:S(2)}, u32[]{:S(2)}) async-start(bf16[16,16,1536]{2,1,0:T(8,128)(2,1)} %get-tuple-element.49), calls=%async_computation.1 | async-start | bytes 1572864 | tf_op jit(solution)/shard_map/all_to_all | solution.py:630
  61.9 12.2 %copy-start.20 = (bf16[16,128]{1,0:T(8,128)(2,1)S(1)}, bf16[16,128]{1,0:T(8,128)(2,1)}, u32[]{:S(2)}) copy-start(bf16[16,128]{1,0:T(8,128)(2,1)} %get-tuple-element.61) | copy-start | bytes 12292
  61.9 12.2 %copy-start.21 = (bf16[16,128]{1,0:T(8,128)(2,1)S(1)}, bf16[16,128]{1,0:T(8,128)(2,1)}, u32[]{:S(2)}) copy-start(bf16[16,128]{1,0:T(8,128)(2,1)} %get-tuple-element.62) | copy-start | bytes 12292
  61.9 15.2 %copy-start.16 = (bf16[256,1024]{1,0:T(8,128)(2,1)}, bf16[256,1024]{1,0:T(8,128)(2,1)S(1)}, u32[]{:S(2)}) copy-start(bf16[256,1024]{1,0:T(8,128)(2,1)S(1)} %collective-permute-done.refs_1_) | copy-start | bytes 1572868
  61.9 15.2 %copy-start.17 = (bf16[256,1024]{1,0:T(8,128)(2,1)}, bf16[256,1024]{1,0:T(8,128)(2,1)S(1)}, u32[]{:S(2)}) copy-start(bf16[256,1024]{1,0:T(8,128)(2,1)S(1)} %collective-permute-done.2.refs_3_) | copy-start | bytes 1572868
  66.6 10.5 %copy-start.3 = (bf16[16,16,1536]{2,1,0:T(8,128)(2,1)}, bf16[16,16,1536]{2,1,0:T(8,128)(2,1)S(1)}, u32[]{:S(2)}) copy-start(bf16[16,16,1536]{2,1,0:T(8,128)(2,1)S(1)} %all-to-all-done.1) | copy-start | bytes 2359300
  66.6 20.8 %all-to-all-start.2 = ((bf16[16,16,1536]{2,1,0:T(8,128)(2,1)}), bf16[16,16,1536]{2,1,0:T(8,128)(2,1)S(1)}, u32[]{:S(2)}, u32[]{:S(2)}) async-start(bf16[16,16,1536]{2,1,0:T(8,128)(2,1)} %get-tuple-element.54), calls=%async_computation.2 | async-start | bytes 1572864 | tf_op jit(solution)/shard_map/all_to_all | solution.py:630
  71.6 5.5 %collective-permute-start.3 = (bf16[256,1024]{1,0:T(8,128)(2,1)S(1)}, bf16[256,1024]{1,0:T(8,128)(2,1)}, u32[]{:S(2)}, u32[]{:S(2)}) collective-permute-start(bf16[256,1024]{1,0:T(8,128)(2,1)S(1)} %collective-permute-done.refs_1_), channel_id=1, source_target_pairs={{0,1},{1,0},{2,3},{3,2},{4,5},{5,4},{6,7},{7,6},{8,9},{9,8},{10,11... | collective-permute-start | bytes 1572872 | tf_op jit(solution)/shard_map/ppermute | solution.py:664
  71.6 5.5 %collective-permute-start.4 = (bf16[256,1024]{1,0:T(8,128)(2,1)}, bf16[256,1024]{1,0:T(8,128)(2,1)}, u32[]{:S(2)}, u32[]{:S(2)}) collective-permute-start(bf16[256,1024]{1,0:T(8,128)(2,1)} %collective-permute-done.1.refs_2_), channel_id=1, source_target_pairs={{0,1},{1,0},{2,3},{3,2},{4,5},{5,4},{6,7},{7,6},{8,9},{9,8},{10,11... | collective-permute-start | bytes 1572872 | tf_op jit(solution)/shard_map/ppermute | solution.py:664
  72.1 5.0 %collective-permute-start.5 = (bf16[256,1024]{1,0:T(8,128)(2,1)S(1)}, bf16[256,1024]{1,0:T(8,128)(2,1)}, u32[]{:S(2)}, u32[]{:S(2)}) collective-permute-start(bf16[256,1024]{1,0:T(8,128)(2,1)S(1)} %collective-permute-done.2.refs_3_), channel_id=1, source_target_pairs={{0,1},{1,0},{2,3},{3,2},{4,5},{5,4},{6,7},{7,6},{8,9},{9,8},{10,11... | collective-permute-start | bytes 1572872 | tf_op jit(solution)/shard_map/ppermute | solution.py:664
  72.3 9.9 %collective-permute-start.6 = (bf16[256,512]{1,0:T(8,128)(2,1)S(1)}, bf16[256,512]{1,0:T(8,128)(2,1)S(1)}, u32[]{:S(2)}, u32[]{:S(2)}) collective-permute-start(bf16[256,512]{1,0:T(8,128)(2,1)S(1)} %pad_maximum_fusion), channel_id=1, source_target_pairs={{0,24},{4,28},{8,16},{12,20},{16,8},{20,12},{24,0},{28,4},{32,56},... | collective-permute-start | bytes 786440 | tf_op jit(solution)/shard_map/ppermute | solution.py:634
  74.1 7.1 %copy-start.18 = (bf16[16,128]{1,0:T(8,128)(2,1)}, bf16[16,128]{1,0:T(8,128)(2,1)S(1)}, u32[]{:S(2)}) copy-start(bf16[16,128]{1,0:T(8,128)(2,1)S(1)} %add.43.refs_8_) | copy-start | bytes 12292
  74.1 7.1 %collective-permute-start.7 = (bf16[16,128]{1,0:T(8,128)(2,1)S(1)}, bf16[16,128]{1,0:T(8,128)(2,1)S(1)}, u32[]{:S(2)}, u32[]{:S(2)}) collective-permute-start(bf16[16,128]{1,0:T(8,128)(2,1)S(1)} %add.43.refs_8_), channel_id=1, source_target_pairs={{0,4},{4,0},{8,12},{12,8},{16,20},{20,16},{24,28},{28,24},{32,36},... | collective-permute-start | bytes 12296 | tf_op jit(solution)/shard_map/ppermute | solution.py:668
  81.2 6.4 %copy-start.19 = (bf16[16,128]{1,0:T(8,128)(2,1)}, bf16[16,128]{1,0:T(8,128)(2,1)S(1)}, u32[]{:S(2)}) copy-start(bf16[16,128]{1,0:T(8,128)(2,1)S(1)} %collective-permute-done.7.refs_9_) | copy-start | bytes 12292
  87.5 0.9 copy-start.5
  87.5 8.7 %collective-permute-start.8 = (bf16[256,512]{1,0:T(8,128)(2,1)S(1)}, bf16[256,512]{1,0:T(8,128)(2,1)S(1)}, u32[]{:S(2)}, u32[]{:S(2)}) collective-permute-start(bf16[256,512]{1,0:T(8,128)(2,1)S(1)} %pad_maximum_fusion.1), channel_id=1, source_target_pairs={{0,24},{4,28},{8,16},{12,20},{16,8},{20,12},{24,0},{28,4},{32,56},... | collective-permute-start | bytes 786440 | tf_op jit(solution)/shard_map/ppermute | solution.py:634
  93.1 6.9 %copy-start.4 = (bf16[16,16,1536]{2,1,0:T(8,128)(2,1)S(1)}, bf16[16,16,1536]{2,1,0:T(8,128)(2,1)}, u32[]{:S(2)}) copy-start(bf16[16,16,1536]{2,1,0:T(8,128)(2,1)} %copy-done.3) | copy-start | bytes 2359300
  96.2 32.9 %all-to-all-start.3 = ((bf16[16,528,128]{2,1,0:T(8,128)(2,1)}), bf16[16,528,128]{2,1,0:T(8,128)(2,1)S(1)}, u32[]{:S(2)}, u32[]{:S(2)}) async-start(bf16[16,528,128]{2,1,0:T(8,128)(2,1)} %shares.3), calls=%async_computation.3 | async-start | bytes 4325376 | tf_op jit(solution)/shard_map/all_to_all | solution.py:630
  100.0 3.4 %copy-start.1 = (bf16[4096,1024]{1,0:T(8,128)(2,1)S(1)}, bf16[4096,1024]{1,0:T(8,128)(2,1)}, u32[]{:S(2)}) copy-start(bf16[4096,1024]{1,0:T(8,128)(2,1)} %refs_4_.3) | copy-start | bytes 25165828
  103.4 1.1 copy-start.6
  108.5 3.1 %copy-start.7 = (bf16[256,1024]{1,0:T(8,128)(2,1)S(1)}, bf16[256,1024]{1,0:T(8,128)(2,1)}, u32[]{:S(2)}) copy-start(bf16[256,1024]{1,0:T(8,128)(2,1)} %gate_ref.1) | copy-start | bytes 1572868
  108.5 3.0 %copy-start.8 = (bf16[256,1024]{1,0:T(8,128)(2,1)S(1)}, bf16[256,1024]{1,0:T(8,128)(2,1)}, u32[]{:S(2)}) copy-start(bf16[256,1024]{1,0:T(8,128)(2,1)} %grad_ref.1) | copy-start | bytes 1572868
  108.5 2.7 %collective-permute-start.9 = (bf16[2,1024,256]{2,1,0:T(8,128)(2,1)S(1)}, bf16[2,1024,256]{2,1,0:T(8,128)(2,1)S(1)}, u32[]{:S(2)}, u32[]{:S(2)}) collective-permute-start(bf16[2,1024,256]{2,1,0:T(8,128)(2,1)S(1)} %get-tuple-element.70), channel_id=1, source_target_pairs={{0,1},{1,0},{2,3},{3,2},{4,5},{5,4},{6,7},{7,6},{8,9},{9,8},{10,11... | collective-permute-start | bytes 3145736 | tf_op jit(solution)/shard_map/ppermute | solution.py:677
  111.4 2.7 %copy-start.11 = (bf16[768,512]{1,0:T(8,128)(2,1)S(1)}, bf16[768,512]{1,0:T(8,128)(2,1)}, u32[]{:S(2)}) copy-start(bf16[768,512]{1,0:T(8,128)(2,1)} %constant.86.clone.both_ref) | copy-start | bytes 2359300
  111.4 2.7 %copy-start.12 = (f32[2,64,128]{2,1,0:T(8,128)S(1)}, f32[2,64,128]{2,1,0:T(8,128)}, u32[]{:S(2)}) copy-start(f32[2,64,128]{2,1,0:T(8,128)} %constant.80.clone.twist_ref) | copy-start | bytes 196612
  111.4 2.7 %copy-start.13 = (bf16[64,384]{1,0:T(8,128)(2,1)S(1)}, bf16[64,384]{1,0:T(8,128)(2,1)}, u32[]{:S(2)}) copy-start(bf16[64,384]{1,0:T(8,128)(2,1)} %constant.87.clone.last_nat_ref) | copy-start | bytes 147460
  111.4 2.7 %copy-start.14 = (bf16[1024,512]{1,0:T(8,128)(2,1)S(1)}, bf16[1024,512]{1,0:T(8,128)(2,1)}, u32[]{:S(2)}) copy-start(bf16[1024,512]{1,0:T(8,128)(2,1)} %get-tuple-element.78.lag_one_ref) | copy-start | bytes 3145732
  111.4 2.7 %copy-start.15 = (bf16[1024,512]{1,0:T(8,128)(2,1)S(1)}, bf16[1024,512]{1,0:T(8,128)(2,1)}, u32[]{:S(2)}) copy-start(bf16[1024,512]{1,0:T(8,128)(2,1)} %get-tuple-element.79.lag_two_ref) | copy-start | bytes 3145732
  111.4 14.0 %collective-permute-start.10 = (bf16[1024,256]{1,0:T(8,128)(2,1)S(1)}, bf16[1024,256]{1,0:T(8,128)(2,1)S(1)}, u32[]{:S(2)}, u32[]{:S(2)}) collective-permute-start(bf16[1024,256]{1,0:T(8,128)(2,1)S(1)} %fusion), channel_id=1, source_target_pairs={{0,2},{2,0},{1,3},{3,1},{4,6},{6,4},{5,7},{7,5},{8,10},{10,8},{9,1... | collective-permute-start | bytes 1572872 | tf_op jit(solution)/shard_map/ppermute | solution.py:680
